TPU v7x, 32 devices: a whole 2x2x4 slice. The times are simulated.
32 devices in a mesh: blk: 8 (over y, x, core), uly: 4 (over z).
Axes of the slice: x: 2, y: 2, z: 4, core: 2. Of those that a mesh axis runs over, the one named last changes fastest.
Arguments:
- inputs: bfloat16 [2, 2048, 768], P(None, ('blk', 'uly')), may hold values from -6 to 6
- doc_starts: int32 [2, 2048], P(None, ('blk', 'uly')), may hold values from 0 to 2046, as said below
- out_grad: bfloat16 [2, 2048, 768], P(None, ('blk', 'uly')), may hold values from -6 to 6
- first_gain: bfloat16 [768], P('blk'), may hold values from 0.099609375 to 1.8984375
- first_bias: bfloat16 [768], P('blk'), may hold values from -3 to 3
- query_key_value_weight: bfloat16 [768, 2304], P('blk', 'uly'), may hold values from -0.21875 to 0.21875
- attention_out_weight: bfloat16 [768, 768], P('blk', 'uly'), may hold values from -6 to 6
- second_gain: bfloat16 [768], P('blk'), may hold values from 0.099609375 to 1.8984375
- second_bias: bfloat16 [768], P('blk'), may hold values from -3 to 3
- up_weight: bfloat16 [768, 3072], P('blk', 'uly'), may hold values from -0.21875 to 0.21875
- down_weight: bfloat16 [3072, 768], P('blk', 'uly'), may hold values from -0.75 to 0.75
Outputs:
- output: bfloat16 [2, 2048, 768], P(None, ('blk', 'uly'))
- grad_inputs: float32 [2, 2048, 768], P(None, ('blk', 'uly'))
- grad_first_gain: float32 [768], P('blk')
- grad_first_bias: float32 [768], P('blk')
- grad_w_qkv: float32 [768, 2304], P('blk', 'uly')
- grad_w_attn_out: float32 [768, 768], P('blk', 'uly')
- grad_second_gain: float32 [768], P('blk')
- grad_second_bias: float32 [768], P('blk')
- grad_w_up: float32 [768, 3072], P('blk', 'uly')
- grad_w_down: float32 [3072, 768], P('blk', 'uly')
Inputs may be any that keep to these rules, and one draw needn't show every extreme that they name: `doc_starts`: each entry is the position, within its sequence, of the first token of that token's document: it never exceeds the token's own position, and entries never fall along a sequence.
All inputs are finite; a program needn't handle non-finite values.
Results may differ from a plain program's by a relative error of at most 0.039.
Values may be sent and summed in bfloat16 or wider, within the bound.
No kernel may reach another device: no remote copies, remote signals or barrier semaphores. Data moves between devices by JAX's collectives and lax.ppermute only.
A program may use at most 192 MiB of HBM per device.

v0:
```python
import math

import jax
import jax.numpy as jnp
from jax import lax
from jax.sharding import PartitionSpec as P

HEAD_DIM = 64


branch_scale = 48.0 ** (-0.5)
norm_epsilon = 1e-05
neg_large = -1e30


def layer_norm(values, gain_vec, shift_vec):
    center = values - jnp.mean(values, axis=-1, keepdims=True)
    spread = jnp.mean(center * center, axis=-1, keepdims=True)
    return center * lax.rsqrt(spread + norm_epsilon) * gain_vec + shift_vec


def smooth_gate(values):
    return jax.nn.gelu(values, approximate=True)


def project(left, right):
    return jnp.einsum("stk,kn->stn", left, right, preferred_element_type=jnp.float32)


def project_back(left, right):
    return jnp.einsum("stn,kn->stk", left, right, preferred_element_type=jnp.float32)


def weight_grad(left, right):
    return jnp.einsum("stk,stn->kn", left, right, preferred_element_type=jnp.float32)


def visible(query_pos, query_first, key_pos):
    return (key_pos[None, :] <= query_pos[:, None]) & (key_pos[None, :] >= query_first[:, None])


def live_pair(query_pos, query_first, key_pos):
    return (key_pos[0] <= query_pos[-1]) & (key_pos[-1] >= query_first[0])


def forward_pair(carried, queries, key_rows, value_rows, query_pos, query_first, key_pos):
    run_max, run_sum, run_acc = carried
    score_scale = queries.shape[-1] ** (-0.5)
    scores = (
        jnp.einsum("qhd,khd->hqk", queries, key_rows, preferred_element_type=jnp.float32)
        * score_scale
    )
    allowed = visible(query_pos, query_first, key_pos)[None]
    scores = jnp.where(allowed, scores, neg_large)
    new_max = jnp.maximum(run_max, jnp.max(scores, axis=-1))
    weights = jnp.where(allowed, jnp.exp(scores - new_max[..., None]), 0.0)
    factor = jnp.exp(run_max - new_max)
    new_sum = factor * run_sum + jnp.sum(weights, axis=-1)
    attention_mixed = jnp.einsum(
        "hqk,khd->hqd", weights.astype(jnp.bfloat16), value_rows, preferred_element_type=jnp.float32
    )
    return (new_max, new_sum, factor[..., None] * run_acc + attention_mixed)


def backward_pair(
    queries,
    grad_rows,
    log_sum,
    delta_rows,
    key_rows,
    value_rows,
    query_pos,
    query_first,
    key_pos,
    want_query,
    want_keys,
):
    score_scale = queries.shape[-1] ** (-0.5)
    scores = (
        jnp.einsum("qhd,khd->hqk", queries, key_rows, preferred_element_type=jnp.float32)
        * score_scale
    )
    allowed = visible(query_pos, query_first, key_pos)[None]
    probs = jnp.where(
        allowed, jnp.exp(jnp.where(allowed, scores, neg_large) - log_sum[..., None]), 0.0
    )
    grad_probs = jnp.einsum(
        "qhd,khd->hqk", grad_rows, value_rows, preferred_element_type=jnp.float32
    )
    grad_scores = (probs * (grad_probs - delta_rows[..., None])).astype(jnp.bfloat16)
    results = ()
    if want_query:
        results = results + (
            jnp.einsum("hqk,khd->qhd", grad_scores, key_rows, preferred_element_type=jnp.float32)
            * score_scale,
        )
    if want_keys:
        grad_key_rows = (
            jnp.einsum("hqk,qhd->khd", grad_scores, queries, preferred_element_type=jnp.float32)
            * score_scale
        )
        grad_value_rows = jnp.einsum(
            "hqk,qhd->khd",
            probs.astype(jnp.bfloat16),
            grad_rows,
            preferred_element_type=jnp.float32,
        )
        results = results + (grad_key_rows, grad_value_rows)
    return results


def each_block(update, carried, arrays, row_limit):
    total_rows = arrays[0].shape[1]
    span_rows = math.gcd(total_rows, row_limit)
    block_count = total_rows // span_rows
    split_arrays = tuple(
        (
            jnp.swapaxes(
                member.reshape((member.shape[0], block_count, span_rows) + member.shape[2:]), 0, 1
            )
            for member in arrays
        )
    )

    def advance(running, inputs):
        number, blocks = inputs
        return (update(running, blocks, number * span_rows), None)

    result, unused = lax.scan(
        advance, carried, (jnp.arange(block_count, dtype=jnp.int32), split_arrays)
    )
    return result


def local(
    inputs,
    doc_starts,
    out_grad,
    first_gain,
    first_bias,
    query_key_value_weight,
    attention_out_weight,
    second_gain,
    second_bias,
    up_weight,
    down_weight,
):
    groups = lax.axis_size("uly")
    cycle_place = lax.axis_index("blk")
    seq_count, tok_dev, model_width = inputs.shape
    block_rows = tok_dev * groups
    group_width = model_width // groups
    heads_here = group_width // HEAD_DIM
    qkv_cols, attn_cols, up_cols, down_cols = (
        lax.all_gather(query_key_value_weight, "uly", axis=1, tiled=True),
        lax.all_gather(attention_out_weight, "uly", axis=1, tiled=True),
        lax.all_gather(up_weight, "uly", axis=1, tiled=True),
        lax.all_gather(down_weight, "uly", axis=1, tiled=True),
    )
    gathered = (
        lax.all_gather(qkv_cols, "blk", axis=0, tiled=True),
        lax.all_gather(attn_cols, "blk", axis=0, tiled=True),
        lax.all_gather(up_cols, "blk", axis=0, tiled=True),
        lax.all_gather(down_cols, "blk", axis=0, tiled=True),
        lax.all_gather(first_gain, "blk", axis=0, tiled=True),
        lax.all_gather(first_bias, "blk", axis=0, tiled=True),
        lax.all_gather(second_gain, "blk", axis=0, tiled=True),
        lax.all_gather(second_bias, "blk", axis=0, tiled=True),
    )
    wide_qkv, wide_attn, wide_up, wide_down = (gathered[0], gathered[1], gathered[2], gathered[3])
    gain_one = gathered[4].astype(jnp.float32)
    bias_one = gathered[5].astype(jnp.float32)
    gain_two = gathered[6].astype(jnp.float32)
    bias_two = gathered[7].astype(jnp.float32)
    residual = inputs.astype(jnp.float32)
    first_normalized, norm_one_back = jax.vjp(layer_norm, residual, gain_one, bias_one)
    normed_low = first_normalized.astype(jnp.bfloat16)
    query_key_value = project(normed_low, wide_qkv).astype(jnp.bfloat16)
    packed = query_key_value.reshape(seq_count, tok_dev, 3, groups, group_width)
    spread = lax.all_to_all(packed, "uly", split_axis=3, concat_axis=1, tiled=True)
    query_flat = spread[:, :, 0, 0]
    key_flat = spread[:, :, 1, 0]
    value_flat = spread[:, :, 2, 0]
    queries = query_flat.reshape(seq_count, block_rows, heads_here, HEAD_DIM)
    key_heads = key_flat.reshape(seq_count, block_rows, heads_here, HEAD_DIM)
    value_heads = value_flat.reshape(seq_count, block_rows, heads_here, HEAD_DIM)
    firsts = lax.all_gather(doc_starts, "uly", axis=1, tiled=True)
    query_pos = cycle_place * block_rows + jnp.arange(block_rows, dtype=jnp.int32)

    def forward_update(carried, blocks, first_row):
        span_rows = blocks[0].shape[1]
        key_pos = first_row + jnp.arange(span_rows, dtype=jnp.int32)
        new_max, new_sum, new_acc = ([], [], [])
        for seq_index in range(seq_count):
            one_state = (carried[0][seq_index], carried[1][seq_index], carried[2][seq_index])
            key_one = blocks[0][seq_index].reshape(span_rows, heads_here, HEAD_DIM)
            value_one = blocks[1][seq_index].reshape(span_rows, heads_here, HEAD_DIM)

            def advance_state(state_in):
                return forward_pair(
                    state_in,
                    queries[seq_index],
                    key_one,
                    value_one,
                    query_pos,
                    firsts[seq_index],
                    key_pos,
                )

            def keep_state(state_in):
                return state_in

            updated = lax.cond(
                live_pair(query_pos, firsts[seq_index], key_pos),
                advance_state,
                keep_state,
                one_state,
            )
            new_max.append(updated[0])
            new_sum.append(updated[1])
            new_acc.append(updated[2])
        return (jnp.stack(new_max), jnp.stack(new_sum), jnp.stack(new_acc))

    start_state = (
        jnp.full((seq_count, heads_here, block_rows), neg_large, jnp.float32),
        jnp.zeros((seq_count, heads_here, block_rows), jnp.float32),
        jnp.zeros((seq_count, heads_here, block_rows, HEAD_DIM), jnp.float32),
    )
    run_max, run_sum, run_acc = each_block(
        forward_update,
        start_state,
        (
            lax.all_gather(key_flat, "blk", axis=1, tiled=True),
            lax.all_gather(value_flat, "blk", axis=1, tiled=True),
        ),
        block_rows,
    )
    attn_heads = jnp.swapaxes(run_acc / run_sum[..., None], 1, 2)
    log_sum = run_max + jnp.log(run_sum)
    attn_low = attn_heads.reshape(seq_count, block_rows, 1, group_width).astype(jnp.bfloat16)
    back_rows = lax.all_to_all(attn_low, "uly", split_axis=1, concat_axis=2, tiled=True).reshape(
        seq_count, tok_dev, model_width
    )
    attention_projected = project(back_rows, wide_attn)
    middle = residual + branch_scale * attention_projected
    second_normalized, norm_two_back = jax.vjp(layer_norm, middle, gain_two, bias_two)
    normed_two_low = second_normalized.astype(jnp.bfloat16)
    before_activation = project(normed_two_low, wide_up)
    act_value, gate_back = jax.vjp(smooth_gate, before_activation)
    act_low = act_value.astype(jnp.bfloat16)
    feedforward_output = project(act_low, wide_down)
    output = (middle + branch_scale * feedforward_output).astype(jnp.bfloat16)
    grad_res = out_grad.astype(jnp.float32)
    grad_branch = (branch_scale * grad_res).astype(jnp.bfloat16)
    grad_w_down = weight_grad(act_low, grad_branch)
    grad_act = project_back(grad_branch, wide_down)
    grad_pre = gate_back(grad_act)[0].astype(jnp.bfloat16)
    grad_w_up = weight_grad(normed_two_low, grad_pre)
    grad_norm_two = project_back(grad_pre, wide_up)
    grad_mid_part, grad_gain_two, grad_bias_two = norm_two_back(grad_norm_two)
    grad_middle = grad_res + grad_mid_part
    grad_attn = (branch_scale * grad_middle).astype(jnp.bfloat16)
    grad_w_attn = weight_grad(back_rows, grad_attn)
    grad_mixed = project_back(grad_attn, wide_attn).astype(jnp.bfloat16)
    grad_spread = lax.all_to_all(
        grad_mixed.reshape(seq_count, tok_dev, groups, group_width),
        "uly",
        split_axis=2,
        concat_axis=1,
        tiled=True,
    )
    grad_flat = grad_spread[:, :, 0]
    grad_heads = grad_flat.reshape(seq_count, block_rows, heads_here, HEAD_DIM)
    delta_rows = jnp.swapaxes(jnp.sum(attn_heads * grad_heads.astype(jnp.float32), axis=-1), 1, 2)

    def query_update(grad_query, blocks, first_row):
        span_rows = blocks[0].shape[1]
        key_pos = first_row + jnp.arange(span_rows, dtype=jnp.int32)
        new_terms = []
        for seq_index in range(seq_count):
            key_one = blocks[0][seq_index].reshape(span_rows, heads_here, HEAD_DIM)
            value_one = blocks[1][seq_index].reshape(span_rows, heads_here, HEAD_DIM)

            def query_compute_terms(unused):
                return backward_pair(
                    queries[seq_index],
                    grad_heads[seq_index],
                    log_sum[seq_index],
                    delta_rows[seq_index],
                    key_one,
                    value_one,
                    query_pos,
                    firsts[seq_index],
                    key_pos,
                    True,
                    False,
                )[0]

            def query_zero_terms(unused):
                return jnp.zeros((block_rows, heads_here, HEAD_DIM), jnp.float32)

            new_terms.append(
                grad_query[seq_index]
                + lax.cond(
                    live_pair(query_pos, firsts[seq_index], key_pos),
                    query_compute_terms,
                    query_zero_terms,
                    0,
                )
            )
        return jnp.stack(new_terms)

    grad_query = each_block(
        query_update,
        jnp.zeros((seq_count, block_rows, heads_here, HEAD_DIM), jnp.float32),
        (
            lax.all_gather(key_flat, "blk", axis=1, tiled=True),
            lax.all_gather(value_flat, "blk", axis=1, tiled=True),
        ),
        block_rows,
    )

    def key_update(carried, blocks, first_row):
        span_rows = blocks[0].shape[1]
        other_pos = first_row + jnp.arange(span_rows, dtype=jnp.int32)
        key_sums, value_sums = ([], [])
        for seq_index in range(seq_count):
            query_one = blocks[0][seq_index].reshape(span_rows, heads_here, HEAD_DIM)
            grad_one = blocks[1][seq_index].reshape(span_rows, heads_here, HEAD_DIM)
            lse_one = jnp.transpose(blocks[2][seq_index])
            delta_one = jnp.transpose(blocks[3][seq_index])
            first_one = blocks[4][seq_index]

            def key_compute_terms(unused):
                return backward_pair(
                    query_one,
                    grad_one,
                    lse_one,
                    delta_one,
                    key_heads[seq_index],
                    value_heads[seq_index],
                    other_pos,
                    first_one,
                    query_pos,
                    False,
                    True,
                )

            def key_zero_terms(unused):
                zero_rows = jnp.zeros((block_rows, heads_here, HEAD_DIM), jnp.float32)
                return (zero_rows, zero_rows)

            terms = lax.cond(
                live_pair(other_pos, first_one, query_pos), key_compute_terms, key_zero_terms, 0
            )
            key_sums.append(carried[0][seq_index] + terms[0])
            value_sums.append(carried[1][seq_index] + terms[1])
        return (jnp.stack(key_sums), jnp.stack(value_sums))

    zero_heads = jnp.zeros((seq_count, block_rows, heads_here, HEAD_DIM), jnp.float32)
    grad_keys, grad_values = each_block(
        key_update,
        (zero_heads, zero_heads),
        (
            lax.all_gather(query_flat, "blk", axis=1, tiled=True),
            lax.all_gather(grad_flat, "blk", axis=1, tiled=True),
            lax.all_gather(
                jnp.swapaxes(log_sum, 1, 2).astype(jnp.bfloat16), "blk", axis=1, tiled=True
            ).astype(jnp.float32),
            lax.all_gather(
                jnp.swapaxes(delta_rows, 1, 2).astype(jnp.bfloat16), "blk", axis=1, tiled=True
            ).astype(jnp.float32),
            lax.all_gather(firsts, "blk", axis=1, tiled=True),
        ),
        block_rows,
    )
    grad_query_flat = grad_query.reshape(seq_count, block_rows, group_width)
    grad_key_flat = grad_keys.reshape(seq_count, block_rows, group_width)
    grad_value_flat = grad_values.reshape(seq_count, block_rows, group_width)
    stacked = jnp.stack([grad_query_flat, grad_key_flat, grad_value_flat], axis=2).astype(
        jnp.bfloat16
    )
    stacked = stacked.reshape(seq_count, block_rows, 3, 1, group_width)
    grad_qkv = lax.all_to_all(stacked, "uly", split_axis=1, concat_axis=3, tiled=True).reshape(
        seq_count, tok_dev, 3 * model_width
    )
    grad_w_qkv = weight_grad(normed_low, grad_qkv)
    grad_norm_one = project_back(grad_qkv, wide_qkv)
    grad_in_part, grad_gain_one, grad_bias_one = norm_one_back(grad_norm_one)
    grad_inputs = grad_middle + grad_in_part
    column_sums = (
        lax.psum_scatter(
            grad_w_qkv.astype(jnp.bfloat16), "uly", scatter_dimension=1, tiled=True
        ).astype(jnp.float32),
        lax.psum_scatter(
            grad_w_attn.astype(jnp.bfloat16), "uly", scatter_dimension=1, tiled=True
        ).astype(jnp.float32),
        lax.psum_scatter(
            grad_w_up.astype(jnp.bfloat16), "uly", scatter_dimension=1, tiled=True
        ).astype(jnp.float32),
        lax.psum_scatter(
            grad_w_down.astype(jnp.bfloat16), "uly", scatter_dimension=1, tiled=True
        ).astype(jnp.float32),
        lax.psum_scatter(
            jnp.tile(grad_gain_one, groups).astype(jnp.bfloat16),
            "uly",
            scatter_dimension=0,
            tiled=True,
        ).astype(jnp.float32),
        lax.psum_scatter(
            jnp.tile(grad_bias_one, groups).astype(jnp.bfloat16),
            "uly",
            scatter_dimension=0,
            tiled=True,
        ).astype(jnp.float32),
        lax.psum_scatter(
            jnp.tile(grad_gain_two, groups).astype(jnp.bfloat16),
            "uly",
            scatter_dimension=0,
            tiled=True,
        ).astype(jnp.float32),
        lax.psum_scatter(
            jnp.tile(grad_bias_two, groups).astype(jnp.bfloat16),
            "uly",
            scatter_dimension=0,
            tiled=True,
        ).astype(jnp.float32),
    )
    owned = (
        lax.psum_scatter(column_sums[0], "blk", scatter_dimension=0, tiled=True),
        lax.psum_scatter(column_sums[1], "blk", scatter_dimension=0, tiled=True),
        lax.psum_scatter(column_sums[2], "blk", scatter_dimension=0, tiled=True),
        lax.psum_scatter(column_sums[3], "blk", scatter_dimension=0, tiled=True),
        lax.psum_scatter(column_sums[4], "blk", scatter_dimension=0, tiled=True),
        lax.psum_scatter(column_sums[5], "blk", scatter_dimension=0, tiled=True),
        lax.psum_scatter(column_sums[6], "blk", scatter_dimension=0, tiled=True),
        lax.psum_scatter(column_sums[7], "blk", scatter_dimension=0, tiled=True),
    )
    return (
        output,
        grad_inputs,
        owned[4],
        owned[5],
        owned[0],
        owned[1],
        owned[6],
        owned[7],
        owned[2],
        owned[3],
    )


def solution(mesh):
    placed = (
        P(None, ("blk", "uly"), None),
        P(None, ("blk", "uly")),
        P(None, ("blk", "uly"), None),
        P("blk"),
        P("blk"),
        P("blk", "uly"),
        P("blk", "uly"),
        P("blk"),
        P("blk"),
        P("blk", "uly"),
        P("blk", "uly"),
    )
    return jax.shard_map(
        local,
        mesh=mesh,
        in_specs=placed,
        out_specs=(
            P(None, ("blk", "uly"), None),
            P(None, ("blk", "uly"), None),
            P("blk"),
            P("blk"),
            P("blk", "uly"),
            P("blk", "uly"),
            P("blk"),
            P("blk"),
            P("blk", "uly"),
            P("blk", "uly"),
        ),
        check_vma=False,
    )
```

profile of v0, /device:TPU:4, one launch (start us, length us, event | category | flops | bytes accessed | tf_op | source)
XLA Modules:
  0.0 820.6 jit_solution(2636758922997852088)
XLA Ops:
  7.3 15.9 %all-gather.4 = bf16[4,576,96]{1,2,0:T(8,128)(2,1)S(1)} all-gather(bf16[1,576,96]{1,2,0:T(8,128)(2,1)} %bitcast.423), channel_id=1, replica_groups=mesh['blk'=8,'uly'=4] {'uly'}, dimensions={0}, use_global_device_ids=true | all-gather | bytes 552960 | tf_op jit(solution)/shard_map/all_gather | solution.py:155
  26.9 12.3 %all-reduce.13 = (bf16[768]{0:T(1024)(128)(2,1)S(1)}, bf16[768]{0:T(1024)(128)(2,1)S(1)}, bf16[768]{0:T(1024)(128)(2,1)S(1)}, bf16[768]{0:T(1024)(128)(2,1)S(1)}) all-reduce(bf16[768]{0:T(1024)(128)(2,1)S(1)} %dynamic-update-slice.1, bf16[768]{0:T(1024)(128)(2,1)S(1)} %dynamic-update-slice, ...), channel_id=1, replica_groups=mesh['blk'=8,'uly'=4] {'blk'}, use_global_device_ids=true, to_apply=%add.1 | all-reduce | flops 3072 | bytes 12288
  39.6 20.9 %all-gather.14.cloned.1.call-done = bf16[768,2304]{1,0:T(8,128)(2,1)} async-done(((bf16[96,2304]{1,0:T(8,128)(2,1)}), bf16[768,2304]{1,0:T(8,128)(2,1)}) %all-gather.14.cloned.1.call-update) | async-done | bytes 3538960 | tf_op jit(solution)/shard_map/all_gather | solution.py:161
  60.5 2.7 convolution_convert_fusion
  64.1 24.9 %all_to_all.63 = bf16[2,64,3,4,192]{4,1,2,0,3:T(8,128)(2,1)S(1)} all-to-all(bf16[2,64,3,4,192]{4,1,2,0,3:T(8,128)(2,1)S(1)} %copy.106), channel_id=1, replica_groups=mesh['blk'=8,'uly'=4] {'uly'}, dimensions={3} | all-to-all | bytes 1179648 | tf_op jit(solution)/shard_map/all_to_all | solution.py:180
  90.9 14.0 %all_gather.69 = bf16[96,768]{0,1:T(8,128)(2,1)S(1)} all-gather(bf16[96,192]{0,1:T(8,128)(2,1)S(1)} %copy.116), channel_id=1, replica_groups=mesh['blk'=8,'uly'=4] {'uly'}, dimensions={1}, use_global_device_ids=true | all-gather | bytes 184320 | tf_op jit(solution)/shard_map/all_gather | solution.py:156
  105.8 17.1 %all_gather.73 = bf16[96,3072]{1,0:T(8,128)(2,1)} all-gather(bf16[96,768]{1,0:T(8,128)(2,1)S(1)} %copy-done.26), channel_id=1, replica_groups=mesh['blk'=8,'uly'=4] {'uly'}, dimensions={1}, use_global_device_ids=true | all-gather | bytes 737280 | tf_op jit(solution)/shard_map/all_gather | solution.py:157
  122.9 15.0 %all_gather.75 = bf16[384,768]{0,1:T(8,128)(2,1)S(1)} all-gather(bf16[384,192]{0,1:T(8,128)(2,1)S(1)} %copy-done.27), channel_id=1, replica_groups=mesh['blk'=8,'uly'=4] {'uly'}, dimensions={1}, use_global_device_ids=true | all-gather | bytes 737280 | tf_op jit(solution)/shard_map/all_gather | solution.py:158
  139.0 9.5 %all-gather.3 = s32[4,64,2]{1,2,0:T(2,128)S(1)} all-gather(s32[1,64,2]{1,2,0:T(2,128)S(1)} %bitcast.433), channel_id=1, replica_groups=mesh['blk'=8,'uly'=4] {'uly'}, dimensions={0}, use_global_device_ids=true | all-gather | bytes 2560 | tf_op jit(solution)/shard_map/all_gather | solution.py:187
  148.8 3.1 copy.111
  151.9 3.9 copy.112
  155.9 113.8 %while.36 = (s32[]{:T(128)}, f32[2,3,256]{2,1,0:T(4,128)S(1)}, f32[2,3,256]{2,1,0:T(4,128)S(1)}, f32[2,3,256,64]{2,3,1,0:T(8,128)S(1)}, s32[8]{0:T(128)S(1)}, /*...) while((s32[]{:T(128)}, f32[2,3,256]{2,1,0:T(4,128)S(1)}, ...), condition=%wide.region_11.12_spmd, body=%wide.region_2.11_spmd.sunk | while | flops 104896776 | bytes 9924064 | solution.py:129
  165.7 3.6 conditional.13
  179.9 3.6 conditional.13
  192.2 3.6 conditional.12
  197.8 3.6 conditional.13
  210.1 3.6 conditional.12
  215.7 3.6 conditional.13
  227.9 3.6 conditional.12
  233.5 3.6 conditional.13
  271.2 3.4 all-to-all-start.1
  275.6 5.8 all-to-all-done.1
  281.9 1.7 fusion.163
  283.9 3.2 fusion.100
  287.3 4.8 fusion.111
  292.1 2.3 multiply_reduce_fusion
  298.3 10.4 %all_to_all.64 = bf16[2,64,4,192]{3,1,0,2:T(8,128)(2,1)S(1)} all-to-all(bf16[2,64,4,192]{3,1,0,2:T(8,128)(2,1)S(1)} %copy.119), channel_id=1, replica_groups=mesh['blk'=8,'uly'=4] {'uly'}, dimensions={2} | all-to-all | bytes 393216 | tf_op jit(solution)/shard_map/all_to_all | solution.py:265
  310.2 1.6 bitcast_convert_fusion.3
  311.9 4.7 bitcast_convert_fusion.1
  316.7 16.4 %all_gather.77 = s32[2,2048]{1,0:T(2,128)} all-gather(s32[2,256]{1,0:T(2,128)S(1)} %get-tuple-element.1271), channel_id=1, replica_groups=mesh['blk'=8,'uly'=4] {'blk'}, dimensions={1}, use_global_device_ids=true | all-gather | bytes 18432 | tf_op jit(solution)/shard_map/all_gather | solution.py:373
  335.1 3.9 copy.131
  339.0 7.9 all_gather.79
  347.0 3.7 bitcast_convert_fusion
  352.2 9.1 %all_gather.81 = bf16[2,2048,3]{1,2,0:T(4,128)(2,1)S(1)} all-gather(bf16[2,256,3]{1,2,0:T(4,128)(2,1)S(1)} %convert_element_type.207), channel_id=1, replica_groups=mesh['blk'=8,'uly'=4] {'blk'}, dimensions={1}, use_global_device_ids=true | all-gather | bytes 27648 | tf_op jit(solution)/shard_map/all_gather | solution.py:370
  361.4 73.6 %while.37 = (s32[]{:T(128)}, f32[2,256,3,64]{1,3,2,0:T(8,128)S(1)}, s32[8]{0:T(128)S(1)}, s32[256]{0:T(256)S(1)}, s32[2,256]{1,0:T(2,128)S(1)}, /*index=5*/bf16[...) while((s32[]{:T(128)}, f32[2,256,3,64]{1,3,2,0:T(8,128)S(1)}, ...), condition=%wide.region_22.23_spmd, body=%wide.region_17.22_spmd.sunk | while | flops 154435840 | bytes 8375632 | solution.py:129
  435.7 3.9 copy.133
  439.7 104.9 %while.38 = (s32[]{:T(128)}, f32[2,256,3,64]{1,3,2,0:T(8,128)S(1)}, f32[2,256,3,64]{1,3,2,0:T(8,128)S(1)}, s32[256]{0:T(256)S(1)}, s32[8]{0:T(128)S(1)}, /*index...) while((s32[]{:T(128)}, f32[2,256,3,64]{1,3,2,0:T(8,128)S(1)}, ...), condition=%wide.region_28.29_spmd, body=%wide.region_23.28_spmd.sunk | while | flops 205357312 | bytes 13318036 | solution.py:129
  493.8 2.2 conditional.16
  494.0 1.3 fusion.60
  497.3 2.2 conditional.17
  509.2 2.2 conditional.16
  509.4 1.3 fusion.60
  512.8 2.2 conditional.17
  513.0 1.3 fusion.77
  524.8 2.2 conditional.16
  524.9 1.3 fusion.60
  528.3 2.2 conditional.17
  528.5 1.3 fusion.77
  540.2 2.2 conditional.16
  540.4 1.3 fusion.60
  546.5 19.7 %all_to_all.65 = bf16[2,256,3,1,192]{4,0,3,2,1:T(2,128)(2,1)S(1)} all-to-all(bf16[2,256,3,1,192]{4,0,3,2,1:T(2,128)(2,1)S(1)} %copy.135), channel_id=1, replica_groups=mesh['blk'=8,'uly'=4] {'uly'}, dimensions={1} | all-to-all | bytes 1179648 | tf_op jit(solution)/shard_map/all_to_all | solution.py:384
  567.6 3.0 bitcast_convert_fusion.2
  570.8 2.0 copy.158
  572.9 2.9 convert_element_type.225
  576.0 2.9 convert_element_type.227
  578.9 59.0 %reduce-scatter.13.cloned.1.call-done = bf16[768,576]{0,1:T(8,128)(2,1)} async-done(((bf16[768,2304]{0,1:T(8,128)(2,1)}), bf16[768,576]{0,1:T(8,128)(2,1)}) %reduce-scatter.13.cloned.1.call-update) | async-done | bytes 884752 | tf_op jit(solution)/shard_map/reduce_scatter | solution.py:392
  637.9 2.5 copy.156
  643.1 4.2 fusion.127
  647.3 1.4 fusion.152
  649.0 18.2 %all-reduce.14 = (bf16[3072]{0:T(1024)(128)(2,1)S(1)}, bf16[3072]{0:T(1024)(128)(2,1)S(1)}, bf16[3072]{0:T(1024)(128)(2,1)S(1)}, bf16[3072]{0:T(1024)(128)(2,1)S(1)}) all-reduce(bf16[3072]{0:T(1024)(128)(2,1)S(1)} %convert_element_type.209, ...), channel_id=5, replica_groups=mesh['blk'=8,'uly'=4] {'uly'}, use_global_device_ids=true, to_apply=%region_32.33.clone | all-reduce | flops 12288 | bytes 49152
  667.4 22.5 %all-reduce.12 = (f32[768]{0:T(1024)S(1)}, f32[768]{0:T(1024)S(1)}, f32[768]{0:T(1024)S(1)}, f32[768]{0:T(1024)S(1)}) all-reduce(f32[768]{0:T(1024)S(1)} %get-tuple-element.754, f32[768]{0:T(1024)S(1)} %get-tuple-element.753, f32[768]{0:T(1024)S(1)} %get-tuple-element.752, ...), channel_id=6, replica_groups=mesh['blk'=8,'uly'=4] {'blk'}, use_global_device_ids=true, to_apply=%region_33.34.clone | all-reduce | flops 3072 | bytes 24576
  693.2 30.0 %reduce-scatter.19.cloned.1.call-done = f32[96,768]{1,0:T(8,128)} async-done(((f32[768,768]{1,0:T(8,128)}), f32[96,768]{1,0:T(8,128)}) %reduce-scatter.19.cloned.1.call-update) | async-done | bytes 294928 | tf_op jit(solution)/shard_map/reduce_scatter | solution.py:432
  723.2 46.6 %reduce-scatter.23.cloned.1.call-done = f32[384,192]{0,1:T(8,128)} async-done(((f32[3072,192]{0,1:T(8,128)}), f32[384,192]{0,1:T(8,128)}) %reduce-scatter.23.cloned.1.call-update) | async-done | bytes 294928 | tf_op jit(solution)/shard_map/reduce_scatter | solution.py:433
  769.9 44.2 %reduce-scatter.25.cloned.1.call-done = f32[96,576]{1,0:T(8,128)} async-done(((f32[768,576]{1,0:T(8,128)}), f32[96,576]{1,0:T(8,128)}) %reduce-scatter.25.cloned.1.call-update) | async-done | bytes 221200
  (872 shorter events, 211.2 us)
Async XLA Ops:
  7.2 17.5 %copy-start.51 = (u32[32]{0:T(128)S(1)}, u32[32]{0:T(128)}, u32[]{:S(2)}) copy-start(u32[32]{0:T(128)} %constant.135) | copy-start | bytes 388
  7.2 18.8 %copy-start.53 = (bf16[96]{0:T(256)(128)(2,1)S(1)}, bf16[96]{0:T(256)(128)(2,1)}, u32[]{:S(2)}) copy-start(bf16[96]{0:T(256)(128)(2,1)} %param.33) | copy-start | bytes 580
  7.2 19.0 %copy-start.54 = (bf16[96]{0:T(256)(128)(2,1)S(1)}, bf16[96]{0:T(256)(128)(2,1)}, u32[]{:S(2)}) copy-start(bf16[96]{0:T(256)(128)(2,1)} %param.32) | copy-start | bytes 580
  7.2 19.2 %copy-start.55 = (bf16[96]{0:T(256)(128)(2,1)S(1)}, bf16[96]{0:T(256)(128)(2,1)}, u32[]{:S(2)}) copy-start(bf16[96]{0:T(256)(128)(2,1)} %param.37) | copy-start | bytes 580
  7.2 19.5 %copy-start.56 = (bf16[96]{0:T(256)(128)(2,1)S(1)}, bf16[96]{0:T(256)(128)(2,1)}, u32[]{:S(2)}) copy-start(bf16[96]{0:T(256)(128)(2,1)} %param.36) | copy-start | bytes 580
  7.2 32.0 %copy-start.2 = (bf16[2,64,768]{2,1,0:T(8,128)(2,1)S(1)}, bf16[2,64,768]{2,1,0:T(8,128)(2,1)}, u32[]{:S(2)}) copy-start(bf16[2,64,768]{2,1,0:T(8,128)(2,1)} %param.29) | copy-start | bytes 589828
  7.2 53.3 %all-gather.14.cloned.1.call-start = ((), (), s32[]{:S(2)}) async-start(), calls=%async_computation.12 | async-start | bytes 3981312 | tf_op jit(solution)/shard_map/all_gather | solution.py:161
  24.6 124.1 %all-gather.24.cloned.1.call-start = ((), (), s32[]{:S(2)}) async-start(), calls=%async_computation.23 | async-start | bytes 2359296 | tf_op jit(solution)/shard_map/all_gather | solution.py:233
  39.2 24.0 %copy-start.22 = (f32[768]{0:T(1024)}, f32[768]{0:T(1024)S(1)}, u32[]{:S(2)}) copy-start(f32[768]{0:T(1024)S(1)} %convert_element_type.189) | copy-start | bytes 9220
  39.2 24.0 %copy-start.15 = (f32[768]{0:T(1024)}, f32[768]{0:T(1024)S(1)}, u32[]{:S(2)}) copy-start(f32[768]{0:T(1024)S(1)} %convert_element_type.188) | copy-start | bytes 9220
  39.4 23.9 %copy-start.32 = (f32[2,64]{1,0:T(2,128)}, f32[2,64]{1,0:T(2,128)S(1)}, u32[]{:S(2)}) copy-start(f32[2,64]{1,0:T(2,128)S(1)} %broadcast_multiply_fusion.1) | copy-start | bytes 1540
  39.6 23.7 %copy-start.43 = (f32[2,64]{1,0:T(2,128)}, f32[2,64]{1,0:T(2,128)S(1)}, u32[]{:S(2)}) copy-start(f32[2,64]{1,0:T(2,128)S(1)} %fusion.140) | copy-start | bytes 1540
  39.6 23.7 %copy-start.40 = (f32[2,64]{1,0:T(2,128)}, f32[2,64]{1,0:T(2,128)S(1)}, u32[]{:S(2)}) copy-start(f32[2,64]{1,0:T(2,128)S(1)} %fusion.148) | copy-start | bytes 1540
  89.1 16.6 %copy-start.26 = (bf16[96,768]{1,0:T(8,128)(2,1)S(1)}, bf16[96,768]{1,0:T(8,128)(2,1)}, u32[]{:S(2)}) copy-start(bf16[96,768]{1,0:T(8,128)(2,1)} %param.38) | copy-start | bytes 442372
  90.0 58.7 %copy-start.12 = (bf16[2,256,1,1,192]{4,1,2,0,3:T(8,128)(2,1)}, bf16[2,256,1,1,192]{4,1,2,0,3:T(8,128)(2,1)S(1)}, u32[]{:S(2)}) copy-start(bf16[2,256,1,1,192]{4,1,2,0,3:T(8,128)(2,1)S(1)} %get-tuple-element.742) | copy-start | bytes 589828
  90.0 32.9 %copy-start.27 = (bf16[384,192]{0,1:T(8,128)(2,1)S(1)}, bf16[384,192]{0,1:T(8,128)(2,1)}, u32[]{:S(2)}) copy-start(bf16[384,192]{0,1:T(8,128)(2,1)} %param.39) | copy-start | bytes 442372
  90.0 61.9 %all-gather.26.cloned.1.call-start = ((), (), s32[]{:S(2)}) async-start(), calls=%async_computation.24 | async-start | bytes 2359296 | tf_op jit(solution)/shard_map/all_gather | solution.py:234
  90.7 191.2 %all-gather.16.cloned.1.call-start = ((), (), s32[]{:S(2)}) async-start(), calls=%async_computation.13 | async-start | bytes 1327104 | tf_op jit(solution)/shard_map/all_gather | solution.py:162
  105.7 178.2 %all-gather.18.cloned.1.call-start = ((), (), s32[]{:S(2)}) async-start(), calls=%async_computation.14 | async-start | bytes 5308416 | tf_op jit(solution)/shard_map/all_gather | solution.py:163
  122.8 16.2 %copy-start.52 = (s32[2,64]{1,0:T(2,128)S(1)}, s32[2,64]{1,0:T(2,128)}, u32[]{:S(2)}) copy-start(s32[2,64]{1,0:T(2,128)} %param.30) | copy-start | bytes 1540
  122.9 164.3 %all-gather.20.cloned.1.call-start = ((), (), s32[]{:S(2)}) async-start(), calls=%async_computation.15 | async-start | bytes 5308416 | tf_op jit(solution)/shard_map/all_gather | solution.py:164
  269.7 12.1 %copy-start.5 = (bf16[8,2,256,192]{2,3,1,0:T(8,128)(2,1)}, bf16[8,2,256,192]{2,3,1,0:T(8,128)(2,1)S(1)}, u32[]{:S(2)}) copy-start(bf16[8,2,256,192]{2,3,1,0:T(8,128)(2,1)S(1)} %get-tuple-element.1237) | copy-start | bytes 4718596
  271.2 10.2 %all-to-all-start.1 = ((bf16[2,256,1,192]{3,0,2,1:T(2,128)(2,1)}), bf16[2,256,1,192]{3,0,2,1:T(2,128)(2,1)S(1)}, u32[]{:S(2)}, u32[]{:S(2)}) async-start(bf16[2,256,1,192]{3,0,2,1:T(2,128)(2,1)} %copy.113), calls=%async_computation.1 | async-start | bytes 524288 | tf_op jit(solution)/shard_map/all_to_all | solution.py:241
  274.6 60.4 %all-gather.28.cloned.1.call-start = ((), (), s32[]{:S(2)}) async-start(), calls=%async_computation.25 | async-start | bytes 2359296 | tf_op jit(solution)/shard_map/all_gather | solution.py:365
  274.7 9.2 %copy-start.24 = (f32[768]{0:T(1024)}, f32[768]{0:T(1024)S(1)}, u32[]{:S(2)}) copy-start(f32[768]{0:T(1024)S(1)} %convert_element_type.195) | copy-start | bytes 9220
  274.7 9.2 %copy-start.17 = (f32[768]{0:T(1024)}, f32[768]{0:T(1024)S(1)}, u32[]{:S(2)}) copy-start(f32[768]{0:T(1024)S(1)} %convert_element_type.194) | copy-start | bytes 9220
  275.4 160.3 %all-gather.22.cloned.1.call-start = ((), (), s32[]{:S(2)}) async-start(), calls=%async_computation.16 | async-start | bytes 2359296 | tf_op jit(solution)/shard_map/all_gather | solution.py:366
  287.2 59.8 %copy-start.3 = (f32[2,64,3072]{2,1,0:T(8,128)}, f32[2,64,3072]{2,1,0:T(8,128)S(1)}, u32[]{:S(2)}) copy-start(f32[2,64,3072]{2,1,0:T(8,128)S(1)} %fusion.100) | copy-start | bytes 4718596
  287.2 4.8 copy-start.1
  310.2 260.6 %reduce-scatter.15.cloned.1.call-start = ((), (), s32[]{:S(2)}) async-start(), calls=%async_computation.18 | async-start | bytes 1474560 | tf_op jit(solution)/shard_map/reduce_scatter | solution.py:395
  311.8 261.1 %reduce-scatter.17.cloned.1.call-start = ((), (), s32[]{:S(2)}) async-start(), calls=%async_computation.19 | async-start | bytes 5898240 | tf_op jit(solution)/shard_map/reduce_scatter | solution.py:398
  316.6 16.5 %copy-start.13 = (bf16[2,256,1,1,192]{4,1,2,0,3:T(8,128)(2,1)S(1)}, bf16[2,256,1,1,192]{4,1,2,0,3:T(8,128)(2,1)}, u32[]{:S(2)}) copy-start(bf16[2,256,1,1,192]{4,1,2,0,3:T(8,128)(2,1)} %get-tuple-element.744) | copy-start | bytes 589828
  316.6 259.3 %reduce-scatter.21.cloned.1.call-start = ((), (), s32[]{:S(2)}) async-start(), calls=%async_computation.21 | async-start | bytes 5898240 | tf_op jit(solution)/shard_map/reduce_scatter | solution.py:401
  350.7 287.3 %reduce-scatter.13.cloned.1.call-start = ((), (), s32[]{:S(2)}) async-start(), calls=%async_computation.17 | async-start | bytes 4423680 | tf_op jit(solution)/shard_map/reduce_scatter | solution.py:392
  439.7 8.9 %copy-start.58 = (s32[8]{0:T(128)}, s32[8]{0:T(128)S(1)}, u32[]{:S(2)}) copy-start(s32[8]{0:T(128)S(1)} %get-tuple-element.1132) | copy-start | bytes 100 | tf_op jit(solution)/shard_map/while
  439.7 9.0 %copy-start.28 = (f32[8,2,256,3]{2,0,3,1:T(8,128)}, f32[8,2,256,3]{2,0,3,1:T(8,128)S(1)}, u32[]{:S(2)}) copy-start(f32[8,2,256,3]{2,0,3,1:T(8,128)S(1)} %get-tuple-element.1135) | copy-start | bytes 147460 | tf_op jit(solution)/shard_map/while
  439.7 9.0 %copy-start.30 = (f32[8,2,256,3]{2,0,3,1:T(8,128)}, f32[8,2,256,3]{2,0,3,1:T(8,128)S(1)}, u32[]{:S(2)}) copy-start(f32[8,2,256,3]{2,0,3,1:T(8,128)S(1)} %get-tuple-element.1137) | copy-start | bytes 147460 | tf_op jit(solution)/shard_map/while
  451.0 8.9 %copy-start.58 = (s32[8]{0:T(128)}, s32[8]{0:T(128)S(1)}, u32[]{:S(2)}) copy-start(s32[8]{0:T(128)S(1)} %get-tuple-element.1132) | copy-start | bytes 100 | tf_op jit(solution)/shard_map/while
  451.0 9.0 %copy-start.28 = (f32[8,2,256,3]{2,0,3,1:T(8,128)}, f32[8,2,256,3]{2,0,3,1:T(8,128)S(1)}, u32[]{:S(2)}) copy-start(f32[8,2,256,3]{2,0,3,1:T(8,128)S(1)} %get-tuple-element.1135) | copy-start | bytes 147460 | tf_op jit(solution)/shard_map/while
  451.0 9.0 %copy-start.30 = (f32[8,2,256,3]{2,0,3,1:T(8,128)}, f32[8,2,256,3]{2,0,3,1:T(8,128)S(1)}, u32[]{:S(2)}) copy-start(f32[8,2,256,3]{2,0,3,1:T(8,128)S(1)} %get-tuple-element.1137) | copy-start | bytes 147460 | tf_op jit(solution)/shard_map/while
  462.2 9.0 %copy-start.58 = (s32[8]{0:T(128)}, s32[8]{0:T(128)S(1)}, u32[]{:S(2)}) copy-start(s32[8]{0:T(128)S(1)} %get-tuple-element.1132) | copy-start | bytes 100 | tf_op jit(solution)/shard_map/while
  462.2 9.0 %copy-start.28 = (f32[8,2,256,3]{2,0,3,1:T(8,128)}, f32[8,2,256,3]{2,0,3,1:T(8,128)S(1)}, u32[]{:S(2)}) copy-start(f32[8,2,256,3]{2,0,3,1:T(8,128)S(1)} %get-tuple-element.1135) | copy-start | bytes 147460 | tf_op jit(solution)/shard_map/while
  462.2 9.0 %copy-start.30 = (f32[8,2,256,3]{2,0,3,1:T(8,128)}, f32[8,2,256,3]{2,0,3,1:T(8,128)S(1)}, u32[]{:S(2)}) copy-start(f32[8,2,256,3]{2,0,3,1:T(8,128)S(1)} %get-tuple-element.1137) | copy-start | bytes 147460 | tf_op jit(solution)/shard_map/while
  473.5 9.0 %copy-start.58 = (s32[8]{0:T(128)}, s32[8]{0:T(128)S(1)}, u32[]{:S(2)}) copy-start(s32[8]{0:T(128)S(1)} %get-tuple-element.1132) | copy-start | bytes 100 | tf_op jit(solution)/shard_map/while
  473.5 9.0 %copy-start.28 = (f32[8,2,256,3]{2,0,3,1:T(8,128)}, f32[8,2,256,3]{2,0,3,1:T(8,128)S(1)}, u32[]{:S(2)}) copy-start(f32[8,2,256,3]{2,0,3,1:T(8,128)S(1)} %get-tuple-element.1135) | copy-start | bytes 147460 | tf_op jit(solution)/shard_map/while
  473.5 9.0 %copy-start.30 = (f32[8,2,256,3]{2,0,3,1:T(8,128)}, f32[8,2,256,3]{2,0,3,1:T(8,128)S(1)}, u32[]{:S(2)}) copy-start(f32[8,2,256,3]{2,0,3,1:T(8,128)S(1)} %get-tuple-element.1137) | copy-start | bytes 147460 | tf_op jit(solution)/shard_map/while
  484.8 8.9 %copy-start.58 = (s32[8]{0:T(128)}, s32[8]{0:T(128)S(1)}, u32[]{:S(2)}) copy-start(s32[8]{0:T(128)S(1)} %get-tuple-element.1132) | copy-start | bytes 100 | tf_op jit(solution)/shard_map/while
  484.8 9.0 %copy-start.28 = (f32[8,2,256,3]{2,0,3,1:T(8,128)}, f32[8,2,256,3]{2,0,3,1:T(8,128)S(1)}, u32[]{:S(2)}) copy-start(f32[8,2,256,3]{2,0,3,1:T(8,128)S(1)} %get-tuple-element.1135) | copy-start | bytes 147460 | tf_op jit(solution)/shard_map/while
  484.8 9.0 %copy-start.30 = (f32[8,2,256,3]{2,0,3,1:T(8,128)}, f32[8,2,256,3]{2,0,3,1:T(8,128)S(1)}, u32[]{:S(2)}) copy-start(f32[8,2,256,3]{2,0,3,1:T(8,128)S(1)} %get-tuple-element.1137) | copy-start | bytes 147460 | tf_op jit(solution)/shard_map/while
  500.3 8.9 %copy-start.58 = (s32[8]{0:T(128)}, s32[8]{0:T(128)S(1)}, u32[]{:S(2)}) copy-start(s32[8]{0:T(128)S(1)} %get-tuple-element.1132) | copy-start | bytes 100 | tf_op jit(solution)/shard_map/while
  500.3 8.9 %copy-start.28 = (f32[8,2,256,3]{2,0,3,1:T(8,128)}, f32[8,2,256,3]{2,0,3,1:T(8,128)S(1)}, u32[]{:S(2)}) copy-start(f32[8,2,256,3]{2,0,3,1:T(8,128)S(1)} %get-tuple-element.1135) | copy-start | bytes 147460 | tf_op jit(solution)/shard_map/while
  500.3 8.9 %copy-start.30 = (f32[8,2,256,3]{2,0,3,1:T(8,128)}, f32[8,2,256,3]{2,0,3,1:T(8,128)S(1)}, u32[]{:S(2)}) copy-start(f32[8,2,256,3]{2,0,3,1:T(8,128)S(1)} %get-tuple-element.1137) | copy-start | bytes 147460 | tf_op jit(solution)/shard_map/while
  515.8 8.9 %copy-start.58 = (s32[8]{0:T(128)}, s32[8]{0:T(128)S(1)}, u32[]{:S(2)}) copy-start(s32[8]{0:T(128)S(1)} %get-tuple-element.1132) | copy-start | bytes 100 | tf_op jit(solution)/shard_map/while
  515.8 9.0 %copy-start.28 = (f32[8,2,256,3]{2,0,3,1:T(8,128)}, f32[8,2,256,3]{2,0,3,1:T(8,128)S(1)}, u32[]{:S(2)}) copy-start(f32[8,2,256,3]{2,0,3,1:T(8,128)S(1)} %get-tuple-element.1135) | copy-start | bytes 147460 | tf_op jit(solution)/shard_map/while
  515.8 9.0 %copy-start.30 = (f32[8,2,256,3]{2,0,3,1:T(8,128)}, f32[8,2,256,3]{2,0,3,1:T(8,128)S(1)}, u32[]{:S(2)}) copy-start(f32[8,2,256,3]{2,0,3,1:T(8,128)S(1)} %get-tuple-element.1137) | copy-start | bytes 147460 | tf_op jit(solution)/shard_map/while
  531.3 8.9 %copy-start.58 = (s32[8]{0:T(128)}, s32[8]{0:T(128)S(1)}, u32[]{:S(2)}) copy-start(s32[8]{0:T(128)S(1)} %get-tuple-element.1132) | copy-start | bytes 100 | tf_op jit(solution)/shard_map/while
  531.3 8.9 %copy-start.28 = (f32[8,2,256,3]{2,0,3,1:T(8,128)}, f32[8,2,256,3]{2,0,3,1:T(8,128)S(1)}, u32[]{:S(2)}) copy-start(f32[8,2,256,3]{2,0,3,1:T(8,128)S(1)} %get-tuple-element.1135) | copy-start | bytes 147460 | tf_op jit(solution)/shard_map/while
  531.3 8.9 %copy-start.30 = (f32[8,2,256,3]{2,0,3,1:T(8,128)}, f32[8,2,256,3]{2,0,3,1:T(8,128)S(1)}, u32[]{:S(2)}) copy-start(f32[8,2,256,3]{2,0,3,1:T(8,128)S(1)} %get-tuple-element.1137) | copy-start | bytes 147460 | tf_op jit(solution)/shard_map/while
  570.7 122.5 %reduce-scatter.27.cloned.1.call-start = ((), (), s32[]{:S(2)}) async-start(), calls=%async_computation.27 | async-start | bytes 884736
  572.8 150.4 %reduce-scatter.19.cloned.1.call-start = ((), (), s32[]{:S(2)}) async-start(), calls=%async_computation.20 | async-start | bytes 2654208 | tf_op jit(solution)/shard_map/reduce_scatter | solution.py:432
  575.9 194.0 %reduce-scatter.23.cloned.1.call-start = ((), (), s32[]{:S(2)}) async-start(), calls=%async_computation.22 | async-start | bytes 2654208 | tf_op jit(solution)/shard_map/reduce_scatter | solution.py:433
  578.9 235.2 %reduce-scatter.25.cloned.1.call-start = ((), (), s32[]{:S(2)}) async-start(), calls=%async_computation.26 | async-start | bytes 2211840
  647.3 44.9 %copy-start.8 = (f32[2,64,768]{2,1,0:T(8,128)S(1)}, f32[2,64,768]{2,1,0:T(8,128)}, u32[]{:S(2)}) copy-start(f32[2,64,768]{2,1,0:T(8,128)} %copy-done.7) | copy-start | bytes 1179652
  647.3 44.9 %copy-start.48 = (f32[2,64]{1,0:T(2,128)S(1)}, f32[2,64]{1,0:T(2,128)}, u32[]{:S(2)}) copy-start(f32[2,64]{1,0:T(2,128)} %copy-done.47) | copy-start | bytes 1540
  (55 other events, 89.3 us)
Sparse Core Ops, SparseCore 0:
  24.8 35.7 all-gather.13
  90.1 26.1 all-gather.23
  118.8 27.8 all-gather.25
  149.0 24.1 all-gather.15
  174.9 38.8 all-gather.17
  215.5 38.8 all-gather.19
  277.4 35.7 all-gather.27
  315.1 28.7 all-gather.21
  346.2 29.2 reduce-scatter.14
  377.7 83.9 reduce-scatter.16
  464.0 86.0 reduce-scatter.20
  570.8 67.0 reduce-scatter.12
  641.6 35.2 reduce-scatter.26
  680.7 42.4 reduce-scatter.18
  727.4 42.4 reduce-scatter.22
  773.7 40.3 reduce-scatter.24
where the time goes:
time: 828 us; the launch traced here: 821 us
  blocking collectives  213 us (26%)
  waiting for transfers between devices  208 us (25%)
  local copies, waits for them, and re-layouts  161 us (19%)
  loops' own time  113 us (14%)
  matrix products  65.1 us (8%)
  other arithmetic  38.4 us (5%)
  between operations  17 us (2%)
    another operation x3, loops' own time, each_block(): lax.scan(advance, carried, (jnp.arange(block_count, dtype=jnp.int32), spl...  112 us
    reduce_scatter x1, waiting for transfers between devices, local(): lax.psum_scatter(grad_w_qkv.astype(jnp.bfloat16), 'uly', scatter_dimensio...  59 us
    unnamed x3, blocking collectives  52.9 us
    dynamic_slice x64, local copies, waits for them, and re-layouts, each_block(): lax.scan(advance, carried, (jnp.arange(block_count, dtype=jnp.int32), spl...  50.8 us
    reduce_scatter x1, waiting for transfers between devices, local(): lax.psum_scatter(column_sums[3], 'blk', scatter_dimension=0, tiled=True)  46.6 us
    slice x72, local copies, waits for them, and re-layouts, live_pair(): return (key_pos[0] <= query_pos[-1]) & (key_pos[-1] >= query_first[0])  46.3 us
    unnamed x18, waiting for transfers between devices  45.8 us
    reduce_scatter x1, waiting for transfers between devices, local(): lax.psum_scatter(column_sums[2], 'blk', scatter_dimension=0, tiled=True)  30 us
  transfers between devices with their start and end apart: 17, of which 6 were waited for; matrix products, arithmetic and copies ran while one was open for 30% of the time, Pallas kernels for 0%

commit v1 on v0

--- a/solution.py
+++ b/solution.py
@@ -1,8 +1,11 @@
+import functools
 import math
 
 import jax
 import jax.numpy as jnp
 from jax import lax
+from jax.experimental import pallas as pl
+from jax.experimental.pallas import tpu as pltpu
 from jax.sharding import PartitionSpec as P
 
 HEAD_DIM = 64
@@ -132,7 +135,7 @@
     return result
 
 
-def local(
+def local_general(
     inputs,
     doc_starts,
     out_grad,
@@ -450,7 +453,375 @@
     )
 
 
+UNITS = 4
+FULL_TOK = 2048
+TILE = 256
+LOG2E = 1.4426950408889634
+
+
+def fits_fast(mesh):
+    return dict(mesh.shape) == {"blk": 8, "uly": 4}
+
+
+def halves_in(rows):
+    half = rows.shape[-2] // 2
+    return jnp.concatenate([rows[..., :half, :], rows[..., half:, :]], axis=-1)
+
+
+def halves_out(packed):
+    half = packed.shape[-1] // 2
+    return jnp.concatenate([packed[..., :half], packed[..., half:]], axis=-2)
+
+
+def attn_forward_kernel(pack_ref, first_ref, out_ref, log_ref, q_rows, k_rows, v_cols):
+    tiles = FULL_TOK // TILE
+    scale = LOG2E * HEAD_DIM**-0.5
+    for t in range(tiles):
+        rows = pl.ds(t * TILE, TILE)
+        pair = pack_ref[t, :TILE, :]
+        q_rows[rows, :] = pair[:, :HEAD_DIM]
+        k_rows[rows, :] = pair[:, HEAD_DIM:]
+        v_cols[:, rows] = halves_out(pack_ref[t, TILE:, :]).T
+    key_iota = lax.broadcasted_iota(jnp.int32, (TILE, TILE), 0)
+    query_iota = lax.broadcasted_iota(jnp.int32, (TILE, TILE), 1)
+    causal = key_iota <= query_iota
+    for i in range(tiles):
+        q_rows_i = pl.ds(i * TILE, TILE)
+        queries = q_rows[q_rows_i, :]
+        first = first_ref[:, q_rows_i]
+        top = total = acc = None
+        for j in range(i, -1, -1):
+            k_at = pl.ds(j * TILE, TILE)
+            scores = lax.dot_general(
+                k_rows[k_at, :], queries, (((1,), (1,)), ((), ())), preferred_element_type=jnp.float32
+            )
+            allowed = key_iota >= first - j * TILE
+            if j == i:
+                allowed = allowed & causal
+            scores = jnp.where(allowed, scores * scale, neg_large)
+            tile_top = jnp.max(scores, axis=0, keepdims=True)
+            new_top = tile_top if top is None else jnp.maximum(top, tile_top)
+            weights = jnp.exp2(scores - new_top)
+            tile_sum = jnp.sum(weights, axis=0, keepdims=True)
+            tile_acc = jnp.dot(
+                v_cols[:, k_at], weights.astype(jnp.bfloat16), preferred_element_type=jnp.float32
+            )
+            if top is None:
+                total, acc = tile_sum, tile_acc
+            else:
+                factor = jnp.exp2(top - new_top)
+                total = factor * total + tile_sum
+                acc = factor * acc + tile_acc
+            top = new_top
+        out_ref[:, q_rows_i] = acc / total
+        log_ref[:, q_rows_i] = top + jnp.log2(total)
+
+
+def attn_backward_kernel(
+    pack_ref, grad_ref, out_cols, log_ref, first_ref, dpack_ref, q_rows, k_rows, v_rows, g_rows, k_cols, delta, dq_cols
+):
+    tiles = FULL_TOK // TILE
+    scale = LOG2E * HEAD_DIM**-0.5
+    for t in range(tiles):
+        rows = pl.ds(t * TILE, TILE)
+        pair = pack_ref[t, :TILE, :]
+        q_rows[rows, :] = pair[:, :HEAD_DIM]
+        keys = pair[:, HEAD_DIM:]
+        k_rows[rows, :] = keys
+        k_cols[:, rows] = keys.T
+        v_rows[rows, :] = halves_out(pack_ref[t, TILE:, :])
+        g_tile = halves_out(grad_ref[t])
+        g_rows[rows, :] = g_tile
+        g_cols = g_tile.T.astype(jnp.float32)
+        delta[:, rows] = jnp.sum(g_cols * out_cols[:, rows], axis=0, keepdims=True)
+    key_iota = lax.broadcasted_iota(jnp.int32, (TILE, TILE), 0)
+    query_iota = lax.broadcasted_iota(jnp.int32, (TILE, TILE), 1)
+    causal = key_iota <= query_iota
+    across = (((1,), (1,)), ((), ()))
+    for j in range(tiles):
+        k_at = pl.ds(j * TILE, TILE)
+        keys, values, keys_t = k_rows[k_at, :], v_rows[k_at, :], k_cols[:, k_at]
+        dk = dv = None
+        for i in range(j, tiles):
+            q_at = pl.ds(i * TILE, TILE)
+            queries, grads = q_rows[q_at, :], g_rows[q_at, :]
+            scores = lax.dot_general(keys, queries, across, preferred_element_type=jnp.float32)
+            allowed = key_iota >= first_ref[:, q_at] - j * TILE
+            if i == j:
+                allowed = allowed & causal
+            probs = jnp.exp2(jnp.where(allowed, scores * scale - log_ref[:, q_at], neg_large))
+            dprobs = lax.dot_general(values, grads, across, preferred_element_type=jnp.float32)
+            dscores = (probs * (dprobs - delta[:, q_at])).astype(jnp.bfloat16)
+            dv_tile = jnp.dot(probs.astype(jnp.bfloat16), grads, preferred_element_type=jnp.float32)
+            dk_tile = jnp.dot(dscores, queries, preferred_element_type=jnp.float32)
+            dq_tile = jnp.dot(keys_t, dscores, preferred_element_type=jnp.float32)
+            dv = dv_tile if dv is None else dv + dv_tile
+            dk = dk_tile if dk is None else dk + dk_tile
+            if j == 0:
+                dq_cols[:, q_at] = dq_tile
+            else:
+                dq_cols[:, q_at] += dq_tile
+        dq = (dq_cols[:, k_at] * HEAD_DIM**-0.5).T
+        dpack_ref[j, :TILE, :HEAD_DIM] = dq.astype(jnp.bfloat16)
+        dpack_ref[j, :TILE, HEAD_DIM:] = (dk * HEAD_DIM**-0.5).astype(jnp.bfloat16)
+        dpack_ref[j, TILE:, :] = halves_in(dv.astype(jnp.bfloat16))
+
+
+def whole(count):
+    return [pl.BlockSpec(memory_space=pltpu.VMEM)] * count
+
+
+def attn_forward(pack, first_row):
+    return pl.pallas_call(
+        attn_forward_kernel,
+        out_shape=(
+            jax.ShapeDtypeStruct((HEAD_DIM, FULL_TOK), jnp.float32),
+            jax.ShapeDtypeStruct((1, FULL_TOK), jnp.float32),
+        ),
+        in_specs=whole(2),
+        out_specs=tuple(whole(2)),
+        scratch_shapes=[
+            pltpu.VMEM((FULL_TOK, HEAD_DIM), jnp.bfloat16),
+            pltpu.VMEM((FULL_TOK, HEAD_DIM), jnp.bfloat16),
+            pltpu.VMEM((HEAD_DIM, FULL_TOK), jnp.bfloat16),
+        ],
+        compiler_params=pltpu.CompilerParams(vmem_limit_bytes=40 * 2**20),
+        cost_estimate=pl.CostEstimate(flops=2**30, bytes_accessed=2**21, transcendentals=2**21),
+        name="attn_forward",
+    )(pack, first_row)
+
+
+def attn_backward(pack, grads, out_cols, log_row, first_row):
+    rows = pltpu.VMEM((FULL_TOK, HEAD_DIM), jnp.bfloat16)
+    return pl.pallas_call(
+        attn_backward_kernel,
+        out_shape=jax.ShapeDtypeStruct(pack.shape, jnp.bfloat16),
+        in_specs=whole(5),
+        out_specs=whole(1)[0],
+        scratch_shapes=[
+            rows,
+            rows,
+            rows,
+            rows,
+            pltpu.VMEM((HEAD_DIM, FULL_TOK), jnp.bfloat16),
+            pltpu.VMEM((1, FULL_TOK), jnp.float32),
+            pltpu.VMEM((HEAD_DIM, FULL_TOK), jnp.float32),
+        ],
+        compiler_params=pltpu.CompilerParams(vmem_limit_bytes=40 * 2**20),
+        cost_estimate=pl.CostEstimate(flops=2**31, bytes_accessed=2**22, transcendentals=2**21),
+        name="attn_backward",
+    )(pack, grads, out_cols, log_row, first_row)
+
+
+def pick(stacked, index):
+    return lax.dynamic_index_in_dim(stacked, index, 0, keepdims=False)
+
+
+def swap_z(value, shift):
+    return lax.ppermute(value, "uly", [(i, i ^ shift) for i in range(4)])
+
+
+def sum_z(parts, place):
+    total = pick(parts, place).astype(jnp.float32)
+    for shift in (1, 2, 3):
+        total = total + swap_z(pick(parts, place ^ shift), shift).astype(jnp.float32)
+    return total
+
+
+SEND_A = ((0, 1), (1, 3), (2, 0), (3, 2))
+SEND_B = ((0, 2), (1, 0), (2, 3), (3, 1))
+PART_SELF, PART_A, PART_B = (0, 2, 0, 2), (1, 0, 2, 1), (2, 1, 1, 0)
+ORDER = ((0, 2, 1), (1, 0, 2), (2, 0, 1), (1, 2, 0))
+
+
+def at_place(table, place):
+    return pick(jnp.asarray(table, jnp.int32), place)
+
+
+def heads_of_place(shard, place):
+    groups = jnp.moveaxis(shard.reshape(shard.shape[0], 3, 192), 1, 0)
+    got = jnp.stack(
+        [
+            pick(groups, at_place(PART_SELF, place)),
+            lax.ppermute(pick(groups, at_place(PART_A, place)), "uly", SEND_A),
+            lax.ppermute(pick(groups, at_place(PART_B, place)), "uly", SEND_B),
+        ]
+    )
+    order = at_place(ORDER, place)
+    parts = jnp.stack([pick(got, order[p]) for p in range(3)], axis=1)
+    return parts.reshape(-1, 3, 3, HEAD_DIM).transpose(0, 2, 1, 3).reshape(-1, 576)
+
+
+def back_to_place(value, place):
+    parts = value.reshape(-1, 3, 3, HEAD_DIM).transpose(2, 0, 1, 3).reshape(3, -1, 192)
+    order = at_place(ORDER, place)
+    inverse = [
+        jnp.where(order[0] == n, 0, jnp.where(order[1] == n, 1, 2)) for n in range(3)
+    ]
+    own = pick(parts, inverse[0])
+    from_a = lax.ppermute(pick(parts, inverse[1]), "uly", [(d, s) for s, d in SEND_A])
+    from_b = lax.ppermute(pick(parts, inverse[2]), "uly", [(d, s) for s, d in SEND_B])
+    got = jnp.stack([own, from_a, from_b])
+    where_self, where_a = at_place(PART_SELF, place), at_place(PART_A, place)
+    groups = [
+        pick(got, jnp.where(where_self == g, 0, jnp.where(where_a == g, 1, 2))) for g in range(3)
+    ]
+    return jnp.concatenate(groups, axis=1)
+
+
+DOWN_MOVES = [(b * 4 + u, (2 * u + b % 2) * 4 + b // 2) for b in range(8) for u in range(4)]
+
+
+def norm_stats(values):
+    center = values - jnp.mean(values, axis=-1, keepdims=True)
+    scale = lax.rsqrt(jnp.mean(center * center, axis=-1, keepdims=True) + norm_epsilon)
+    return center * scale, scale
+
+
+def norm_back(grad_out, normal, scale, gain):
+    grad_normal = grad_out * gain
+    mean_one = jnp.mean(grad_normal, axis=-1, keepdims=True)
+    mean_two = jnp.mean(grad_normal * normal, axis=-1, keepdims=True)
+    return (grad_normal - mean_one - normal * mean_two) * scale
+
+
+def dot32(left, right, dims):
+    return lax.dot_general(left, right, (dims, ((), ())), preferred_element_type=jnp.float32)
+
+
+def local_fast(
+    inputs,
+    doc_starts,
+    out_grad,
+    first_gain,
+    first_bias,
+    query_key_value_weight,
+    attention_out_weight,
+    second_gain,
+    second_bias,
+    up_weight,
+    down_weight,
+):
+    bf16, f32 = jnp.bfloat16, jnp.float32
+    blk, uly = lax.axis_index("blk"), lax.axis_index("uly")
+    width = inputs.shape[2]
+
+    qkv_shard = heads_of_place(query_key_value_weight, uly)
+    vectors = jnp.stack([first_gain, first_bias, second_gain, second_bias], axis=1)
+    qkv_shard = jnp.concatenate([qkv_shard, jnp.pad(vectors, ((0, 0), (0, 60)))], axis=1)
+    qkv_full = lax.all_gather(qkv_shard, "blk", axis=0, tiled=True)
+    w_qkv = qkv_full[:, :576]
+    vectors = qkv_full[:, 576:580].astype(f32).T
+    gain_one, bias_one, gain_two, bias_two = (vectors[n : n + 1] for n in range(4))
+    starts = lax.all_gather(doc_starts, ("blk", "uly"), axis=1, tiled=True)
+    first_row = jnp.where(blk < 4, starts[0:1], starts[1:2])
+    x_rows = lax.all_gather(inputs, "uly", axis=1, tiled=True)
+    out_shard = lax.all_gather(attention_out_weight, "uly", axis=1, tiled=True)
+    down_shard = lax.ppermute(down_weight, ("blk", "uly"), DOWN_MOVES)
+    w_out = lax.all_gather(out_shard, "blk", axis=0, tiled=True)
+    w_up = lax.all_gather(up_weight, "blk", axis=0, tiled=True)
+    w_down = lax.all_gather(down_shard, "blk", axis=0)
+    w_down = w_down.reshape(4, 2, 384, 192).transpose(1, 2, 0, 3).reshape(768, 768)
+    g_rows = lax.all_gather(out_grad, "uly", axis=1, tiled=True)
+
+    residual = x_rows.astype(f32).reshape(512, width)
+    normal_one, scale_one = norm_stats(residual)
+    normed_one = (normal_one * gain_one + bias_one).astype(bf16)
+    qkv = dot32(normed_one, w_qkv, ((1,), (0,))).astype(bf16).reshape(2, 256, 3, 192)
+    qkv = jnp.concatenate([qkv, qkv[:, :, 2:]], axis=2).transpose(0, 2, 1, 3)
+    pack = jnp.concatenate([qkv[..., :128], halves_in(qkv[..., 128:])], axis=2)
+    pack = lax.all_to_all(pack.reshape(8, 384, 128), "blk", 0, 0, tiled=True)
+
+    out_cols, log_row = attn_forward(pack, first_row)
+    attn_pack = halves_in(
+        out_cols.astype(bf16).reshape(HEAD_DIM, 8, 256).transpose(1, 2, 0)
+    )
+    attn_pack = lax.all_to_all(attn_pack, "blk", 0, 0, tiled=True)
+    attn_pack = attn_pack.reshape(2, 4, 128, 128)[:, :3]
+    mixed = lax.all_gather(attn_pack, "uly", axis=0)
+    mixed = halves_out(mixed)
+    mixed = mixed.transpose(1, 3, 0, 2, 4).reshape(512, width)
+
+    middle = residual + branch_scale * dot32(mixed, w_out, ((1,), (0,)))
+    normal_two, scale_two = norm_stats(middle)
+    normed_two = (normal_two * gain_two + bias_two).astype(bf16)
+    pre_act = dot32(normed_two, w_up, ((1,), (0,)))
+    act, gate_back = jax.vjp(smooth_gate, pre_act)
+    act = act.astype(bf16)
+    grad_branch = (branch_scale * g_rows.astype(f32)).astype(bf16).reshape(512, width)
+    grad_act = dot32(grad_branch, w_down, ((1,), (1,)))
+    grad_pre = gate_back(grad_act)[0].astype(bf16)
+    grad_norm_two = dot32(grad_pre, w_up, ((1,), (1,))).astype(bf16)
+    chunks = lambda rows: rows.reshape(2, 4, 64, width).transpose(1, 0, 2, 3)
+    grad_norm_two = sum_z(chunks(grad_norm_two), uly)
+    feed = dot32(act, w_down, ((1,), (0,))).astype(bf16)
+    g_w_up = dot32(normed_two, grad_pre, ((0,), (0,)))
+    g_w_down = dot32(act, grad_branch, ((0,), (0,)))
+    g_w_down = g_w_down.reshape(2, 384, 4, 192).transpose(2, 0, 1, 3).reshape(8 * 384, 192)
+    g_w_up = lax.psum_scatter(g_w_up.astype(bf16), "blk", scatter_dimension=0, tiled=True)
+    g_w_down = lax.psum_scatter(g_w_down.astype(bf16), "blk", scatter_dimension=0, tiled=True)
+    back_moves = [(d, s) for s, d in DOWN_MOVES]
+    g_w_down = lax.ppermute(g_w_down, ("blk", "uly"), back_moves).astype(f32)
+
+    own = lambda rows: pick(chunks(rows), uly)
+    middle_own = own(middle)
+    output = (middle_own + branch_scale * sum_z(chunks(feed), uly)).astype(bf16)
+    normal_two_own, scale_two_own = norm_stats(middle_own)
+    grad_middle = out_grad.astype(f32) + norm_back(
+        grad_norm_two, normal_two_own, scale_two_own, gain_two
+    )
+    d_gain_two = jnp.sum(grad_norm_two * normal_two_own, axis=(0, 1))
+    d_bias_two = jnp.sum(grad_norm_two, axis=(0, 1))
+    grad_attn = (branch_scale * grad_middle).astype(bf16)
+    grad_mixed = dot32(grad_attn, w_out, ((2,), (1,))).astype(bf16)
+    grad_mixed = halves_in(grad_mixed.reshape(2, 64, 4, 3, HEAD_DIM).transpose(2, 0, 3, 1, 4))
+    grad_mixed = lax.all_to_all(grad_mixed, "uly", 0, 0, tiled=True)
+    grad_mixed = halves_out(grad_mixed).transpose(1, 2, 0, 3, 4).reshape(2, 3, 256, HEAD_DIM)
+    grad_mixed = jnp.concatenate([grad_mixed, grad_mixed[:, 2:]], axis=1)
+    grad_pack = halves_in(grad_mixed).reshape(8, 128, 128)
+    grad_pack = lax.all_to_all(grad_pack, "blk", 0, 0, tiled=True)
+
+    grad_cols = grad_attn.reshape(2, 64, 4, 192).transpose(2, 0, 1, 3)
+    grad_cols = lax.all_to_all(grad_cols, "uly", 0, 0, tiled=True)
+    grad_cols = grad_cols.transpose(1, 0, 2, 3).reshape(512, 192)
+    g_w_out = dot32(mixed, grad_cols, ((0,), (0,)))
+    g_w_out = lax.psum_scatter(g_w_out.astype(bf16), "blk", scatter_dimension=0, tiled=True)
+
+    dpack = attn_backward(pack, grad_pack, out_cols, log_row, first_row)
+    dpack = lax.all_to_all(dpack, "blk", 0, 0, tiled=True)
+    dpack = dpack.reshape(2, 4, 384, 128)[:, :3]
+    grad_qkv = jnp.concatenate([dpack[:, :, :256], halves_out(dpack[:, :, 256:])], axis=3)
+    grad_qkv = grad_qkv.transpose(0, 2, 1, 3).reshape(512, 576)
+    grad_norm_one = dot32(grad_qkv, w_qkv, ((1,), (1,)))
+    d_gain_one = jnp.sum(grad_norm_one * normal_one, axis=0)
+    d_bias_one = jnp.sum(grad_norm_one, axis=0)
+    grad_norm_one = sum_z(chunks(grad_norm_one.astype(bf16)), uly)
+    normal_own, scale_own = norm_stats(inputs.astype(f32))
+    grad_inputs = grad_middle + norm_back(grad_norm_one, normal_own, scale_own, gain_one)
+
+    g_w_qkv = dot32(normed_one, grad_qkv, ((0,), (0,)))
+    d_vectors = jnp.stack([d_gain_one, d_bias_one, d_gain_two, d_bias_two], axis=1)
+    tail = jnp.concatenate([g_w_qkv, jnp.pad(d_vectors, ((0, 0), (0, 60)))], axis=1)
+    tail = lax.psum_scatter(tail.astype(bf16), "blk", scatter_dimension=0, tiled=True).astype(f32)
+    g_w_qkv = back_to_place(tail[:, :576], uly)
+    d_vectors = tail[:, 576:580]
+    d_vectors = d_vectors + sum(swap_z(d_vectors, shift) for shift in (1, 2, 3))
+    return (
+        output,
+        grad_inputs,
+        d_vectors[:, 0],
+        d_vectors[:, 1],
+        g_w_qkv,
+        g_w_out.astype(f32),
+        d_vectors[:, 2],
+        d_vectors[:, 3],
+        g_w_up.astype(f32),
+        g_w_down,
+    )
+
+
 def solution(mesh):
+    local = local_fast if fits_fast(mesh) else local_general
     placed = (
         P(None, ("blk", "uly"), None),
         P(None, ("blk", "uly")),

time: 828 us -> 461 us (0.56)
  waiting for transfers between devices: 208 us -> 91.9 us
  local copies, waits for them, and re-layouts: 161 us -> 46 us
  loops' own time: 113 us -> 0 us
  blocking collectives: 213 us -> 155 us
  starting transfers between devices: 4.25 us -> 53.7 us
  matrix products: 65.1 us -> 26.8 us
  Pallas kernels: 0 us -> 20.9 us
  between operations: 17 us -> 35.3 us
  other arithmetic: 38.4 us -> 23.1 us
    reduce_scatter x6 -> x2, waiting for transfers between devices: 136 us -> 1.94 us  [the longest x1 1.94 us: local_fast(): lax.psum_scatter(g_w_up.astype(bf16), 'blk', scatter_dimension=0, tiled=T...]
    another operation x51 -> x0, loops' own time: 113 us -> none  [the longest x3 112 us: each_block(): lax.scan(advance, carried, (jnp.arange(block_count, dtype=jnp.int32), spl...]
    unnamed x3 -> x0, blocking collectives: 52.9 us -> none
    slice x161 -> x15, local copies, waits for them, and re-layouts: 49.9 us -> 4.01 us  [the longest x3 1.27 us: halves_out(): return jnp.concatenate([packed[..., :half], packed[..., half:]], axis=-2)]
    dynamic_slice x64 -> x13, local copies, waits for them, and re-layouts: 50.8 us -> 5.11 us  [pick(): return lax.dynamic_index_in_dim(stacked, index, 0, keepdims=False)]
    all_to_all x3 -> x1, blocking collectives: 55 us -> 9.82 us  [local_fast(): grad_mixed = lax.all_to_all(grad_mixed, 'uly', 0, 0, tiled=True)]
    all_gather x8 -> x6, blocking collectives: 105 us -> 145 us  [the longest x1 64.9 us: local_fast(): starts = lax.all_gather(doc_starts, ('blk', 'uly'), axis=1, tiled=True)]
    dot_general x65 -> x12, matrix products: 65.1 us -> 26.8 us  [dot32(): lax.dot_general(left, right, (dims, ((), ())), preferred_element_type=jnp...]
  transfers between devices with their start and end apart: 17 -> 30, of which waited for: 6 -> 14; matrix products, arithmetic and copies ran while one was open for 30% -> 17% of each run, Pallas kernels for 0% -> 5%
where the time goes in v1:
time: 461 us; the launch traced here: 452 us
  blocking collectives  155 us (34%)
  waiting for transfers between devices  91.9 us (20%)
  starting transfers between devices  53.7 us (12%)
  local copies, waits for them, and re-layouts  46 us (10%)
  between operations  35.3 us (8%)
  matrix products  26.8 us (6%)
  other arithmetic  23.1 us (5%)
  Pallas kernels  20.9 us (5%)
    all_gather x1, blocking collectives, local_fast(): starts = lax.all_gather(doc_starts, ('blk', 'uly'), axis=1, tiled=True)  64.9 us
    unnamed x9, waiting for transfers between devices  36.3 us
    dot_general x12, matrix products, dot32(): lax.dot_general(left, right, (dims, ((), ())), preferred_element_type=jnp...  26.8 us
    ppermute x12, waiting for transfers between devices, swap_z(): return lax.ppermute(value, 'uly', [(i, i ^ shift) for i in range(4)])  25 us
    ppermute x12, starting transfers between devices, swap_z(): return lax.ppermute(value, 'uly', [(i, i ^ shift) for i in range(4)])  20.4 us
    unnamed x124, local copies, waits for them, and re-layouts  19.3 us
    all_gather x1, blocking collectives, local_fast(): x_rows = lax.all_gather(inputs, 'uly', axis=1, tiled=True)  19 us
    all_gather x1, blocking collectives, local_fast(): mixed = lax.all_gather(attn_pack, 'uly', axis=0)  18.7 us
  transfers between devices with their start and end apart: 30, of which 14 were waited for; matrix products, arithmetic and copies ran while one was open for 17% of the time, Pallas kernels for 5%

profile of v1, /device:TPU:4, one launch (start us, length us, event | category | flops | bytes accessed | tf_op | source)
XLA Modules:
  0.0 452.3 jit_solution(15016529424594526732)
XLA Ops:
  8.2 14.0 %all_gather.38 = bf16[96,768]{0,1:T(8,128)(2,1)S(1)} all-gather(bf16[96,192]{0,1:T(8,128)(2,1)S(1)} %copy.140), channel_id=1, replica_groups=mesh['blk'=8,'uly'=4] {'uly'}, dimensions={1}, use_global_device_ids=true | all-gather | bytes 184320 | tf_op jit(solution)/shard_map/all_gather | solution.py:719
  23.1 2.5 collective-permute-start.2
  25.5 6.9 %collective-permute-done.2 = bf16[384,192]{0,1:T(8,128)(2,1)S(1)} collective-permute-done((bf16[384,192]{0,1:T(8,128)(2,1)}, bf16[384,192]{0,1:T(8,128)(2,1)S(1)}, u32[]{:S(2)}, u32[]{:S(2)}) %collective-permute-start.2) | collective-permute-done | bytes 147488 | tf_op jit(solution)/shard_map/ppermute | solution.py:720
  33.2 1.2 dynamic_slice.72
  35.7 1.2 dynamic_slice.75
  38.2 1.2 dynamic_slice.74
  44.2 3.1 collective-permute-start
  48.0 19.0 %all_gather.33 = bf16[2,256,768]{2,1,0:T(8,128)(2,1)S(1)} all-gather(bf16[2,64,768]{2,1,0:T(8,128)(2,1)S(1)} %copy-done.3), channel_id=1, replica_groups=mesh['blk'=8,'uly'=4] {'uly'}, dimensions={1}, use_global_device_ids=true | all-gather | bytes 983040 | tf_op jit(solution)/shard_map/all_gather | solution.py:718
  73.1 64.9 %all-gather.2 = s32[32,64,2]{1,2,0:T(2,128)S(1)} all-gather(s32[1,64,2]{1,2,0:T(2,128)S(1)} %bitcast.279), channel_id=1, replica_groups=mesh['blk'=8,'uly'=4] {'blk','uly'}, dimensions={0}, use_global_device_ids=true | all-gather | bytes 16896 | tf_op jit(solution)/shard_map/all_gather | solution.py:716
  140.8 10.3 %all_gather.34 = bf16[768,640]{1,0:T(8,128)(2,1)S(1)} all-gather(bf16[96,640]{1,0:T(8,128)(2,1)S(1)} %copy.133), channel_id=1, replica_groups=mesh['blk'=8,'uly'=4] {'blk'}, dimensions={0}, use_global_device_ids=true | all-gather | bytes 1105920 | tf_op jit(solution)/shard_map/all_gather | solution.py:712
  156.2 4.5 all-to-all-start
  160.7 17.8 %all_gather.43 = bf16[2,256,768]{2,1,0:T(8,128)(2,1)S(1)} all-gather(bf16[2,64,768]{2,1,0:T(8,128)(2,1)S(1)} %copy-done.8), channel_id=1, replica_groups=mesh['blk'=8,'uly'=4] {'uly'}, dimensions={1}, use_global_device_ids=true | all-gather | bytes 983040 | tf_op jit(solution)/shard_map/all_gather | solution.py:725
  178.5 10.6 %attn_forward.1 = (f32[64,2048]{1,0:T(8,128)S(1)}, f32[1,2048]{1,0:T(1,128)S(1)}) custom-call(bf16[8,384,128]{2,1,0:T(8,128)(2,1)S(1)} %all-to-all-done.pack_ref, s32[1,2048]{1,0:T(1,128)S(1)} %broadcast_select_fusion.first_ref), custom_call_target="tpu_custom_call" | custom-call | flops 1073741824 | bytes 2097152 | tf_op jit(solution)/shard_map/attn_forward/pallas_call | solution.py:575
  190.0 4.2 all-to-all-start.1
  195.2 4.4 all-to-all-done.1
  199.8 18.7 %all-gather = bf16[8,3,128,128]{3,2,1,0:T(8,128)(2,1)S(1)} all-gather(bf16[2,3,128,128]{3,2,1,0:T(8,128)(2,1)S(1)} %copy.169), channel_id=2, replica_groups=mesh['blk'=8,'uly'=4] {'uly'}, dimensions={0}, use_global_device_ids=true | all-gather | bytes 983040 | tf_op jit(solution)/shard_map/all_gather | solution.py:741
  218.9 1.6 maximum_bitcast_fusion
  220.5 3.3 copy.139
  223.9 1.3 copy.179
  225.2 2.5 fusion.93
  229.2 3.3 reshape.324
  234.6 2.0 fusion.94
  236.6 5.1 %fusion.6 = (bf16[512,768]{1,0:T(8,128)(2,1)S(1)}, f32[512,768]{1,0:T(8,128)}) fusion(f32[512,768]{1,0:T(8,128)} %fusion.94, bf16[768,768]{1,0:T(8,128)(2,1)} %all-gather.9.cloned.1.call-done, f32[512,768]{1,0:T(8,128)} %copy-done, f32[768]{0:T(1024)S(1)} %get-tuple-element.23, f32[768]{0:T(1024)S(1)} %get-tuple-element.22, f32[512]{0:T(512)S(1)} %add_rsqrt_fusion, ...), kind=kOutput, calls=%fused_computation.9 | convolution fusion | flops 613810176 | bytes 6694912 | tf_op jit(solution)/shard_map/dot_general | solution.py:689
  242.7 1.8 collective-permute-start.8
  244.4 2.7 collective-permute-start.6
  247.1 4.8 %collective-permute-done.8 = bf16[2,64,768]{2,1,0:T(8,128)(2,1)S(1)} collective-permute-done((bf16[2,64,768]{2,1,0:T(8,128)(2,1)S(1)}, bf16[2,64,768]{2,1,0:T(8,128)(2,1)S(1)}, u32[]{:S(2)}, u32[]{:S(2)}) %collective-permute-start.8) | collective-permute-done | bytes 196640 | tf_op jit(solution)/shard_map/ppermute | solution.py:621
  251.9 6.6 %collective-permute-done.7 = bf16[2,64,768]{2,1,0:T(8,128)(2,1)S(1)} collective-permute-done((bf16[2,64,768]{2,1,0:T(8,128)(2,1)S(1)}, bf16[2,64,768]{2,1,0:T(8,128)(2,1)S(1)}, u32[]{:S(2)}, u32[]{:S(2)}) %collective-permute-start.7) | collective-permute-done | bytes 196640 | tf_op jit(solution)/shard_map/ppermute | solution.py:621
  261.3 3.5 all-to-all-start.5
  266.0 5.9 %all-to-all-done.5 = bf16[4,2,64,192]{3,2,1,0:T(8,128)(2,1)S(1)} async-done(((bf16[4,2,64,192]{3,2,1,0:T(8,128)(2,1)}), bf16[4,2,64,192]{3,2,1,0:T(8,128)(2,1)S(1)}, u32[]{:S(2)}, u32[]{:S(2)}) %all-to-all-start.5) | async-done | bytes 196640 | tf_op jit(solution)/shard_map/all_to_all | solution.py:785
  271.9 2.2 convolution_convert_fusion.6
  274.2 1.9 fusion.14
  276.1 1.2 copy.162
  277.3 3.3 fusion.27
  280.6 2.5 copy.167
  283.1 1.8 fusion.30
  285.9 9.8 %all_to_all.30 = bf16[4,2,3,32,128]{4,3,2,1,0:T(8,128)(2,1)S(1)} all-to-all(bf16[4,2,3,32,128]{4,3,2,1,0:T(8,128)(2,1)S(1)} %copy.145), channel_id=1, replica_groups=mesh['blk'=8,'uly'=4] {'uly'}, dimensions={0} | all-to-all | bytes 393216 | tf_op jit(solution)/shard_map/all_to_all | solution.py:778
  297.5 5.0 %all-to-all-start.3 = ((bf16[8,128,128]{2,1,0:T(8,128)(2,1)}), bf16[8,128,128]{2,1,0:T(8,128)(2,1)S(1)}, u32[]{:S(2)}, u32[]{:S(2)}) async-start(bf16[8,128,128]{2,1,0:T(8,128)(2,1)} %bitcast.49), calls=%async_computation.3 | async-start | bytes 524288 | tf_op jit(solution)/shard_map/all_to_all | solution.py:782
  302.6 5.8 %all-to-all-done.3.grad_ref = bf16[8,128,128]{2,1,0:T(8,128)(2,1)S(1)} async-done(((bf16[8,128,128]{2,1,0:T(8,128)(2,1)}), bf16[8,128,128]{2,1,0:T(8,128)(2,1)S(1)}, u32[]{:S(2)}, u32[]{:S(2)}) %all-to-all-start.3) | async-done | bytes 262176 | tf_op jit(solution)/shard_map/all_to_all | solution.py:782
  308.4 10.3 %attn_backward.1 = bf16[8,384,128]{2,1,0:T(8,128)(2,1)} custom-call(bf16[8,384,128]{2,1,0:T(8,128)(2,1)S(1)} %all-to-all-done.pack_ref, bf16[8,128,128]{2,1,0:T(8,128)(2,1)S(1)} %all-to-all-done.3.grad_ref, f32[64,2048]{1,0:T(8,128)S(1)} %get-tuple-element.12.out_cols, f32[1,2048]{1,0:T(1,128)S(1)} %get-tuple-element.13.log_ref, ...), custom_call_target="tpu_custom_call" | custom-call | flops 2147483648 | bytes 4194304 | tf_op jit(solution)/shard_map/attn_backward/pallas_call | solution.py:596
  318.8 5.1 %all-to-all-start.4 = ((bf16[8,384,128]{2,1,0:T(8,128)(2,1)}), bf16[8,384,128]{2,1,0:T(8,128)(2,1)S(1)}, u32[]{:S(2)}, u32[]{:S(2)}) async-start(bf16[8,384,128]{2,1,0:T(8,128)(2,1)} %attn_backward.1), calls=%async_computation.4 | async-start | bytes 1572864 | tf_op jit(solution)/shard_map/all_to_all | solution.py:791
  324.0 3.2 convolution_convert_fusion.1
  336.2 1.3 fusion.20
  340.9 1.5 copy.172
  343.6 1.9 fusion.26
  346.2 1.3 copy.163
  349.2 1.6 collective-permute-start.10
  350.8 2.0 collective-permute-start.9
  352.8 2.8 convolution_convert_fusion.4
  358.7 1.4 convert_element_type.173
  360.2 5.6 %collective-permute-start.3 = (bf16[2,64,768]{2,1,0:T(8,128)(2,1)S(1)}, bf16[2,64,768]{2,1,0:T(8,128)(2,1)}, u32[]{:S(2)}, u32[]{:S(2)}) collective-permute-start(bf16[2,64,768]{2,1,0:T(8,128)(2,1)S(1)} %get-tuple-element.41), channel_id=1, source_target_pairs={{0,1},{1,0},{2,3},{3,2},{4,5},{5,4},{6,7},{7,6},{8,9},{9,8},{10,11... | collective-permute-start | bytes 589832 | tf_op jit(solution)/shard_map/ppermute | solution.py:621
  365.8 12.1 %collective-permute-done.10 = bf16[2,64,768]{2,1,0:T(8,128)(2,1)S(1)} collective-permute-done((bf16[2,64,768]{2,1,0:T(8,128)(2,1)}, bf16[2,64,768]{2,1,0:T(8,128)(2,1)S(1)}, u32[]{:S(2)}, u32[]{:S(2)}) %collective-permute-start.10) | collective-permute-done | bytes 196640 | tf_op jit(solution)/shard_map/ppermute | solution.py:621
  378.5 1.5 fusion.83
  380.6 1.7 copy.166
  382.3 1.9 collective-permute-start.17
  384.2 1.2 collective-permute-done.4
  385.5 2.2 fusion.47
  387.7 1.9 reduce-scatter.11.cloned.1.call-done
  389.6 1.6 convert_element_type.175
  391.2 2.7 collective-permute-done.17
  394.0 1.6 convert_element_type.180
  395.6 36.2 %reduce-scatter.13.cloned.1.call-done = bf16[96,640]{1,0:T(8,128)(2,1)} async-done(((bf16[768,640]{1,0:T(8,128)(2,1)}), bf16[96,640]{1,0:T(8,128)(2,1)}) %reduce-scatter.13.cloned.1.call-update) | async-done | bytes 122896
  432.9 3.4 collective-permute-start.14
  438.5 2.0 collective-permute-start.15
  441.3 2.0 collective-permute-done.16
  (260 shorter events, 44.4 us)
Async XLA Ops:
  7.2 40.8 %copy-start.3 = (bf16[2,64,768]{2,1,0:T(8,128)(2,1)S(1)}, bf16[2,64,768]{2,1,0:T(8,128)(2,1)}, u32[]{:S(2)}) copy-start(bf16[2,64,768]{2,1,0:T(8,128)(2,1)} %param.18) | copy-start | bytes 589828
  7.2 218.0 %all-gather.7.cloned.1.call-start = ((), (), s32[]{:S(2)}) async-start(), calls=%async_computation.10 | async-start | bytes 1327104 | tf_op jit(solution)/shard_map/all_gather | solution.py:721
  23.0 206.1 %all-gather.11.cloned.1.call-start = ((), (), s32[]{:S(2)}) async-start(), calls=%async_computation.14 | async-start | bytes 1327104 | tf_op jit(solution)/shard_map/all_gather | solution.py:723
  23.1 9.4 %collective-permute-start.2 = (bf16[384,192]{0,1:T(8,128)(2,1)}, bf16[384,192]{0,1:T(8,128)(2,1)S(1)}, u32[]{:S(2)}, u32[]{:S(2)}) collective-permute-start(bf16[384,192]{0,1:T(8,128)(2,1)} %param.28), channel_id=1, source_target_pairs={{0,0},{1,8},{2,16},{3,24},{4,4},{5,12},{6,20},{7,28},{8,1},{9,9},{... | collective-permute-start | bytes 442376 | tf_op jit(solution)/shard_map/ppermute | solution.py:720
  33.1 203.5 %all-gather.9.cloned.1.call-start = ((), (), s32[]{:S(2)}) async-start(), calls=%async_computation.11 | async-start | bytes 1327104 | tf_op jit(solution)/shard_map/all_gather | solution.py:722
  43.8 24.4 %copy-start.48 = (bf16[96]{0:T(256)(128)(2,1)S(1)}, bf16[96]{0:T(256)(128)(2,1)}, u32[]{:S(2)}) copy-start(bf16[96]{0:T(256)(128)(2,1)} %param.26) | copy-start | bytes 580
  43.8 24.4 %copy-start.49 = (bf16[96]{0:T(256)(128)(2,1)S(1)}, bf16[96]{0:T(256)(128)(2,1)}, u32[]{:S(2)}) copy-start(bf16[96]{0:T(256)(128)(2,1)} %param.25) | copy-start | bytes 580
  43.8 24.4 %copy-start.50 = (bf16[96]{0:T(256)(128)(2,1)S(1)}, bf16[96]{0:T(256)(128)(2,1)}, u32[]{:S(2)}) copy-start(bf16[96]{0:T(256)(128)(2,1)} %param.22) | copy-start | bytes 580
  43.8 24.4 %copy-start.51 = (bf16[96]{0:T(256)(128)(2,1)S(1)}, bf16[96]{0:T(256)(128)(2,1)}, u32[]{:S(2)}) copy-start(bf16[96]{0:T(256)(128)(2,1)} %param.21) | copy-start | bytes 580
  43.9 29.2 %copy-start.47 = (s32[2,64]{1,0:T(2,128)S(1)}, s32[2,64]{1,0:T(2,128)}, u32[]{:S(2)}) copy-start(s32[2,64]{1,0:T(2,128)} %param.19) | copy-start | bytes 1540
  44.0 96.1 %collective-permute-start.1 = (bf16[96,192]{1,0:T(8,128)(2,1)S(1)}, bf16[96,192]{1,0:T(8,128)(2,1)S(1)}, u32[]{:S(2)}, u32[]{:S(2)}) collective-permute-start(bf16[96,192]{1,0:T(8,128)(2,1)S(1)} %bitcast.273), channel_id=1, source_target_pairs={{0,2},{1,0},{2,3},{3,1},{4,6},{5,4},{6,7},{7,5},{8,10},{9,8},{10,1... | collective-permute-start | bytes 110600 | tf_op jit(solution)/shard_map/ppermute | solution.py:647
  44.2 95.9 %collective-permute-start = (bf16[96,192]{1,0:T(8,128)(2,1)S(1)}, bf16[96,192]{1,0:T(8,128)(2,1)S(1)}, u32[]{:S(2)}, u32[]{:S(2)}) collective-permute-start(bf16[96,192]{1,0:T(8,128)(2,1)S(1)} %bitcast.274), channel_id=1, source_target_pairs={{0,1},{1,3},{2,0},{3,2},{4,5},{5,7},{6,4},{7,6},{8,9},{9,11},{10,8... | collective-permute-start | bytes 110600 | tf_op jit(solution)/shard_map/ppermute | solution.py:646
  73.0 79.0 %copy-start.35 = (f32[1,2,2,128]{3,1,2,0:T(2,128)}, f32[1,2,2,128]{3,1,2,0:T(2,128)S(1)}, u32[]{:S(2)}) copy-start(f32[1,2,2,128]{3,1,2,0:T(2,128)S(1)} %copy.178) | copy-start | bytes 6148
  73.0 79.0 %copy-start.37 = (f32[1,2,2,128]{3,1,2,0:T(2,128)}, f32[1,2,2,128]{3,1,2,0:T(2,128)S(1)}, u32[]{:S(2)}) copy-start(f32[1,2,2,128]{3,1,2,0:T(2,128)S(1)} %copy.177) | copy-start | bytes 6148
  152.0 84.5 %copy-start.43 = (f32[768]{0:T(1024)}, f32[768]{0:T(1024)S(1)}, u32[]{:S(2)}) copy-start(f32[768]{0:T(1024)S(1)} %get-tuple-element.23) | copy-start | bytes 9220
  152.0 107.3 %copy-start.20 = (f32[768]{0:T(1024)}, f32[768]{0:T(1024)S(1)}, u32[]{:S(2)}) copy-start(f32[768]{0:T(1024)S(1)} %get-tuple-element.22) | copy-start | bytes 9220
  155.1 5.6 %copy-start.8 = (bf16[2,64,768]{2,1,0:T(8,128)(2,1)S(1)}, bf16[2,64,768]{2,1,0:T(8,128)(2,1)}, u32[]{:S(2)}) copy-start(bf16[2,64,768]{2,1,0:T(8,128)(2,1)} %param.20) | copy-start | bytes 589828
  156.2 22.3 %all-to-all-start = ((bf16[8,384,128]{2,1,0:T(8,128)(2,1)}), bf16[8,384,128]{2,1,0:T(8,128)(2,1)S(1)}, u32[]{:S(2)}, u32[]{:S(2)}) async-start(bf16[8,384,128]{2,1,0:T(8,128)(2,1)} %bitcast.24), calls=%async_computation | async-start | bytes 1572864 | tf_op jit(solution)/shard_map/all_to_all | solution.py:733
  190.0 9.7 %all-to-all-start.1 = ((bf16[8,128,128]{1,2,0:T(8,128)(2,1)}), bf16[8,128,128]{1,2,0:T(8,128)(2,1)S(1)}, u32[]{:S(2)}, u32[]{:S(2)}) async-start(bf16[8,128,128]{1,2,0:T(8,128)(2,1)} %pad_maximum_fusion.3), calls=%async_computation.1 | async-start | bytes 524288 | tf_op jit(solution)/shard_map/all_to_all | solution.py:739
  225.2 2.5 copy-start.7
  227.8 31.6 %copy-start.26 = (f32[2,64]{1,0:T(2,128)}, f32[2,64]{1,0:T(2,128)S(1)}, u32[]{:S(2)}) copy-start(f32[2,64]{1,0:T(2,128)S(1)} %broadcast_multiply_fusion.6) | copy-start | bytes 1540
  228.8 7.8 %copy-start.41 = (f32[512]{0:T(512)}, f32[512]{0:T(512)S(1)}, u32[]{:S(2)}) copy-start(f32[512]{0:T(512)S(1)} %broadcast_multiply_fusion) | copy-start | bytes 6148
  229.1 7.5 %copy-start.45 = (f32[512]{0:T(512)}, f32[512]{0:T(512)S(1)}, u32[]{:S(2)}) copy-start(f32[512]{0:T(512)S(1)} %add_rsqrt_fusion) | copy-start | bytes 6148
  236.6 5.1 %copy-start.52 = (bf16[768,768]{1,0:T(8,128)(2,1)S(1)}, bf16[768,768]{1,0:T(8,128)(2,1)}, u32[]{:S(2)}) copy-start(bf16[768,768]{1,0:T(8,128)(2,1)} %all-gather.9.cloned.1.call-done) | copy-start | bytes 3538948
  241.7 16.8 %copy-start.1 = (f32[512,768]{1,0:T(8,128)S(1)}, f32[512,768]{1,0:T(8,128)}, u32[]{:S(2)}) copy-start(f32[512,768]{1,0:T(8,128)} %copy-done) | copy-start | bytes 4718596
  242.6 17.5 %copy-start.9 = (bf16[2,64,768]{2,1,0:T(8,128)(2,1)S(1)}, bf16[2,64,768]{2,1,0:T(8,128)(2,1)}, u32[]{:S(2)}) copy-start(bf16[2,64,768]{2,1,0:T(8,128)(2,1)} %param.20) | copy-start | bytes 589828
  242.7 9.2 %collective-permute-start.8 = (bf16[2,64,768]{2,1,0:T(8,128)(2,1)S(1)}, bf16[2,64,768]{2,1,0:T(8,128)(2,1)S(1)}, u32[]{:S(2)}, u32[]{:S(2)}) collective-permute-start(bf16[2,64,768]{2,1,0:T(8,128)(2,1)S(1)} %get-tuple-element.39), channel_id=1, source_target_pairs={{0,3},{1,2},{2,1},{3,0},{4,7},{5,6},{6,5},{7,4},{8,11},{9,10},{10,... | collective-permute-start | bytes 589832 | tf_op jit(solution)/shard_map/ppermute | solution.py:621
  244.4 14.1 %collective-permute-start.7 = (bf16[2,64,768]{2,1,0:T(8,128)(2,1)S(1)}, bf16[2,64,768]{2,1,0:T(8,128)(2,1)S(1)}, u32[]{:S(2)}, u32[]{:S(2)}) collective-permute-start(bf16[2,64,768]{2,1,0:T(8,128)(2,1)S(1)} %get-tuple-element.40), channel_id=1, source_target_pairs={{0,2},{1,3},{2,0},{3,1},{4,6},{5,7},{6,4},{7,5},{8,10},{9,11},{10,... | collective-permute-start | bytes 589832 | tf_op jit(solution)/shard_map/ppermute | solution.py:621
  244.4 14.1 %collective-permute-start.6 = (bf16[2,64,768]{2,1,0:T(8,128)(2,1)S(1)}, bf16[2,64,768]{2,1,0:T(8,128)(2,1)S(1)}, u32[]{:S(2)}, u32[]{:S(2)}) collective-permute-start(bf16[2,64,768]{2,1,0:T(8,128)(2,1)S(1)} %get-tuple-element.38), channel_id=1, source_target_pairs={{0,1},{1,0},{2,3},{3,2},{4,5},{5,4},{6,7},{7,6},{8,9},{9,8},{10,11... | collective-permute-start | bytes 589832 | tf_op jit(solution)/shard_map/ppermute | solution.py:621
  247.1 12.3 %copy-start.30 = (f32[2,64]{1,0:T(2,128)}, f32[2,64]{1,0:T(2,128)S(1)}, u32[]{:S(2)}) copy-start(f32[2,64]{1,0:T(2,128)S(1)} %add_rsqrt_fusion.3) | copy-start | bytes 1540
  261.3 10.5 %all-to-all-start.5 = ((bf16[4,2,64,192]{3,2,1,0:T(8,128)(2,1)}), bf16[4,2,64,192]{3,2,1,0:T(8,128)(2,1)S(1)}, u32[]{:S(2)}, u32[]{:S(2)}) async-start(bf16[4,2,64,192]{3,2,1,0:T(8,128)(2,1)} %copy.156), calls=%async_computation.5 | async-start | bytes 524288 | tf_op jit(solution)/shard_map/all_to_all | solution.py:785
  264.8 93.9 %reduce-scatter.9.cloned.1.call-start = ((), (), s32[]{:S(2)}) async-start(), calls=%async_computation.12 | async-start | bytes 442368 | tf_op jit(solution)/shard_map/reduce_scatter | solution.py:788
  274.1 106.5 %reduce-scatter.15.cloned.1.call-start = ((), (), s32[]{:S(2)}) async-start(), calls=%async_computation.16 | async-start | bytes 1769472
  297.5 11.0 %all-to-all-start.3 = ((bf16[8,128,128]{2,1,0:T(8,128)(2,1)}), bf16[8,128,128]{2,1,0:T(8,128)(2,1)S(1)}, u32[]{:S(2)}, u32[]{:S(2)}) async-start(bf16[8,128,128]{2,1,0:T(8,128)(2,1)} %bitcast.49), calls=%async_computation.3 | async-start | bytes 524288 | tf_op jit(solution)/shard_map/all_to_all | solution.py:782
  308.4 15.5 %copy-start.21 = (f32[768]{0:T(1024)S(1)}, f32[768]{0:T(1024)}, u32[]{:S(2)}) copy-start(f32[768]{0:T(1024)} %copy-done.20) | copy-start | bytes 9220
  308.4 15.5 %copy-start.42 = (f32[512]{0:T(512)S(1)}, f32[512]{0:T(512)}, u32[]{:S(2)}) copy-start(f32[512]{0:T(512)} %copy-done.41) | copy-start | bytes 6148
  308.4 15.5 %copy-start.44 = (f32[768]{0:T(1024)S(1)}, f32[768]{0:T(1024)}, u32[]{:S(2)}) copy-start(f32[768]{0:T(1024)} %copy-done.43) | copy-start | bytes 9220
  308.4 15.5 %copy-start.46 = (f32[512]{0:T(512)S(1)}, f32[512]{0:T(512)}, u32[]{:S(2)}) copy-start(f32[512]{0:T(512)} %copy-done.45) | copy-start | bytes 6148
  318.8 5.2 %copy-start.2 = (f32[512,768]{1,0:T(8,128)S(1)}, f32[512,768]{1,0:T(8,128)}, u32[]{:S(2)}) copy-start(f32[512,768]{1,0:T(8,128)} %copy-done) | copy-start | bytes 4718596
  318.8 19.3 %all-to-all-start.4 = ((bf16[8,384,128]{2,1,0:T(8,128)(2,1)}), bf16[8,384,128]{2,1,0:T(8,128)(2,1)S(1)}, u32[]{:S(2)}, u32[]{:S(2)}) async-start(bf16[8,384,128]{2,1,0:T(8,128)(2,1)} %attn_backward.1), calls=%async_computation.4 | async-start | bytes 1572864 | tf_op jit(solution)/shard_map/all_to_all | solution.py:791
  323.9 12.3 %copy-start.23 = (f32[768]{0:T(1024)S(1)}, f32[768]{0:T(1024)}, u32[]{:S(2)}) copy-start(f32[768]{0:T(1024)} %copy-done.22) | copy-start | bytes 9220
  323.9 12.3 %copy-start.25 = (f32[768]{0:T(1024)S(1)}, f32[768]{0:T(1024)}, u32[]{:S(2)}) copy-start(f32[768]{0:T(1024)} %copy-done.24) | copy-start | bytes 9220
  323.9 12.3 %copy-start.29 = (f32[2,256]{1,0:T(2,128)S(1)}, f32[2,256]{1,0:T(2,128)}, u32[]{:S(2)}) copy-start(f32[2,256]{1,0:T(2,128)} %copy-done.28) | copy-start | bytes 6148
  323.9 12.3 %copy-start.34 = (f32[2,256]{1,0:T(2,128)S(1)}, f32[2,256]{1,0:T(2,128)}, u32[]{:S(2)}) copy-start(f32[2,256]{1,0:T(2,128)} %get-tuple-element.68) | copy-start | bytes 6148
  323.9 65.7 %reduce-scatter.11.cloned.1.call-start = ((), (), s32[]{:S(2)}) async-start(), calls=%async_computation.13 | async-start | bytes 1327104 | tf_op jit(solution)/shard_map/reduce_scatter | solution.py:761
  327.1 10.3 %copy-start.40 = (bf16[768]{0:T(1024)(128)(2,1)S(1)}, bf16[768]{0:T(1024)(128)(2,1)}, u32[]{:S(2)}) copy-start(bf16[768]{0:T(1024)(128)(2,1)} %get-tuple-element.19) | copy-start | bytes 4612
  327.1 10.3 %copy-start.39 = (bf16[768]{0:T(1024)(128)(2,1)S(1)}, bf16[768]{0:T(1024)(128)(2,1)}, u32[]{:S(2)}) copy-start(bf16[768]{0:T(1024)(128)(2,1)} %get-tuple-element.14) | copy-start | bytes 4612
  327.2 104.6 %reduce-scatter.13.cloned.1.call-start = ((), (), s32[]{:S(2)}) async-start(), calls=%async_computation.15 | async-start | bytes 1105920
  348.4 11.8 %collective-permute-start.11 = (bf16[2,64,768]{2,1,0:T(8,128)(2,1)}, bf16[2,64,768]{2,1,0:T(8,128)(2,1)S(1)}, u32[]{:S(2)}, u32[]{:S(2)}) collective-permute-start(bf16[2,64,768]{2,1,0:T(8,128)(2,1)} %get-tuple-element.34), channel_id=1, source_target_pairs={{0,3},{1,2},{2,1},{3,0},{4,7},{5,6},{6,5},{7,4},{8,11},{9,10},{10,... | collective-permute-start | bytes 589832 | tf_op jit(solution)/shard_map/ppermute | solution.py:621
  349.2 28.7 %collective-permute-start.10 = (bf16[2,64,768]{2,1,0:T(8,128)(2,1)}, bf16[2,64,768]{2,1,0:T(8,128)(2,1)S(1)}, u32[]{:S(2)}, u32[]{:S(2)}) collective-permute-start(bf16[2,64,768]{2,1,0:T(8,128)(2,1)} %get-tuple-element.35), channel_id=1, source_target_pairs={{0,2},{1,3},{2,0},{3,1},{4,6},{5,7},{6,4},{7,5},{8,10},{9,11},{10,... | collective-permute-start | bytes 589832 | tf_op jit(solution)/shard_map/ppermute | solution.py:621
  350.8 27.7 %collective-permute-start.9 = (bf16[2,64,768]{2,1,0:T(8,128)(2,1)}, bf16[2,64,768]{2,1,0:T(8,128)(2,1)}, u32[]{:S(2)}, u32[]{:S(2)}) collective-permute-start(bf16[2,64,768]{2,1,0:T(8,128)(2,1)} %get-tuple-element.33), channel_id=1, source_target_pairs={{0,1},{1,0},{2,3},{3,2},{4,5},{5,4},{6,7},{7,6},{8,9},{9,8},{10,11... | collective-permute-start | bytes 589832 | tf_op jit(solution)/shard_map/ppermute | solution.py:621
  355.6 29.8 %copy-start.5 = (f32[2,64,768]{2,1,0:T(8,128)S(1)}, f32[2,64,768]{2,1,0:T(8,128)}, u32[]{:S(2)}) copy-start(f32[2,64,768]{2,1,0:T(8,128)} %copy-done.4) | copy-start | bytes 1179652
  355.6 29.8 %copy-start.10 = (bf16[2,64,768]{2,1,0:T(8,128)(2,1)S(1)}, bf16[2,64,768]{2,1,0:T(8,128)(2,1)}, u32[]{:S(2)}) copy-start(bf16[2,64,768]{2,1,0:T(8,128)(2,1)} %param.20) | copy-start | bytes 589828
  355.6 29.8 %copy-start.27 = (f32[2,64]{1,0:T(2,128)S(1)}, f32[2,64]{1,0:T(2,128)}, u32[]{:S(2)}) copy-start(f32[2,64]{1,0:T(2,128)} %copy-done.26) | copy-start | bytes 1540
  357.2 27.0 %collective-permute-start.5 = (bf16[2,64,768]{2,1,0:T(8,128)(2,1)}, bf16[2,64,768]{2,1,0:T(8,128)(2,1)S(1)}, u32[]{:S(2)}, u32[]{:S(2)}) collective-permute-start(bf16[2,64,768]{2,1,0:T(8,128)(2,1)} %get-tuple-element.42), channel_id=1, source_target_pairs={{0,3},{1,2},{2,1},{3,0},{4,7},{5,6},{6,5},{7,4},{8,11},{9,10},{10,... | collective-permute-start | bytes 589832 | tf_op jit(solution)/shard_map/ppermute | solution.py:621
  358.0 27.5 %collective-permute-start.4 = (bf16[2,64,768]{2,1,0:T(8,128)(2,1)S(1)}, bf16[2,64,768]{2,1,0:T(8,128)(2,1)S(1)}, u32[]{:S(2)}, u32[]{:S(2)}) collective-permute-start(bf16[2,64,768]{2,1,0:T(8,128)(2,1)S(1)} %get-tuple-element.43), channel_id=1, source_target_pairs={{0,2},{1,3},{2,0},{3,1},{4,6},{5,7},{6,4},{7,5},{8,10},{9,11},{10,... | collective-permute-start | bytes 589832 | tf_op jit(solution)/shard_map/ppermute | solution.py:621
  360.2 17.7 %copy-start.17 = (bf16[2,64,768]{2,1,0:T(8,128)(2,1)}, bf16[2,64,768]{2,1,0:T(8,128)(2,1)S(1)}, u32[]{:S(2)}) copy-start(bf16[2,64,768]{2,1,0:T(8,128)(2,1)S(1)} %collective-permute-done.11) | copy-start | bytes 589828
  360.2 25.3 %collective-permute-start.3 = (bf16[2,64,768]{2,1,0:T(8,128)(2,1)S(1)}, bf16[2,64,768]{2,1,0:T(8,128)(2,1)}, u32[]{:S(2)}, u32[]{:S(2)}) collective-permute-start(bf16[2,64,768]{2,1,0:T(8,128)(2,1)S(1)} %get-tuple-element.41), channel_id=1, source_target_pairs={{0,1},{1,0},{2,3},{3,2},{4,5},{5,4},{6,7},{7,6},{8,9},{9,8},{10,11... | collective-permute-start | bytes 589832 | tf_op jit(solution)/shard_map/ppermute | solution.py:621
  382.3 11.7 %collective-permute-start.17 = (bf16[384,192]{0,1:T(8,128)(2,1)}, bf16[384,192]{0,1:T(8,128)(2,1)}, u32[]{:S(2)}, u32[]{:S(2)}) collective-permute-start(bf16[384,192]{0,1:T(8,128)(2,1)} %copy.166), channel_id=1, source_target_pairs={{0,0},{8,1},{16,2},{24,3},{4,4},{12,5},{20,6},{28,7},{1,8},{9,9},{... | collective-permute-start | bytes 442376 | tf_op jit(solution)/shard_map/ppermute | solution.py:764
  432.9 7.6 %collective-permute-start.14 = (f32[96,4]{0,1:T(4,128)S(1)}, f32[96,4]{0,1:T(4,128)S(1)}, u32[]{:S(2)}, u32[]{:S(2)}) collective-permute-start(f32[96,4]{0,1:T(4,128)S(1)} %slice.197), channel_id=1, source_target_pairs={{0,3},{1,2},{2,1},{3,0},{4,7},{5,6},{6,5},{7,4},{8,11},{9,10},{10,... | collective-permute-start | bytes 4616 | tf_op jit(solution)/shard_map/ppermute | solution.py:621
  436.3 4.2 collective-permute-start.12
  436.3 4.5 collective-permute-start.13
  437.5 5.8 %collective-permute-start.16 = (f32[96,192]{0,1:T(8,128)S(1)}, f32[96,192]{0,1:T(8,128)S(1)}, u32[]{:S(2)}, u32[]{:S(2)}) collective-permute-start(f32[96,192]{0,1:T(8,128)S(1)} %get-tuple-element.52), channel_id=1, source_target_pairs={{2,0},{0,1},{3,2},{1,3},{6,4},{4,5},{7,6},{5,7},{10,8},{8,9},{11,1... | collective-permute-start | bytes 221192 | tf_op jit(solution)/shard_map/ppermute | solution.py:663
  438.5 5.6 %collective-permute-start.15 = (f32[96,192]{0,1:T(8,128)S(1)}, f32[96,192]{0,1:T(8,128)S(1)}, u32[]{:S(2)}, u32[]{:S(2)}) collective-permute-start(f32[96,192]{0,1:T(8,128)S(1)} %get-tuple-element.53), channel_id=1, source_target_pairs={{1,0},{3,1},{0,2},{2,3},{5,4},{7,5},{4,6},{6,7},{9,8},{11,9},{8,10... | collective-permute-start | bytes 221192 | tf_op jit(solution)/shard_map/ppermute | solution.py:662
  (20 other events, 24.8 us)
Sparse Core Ops, SparseCore 0:
  23.1 25.7 all-gather.6
  51.4 24.0 all-gather.10
  77.3 24.1 all-gather.8
  274.3 33.7 reduce-scatter.8
  311.2 38.4 reduce-scatter.14
  352.8 36.7 reduce-scatter.10
  393.1 38.6 reduce-scatter.12

commit v2 on v0

--- a/solution.py
+++ b/solution.py
@@ -1,8 +1,11 @@
+import functools
 import math
 
 import jax
 import jax.numpy as jnp
 from jax import lax
+from jax.experimental import pallas as pl
+from jax.experimental.pallas import tpu as pltpu
 from jax.sharding import PartitionSpec as P
 
 HEAD_DIM = 64
@@ -132,7 +135,7 @@
     return result
 
 
-def local(
+def local_general(
     inputs,
     doc_starts,
     out_grad,
@@ -450,7 +453,647 @@
     )
 
 
+FULL_TOK = 2048
+TILE = 256
+TILES = FULL_TOK // TILE
+LOG2E = 1.4426950408889634
+WIDE = 768
+PACK = 400
+ACROSS = (((1,), (1,)), ((), ()))
+
+
+def fits_fast(mesh):
+    return dict(mesh.shape) == {"blk": 8, "uly": 4}
+
+
+def halves_in(rows):
+    half = rows.shape[-2] // 2
+    return jnp.concatenate([rows[..., :half, :], rows[..., half:, :]], axis=-1)
+
+
+def halves_out(packed):
+    half = packed.shape[-1] // 2
+    return jnp.concatenate([packed[..., :half], packed[..., half:]], axis=-2)
+
+
+def in_f32(value):
+    return value.astype(jnp.float32)
+
+
+def in_bf16(value):
+    return value.astype(jnp.bfloat16)
+
+
+def norm_stats(values):
+    center = values - jnp.mean(values, axis=-1, keepdims=True)
+    scale = lax.rsqrt(jnp.mean(center * center, axis=-1, keepdims=True) + norm_epsilon)
+    return center * scale, scale
+
+
+def norm_back(grad_out, normal, scale, gain):
+    grad_normal = grad_out * gain
+    mean_one = jnp.mean(grad_normal, axis=-1, keepdims=True)
+    mean_two = jnp.mean(grad_normal * normal, axis=-1, keepdims=True)
+    return (grad_normal - mean_one - normal * mean_two) * scale
+
+
+def mul(left, right):
+    return jnp.dot(left, right, preferred_element_type=jnp.float32)
+
+
+def mul_t(left, right):
+    return lax.dot_general(left, right, ACROSS, preferred_element_type=jnp.float32)
+
+
+def copies(pairs, sems):
+    moves = [pltpu.make_async_copy(source, target, sems.at[n]) for n, (source, target) in enumerate(pairs)]
+    for move in moves:
+        move.start()
+    return moves
+
+
+def finish(moves):
+    for move in moves:
+        move.wait()
+
+
+def group_places(uly):
+    query = jnp.minimum(uly, 2)
+    key = 1 - lax.rem((uly + 1) // 2, 2)
+    return query, key, 3 - query - key
+
+
+def first_kernel(place, x0, x1, x2, x3, starts, weight_in, pack, normed, rows_out, vectors, weight, rows, parts, sems):
+    uly = place[1]
+    moves = copies(
+        [(weight_in, weight)]
+        + [
+            (part.at[seq], rows.at[seq, uly ^ shift])
+            for shift, part in enumerate((x0, x1, x2))
+            for seq in range(2)
+        ]
+        + [(x3.at[pl.ds(64 * seq, 64)], rows.at[seq, uly ^ 3]) for seq in range(2)],
+        sems,
+    )
+    known = in_f32(starts[...])
+    even, low_half = lax.rem(uly, 2) == 0, uly < 2
+    for seq in range(2):
+        chunks = [known[2 * shift + seq : 2 * shift + seq + 1] for shift in range(4)]
+        lines = []
+        for part in (slice(0, 64), slice(64, 128)):
+            near, next_to, far, far_next = (chunk[:, part] for chunk in chunks)
+            near = jnp.where(
+                even, jnp.concatenate([near, next_to], axis=1), jnp.concatenate([next_to, near], axis=1)
+            )
+            far = jnp.where(
+                even, jnp.concatenate([far, far_next], axis=1), jnp.concatenate([far_next, far], axis=1)
+            )
+            lines += [jnp.where(low_half, near, far), jnp.where(low_half, far, near)]
+        lines = in_bf16(jnp.concatenate(lines + [jnp.zeros((12, 128), jnp.float32)], axis=0))
+        for head in range(3):
+            pack[4 * seq + head, 384:, :] = lines
+        pack[4 * seq + 3] = jnp.zeros((PACK, 128), jnp.bfloat16)
+    finish(moves)
+    rows_out[...] = rows[...]
+    vector_rows = in_f32(weight[:, 512:640]).T[64:72]
+    vectors[...] = vector_rows
+    normal, unused = norm_stats(in_f32(rows[...].reshape(512, WIDE)))
+    value = in_bf16(normal * vector_rows[0:1] + vector_rows[1:2])
+    normed[...] = value
+    product = in_bf16(mul(value, weight[:, :576]))
+    for number in range(3):
+        parts[number] = product[:, 192 * number : 192 * (number + 1)]
+    queries, keys, values = (parts[at] for at in group_places(uly))
+    for seq in range(2):
+        at_rows = slice(256 * seq, 256 * (seq + 1))
+        for head in range(3):
+            at = slice(HEAD_DIM * head, HEAD_DIM * (head + 1))
+            pack[4 * seq + head, :256, :] = jnp.concatenate([queries[at_rows, at], keys[at_rows, at]], axis=1)
+            pack[4 * seq + head, 256:384, :] = halves_in(values[at_rows, at])
+
+
+def first_row(pack, tile):
+    high, low = (
+        jnp.concatenate([rows[0:1], rows[1:2]], axis=1)
+        for rows in (in_f32(pack[tile, 384:386, :]), in_f32(pack[tile, 386:388, :]))
+    )
+    return high * 128.0 + low
+
+
+def iotas():
+    key_at = lax.broadcasted_iota(jnp.int32, (TILE, TILE), 0)
+    query_at = lax.broadcasted_iota(jnp.int32, (TILE, TILE), 1)
+    return in_f32(key_at), key_at <= query_at
+
+
+def attn_forward_kernel(pack, packed_out, out_cols, log_row, q_rows, k_rows, v_cols):
+    scale = LOG2E * HEAD_DIM**-0.5
+    for t in range(TILES):
+        rows = pl.ds(t * TILE, TILE)
+        pair = pack[t, :TILE, :]
+        q_rows[rows, :] = pair[:, :HEAD_DIM]
+        k_rows[rows, :] = pair[:, HEAD_DIM:]
+        v_cols[:, rows] = halves_out(pack[t, TILE:384, :]).T
+    key_at, causal = iotas()
+    for i in range(TILES):
+        q_at = pl.ds(i * TILE, TILE)
+        queries = q_rows[q_at, :]
+        first = first_row(pack, i)
+        top = total = acc = None
+        for j in range(i, -1, -1):
+            k_at = pl.ds(j * TILE, TILE)
+            scores = mul_t(k_rows[k_at, :], queries)
+            allowed = key_at >= first - float(j * TILE)
+            if j == i:
+                allowed = allowed & causal
+            scores = jnp.where(allowed, scores * scale, neg_large)
+            tile_top = jnp.max(scores, axis=0, keepdims=True)
+            new_top = tile_top if top is None else jnp.maximum(top, tile_top)
+            weights = jnp.exp2(scores - new_top)
+            tile_sum = jnp.sum(weights, axis=0, keepdims=True)
+            tile_acc = mul(v_cols[:, k_at], in_bf16(weights))
+            if top is None:
+                total, acc = tile_sum, tile_acc
+            else:
+                factor = jnp.exp2(top - new_top)
+                total = factor * total + tile_sum
+                acc = factor * acc + tile_acc
+            top = new_top
+        acc = acc / total
+        out_cols[:, q_at] = acc
+        log_row[:, q_at] = top + jnp.log2(total)
+        packed_out[i] = in_bf16(halves_in(acc.T))
+
+
+def attn_backward_kernel(
+    pack, grad, out_cols, log_row, dpack, q_rows, k_rows, v_rows, g_rows, k_cols, delta, firsts, dq_cols
+):
+    scale = LOG2E * HEAD_DIM**-0.5
+    for t in range(TILES):
+        rows = pl.ds(t * TILE, TILE)
+        pair = pack[t, :TILE, :]
+        q_rows[rows, :] = pair[:, :HEAD_DIM]
+        keys = pair[:, HEAD_DIM:]
+        k_rows[rows, :] = keys
+        k_cols[:, rows] = keys.T
+        v_rows[rows, :] = halves_out(pack[t, TILE:384, :])
+        g_tile = halves_out(grad[pl.ds(4 * t, 4)]).reshape(TILE, HEAD_DIM)
+        g_rows[rows, :] = g_tile
+        delta[:, rows] = jnp.sum(in_f32(g_tile.T) * out_cols[:, rows], axis=0, keepdims=True)
+        firsts[:, rows] = first_row(pack, t)
+    key_at, causal = iotas()
+    for j in range(TILES):
+        k_at = pl.ds(j * TILE, TILE)
+        keys, values, keys_t = k_rows[k_at, :], v_rows[k_at, :], k_cols[:, k_at]
+        dk = dv = None
+        for i in range(j, TILES):
+            q_at = pl.ds(i * TILE, TILE)
+            queries, grads = q_rows[q_at, :], g_rows[q_at, :]
+            allowed = key_at >= firsts[:, q_at] - float(j * TILE)
+            if i == j:
+                allowed = allowed & causal
+            scores = mul_t(keys, queries) * scale - log_row[:, q_at]
+            probs = jnp.exp2(jnp.where(allowed, scores, neg_large))
+            dscores = in_bf16(probs * (mul_t(values, grads) - delta[:, q_at]))
+            dv_tile = mul(in_bf16(probs), grads)
+            dk_tile = mul(dscores, queries)
+            dq_tile = mul(keys_t, dscores)
+            dv = dv_tile if dv is None else dv + dv_tile
+            dk = dk_tile if dk is None else dk + dk_tile
+            if j == 0:
+                dq_cols[:, q_at] = dq_tile
+            else:
+                dq_cols[:, q_at] += dq_tile
+        dq = (dq_cols[:, k_at] * HEAD_DIM**-0.5).T
+        dk = dk * HEAD_DIM**-0.5
+        dpack[j, :TILE, :] = in_bf16(jnp.concatenate([dq, dk], axis=1))
+        dpack[j, TILE:, :] = halves_in(in_bf16(dv))
+
+
+def down_from(weights, columns, full):
+    for at in range(8):
+        for number in range(4):
+            lane = WIDE + 192 * number
+            columns[at // 2, pl.ds(384 * (at % 2) + 96 * number, 96), :] = weights[at, :, lane : lane + 192]
+    for group in range(4):
+        full[:, 192 * group : 192 * (group + 1)] = columns[group]
+
+
+def out_from(weights, uly, columns, full):
+    for shift in range(4):
+        lane = 2 * WIDE + 192 * shift
+        columns[uly ^ shift] = weights[:, :, lane : lane + 192].reshape(WIDE, 192)
+    for group in range(4):
+        full[:, 192 * group : 192 * (group + 1)] = columns[group]
+
+
+def middle_kernel(place, mixed_pack, rows_in, g0, g1, g2, g3, weights_in, vectors, *refs):
+    outs, (weights, columns, down, w_out, rows, parts, slots, sems) = refs[:10], refs[10:]
+    grad_outs, (mixed, middle_own, normed, act_out, pre_out, grad_branch) = outs[:4], outs[4:]
+    uly = place[1]
+    moves = copies(
+        [(weights_in, weights), (rows_in, rows)]
+        + [
+            (part.at[seq], parts.at[seq, uly ^ shift])
+            for shift, part in enumerate((g0, g1, g2, g3))
+            for seq in range(2)
+        ],
+        sems,
+    )
+    for group in range(4):
+        for seq in range(2):
+            for head in range(3):
+                at = 192 * group + HEAD_DIM * head
+                mixed[pl.ds(256 * seq, 256), at : at + HEAD_DIM] = halves_out(mixed_pack[group, seq, head])
+    finish(moves)
+    out_from(weights, uly, columns, w_out)
+    middle = in_f32(rows[...].reshape(512, WIDE)) + branch_scale * mul(mixed[...], w_out[...])
+    normal, unused = norm_stats(middle)
+    normed[...] = in_bf16(normal * vectors[2:3] + vectors[3:4])
+    chunks = middle.reshape(2, 4, 64, WIDE)
+    middle_own[...] = jnp.where(
+        uly < 2,
+        jnp.where(uly == 0, chunks[:, 0], chunks[:, 1]),
+        jnp.where(uly == 2, chunks[:, 2], chunks[:, 3]),
+    )
+    down_from(weights, columns, down)
+    grad_branch[...] = in_bf16(branch_scale * in_f32(parts[...])).reshape(512, WIDE)
+    up_full = weights[:, :, :WIDE].reshape(WIDE, WIDE)
+    pre = mul(normed[...], up_full)
+    grad_act = mul_t(grad_branch[...], down[...])
+    square = pre * pre
+    bend = jnp.tanh(math.sqrt(2.0 / math.pi) * pre * (1.0 + 0.044715 * square))
+    half = 0.5 * (1.0 + bend)
+    act_out[...] = in_bf16(pre * half)
+    slope = math.sqrt(2.0 / math.pi) * (1.0 + 3 * 0.044715 * square)
+    gate = half + 0.5 * pre * (1.0 - bend * bend) * slope
+    pre_out[...] = in_bf16(grad_act * gate)
+    result = in_bf16(mul_t(pre_out[...], up_full)).reshape(2, 4, 64, WIDE)
+    for to in range(4):
+        slots[to] = result[:, to]
+    for shift, out in enumerate(grad_outs):
+        out[...] = slots[uly ^ shift]
+
+
+def feed_grads_kernel(place, normed, act, grad_pre, grad_branch, weights_in, *refs):
+    feed, keep, send, w_out, weights, up_grad, down_grad, columns, down, sems = refs
+    blk, uly = place[0], place[1]
+    moves = copies([(weights_in, weights)], sems)
+    chip, core = blk // 2, lax.rem(blk, 2)
+    up_grad[...] = in_bf16(mul(normed[...].T, grad_pre[...])).reshape(8, 96, WIDE)
+    grad = in_bf16(mul(act[...].T, grad_branch[...]))
+    for group in range(4):
+        for half in range(2):
+            for number in range(4):
+                at = 384 * half + 96 * number
+                down_grad[2 * group + half, :, 192 * number : 192 * (number + 1)] = grad[
+                    at : at + 96, 192 * group : 192 * (group + 1)
+                ]
+    for shift in range(4):
+        same, other = 2 * (chip ^ shift) + core, 2 * (chip ^ shift) + 1 - core
+        keep[shift, 0], keep[shift, 1] = up_grad[same], down_grad[same]
+        send[shift, 0], send[shift, 1] = up_grad[other], down_grad[other]
+    finish(moves)
+    out_from(weights, uly, columns, w_out)
+    down_from(weights, columns, down)
+    feed[...] = in_bf16(mul(act[...], down[...])).reshape(2, 256, WIDE)
+
+
+def second_back_kernel(
+    place, g0, g1, g2, g3, middle, out_grad, w_out, vectors, grad_middle, pack, sums, a0, a1, a2, a3, columns
+):
+    uly = place[1]
+    grad = in_f32(g0[...]) + in_f32(g1[...]) + in_f32(g2[...]) + in_f32(g3[...])
+    grad = grad.reshape(128, WIDE)
+    normal, scale = norm_stats(middle[...].reshape(128, WIDE))
+    sums[...] = jnp.concatenate(
+        [
+            jnp.sum(grad * normal, axis=0, keepdims=True),
+            jnp.sum(grad, axis=0, keepdims=True),
+            jnp.zeros((6, WIDE), jnp.float32),
+        ],
+        axis=0,
+    )
+    result = in_f32(out_grad[...].reshape(128, WIDE)) + norm_back(grad, normal, scale, vectors[2:3])
+    grad_middle[...] = result.reshape(2, 64, WIDE)
+    low = in_bf16(branch_scale * result)
+    mixed = in_bf16(mul_t(low, w_out[...]))
+    for group in range(4):
+        columns[group] = low[:, 192 * group : 192 * (group + 1)]
+        for seq in range(2):
+            rows = mixed[64 * seq : 64 * (seq + 1)]
+            for head in range(3):
+                at = 192 * group + HEAD_DIM * head
+                pack[4 * seq + head, group] = halves_in(rows[:, at : at + HEAD_DIM])
+            pack[4 * seq + 3, group] = jnp.zeros((32, 128), jnp.bfloat16)
+    for shift, out in enumerate((a0, a1, a2, a3)):
+        out[...] = columns[uly ^ shift]
+
+
+def last_kernel(place, dpack, weight_in, rows_in, *refs):
+    grad_norm, grad_qkv, sums, weight, rows_low, parts, sems = refs
+    uly = place[1]
+    moves = copies([(weight_in, weight), (rows_in, rows_low)], sems)
+    for seq in range(2):
+        rows = pl.ds(256 * seq, 256)
+        for head in range(3):
+            at = slice(HEAD_DIM * head, HEAD_DIM * (head + 1))
+            pair = dpack[4 * seq + head, :256, :]
+            parts[0, rows, at] = pair[:, :HEAD_DIM]
+            parts[1, rows, at] = pair[:, HEAD_DIM:]
+            parts[2, rows, at] = halves_out(dpack[4 * seq + head, 256:, :])
+    query, key, value = group_places(uly)
+    for number in range(3):
+        part = jnp.where(query == number, 0, jnp.where(key == number, 1, 2))
+        grad_qkv[:, 192 * number : 192 * (number + 1)] = parts[part]
+    finish(moves)
+    grad = mul_t(grad_qkv[...], weight[:, :576])
+    grad_norm[...] = in_bf16(grad).reshape(2, 256, WIDE)
+    normal, unused = norm_stats(in_f32(rows_low[...].reshape(512, WIDE)))
+    sums[...] = jnp.concatenate(
+        [
+            jnp.sum(grad * normal, axis=0, keepdims=True),
+            jnp.sum(grad, axis=0, keepdims=True),
+            jnp.zeros((6, WIDE), jnp.float32),
+        ],
+        axis=0,
+    )
+
+
+TAIL = 832
+
+
+def late_grads_kernel(
+    place, normed, grad_qkv, sums_one, sums_two, mixed, a0, a1, a2, a3, keep, send, full, columns
+):
+    blk, uly = place[0], place[1]
+    chip, core = blk // 2, lax.rem(blk, 2)
+    for shift, part in enumerate((a0, a1, a2, a3)):
+        for seq in range(2):
+            columns[seq, uly ^ shift] = part[64 * seq : 64 * (seq + 1)]
+    grad = mul(normed[...].T, grad_qkv[...])
+    out_grad = mul(mixed[...].T, columns[...].reshape(512, 192))
+    sums = jnp.concatenate([sums_one[0:2], sums_two[0:2], jnp.zeros((60, WIDE), jnp.float32)], axis=0)
+    full[...] = in_bf16(jnp.concatenate([grad, sums.T, out_grad], axis=1)).reshape(8, 96, TAIL)
+    for shift in range(4):
+        keep[shift] = full[2 * (chip ^ shift) + core]
+        send[shift] = full[2 * (chip ^ shift) + 1 - core]
+
+
+def chip_sum_kernel(keep, got, own, to_x, to_y, to_xy):
+    own[...] = in_f32(keep[0]) + in_f32(got[0])
+    for shift, out in ((1, to_x), (2, to_y), (3, to_xy)):
+        out[...] = in_bf16(in_f32(keep[shift]) + in_f32(got[shift]))
+
+
+VMEM_SPEC = pl.BlockSpec(memory_space=pltpu.VMEM)
+FREE_SPEC = pl.BlockSpec(memory_space=pl.ANY)
+
+
+def on_core(kernel, outs, operands, scratch=(), flops=0, place=False, free=(), sems=0):
+    size = lambda item: math.prod(item.shape) * item.dtype.itemsize
+    shapes = [jax.ShapeDtypeStruct(shape, dtype) for shape, dtype in outs]
+    specs = [FREE_SPEC if n in free else VMEM_SPEC for n in range(len(operands))]
+    if place:
+        specs[0] = pl.BlockSpec(memory_space=pltpu.SMEM)
+    scratch = [pltpu.VMEM(shape, dtype) for shape, dtype in scratch]
+    if sems:
+        scratch.append(pltpu.SemaphoreType.DMA((sems,)))
+    moved = sum(size(item) for item in operands) + sum(size(item) for item in shapes)
+    return pl.pallas_call(
+        kernel,
+        out_shape=shapes,
+        in_specs=specs,
+        out_specs=[VMEM_SPEC] * len(shapes),
+        scratch_shapes=scratch,
+        compiler_params=pltpu.CompilerParams(vmem_limit_bytes=(VMEM_MB if free else 24) * 2**20),
+        cost_estimate=pl.CostEstimate(flops=flops, bytes_accessed=moved, transcendentals=0),
+        name=kernel.__name__,
+    )(*operands)
+
+
+VMEM_MB = 56
+
+
+def swap_z(value, shift):
+    return lax.ppermute(value, "uly", [(i, i ^ shift) for i in range(4)])
+
+
+def swap_blk(value, mask):
+    return lax.ppermute(value, "blk", [(i, i ^ mask) for i in range(8)])
+
+
+def swap_parts(parts):
+    return [parts[0]] + [swap_z(parts[shift], shift) for shift in (1, 2, 3)]
+
+
+def sum_blk(keep, send):
+    got = swap_blk(send, 1)
+    shape = keep.shape[1:]
+    own, to_x, to_y, to_xy = on_core(
+        chip_sum_kernel, [(shape, jnp.float32)] + [(shape, jnp.bfloat16)] * 3, (keep, got)
+    )
+    return own, to_x, to_y, to_xy
+
+
+def finish_sum(own, to_x, to_y, to_xy):
+    return own + in_f32(swap_blk(to_x, 2)) + in_f32(swap_blk(to_y, 4)) + in_f32(swap_blk(to_xy, 6))
+
+
+def after(value, *others):
+    return lax.optimization_barrier((value,) + others)[0]
+
+
+DOWN_MOVES = [(b * 4 + u, (2 * u + b % 2) * 4 + b // 2) for b in range(8) for u in range(4)]
+
+
+def local_fast(
+    inputs,
+    doc_starts,
+    out_grad,
+    first_gain,
+    first_bias,
+    query_key_value_weight,
+    attention_out_weight,
+    second_gain,
+    second_bias,
+    up_weight,
+    down_weight,
+):
+    bf16, f32 = jnp.bfloat16, jnp.float32
+    blk, uly = lax.axis_index("blk"), lax.axis_index("uly")
+    place = jnp.stack([blk, uly]).astype(jnp.int32)
+    even = lax.rem(uly, 2) == 0
+    square = (WIDE, WIDE)
+
+    groups = [query_key_value_weight[:, 192 * n : 192 * (n + 1)] for n in range(3)]
+    own_starts = jnp.concatenate([doc_starts // 128, lax.rem(doc_starts, 128)], axis=1).astype(bf16)
+    shared = jnp.concatenate([attention_out_weight, jnp.pad(own_starts, ((0, 14), (0, 64)))], axis=0)
+    to_one = jnp.concatenate([groups[1], shared], axis=0)
+    to_two = jnp.concatenate([jnp.where(even, groups[2], groups[0]), shared], axis=0)
+    to_three = jnp.concatenate(
+        [inputs.reshape(128, WIDE), jnp.concatenate([shared[28 * n : 28 * (n + 1)] for n in range(4)], axis=1),
+         jnp.zeros((4, WIDE), bf16)], axis=0
+    )
+    got_one, got_two = swap_z(to_one, 1), swap_z(to_two, 2)
+    got_three = swap_z(to_three, 3)
+    x_own = after(inputs, to_one, to_two)
+    x_parts = [inputs, swap_z(x_own, 1), swap_z(x_own, 2), got_three]
+    shared_three = jnp.concatenate([got_three[128:156, 192 * n : 192 * (n + 1)] for n in range(4)], axis=0)
+    vectors = jnp.stack([first_gain, first_bias, second_gain, second_bias], axis=1)
+    qkv_shard = jnp.concatenate(
+        [
+            jnp.where(even, groups[0], groups[2]),
+            got_one[:96],
+            got_two[:96],
+            jnp.pad(vectors, ((0, 0), (0, 60))),
+        ],
+        axis=1,
+    )
+    starts = jnp.concatenate(
+        [own_starts, got_one[192:194, :128], got_two[192:194, :128], shared_three[96:98, :128]], axis=0
+    )
+    w_qkv = lax.all_gather(qkv_shard, "blk", axis=0, tiled=True)
+    down_shard = lax.ppermute(down_weight, ("blk", "uly"), DOWN_MOVES)
+
+    pack, normed_one, rows, vectors = on_core(
+        first_kernel,
+        [((8, PACK, 128), bf16), ((512, WIDE), bf16), ((2, 4, 64, WIDE), bf16), ((8, WIDE), f32)],
+        [place] + x_parts + [starts, w_qkv],
+        scratch=[((WIDE, 640), bf16), ((2, 4, 64, WIDE), bf16), ((3, 512, 192), bf16)],
+        flops=2 * 512 * 768 * 576,
+        place=True,
+        free=(1, 2, 3, 4, 6),
+        sems=9,
+    )
+    weights = jnp.concatenate(
+        [up_weight]
+        + [down_shard[96 * n : 96 * (n + 1)] for n in range(4)]
+        + [attention_out_weight, got_one[96:192], got_two[96:192], shared_three[:96]],
+        axis=1,
+    )
+    pack = lax.all_to_all(pack, "blk", 0, 0, tiled=True)
+    weights = lax.all_gather(after(weights, pack), "blk", axis=0)
+    g_parts = swap_parts([after(out_grad, normed_one)] * 4)
+
+    head_rows = ((FULL_TOK, HEAD_DIM), bf16)
+    head_cols = ((HEAD_DIM, FULL_TOK), bf16)
+    attn_pack, out_cols, log_row = on_core(
+        attn_forward_kernel,
+        [((8, 128, 128), bf16), ((HEAD_DIM, FULL_TOK), f32), ((1, FULL_TOK), f32)],
+        [pack],
+        scratch=[head_rows, head_rows, head_cols],
+        flops=4 * FULL_TOK * FULL_TOK * HEAD_DIM,
+    )
+    attn_pack, *g_parts = lax.optimization_barrier([attn_pack] + g_parts)
+    attn_pack = lax.all_to_all(attn_pack, "blk", 0, 0, tiled=True)
+    attn_pack = lax.all_gather(attn_pack.reshape(2, 4, 128, 128)[:, :3], "uly", axis=0)
+
+    big = [((8, 96, 3 * WIDE), bf16), ((4, WIDE, 192), bf16), (square, bf16)]
+    tok_rows = ((512, WIDE), bf16)
+    own_rows = ((2, 64, WIDE), bf16)
+    *grad_norm, mixed, middle_own, normed_two, act, grad_pre, grad_branch = on_core(
+        middle_kernel,
+        [own_rows] * 4 + [tok_rows, ((2, 64, WIDE), f32)] + [tok_rows] * 4,
+        [place, attn_pack, rows] + g_parts + [weights, vectors],
+        scratch=big + [(square, bf16), ((2, 4, 64, WIDE), bf16), ((2, 4, 64, WIDE), bf16), ((4, 2, 64, WIDE), bf16)],
+        flops=8 * 512 * 768 * 768,
+        place=True,
+        free=(2, 3, 4, 5, 6, 7),
+        sems=10,
+    )
+    grad_norm = swap_parts(grad_norm)
+    feed, keep, send, w_out = on_core(
+        feed_grads_kernel,
+        [((2, 256, WIDE), bf16), ((4, 2, 96, WIDE), bf16), ((4, 2, 96, WIDE), bf16), (square, bf16)],
+        [place, normed_two, act, grad_pre, grad_branch, weights],
+        scratch=[big[0], ((8, 96, WIDE), bf16), ((8, 96, WIDE), bf16)] + big[1:],
+        flops=6 * 512 * 768 * 768,
+        place=True,
+        free=(5,),
+        sems=1,
+    )
+    grad_middle, grad_pack, sums_two, *grad_cols = on_core(
+        second_back_kernel,
+        [((2, 64, WIDE), f32), ((8, 4, 32, 128), bf16), ((8, WIDE), f32)] + [((128, 192), bf16)] * 4,
+        [place] + grad_norm + [middle_own, out_grad, w_out, vectors],
+        scratch=[((4, 128, 192), bf16)],
+        flops=2 * 128 * 768 * 768,
+        place=True,
+    )
+    grad_pack = lax.all_to_all(grad_pack.reshape(32, 32, 128), ("blk", "uly"), 0, 0, tiled=True)
+    feed = in_f32(lax.psum_scatter(after(feed, grad_pack), "uly", scatter_dimension=1, tiled=True))
+    output = in_bf16(middle_own + branch_scale * feed)
+    sums = sum_blk(keep, after(send, sums_two))
+    grad_pack, *sums = lax.optimization_barrier([grad_pack] + list(sums))
+
+    (dpack,) = on_core(
+        attn_backward_kernel,
+        [((8, 384, 128), bf16)],
+        [pack, grad_pack, out_cols, log_row],
+        scratch=[head_rows] * 4 + [head_cols] + [((1, FULL_TOK), f32)] * 2 + [((HEAD_DIM, FULL_TOK), f32)],
+        flops=10 * FULL_TOK * FULL_TOK * HEAD_DIM,
+    )
+    up_down, dpack = lax.optimization_barrier((finish_sum(*sums), dpack))
+    g_w_up = up_down[0]
+    g_w_down = jnp.concatenate([up_down[1][:, 192 * n : 192 * (n + 1)] for n in range(4)], axis=0)
+    g_w_down = lax.ppermute(in_bf16(g_w_down), ("blk", "uly"), [(to, at) for at, to in DOWN_MOVES])
+    grad_cols = swap_parts([after(part, dpack) for part in grad_cols])
+    dpack = lax.all_to_all(dpack, "blk", 0, 0, tiled=True)
+    dpack, g_w_down, *grad_cols = lax.optimization_barrier([dpack, g_w_down] + grad_cols)
+    grad_norm, grad_qkv, sums_one = on_core(
+        last_kernel,
+        [((2, 256, WIDE), bf16)] + [((512, 576), bf16), ((8, WIDE), f32)],
+        [place, dpack, w_qkv, rows],
+        scratch=[((WIDE, 640), bf16), ((2, 4, 64, WIDE), bf16), ((3, 512, 192), bf16)],
+        flops=2 * 512 * 768 * 576,
+        place=True,
+        free=(2, 3),
+        sems=2,
+    )
+    grad_norm = lax.psum_scatter(grad_norm, "uly", scatter_dimension=1, tiled=True)
+    keep, send = on_core(
+        late_grads_kernel,
+        [((4, 96, TAIL), bf16)] * 2,
+        [place, normed_one, grad_qkv, sums_one, sums_two, mixed] + grad_cols,
+        scratch=[((8, 96, TAIL), bf16), ((2, 4, 64, 192), bf16)],
+        flops=2 * 512 * 768 * 768,
+        place=True,
+    )
+    tail = finish_sum(*sum_blk(keep, send))
+    d_vectors = tail[:, 576:580]
+    got_one = in_f32(swap_z(in_bf16(jnp.concatenate([tail[:, 192:384], d_vectors], axis=1)), 1))
+    d_vectors = d_vectors + got_one[:, 192:]
+    got_two = in_f32(swap_z(in_bf16(jnp.concatenate([tail[:, 384:576], d_vectors], axis=1)), 2))
+    d_vectors = (d_vectors + got_two[:, 192:]).T
+    g_w_qkv = jnp.concatenate(
+        [
+            jnp.where(even, tail[:, :192], got_two[:, :192]),
+            got_one[:, :192],
+            jnp.where(even, got_two[:, :192], tail[:, :192]),
+        ],
+        axis=1,
+    )
+
+    grad_norm = in_f32(grad_norm)
+    normal, scale = norm_stats(in_f32(inputs))
+    grad_inputs = grad_middle + norm_back(grad_norm, normal, scale, vectors[0:1])
+    return (
+        output,
+        grad_inputs,
+        d_vectors[0],
+        d_vectors[1],
+        g_w_qkv,
+        tail[:, 640:],
+        d_vectors[2],
+        d_vectors[3],
+        g_w_up,
+        in_f32(g_w_down),
+    )
+
+
 def solution(mesh):
+    local = local_fast if fits_fast(mesh) else local_general
     placed = (
         P(None, ("blk", "uly"), None),
         P(None, ("blk", "uly")),

time: 828 us -> 253 us (0.31)
  blocking collectives: 213 us -> 45.4 us
  waiting for transfers between devices: 208 us -> 52.9 us
  local copies, waits for them, and re-layouts: 161 us -> 17.8 us
  loops' own time: 113 us -> 0 us
  matrix products: 65.1 us -> 0 us
  Pallas kernels: 0 us -> 53.1 us
  starting transfers between devices: 4.25 us -> 54.5 us
  other arithmetic: 38.4 us -> 12.2 us
    reduce_scatter x6 -> x2, waiting for transfers between devices: 136 us -> 0.02 us  [the longest x1 0.02 us: local_fast(): lax.psum_scatter(after(feed, grad_pack), 'uly', scatter_dimension=1, tile...]
    another operation x51 -> x0, loops' own time: 113 us -> none  [the longest x3 112 us: each_block(): lax.scan(advance, carried, (jnp.arange(block_count, dtype=jnp.int32), spl...]
    all_gather x8 -> x2, blocking collectives: 105 us -> 32.4 us  [the longest x1 20.5 us: local_fast(): lax.all_gather(attn_pack.reshape(2, 4, 128, 128)[:, :3], 'uly', axis=0)]
    dot_general x65 -> x0, matrix products: 65.1 us -> none  [the longest x4 13 us: weight_grad(): jnp.einsum('stk,stn->kn', left, right, preferred_element_type=jnp.float32)]
    pallas_call x0 -> x10, Pallas kernels: none -> 53.1 us  [on_core(): pl.pallas_call(kernel, out_shape=shapes, in_specs=specs, out_specs=[VMEM_...]
    unnamed x3 -> x0, blocking collectives: 52.9 us -> none
    dynamic_slice x64 -> x0, local copies, waits for them, and re-layouts: 50.8 us -> none  [each_block(): lax.scan(advance, carried, (jnp.arange(block_count, dtype=jnp.int32), spl...]
    slice x161 -> x19, local copies, waits for them, and re-layouts: 49.9 us -> 3.33 us  [the longest x1 0.9 us: local_fast(): got_three[128:156, 192 * n:192 * (n + 1)]]
  transfers between devices with their start and end apart: 17 -> 32, of which waited for: 6 -> 12; matrix products, arithmetic and copies ran while one was open for 30% -> 5% of each run, Pallas kernels for 0% -> 17%
where the time goes in v2:
time: 253 us; the launch traced here: 250 us
  starting transfers between devices  54.5 us (22%)
  Pallas kernels  53.1 us (21%)
  waiting for transfers between devices  52.9 us (21%)
  blocking collectives  45.4 us (18%)
  local copies, waits for them, and re-layouts  17.8 us (7%)
  between operations  14.4 us (6%)
  other arithmetic  12.2 us (5%)
    pallas_call x10, Pallas kernels, on_core(): pl.pallas_call(kernel, out_shape=shapes, in_specs=specs, out_specs=[VMEM_...  53.1 us
    ppermute x16, starting transfers between devices, swap_z(): return lax.ppermute(value, 'uly', [(i, i ^ shift) for i in range(4)])  21.6 us
    ppermute x16, waiting for transfers between devices, swap_z(): return lax.ppermute(value, 'uly', [(i, i ^ shift) for i in range(4)])  21.2 us
    all_gather x1, blocking collectives, local_fast(): lax.all_gather(attn_pack.reshape(2, 4, 128, 128)[:, :3], 'uly', axis=0)  20.5 us
    all_to_all x1, blocking collectives, local_fast(): attn_pack = lax.all_to_all(attn_pack, 'blk', 0, 0, tiled=True)  13 us
    unnamed x87, local copies, waits for them, and re-layouts  12.6 us
    all_gather x1, blocking collectives, local_fast(): w_qkv = lax.all_gather(qkv_shard, 'blk', axis=0, tiled=True)  11.9 us
    ppermute x8, waiting for transfers between devices, swap_blk(): return lax.ppermute(value, 'blk', [(i, i ^ mask) for i in range(8)])  9.83 us
  transfers between devices with their start and end apart: 32, of which 12 were waited for; matrix products, arithmetic and copies ran while one was open for 5% of the time, Pallas kernels for 17%

profile of v2, /device:TPU:4, one launch (start us, length us, event | category | flops | bytes accessed | tf_op | source)
XLA Modules:
  0.0 250.5 jit_solution(4086692452056094054)
XLA Ops:
  7.2 0.7 fusion.29
  8.0 1.1 broadcast_select_fusion
  9.1 0.8 pad_maximum_fusion.2
  9.9 2.7 %collective-permute-start.4 = (bf16[208,192]{1,0:T(8,128)(2,1)S(1)}, bf16[208,192]{1,0:T(8,128)(2,1)S(1)}, u32[]{:S(2)}, u32[]{:S(2)}) collective-permute-start(bf16[208,192]{1,0:T(8,128)(2,1)S(1)} %get-tuple-element.208), channel_id=1, source_target_pairs={{0,2},{1,3},{2,0},{3,1},{4,6},{5,7},{6,4},{7,5},{8,10},{9,11},{10,... | collective-permute-start | bytes 239624 | tf_op jit(solution)/shard_map/ppermute | solution.py:879
  12.6 1.6 collective-permute-start.3
  15.0 0.8 fusion.38
  15.8 1.1 fusion.17
  16.9 3.7 %collective-permute-start.2 = (bf16[160,768]{1,0:T(8,128)(2,1)S(1)}, bf16[160,768]{1,0:T(8,128)(2,1)S(1)}, u32[]{:S(2)}, u32[]{:S(2)}) collective-permute-start(bf16[160,768]{1,0:T(8,128)(2,1)S(1)} %fusion.17), channel_id=1, source_target_pairs={{0,3},{1,2},{2,1},{3,0},{4,7},{5,6},{6,5},{7,4},{8,11},{9,10},{10,... | collective-permute-start | bytes 737288 | tf_op jit(solution)/shard_map/ppermute | solution.py:879
  21.3 1.9 collective-permute-start.8
  23.4 11.9 %all_gather.15.weight_in = bf16[768,640]{1,0:T(8,128)(2,1)} all-gather(bf16[96,640]{1,0:T(8,128)(2,1)S(1)} %fusion.20), channel_id=1, replica_groups=mesh['blk'=8,'uly'=4] {'blk'}, dimensions={0}, use_global_device_ids=true | all-gather | bytes 1105920 | tf_op jit(solution)/shard_map/all_gather | solution.py:956
  37.4 4.8 %first_kernel.1 = (bf16[8,400,128]{2,1,0:T(8,128)(2,1)}, bf16[512,768]{1,0:T(8,128)(2,1)}, bf16[2,4,64,768]{3,2,1,0:T(8,128)(2,1)}, f32[8,768]{1,0:T(8,128)}) custom-call(s32[2]{0:T(128)} %pad_add_fusion.place, bf16[2,64,768]{2,1,0:T(8,128)(2,1)} %x0.1, bf16[2,64,768]{2,1,0:T(8,128)(2,1)} %copy-done.32, bf16[2,64,768]{2,1,0:T(8,128)(2,1)} %copy-done.33, ...), custom_call_target="tpu_custom_call" | custom-call | flops 452984832 | bytes 4237320 | tf_op jit(solution)/shard_map/first_kernel/pallas_call | solution.py:863
  42.3 8.2 %all-to-all-start = ((bf16[8,400,128]{2,1,0:T(8,128)(2,1)}), bf16[8,400,128]{2,1,0:T(8,128)(2,1)S(1)}, u32[]{:S(2)}, u32[]{:S(2)}) async-start(bf16[8,400,128]{2,1,0:T(8,128)(2,1)} %get-tuple-element.79), calls=%async_computation | async-start | bytes 1638400 | tf_op jit(solution)/shard_map/all_to_all | solution.py:975
  51.0 0.9 fusion.32
  51.9 0.9 concatenate.57
  52.8 9.5 %all-to-all-done.pack = bf16[8,400,128]{2,1,0:T(8,128)(2,1)S(1)} async-done(((bf16[8,400,128]{2,1,0:T(8,128)(2,1)}), bf16[8,400,128]{2,1,0:T(8,128)(2,1)S(1)}, u32[]{:S(2)}, u32[]{:S(2)}) %all-to-all-start) | async-done | bytes 819232 | tf_op jit(solution)/shard_map/all_to_all | solution.py:975
  62.3 2.4 collective-permute-start.5
  64.8 1.8 collective-permute-start.6
  67.2 10.7 %attn_forward_kernel.1 = (bf16[8,128,128]{2,1,0:T(8,128)(2,1)S(1)}, f32[64,2048]{1,0:T(8,128)S(1)}, f32[1,2048]{1,0:T(1,128)S(1)}) custom-call(bf16[8,400,128]{2,1,0:T(8,128)(2,1)S(1)} %all-to-all-done.pack), custom_call_target="tpu_custom_call" | custom-call | flops 1073741824 | bytes 1613824 | tf_op jit(solution)/shard_map/attn_forward_kernel/pallas_call | solution.py:863
  78.0 2.6 %collective-permute-done.6.g2 = bf16[2,64,768]{2,1,0:T(8,128)(2,1)S(1)} collective-permute-done((bf16[2,64,768]{2,1,0:T(8,128)(2,1)S(1)}, bf16[2,64,768]{2,1,0:T(8,128)(2,1)S(1)}, u32[]{:S(2)}, u32[]{:S(2)}) %collective-permute-start.6) | collective-permute-done | bytes 196640 | tf_op jit(solution)/shard_map/ppermute | solution.py:879
  80.6 13.0 %all_to_all.20 = bf16[8,128,128]{2,1,0:T(8,128)(2,1)S(1)} all-to-all(bf16[8,128,128]{2,1,0:T(8,128)(2,1)S(1)} %get-tuple-element.83), channel_id=1, replica_groups=mesh['blk'=8,'uly'=4] {'blk'}, dimensions={0} | all-to-all | bytes 524288 | tf_op jit(solution)/shard_map/all_to_all | solution.py:989
  93.7 20.5 %all-gather = bf16[8,3,128,128]{3,2,1,0:T(8,128)(2,1)} all-gather(bf16[2,3,128,128]{3,2,1,0:T(8,128)(2,1)S(1)} %slice.193), channel_id=2, replica_groups=mesh['blk'=8,'uly'=4] {'uly'}, dimensions={0}, use_global_device_ids=true | all-gather | bytes 983040 | tf_op jit(solution)/shard_map/all_gather | solution.py:990
  114.2 9.1 %middle_kernel.1 = (bf16[2,64,768]{2,1,0:T(8,128)(2,1)}, bf16[2,64,768]{2,1,0:T(8,128)(2,1)}, bf16[2,64,768]{2,1,0:T(8,128)(2,1)}, bf16[2,64,768]{2,1,0:T(8,128)...) custom-call(s32[2]{0:T(128)} %pad_add_fusion.place, ...), custom_call_target="tpu_custom_call" | custom-call | flops 2415919104 | bytes 11034632 | tf_op jit(solution)/shard_map/middle_kernel/pallas_call | solution.py:863
  123.3 0.9 collective-permute-start.10
  124.2 1.3 collective-permute-start.11
  125.5 1.3 collective-permute-start.9
  126.9 8.2 %feed_grads_kernel.1 = (bf16[2,256,768]{2,1,0:T(8,128)(2,1)}, bf16[4,2,96,768]{3,2,1,0:T(8,128)(2,1)}, bf16[4,2,96,768]{3,2,1,0:T(8,128)(2,1)}, bf16[768,768]{1,0:T(8,128)(2,1)}) custom-call(s32[2]{0:T(128)} %pad_add_fusion.place, bf16[512,768]{1,0:T(8,128)(2,1)} %get-tuple-element.92.normed, bf16[512,768]{1,0:T(8,128)(2,1)} %get-tuple-element.93.act, ...), custom_call_target="tpu_custom_call" | custom-call | flops 1811939328 | bytes 11010056 | tf_op jit(solution)/shard_map/feed_grads_kernel/pallas_call | solution.py:863
  135.1 1.1 collective-permute-done.10.g2
  136.3 1.3 copy-done.2
  137.5 2.2 second_back_kernel.1
  139.7 0.7 copy-done.8
  141.7 6.2 %all-to-all-start.2 = ((bf16[32,32,128]{2,1,0:T(8,128)(2,1)}), bf16[32,32,128]{2,1,0:T(8,128)(2,1)}, u32[]{:S(2)}, u32[]{:S(2)}) async-start(bf16[32,32,128]{2,1,0:T(8,128)(2,1)} %bitcast.10), calls=%async_computation.2 | async-start | bytes 524288 | tf_op jit(solution)/shard_map/all_to_all | solution.py:1024
  149.3 0.7 copy-done.18
  150.0 0.7 copy-done.19
  150.7 6.8 %all-to-all-done.2.grad = bf16[32,32,128]{2,1,0:T(8,128)(2,1)} async-done(((bf16[32,32,128]{2,1,0:T(8,128)(2,1)}), bf16[32,32,128]{2,1,0:T(8,128)(2,1)}, u32[]{:S(2)}, u32[]{:S(2)}) %all-to-all-start.2) | async-done | bytes 262176 | tf_op jit(solution)/shard_map/all_to_all | solution.py:1024
  158.0 1.5 collective-permute-start.14
  159.5 1.5 collective-permute-start.15
  161.0 1.1 copy-done.4
  162.2 1.0 copy-done.25
  163.2 11.3 %attn_backward_kernel.1 = bf16[8,384,128]{2,1,0:T(8,128)(2,1)} custom-call(bf16[8,400,128]{2,1,0:T(8,128)(2,1)S(1)} %copy-done.4, bf16[32,32,128]{2,1,0:T(8,128)(2,1)} %all-to-all-done.2.grad, f32[64,2048]{1,0:T(8,128)S(1)} %copy-done.25, f32[1,2048]{1,0:T(1,128)S(1)} %get-tuple-element.119.log_row), custom_call_target="tpu_custom_call" | custom-call | flops 2684354560 | bytes 2400256 | tf_op jit(solution)/shard_map/attn_backward_kernel/pallas_call | solution.py:863
  174.7 4.6 %all-to-all-start.3 = ((bf16[8,384,128]{2,1,0:T(8,128)(2,1)}), bf16[8,384,128]{2,1,0:T(8,128)(2,1)S(1)}, u32[]{:S(2)}, u32[]{:S(2)}) async-start(bf16[8,384,128]{2,1,0:T(8,128)(2,1)} %attn_backward_kernel.1), calls=%async_computation.4 | async-start | bytes 1572864 | tf_op jit(solution)/shard_map/all_to_all | solution.py:1042
  179.5 2.5 collective-permute-start.16
  182.0 2.9 %collective-permute-start.19 = (bf16[128,192]{1,0:T(8,128)(2,1)S(1)}, bf16[128,192]{1,0:T(8,128)(2,1)S(1)}, u32[]{:S(2)}, u32[]{:S(2)}) collective-permute-start(bf16[128,192]{1,0:T(8,128)(2,1)S(1)} %copy-done.23), channel_id=1, source_target_pairs={{0,3},{1,2},{2,1},{3,0},{4,7},{5,6},{6,5},{7,4},{8,11},{9,10},{10,... | collective-permute-start | bytes 147464 | tf_op jit(solution)/shard_map/ppermute | solution.py:879
  185.4 1.1 collective-permute-start.17
  186.4 6.3 %collective-permute-done.19.a3 = bf16[128,192]{1,0:T(8,128)(2,1)S(1)} collective-permute-done((bf16[128,192]{1,0:T(8,128)(2,1)S(1)}, bf16[128,192]{1,0:T(8,128)(2,1)S(1)}, u32[]{:S(2)}, u32[]{:S(2)}) %collective-permute-start.19) | collective-permute-done | bytes 49184 | tf_op jit(solution)/shard_map/ppermute | solution.py:879
  192.8 5.5 %collective-permute-done.16 = bf16[384,192]{1,0:T(8,128)(2,1)S(1)} collective-permute-done((bf16[384,192]{1,0:T(8,128)(2,1)S(1)}, bf16[384,192]{1,0:T(8,128)(2,1)S(1)}, u32[]{:S(2)}, u32[]{:S(2)}) %collective-permute-start.16) | collective-permute-done | bytes 147488 | tf_op jit(solution)/shard_map/ppermute | solution.py:1040
  198.2 0.9 copy-done.27
  199.2 4.7 %last_kernel.1 = (bf16[2,256,768]{2,1,0:T(8,128)(2,1)}, bf16[512,576]{1,0:T(8,128)(2,1)}, f32[8,768]{1,0:T(8,128)}) custom-call(s32[2]{0:T(128)} %pad_add_fusion.place, bf16[8,384,128]{2,1,0:T(8,128)(2,1)} %copy-done.27, bf16[768,640]{1,0:T(8,128)(2,1)} %all_gather.15.weight_in, bf16[2,4,64,768]{3,2,1,0:T(8,128)(2,1)} %get-tuple-element.84.rows_in), custom_call_target="tpu_custom_call" | custom-call | flops 452984832 | bytes 3956744 | tf_op jit(solution)/shard_map/last_kernel/pallas_call | solution.py:863
  203.9 1.1 copy-done.7
  205.0 0.7 copy-done.14
  205.7 1.7 late_grads_kernel.1
  207.8 1.8 collective-permute-done.20.got
  209.8 4.9 %collective-permute-start.22 = (bf16[96,832]{1,0:T(8,128)(2,1)S(1)}, bf16[96,832]{1,0:T(8,128)(2,1)S(1)}, u32[]{:S(2)}, u32[]{:S(2)}) collective-permute-start(bf16[96,832]{1,0:T(8,128)(2,1)S(1)} %get-tuple-element.143), channel_id=1, source_target_pairs={{0,16},{4,20},{8,24},{12,28},{16,0},{20,4},{24,8},{28,12},{1,17},{... | collective-permute-start | bytes 479240 | tf_op jit(solution)/shard_map/ppermute | solution.py:883
  215.5 0.7 collective-permute-done.21
  216.2 5.8 %collective-permute-done.22 = bf16[96,832]{1,0:T(8,128)(2,1)S(1)} collective-permute-done((bf16[96,832]{1,0:T(8,128)(2,1)S(1)}, bf16[96,832]{1,0:T(8,128)(2,1)S(1)}, u32[]{:S(2)}, u32[]{:S(2)}) %collective-permute-start.22) | collective-permute-done | bytes 159776 | tf_op jit(solution)/shard_map/ppermute | solution.py:883
  222.1 1.4 collective-permute-done.23
  223.9 0.7 slice_bitcast_fusion
  224.6 5.2 %collective-permute-done.24 = bf16[96,196]{1,0:T(8,128)(2,1)S(1)} collective-permute-done((bf16[96,196]{1,0:T(8,128)(2,1)S(1)}, bf16[96,196]{1,0:T(8,128)(2,1)S(1)}, u32[]{:S(2)}, u32[]{:S(2)}) %collective-permute-start.24) | collective-permute-done | bytes 37664 | tf_op jit(solution)/shard_map/ppermute | solution.py:879
  230.1 1.7 add_convert_fusion
  231.7 0.8 copy.44
  232.6 6.0 %collective-permute-done.25 = bf16[96,196]{1,0:T(8,128)(2,1)S(1)} collective-permute-done((bf16[96,196]{1,0:T(8,128)(2,1)S(1)}, bf16[96,196]{1,0:T(8,128)(2,1)S(1)}, u32[]{:S(2)}, u32[]{:S(2)}) %collective-permute-start.25) | collective-permute-done | bytes 37664 | tf_op jit(solution)/shard_map/ppermute | solution.py:879
  238.7 0.7 slice_reduce_fusion
  240.1 0.8 pad_maximum_fusion
  240.9 1.1 fusion.12
  242.1 1.9 fusion.10
  (157 shorter events, 11.8 us)
Async XLA Ops:
  7.2 13.4 %copy-start.38 = (bf16[96]{0:T(256)(128)(2,1)S(1)}, bf16[96]{0:T(256)(128)(2,1)}, u32[]{:S(2)}) copy-start(bf16[96]{0:T(256)(128)(2,1)} %param.14) | copy-start | bytes 580
  7.2 13.4 %copy-start.37 = (bf16[96]{0:T(256)(128)(2,1)S(1)}, bf16[96]{0:T(256)(128)(2,1)}, u32[]{:S(2)}) copy-start(bf16[96]{0:T(256)(128)(2,1)} %param.15) | copy-start | bytes 580
  7.2 13.4 %copy-start.36 = (bf16[96]{0:T(256)(128)(2,1)S(1)}, bf16[96]{0:T(256)(128)(2,1)}, u32[]{:S(2)}) copy-start(bf16[96]{0:T(256)(128)(2,1)} %param.18) | copy-start | bytes 580
  7.2 13.4 %copy-start.35 = (bf16[96]{0:T(256)(128)(2,1)S(1)}, bf16[96]{0:T(256)(128)(2,1)}, u32[]{:S(2)}) copy-start(bf16[96]{0:T(256)(128)(2,1)} %param.19) | copy-start | bytes 580
  7.2 14.1 %copy-start.42 = (bf16[384,192]{0,1:T(8,128)(2,1)S(1)}, bf16[384,192]{0,1:T(8,128)(2,1)}, u32[]{:S(2)}) copy-start(bf16[384,192]{0,1:T(8,128)(2,1)} %param.21) | copy-start | bytes 442372
  9.9 11.4 %collective-permute-start.4 = (bf16[208,192]{1,0:T(8,128)(2,1)S(1)}, bf16[208,192]{1,0:T(8,128)(2,1)S(1)}, u32[]{:S(2)}, u32[]{:S(2)}) collective-permute-start(bf16[208,192]{1,0:T(8,128)(2,1)S(1)} %get-tuple-element.208), channel_id=1, source_target_pairs={{0,2},{1,3},{2,0},{3,1},{4,6},{5,7},{6,4},{7,5},{8,10},{9,11},{10,... | collective-permute-start | bytes 239624 | tf_op jit(solution)/shard_map/ppermute | solution.py:879
  12.6 10.7 %collective-permute-start.3 = (bf16[208,192]{1,0:T(8,128)(2,1)S(1)}, bf16[208,192]{1,0:T(8,128)(2,1)S(1)}, u32[]{:S(2)}, u32[]{:S(2)}) collective-permute-start(bf16[208,192]{1,0:T(8,128)(2,1)S(1)} %get-tuple-element.209), channel_id=1, source_target_pairs={{0,1},{1,0},{2,3},{3,2},{4,5},{5,4},{6,7},{7,6},{8,9},{9,8},{10,11... | collective-permute-start | bytes 239624 | tf_op jit(solution)/shard_map/ppermute | solution.py:879
  14.2 21.9 %collective-permute-start = (bf16[2,64,768]{2,1,0:T(8,128)(2,1)}, bf16[2,64,768]{2,1,0:T(8,128)(2,1)S(1)}, u32[]{:S(2)}, u32[]{:S(2)}) collective-permute-start(bf16[2,64,768]{2,1,0:T(8,128)(2,1)} %x0.1), channel_id=1, source_target_pairs={{0,1},{1,0},{2,3},{3,2},{4,5},{5,4},{6,7},{7,6},{8,9},{9,8},{10,11... | collective-permute-start | bytes 589832 | tf_op jit(solution)/shard_map/ppermute | solution.py:879
  14.6 21.5 %collective-permute-start.1 = (bf16[2,64,768]{2,1,0:T(8,128)(2,1)}, bf16[2,64,768]{2,1,0:T(8,128)(2,1)S(1)}, u32[]{:S(2)}, u32[]{:S(2)}) collective-permute-start(bf16[2,64,768]{2,1,0:T(8,128)(2,1)} %x0.1), channel_id=1, source_target_pairs={{0,2},{1,3},{2,0},{3,1},{4,6},{5,7},{6,4},{7,5},{8,10},{9,11},{10,... | collective-permute-start | bytes 589832 | tf_op jit(solution)/shard_map/ppermute | solution.py:879
  16.9 18.4 %collective-permute-start.2 = (bf16[160,768]{1,0:T(8,128)(2,1)S(1)}, bf16[160,768]{1,0:T(8,128)(2,1)S(1)}, u32[]{:S(2)}, u32[]{:S(2)}) collective-permute-start(bf16[160,768]{1,0:T(8,128)(2,1)S(1)} %fusion.17), channel_id=1, source_target_pairs={{0,3},{1,2},{2,1},{3,0},{4,7},{5,6},{6,5},{7,4},{8,11},{9,10},{10,... | collective-permute-start | bytes 737288 | tf_op jit(solution)/shard_map/ppermute | solution.py:879
  21.3 29.1 %collective-permute-start.8 = (bf16[384,192]{0,1:T(8,128)(2,1)S(1)}, bf16[384,192]{0,1:T(8,128)(2,1)S(1)}, u32[]{:S(2)}, u32[]{:S(2)}) collective-permute-start(bf16[384,192]{0,1:T(8,128)(2,1)S(1)} %copy-done.42), channel_id=1, source_target_pairs={{0,0},{1,8},{2,16},{3,24},{4,4},{5,12},{6,20},{7,28},{8,1},{9,9},{... | collective-permute-start | bytes 442376 | tf_op jit(solution)/shard_map/ppermute | solution.py:957
  42.3 9.7 %copy-start.30 = (bf16[96,192]{1,0:T(8,128)(2,1)S(1)}, bf16[96,192]{1,0:T(8,128)(2,1)}, u32[]{:S(2)}) copy-start(bf16[96,192]{1,0:T(8,128)(2,1)} %param.17) | copy-start | bytes 110596
  42.3 9.7 %copy-start.34 = (bf16[96,768]{1,0:T(8,128)(2,1)S(1)}, bf16[96,768]{1,0:T(8,128)(2,1)}, u32[]{:S(2)}) copy-start(bf16[96,768]{1,0:T(8,128)(2,1)} %param.20) | copy-start | bytes 442372
  42.3 20.0 %all-to-all-start = ((bf16[8,400,128]{2,1,0:T(8,128)(2,1)}), bf16[8,400,128]{2,1,0:T(8,128)(2,1)S(1)}, u32[]{:S(2)}, u32[]{:S(2)}) async-start(bf16[8,400,128]{2,1,0:T(8,128)(2,1)} %get-tuple-element.79), calls=%async_computation | async-start | bytes 1638400 | tf_op jit(solution)/shard_map/all_to_all | solution.py:975
  50.4 11.9 %copy-start.10 = (bf16[2,64,768]{2,1,0:T(8,128)(2,1)S(1)}, bf16[2,64,768]{2,1,0:T(8,128)(2,1)}, u32[]{:S(2)}) copy-start(bf16[2,64,768]{2,1,0:T(8,128)(2,1)} %out_grad.1) | copy-start | bytes 589828
  50.4 63.7 %all-gather.4.cloned.1.call-start = ((), (), s32[]{:S(2)}) async-start(), calls=%async_computation.8 | async-start | bytes 3981312 | tf_op jit(solution)/shard_map/all_gather | solution.py:976
  62.3 15.6 %copy-start.3 = (bf16[8,400,128]{2,1,0:T(8,128)(2,1)}, bf16[8,400,128]{2,1,0:T(8,128)(2,1)S(1)}, u32[]{:S(2)}) copy-start(bf16[8,400,128]{2,1,0:T(8,128)(2,1)S(1)} %all-to-all-done.pack) | copy-start | bytes 2457604
  62.3 15.6 %collective-permute-start.5 = (bf16[2,64,768]{2,1,0:T(8,128)(2,1)S(1)}, bf16[2,64,768]{2,1,0:T(8,128)(2,1)S(1)}, u32[]{:S(2)}, u32[]{:S(2)}) collective-permute-start(bf16[2,64,768]{2,1,0:T(8,128)(2,1)S(1)} %copy-done.10), channel_id=1, source_target_pairs={{0,1},{1,0},{2,3},{3,2},{4,5},{5,4},{6,7},{7,6},{8,9},{9,8},{10,11... | collective-permute-start | bytes 589832 | tf_op jit(solution)/shard_map/ppermute | solution.py:879
  64.8 15.8 %collective-permute-start.6 = (bf16[2,64,768]{2,1,0:T(8,128)(2,1)S(1)}, bf16[2,64,768]{2,1,0:T(8,128)(2,1)S(1)}, u32[]{:S(2)}, u32[]{:S(2)}) collective-permute-start(bf16[2,64,768]{2,1,0:T(8,128)(2,1)S(1)} %copy-done.10), channel_id=1, source_target_pairs={{0,2},{1,3},{2,0},{3,1},{4,6},{5,7},{6,4},{7,5},{8,10},{9,11},{10,... | collective-permute-start | bytes 589832 | tf_op jit(solution)/shard_map/ppermute | solution.py:879
  66.6 14.0 %collective-permute-start.7 = (bf16[2,64,768]{2,1,0:T(8,128)(2,1)S(1)}, bf16[2,64,768]{2,1,0:T(8,128)(2,1)S(1)}, u32[]{:S(2)}, u32[]{:S(2)}) collective-permute-start(bf16[2,64,768]{2,1,0:T(8,128)(2,1)S(1)} %copy-done.10), channel_id=1, source_target_pairs={{0,3},{1,2},{2,1},{3,0},{4,7},{5,6},{6,5},{7,4},{8,11},{9,10},{10,... | collective-permute-start | bytes 589832 | tf_op jit(solution)/shard_map/ppermute | solution.py:879
  77.9 45.4 %copy-start.24 = (f32[64,2048]{1,0:T(8,128)}, f32[64,2048]{1,0:T(8,128)S(1)}, u32[]{:S(2)}) copy-start(f32[64,2048]{1,0:T(8,128)S(1)} %get-tuple-element.118.out_cols) | copy-start | bytes 1572868
  78.0 36.2 %copy-start.39 = (bf16[2,64,768]{2,1,0:T(8,128)(2,1)}, bf16[2,64,768]{2,1,0:T(8,128)(2,1)S(1)}, u32[]{:S(2)}) copy-start(bf16[2,64,768]{2,1,0:T(8,128)(2,1)S(1)} %collective-permute-done.5.g1) | copy-start | bytes 589828
  80.6 33.5 %copy-start.40 = (bf16[2,64,768]{2,1,0:T(8,128)(2,1)}, bf16[2,64,768]{2,1,0:T(8,128)(2,1)S(1)}, u32[]{:S(2)}) copy-start(bf16[2,64,768]{2,1,0:T(8,128)(2,1)S(1)} %collective-permute-done.6.g2) | copy-start | bytes 589828
  80.6 33.5 %copy-start.41 = (bf16[2,64,768]{2,1,0:T(8,128)(2,1)}, bf16[2,64,768]{2,1,0:T(8,128)(2,1)S(1)}, u32[]{:S(2)}) copy-start(bf16[2,64,768]{2,1,0:T(8,128)(2,1)S(1)} %collective-permute-done.7.g3) | copy-start | bytes 589828
  123.3 12.9 %collective-permute-start.10 = (bf16[2,64,768]{2,1,0:T(8,128)(2,1)}, bf16[2,64,768]{2,1,0:T(8,128)(2,1)S(1)}, u32[]{:S(2)}, u32[]{:S(2)}) collective-permute-start(bf16[2,64,768]{2,1,0:T(8,128)(2,1)} %get-tuple-element.99), channel_id=1, source_target_pairs={{0,2},{1,3},{2,0},{3,1},{4,6},{5,7},{6,4},{7,5},{8,10},{9,11},{10,... | collective-permute-start | bytes 589832 | tf_op jit(solution)/shard_map/ppermute | solution.py:879
  124.2 12.0 %collective-permute-start.11 = (bf16[2,64,768]{2,1,0:T(8,128)(2,1)}, bf16[2,64,768]{2,1,0:T(8,128)(2,1)S(1)}, u32[]{:S(2)}, u32[]{:S(2)}) collective-permute-start(bf16[2,64,768]{2,1,0:T(8,128)(2,1)} %get-tuple-element.100), channel_id=1, source_target_pairs={{0,3},{1,2},{2,1},{3,0},{4,7},{5,6},{6,5},{7,4},{8,11},{9,10},{10,... | collective-permute-start | bytes 589832 | tf_op jit(solution)/shard_map/ppermute | solution.py:879
  125.5 10.7 %collective-permute-start.9 = (bf16[2,64,768]{2,1,0:T(8,128)(2,1)}, bf16[2,64,768]{2,1,0:T(8,128)(2,1)S(1)}, u32[]{:S(2)}, u32[]{:S(2)}) collective-permute-start(bf16[2,64,768]{2,1,0:T(8,128)(2,1)} %get-tuple-element.98), channel_id=1, source_target_pairs={{0,1},{1,0},{2,3},{3,2},{4,5},{5,4},{6,7},{7,6},{8,9},{9,8},{10,11... | collective-permute-start | bytes 589832 | tf_op jit(solution)/shard_map/ppermute | solution.py:879
  126.9 9.4 %copy-start = (f32[2,64,768]{2,1,0:T(8,128)S(1)}, f32[2,64,768]{2,1,0:T(8,128)}, u32[]{:S(2)}) copy-start(f32[2,64,768]{2,1,0:T(8,128)} %get-tuple-element.91.middle) | copy-start | bytes 1179652
  126.9 9.4 %copy-start.11 = (bf16[2,64,768]{2,1,0:T(8,128)(2,1)S(1)}, bf16[2,64,768]{2,1,0:T(8,128)(2,1)}, u32[]{:S(2)}) copy-start(bf16[2,64,768]{2,1,0:T(8,128)(2,1)} %out_grad.1) | copy-start | bytes 589828
  126.9 9.4 %copy-start.12 = (bf16[2,64,768]{2,1,0:T(8,128)(2,1)S(1)}, bf16[2,64,768]{2,1,0:T(8,128)(2,1)}, u32[]{:S(2)}) copy-start(bf16[2,64,768]{2,1,0:T(8,128)(2,1)} %get-tuple-element.97.g0) | copy-start | bytes 589828
  126.9 9.4 %copy-start.13 = (f32[8,768]{1,0:T(8,128)S(1)}, f32[8,768]{1,0:T(8,128)}, u32[]{:S(2)}) copy-start(f32[8,768]{1,0:T(8,128)} %get-tuple-element.90.vectors) | copy-start | bytes 73732
  126.9 9.4 %copy-start.15 = (s32[2]{0:T(128)S(1)}, s32[2]{0:T(128)}, u32[]{:S(2)}) copy-start(s32[2]{0:T(128)} %pad_add_fusion.place) | copy-start | bytes 28
  136.3 1.3 copy-start.2
  137.5 10.7 %copy-start.1 = (bf16[4,2,96,768]{3,2,1,0:T(8,128)(2,1)S(1)}, bf16[4,2,96,768]{3,2,1,0:T(8,128)(2,1)}, u32[]{:S(2)}) copy-start(bf16[4,2,96,768]{3,2,1,0:T(8,128)(2,1)} %get-tuple-element.105.keep) | copy-start | bytes 3538948
  141.7 6.5 %collective-permute-start.12 = (bf16[4,2,96,768]{3,2,1,0:T(8,128)(2,1)}, bf16[4,2,96,768]{3,2,1,0:T(8,128)(2,1)S(1)}, u32[]{:S(2)}, u32[]{:S(2)}) collective-permute-start(bf16[4,2,96,768]{3,2,1,0:T(8,128)(2,1)} %get-tuple-element.108), channel_id=1, source_target_pairs={{0,4},{4,0},{8,12},{12,8},{16,20},{20,16},{24,28},{28,24},{1,5},{5... | collective-permute-start | bytes 3538952 | tf_op jit(solution)/shard_map/ppermute | solution.py:883
  141.7 15.8 %all-to-all-start.2 = ((bf16[32,32,128]{2,1,0:T(8,128)(2,1)}), bf16[32,32,128]{2,1,0:T(8,128)(2,1)}, u32[]{:S(2)}, u32[]{:S(2)}) async-start(bf16[32,32,128]{2,1,0:T(8,128)(2,1)} %bitcast.10), calls=%async_computation.2 | async-start | bytes 524288 | tf_op jit(solution)/shard_map/all_to_all | solution.py:1024
  148.0 82.1 %reduce-scatter.3.cloned.1.call-start = ((), (), s32[]{:S(2)}) async-start(), calls=%async_computation.6 | async-start | bytes 983040 | tf_op jit(solution)/shard_map/reduce_scatter | solution.py:1025
  157.5 17.0 %collective-permute-start.13 = (bf16[2,96,768]{2,1,0:T(8,128)(2,1)}, bf16[2,96,768]{2,1,0:T(8,128)(2,1)S(1)}, u32[]{:S(2)}, u32[]{:S(2)}) collective-permute-start(bf16[2,96,768]{2,1,0:T(8,128)(2,1)} %copy-done.19), channel_id=1, source_target_pairs={{0,8},{4,12},{8,0},{12,4},{16,24},{20,28},{24,16},{28,20},{1,9},{5... | collective-permute-start | bytes 884744 | tf_op jit(solution)/shard_map/ppermute | solution.py:883
  158.0 16.5 %collective-permute-start.14 = (bf16[2,96,768]{2,1,0:T(8,128)(2,1)}, bf16[2,96,768]{2,1,0:T(8,128)(2,1)S(1)}, u32[]{:S(2)}, u32[]{:S(2)}) collective-permute-start(bf16[2,96,768]{2,1,0:T(8,128)(2,1)} %copy-done.18), channel_id=1, source_target_pairs={{0,16},{4,20},{8,24},{12,28},{16,0},{20,4},{24,8},{28,12},{1,17},{... | collective-permute-start | bytes 884744 | tf_op jit(solution)/shard_map/ppermute | solution.py:883
  159.5 15.0 %collective-permute-start.15 = (bf16[2,96,768]{2,1,0:T(8,128)(2,1)}, bf16[2,96,768]{2,1,0:T(8,128)(2,1)S(1)}, u32[]{:S(2)}, u32[]{:S(2)}) collective-permute-start(bf16[2,96,768]{2,1,0:T(8,128)(2,1)} %copy-done.17), channel_id=1, source_target_pairs={{0,24},{4,28},{8,16},{12,20},{16,8},{20,12},{24,0},{28,4},{1,25},{... | collective-permute-start | bytes 884744 | tf_op jit(solution)/shard_map/ppermute | solution.py:883
  161.0 1.1 copy-start.4
  162.2 1.0 copy-start.25
  174.7 4.8 %copy-start.28 = (f32[2,96,768]{2,1,0:T(8,128)}, f32[2,96,768]{2,1,0:T(8,128)S(1)}, u32[]{:S(2)}) copy-start(f32[2,96,768]{2,1,0:T(8,128)S(1)} %convert_add_fusion) | copy-start | bytes 1769476
  174.7 7.3 %copy-start.23 = (bf16[128,192]{1,0:T(8,128)(2,1)S(1)}, bf16[128,192]{1,0:T(8,128)(2,1)}, u32[]{:S(2)}) copy-start(bf16[128,192]{1,0:T(8,128)(2,1)} %copy-done.22) | copy-start | bytes 147460
  174.7 10.2 %copy-start.21 = (bf16[128,192]{1,0:T(8,128)(2,1)S(1)}, bf16[128,192]{1,0:T(8,128)(2,1)}, u32[]{:S(2)}) copy-start(bf16[128,192]{1,0:T(8,128)(2,1)} %copy-done.20) | copy-start | bytes 147460
  174.7 23.6 %all-to-all-start.3 = ((bf16[8,384,128]{2,1,0:T(8,128)(2,1)}), bf16[8,384,128]{2,1,0:T(8,128)(2,1)S(1)}, u32[]{:S(2)}, u32[]{:S(2)}) async-start(bf16[8,384,128]{2,1,0:T(8,128)(2,1)} %attn_backward_kernel.1), calls=%async_computation.4 | async-start | bytes 1572864 | tf_op jit(solution)/shard_map/all_to_all | solution.py:1042
  179.3 61.6 %reduce-scatter.5.cloned.1.call-start = ((), (), s32[]{:S(2)}) async-start(), calls=%async_computation.7 | async-start | bytes 983040 | tf_op jit(solution)/shard_map/reduce_scatter | solution.py:1054
  179.5 18.8 %collective-permute-start.16 = (bf16[384,192]{1,0:T(8,128)(2,1)S(1)}, bf16[384,192]{1,0:T(8,128)(2,1)S(1)}, u32[]{:S(2)}, u32[]{:S(2)}) collective-permute-start(bf16[384,192]{1,0:T(8,128)(2,1)S(1)} %pad_maximum_fusion.1), channel_id=1, source_target_pairs={{0,0},{8,1},{16,2},{24,3},{4,4},{12,5},{20,6},{28,7},{1,8},{9,9},{... | collective-permute-start | bytes 442376 | tf_op jit(solution)/shard_map/ppermute | solution.py:1040
  182.0 10.8 %collective-permute-start.19 = (bf16[128,192]{1,0:T(8,128)(2,1)S(1)}, bf16[128,192]{1,0:T(8,128)(2,1)S(1)}, u32[]{:S(2)}, u32[]{:S(2)}) collective-permute-start(bf16[128,192]{1,0:T(8,128)(2,1)S(1)} %copy-done.23), channel_id=1, source_target_pairs={{0,3},{1,2},{2,1},{3,0},{4,7},{5,6},{6,5},{7,4},{8,11},{9,10},{10,... | collective-permute-start | bytes 147464 | tf_op jit(solution)/shard_map/ppermute | solution.py:879
  184.8 7.9 %collective-permute-start.18 = (bf16[128,192]{1,0:T(8,128)(2,1)S(1)}, bf16[128,192]{1,0:T(8,128)(2,1)S(1)}, u32[]{:S(2)}, u32[]{:S(2)}) collective-permute-start(bf16[128,192]{1,0:T(8,128)(2,1)S(1)} %copy-done.21), channel_id=1, source_target_pairs={{0,2},{1,3},{2,0},{3,1},{4,6},{5,7},{6,4},{7,5},{8,10},{9,11},{10,... | collective-permute-start | bytes 147464 | tf_op jit(solution)/shard_map/ppermute | solution.py:879
  185.4 7.4 %collective-permute-start.17 = (bf16[128,192]{1,0:T(8,128)(2,1)S(1)}, bf16[128,192]{1,0:T(8,128)(2,1)S(1)}, u32[]{:S(2)}, u32[]{:S(2)}) collective-permute-start(bf16[128,192]{1,0:T(8,128)(2,1)S(1)} %get-tuple-element.125), channel_id=1, source_target_pairs={{0,1},{1,0},{2,3},{3,2},{4,5},{5,4},{6,7},{7,6},{8,9},{9,8},{10,11... | collective-permute-start | bytes 147464 | tf_op jit(solution)/shard_map/ppermute | solution.py:879
  186.4 17.4 %copy-start.5 = (bf16[512,768]{1,0:T(8,128)(2,1)S(1)}, bf16[512,768]{1,0:T(8,128)(2,1)}, u32[]{:S(2)}) copy-start(bf16[512,768]{1,0:T(8,128)(2,1)} %get-tuple-element.81.normed) | copy-start | bytes 2359300
  186.4 17.4 %copy-start.6 = (bf16[512,768]{1,0:T(8,128)(2,1)S(1)}, bf16[512,768]{1,0:T(8,128)(2,1)}, u32[]{:S(2)}) copy-start(bf16[512,768]{1,0:T(8,128)(2,1)} %get-tuple-element.134.mixed) | copy-start | bytes 2359300
  186.4 17.4 %copy-start.16 = (s32[2]{0:T(128)S(1)}, s32[2]{0:T(128)}, u32[]{:S(2)}) copy-start(s32[2]{0:T(128)} %pad_add_fusion.place) | copy-start | bytes 28
  203.9 1.1 copy-start.7
  205.7 1.7 copy-start.26
  207.4 2.2 collective-permute-start.20
  209.7 6.5 %collective-permute-start.21 = (bf16[96,832]{1,0:T(8,128)(2,1)S(1)}, bf16[96,832]{1,0:T(8,128)(2,1)S(1)}, u32[]{:S(2)}, u32[]{:S(2)}) collective-permute-start(bf16[96,832]{1,0:T(8,128)(2,1)S(1)} %get-tuple-element.142), channel_id=1, source_target_pairs={{0,8},{4,12},{8,0},{12,4},{16,24},{20,28},{24,16},{28,20},{1,9},{5... | collective-permute-start | bytes 479240 | tf_op jit(solution)/shard_map/ppermute | solution.py:883
  209.8 12.2 %collective-permute-start.22 = (bf16[96,832]{1,0:T(8,128)(2,1)S(1)}, bf16[96,832]{1,0:T(8,128)(2,1)S(1)}, u32[]{:S(2)}, u32[]{:S(2)}) collective-permute-start(bf16[96,832]{1,0:T(8,128)(2,1)S(1)} %get-tuple-element.143), channel_id=1, source_target_pairs={{0,16},{4,20},{8,24},{12,28},{16,0},{20,4},{24,8},{28,12},{1,17},{... | collective-permute-start | bytes 479240 | tf_op jit(solution)/shard_map/ppermute | solution.py:883
  214.7 8.8 %collective-permute-start.23 = (bf16[96,832]{1,0:T(8,128)(2,1)S(1)}, bf16[96,832]{1,0:T(8,128)(2,1)S(1)}, u32[]{:S(2)}, u32[]{:S(2)}) collective-permute-start(bf16[96,832]{1,0:T(8,128)(2,1)S(1)} %get-tuple-element.144), channel_id=1, source_target_pairs={{0,24},{4,28},{8,16},{12,20},{16,8},{20,12},{24,0},{28,4},{1,25},{... | collective-permute-start | bytes 479240 | tf_op jit(solution)/shard_map/ppermute | solution.py:883
  215.5 8.4 %copy-start.29 = (f32[2,96,768]{2,1,0:T(8,128)S(1)}, f32[2,96,768]{2,1,0:T(8,128)}, u32[]{:S(2)}) copy-start(f32[2,96,768]{2,1,0:T(8,128)} %copy-done.28) | copy-start | bytes 1769476
  223.9 6.0 %collective-permute-start.24 = (bf16[96,196]{1,0:T(8,128)(2,1)S(1)}, bf16[96,196]{1,0:T(8,128)(2,1)S(1)}, u32[]{:S(2)}, u32[]{:S(2)}) collective-permute-start(bf16[96,196]{1,0:T(8,128)(2,1)S(1)} %pad_maximum_fusion.9), channel_id=1, source_target_pairs={{0,1},{1,0},{2,3},{3,2},{4,5},{5,4},{6,7},{7,6},{8,9},{9,8},{10,11... | collective-permute-start | bytes 112904 | tf_op jit(solution)/shard_map/ppermute | solution.py:879
  230.0 8.6 %collective-permute-start.25 = (bf16[96,196]{1,0:T(8,128)(2,1)S(1)}, bf16[96,196]{1,0:T(8,128)(2,1)S(1)}, u32[]{:S(2)}, u32[]{:S(2)}) collective-permute-start(bf16[96,196]{1,0:T(8,128)(2,1)S(1)} %pad_maximum_fusion.10), channel_id=1, source_target_pairs={{0,2},{1,3},{2,0},{3,1},{4,6},{5,7},{6,4},{7,5},{8,10},{9,11},{10,... | collective-permute-start | bytes 112904 | tf_op jit(solution)/shard_map/ppermute | solution.py:879
  232.6 9.5 %copy-start.9 = (f32[2,64,768]{2,1,0:T(8,128)S(1)}, f32[2,64,768]{2,1,0:T(8,128)}, u32[]{:S(2)}) copy-start(f32[2,64,768]{2,1,0:T(8,128)} %copy-done.8) | copy-start | bytes 1179652
  (11 other events, 7.9 us)
Sparse Core Ops, SparseCore 0:
  62.5 37.3 all-gather.3
  161.2 21.8 reduce-scatter.2
  215.6 25.0 reduce-scatter.4

commit v3 on v2

--- a/solution.py
+++ b/solution.py
@@ -505,14 +505,14 @@
     return lax.dot_general(left, right, ACROSS, preferred_element_type=jnp.float32)
 
 
-def copies(pairs, sems):
+def copies(sems, *pairs):
     moves = [pltpu.make_async_copy(source, target, sems.at[n]) for n, (source, target) in enumerate(pairs)]
     for move in moves:
         move.start()
     return moves
 
 
-def finish(moves):
+def finish(*moves):
     for move in moves:
         move.wait()
 
@@ -523,19 +523,69 @@
     return query, key, 3 - query - key
 
 
-def first_kernel(place, x0, x1, x2, x3, starts, weight_in, pack, normed, rows_out, vectors, weight, rows, parts, sems):
+def send_kernel(place, weight_in, out_in, starts_in, to_one, to_two, shared, weight, out_weight, doc_starts, sems):
+    finish(*copies(sems, (weight_in, weight), (out_in, out_weight), (starts_in, doc_starts)))
+    even = lax.rem(place[1], 2) == 0
+    groups = [weight[:, 192 * number : 192 * (number + 1)] for number in range(3)]
+    starts = doc_starts[...]
+    starts = in_f32(jnp.concatenate([starts // 128, lax.rem(starts, 128), jnp.zeros_like(starts)], axis=1))
+    lines = jnp.concatenate([in_f32(out_weight[...]), starts, jnp.zeros((30, 192), jnp.float32)], axis=0)
+    lines = in_bf16(lines)
+    to_one[:96, :] = groups[1]
+    to_two[:96, :] = jnp.where(even, groups[2], groups[0])
+    to_one[96:, :] = lines[:112]
+    to_two[96:, :] = lines[:112]
+    shared[...] = lines
+
+
+def third_kernel(inputs, shared, to_three, sems):
+    moves = copies(
+        sems,
+        (inputs.at[0], to_three.at[pl.ds(0, 64)]),
+        (inputs.at[1], to_three.at[pl.ds(64, 64)]),
+    )
+    for number in range(4):
+        to_three[128:, 192 * number : 192 * (number + 1)] = shared[32 * number : 32 * (number + 1)]
+    finish(*moves)
+
+
+def shard_kernel(place, weight, got_one, got_two, vectors, shard):
+    even = lax.rem(place[1], 2) == 0
+    shard[:, :192] = jnp.where(even, weight[:, :192], weight[:, 384:])
+    shard[:, 192:384] = got_one[:96, :]
+    shard[:, 384:576] = got_two[:96, :]
+    lines = jnp.concatenate([in_f32(vectors[...]), jnp.zeros((60, 96), jnp.float32)], axis=0)
+    shard[:, 576:] = in_bf16(lines.T)
+
+
+def weights_kernel(down, out_weight, got_one, got_two, got_three, weights):
+    for number in range(4):
+        at = slice(192 * number, 192 * (number + 1))
+        weights[:, at] = down[96 * number : 96 * (number + 1), :]
+        at = slice(WIDE + 192 * number, WIDE + 192 * (number + 1))
+        if number < 3:
+            weights[:, at] = (out_weight[...], got_one[96:192, :], got_two[96:192, :])[number]
+        else:
+            for part in range(3):
+                weights[32 * part : 32 * (part + 1), at] = got_three[128:, 192 * part : 192 * (part + 1)]
+
+
+def first_kernel(place, x0, x1, x2, x3, got_one, got_two, doc_starts, weight, pack, normed, rows, vectors, parts):
     uly = place[1]
-    moves = copies(
-        [(weight_in, weight)]
-        + [
-            (part.at[seq], rows.at[seq, uly ^ shift])
-            for shift, part in enumerate((x0, x1, x2))
-            for seq in range(2)
-        ]
-        + [(x3.at[pl.ds(64 * seq, 64)], rows.at[seq, uly ^ 3]) for seq in range(2)],
-        sems,
-    )
-    known = in_f32(starts[...])
+    for shift, part in enumerate((x0, x1, x2, x3)):
+        for seq in range(2):
+            rows[seq, uly ^ shift] = part[64 * seq : 64 * (seq + 1)] if shift == 3 else part[seq]
+    full = weight[...].reshape(WIDE, 640)
+    own = doc_starts[...]
+    known = jnp.concatenate(
+        [
+            in_f32(jnp.concatenate([own // 128, lax.rem(own, 128)], axis=1)),
+            in_f32(got_one[192:208, :128])[:2],
+            in_f32(got_two[192:208, :128])[:2],
+            in_f32(x3[128:144, 576:704])[:2],
+        ],
+        axis=0,
+    )
     even, low_half = lax.rem(uly, 2) == 0, uly < 2
     for seq in range(2):
         chunks = [known[2 * shift + seq : 2 * shift + seq + 1] for shift in range(4)]
@@ -553,14 +603,12 @@
         for head in range(3):
             pack[4 * seq + head, 384:, :] = lines
         pack[4 * seq + 3] = jnp.zeros((PACK, 128), jnp.bfloat16)
-    finish(moves)
-    rows_out[...] = rows[...]
-    vector_rows = in_f32(weight[:, 512:640]).T[64:72]
+    vector_rows = in_f32(full[:, 512:640]).T[64:72]
     vectors[...] = vector_rows
     normal, unused = norm_stats(in_f32(rows[...].reshape(512, WIDE)))
     value = in_bf16(normal * vector_rows[0:1] + vector_rows[1:2])
     normed[...] = value
-    product = in_bf16(mul(value, weight[:, :576]))
+    product = in_bf16(mul(value, full[:, :576]))
     for number in range(3):
         parts[number] = product[:, 192 * number : 192 * (number + 1)]
     queries, keys, values = (parts[at] for at in group_places(uly))
@@ -586,7 +634,7 @@
     return in_f32(key_at), key_at <= query_at
 
 
-def attn_forward_kernel(pack, packed_out, out_cols, log_row, q_rows, k_rows, v_cols):
+def attn_forward_kernel(pack, packed_out, out_cols, log_row, q_rows, k_rows, v_cols, held, probs):
     scale = LOG2E * HEAD_DIM**-0.5
     for t in range(TILES):
         rows = pl.ds(t * TILE, TILE)
@@ -599,26 +647,26 @@
         q_at = pl.ds(i * TILE, TILE)
         queries = q_rows[q_at, :]
         first = first_row(pack, i)
-        top = total = acc = None
-        for j in range(i, -1, -1):
-            k_at = pl.ds(j * TILE, TILE)
-            scores = mul_t(k_rows[k_at, :], queries)
+        top = None
+        for j in range(i + 1):
+            scores = mul_t(k_rows[pl.ds(j * TILE, TILE), :], queries)
             allowed = key_at >= first - float(j * TILE)
             if j == i:
                 allowed = allowed & causal
             scores = jnp.where(allowed, scores * scale, neg_large)
-            tile_top = jnp.max(scores, axis=0, keepdims=True)
-            new_top = tile_top if top is None else jnp.maximum(top, tile_top)
-            weights = jnp.exp2(scores - new_top)
-            tile_sum = jnp.sum(weights, axis=0, keepdims=True)
-            tile_acc = mul(v_cols[:, k_at], in_bf16(weights))
-            if top is None:
-                total, acc = tile_sum, tile_acc
-            else:
-                factor = jnp.exp2(top - new_top)
-                total = factor * total + tile_sum
-                acc = factor * acc + tile_acc
-            top = new_top
+            held[i % 2, j] = scores
+            tile_top = jnp.max(scores.reshape(TILE // 8, 8, TILE), axis=0)
+            top = tile_top if top is None else jnp.maximum(top, tile_top)
+        top = jnp.max(top, axis=0, keepdims=True)
+        total = None
+        for j in range(i + 1):
+            weights = jnp.exp2(held[i % 2, j] - top)
+            tile_sum = jnp.sum(weights.reshape(TILE // 8, 8, TILE), axis=0)
+            total = tile_sum if total is None else total + tile_sum
+            probs[i % 2, pl.ds(j * TILE, TILE), :] = in_bf16(weights)
+        seen = pl.ds(0, (i + 1) * TILE)
+        acc = mul(v_cols[:, seen], probs[i % 2, seen, :])
+        total = jnp.sum(total, axis=0, keepdims=True)
         acc = acc / total
         out_cols[:, q_at] = acc
         log_row[:, q_at] = top + jnp.log2(total)
@@ -626,7 +674,7 @@
 
 
 def attn_backward_kernel(
-    pack, grad, out_cols, log_row, dpack, q_rows, k_rows, v_rows, g_rows, k_cols, delta, firsts, dq_cols
+    pack, grad, out_cols, log_row, dpack, q_rows, k_rows, v_rows, g_rows, k_cols, delta, firsts, dq_cols, probs, dscores
 ):
     scale = LOG2E * HEAD_DIM**-0.5
     for t in range(TILES):
@@ -645,69 +693,62 @@
     for j in range(TILES):
         k_at = pl.ds(j * TILE, TILE)
         keys, values, keys_t = k_rows[k_at, :], v_rows[k_at, :], k_cols[:, k_at]
-        dk = dv = None
         for i in range(j, TILES):
             q_at = pl.ds(i * TILE, TILE)
-            queries, grads = q_rows[q_at, :], g_rows[q_at, :]
             allowed = key_at >= firsts[:, q_at] - float(j * TILE)
             if i == j:
                 allowed = allowed & causal
-            scores = mul_t(keys, queries) * scale - log_row[:, q_at]
-            probs = jnp.exp2(jnp.where(allowed, scores, neg_large))
-            dscores = in_bf16(probs * (mul_t(values, grads) - delta[:, q_at]))
-            dv_tile = mul(in_bf16(probs), grads)
-            dk_tile = mul(dscores, queries)
-            dq_tile = mul(keys_t, dscores)
-            dv = dv_tile if dv is None else dv + dv_tile
-            dk = dk_tile if dk is None else dk + dk_tile
-            if j == 0:
-                dq_cols[:, q_at] = dq_tile
-            else:
-                dq_cols[:, q_at] += dq_tile
+            scores = mul_t(keys, q_rows[q_at, :]) * scale - log_row[:, q_at]
+            weights = jnp.exp2(jnp.where(allowed, scores, neg_large))
+            probs[j % 2, :, q_at] = in_bf16(weights)
+            dscores[j % 2, :, q_at] = in_bf16(weights * (mul_t(values, g_rows[q_at, :]) - delta[:, q_at]))
+        later = pl.ds(j * TILE, FULL_TOK - j * TILE)
+        dv = mul(probs[j % 2, :, later], g_rows[later, :])
+        dk = mul(dscores[j % 2, :, later], q_rows[later, :])
+        dq = mul(keys_t, dscores[j % 2, :, later])
+        if j == 0:
+            dq_cols[...] = dq
+        else:
+            dq_cols[:, later] += dq
         dq = (dq_cols[:, k_at] * HEAD_DIM**-0.5).T
         dk = dk * HEAD_DIM**-0.5
         dpack[j, :TILE, :] = in_bf16(jnp.concatenate([dq, dk], axis=1))
         dpack[j, TILE:, :] = halves_in(in_bf16(dv))
 
 
-def down_from(weights, columns, full):
-    for at in range(8):
-        for number in range(4):
-            lane = WIDE + 192 * number
-            columns[at // 2, pl.ds(384 * (at % 2) + 96 * number, 96), :] = weights[at, :, lane : lane + 192]
-    for group in range(4):
-        full[:, 192 * group : 192 * (group + 1)] = columns[group]
-
-
-def out_from(weights, uly, columns, full):
-    for shift in range(4):
-        lane = 2 * WIDE + 192 * shift
-        columns[uly ^ shift] = weights[:, :, lane : lane + 192].reshape(WIDE, 192)
-    for group in range(4):
-        full[:, 192 * group : 192 * (group + 1)] = columns[group]
-
-
-def middle_kernel(place, mixed_pack, rows_in, g0, g1, g2, g3, weights_in, vectors, *refs):
-    outs, (weights, columns, down, w_out, rows, parts, slots, sems) = refs[:10], refs[10:]
-    grad_outs, (mixed, middle_own, normed, act_out, pre_out, grad_branch) = outs[:4], outs[4:]
+def middle_kernel(place, mixed_pack, rows_in, weights_in, up_in, g0, g1, g2, g3, vectors, *refs):
+    grad_outs, (mixed_to, middle_to, normed_to, act_to, pre_to) = refs[:4], refs[4:9]
+    w_out_to, w_down_to, branch_to = refs[9:12]
+    slots, mixed, rows, weights, up, parts, columns, w_out, w_down, grad_branch = refs[12:22]
+    middle_own, normed, act_out, pre_out, sems = refs[22:]
     uly = place[1]
     moves = copies(
-        [(weights_in, weights), (rows_in, rows)]
-        + [
-            (part.at[seq], parts.at[seq, uly ^ shift])
-            for shift, part in enumerate((g0, g1, g2, g3))
-            for seq in range(2)
-        ],
-        sems,
+        sems.at[pl.ds(0, 4)],
+        (weights_in.at[:, :, pl.ds(WIDE, WIDE)], weights.at[1]),
+        (rows_in, rows),
+        (up_in, up),
+        (weights_in.at[:, :, pl.ds(0, WIDE)], weights.at[0]),
     )
     for group in range(4):
         for seq in range(2):
             for head in range(3):
                 at = 192 * group + HEAD_DIM * head
                 mixed[pl.ds(256 * seq, 256), at : at + HEAD_DIM] = halves_out(mixed_pack[group, seq, head])
-    finish(moves)
-    out_from(weights, uly, columns, w_out)
-    middle = in_f32(rows[...].reshape(512, WIDE)) + branch_scale * mul(mixed[...], w_out[...])
+    out_moves = copies(sems.at[pl.ds(4, 1)], (mixed, mixed_to))
+    for shift, part in enumerate((g0, g1, g2, g3)):
+        for seq in range(2):
+            parts[seq, uly ^ shift] = in_bf16(branch_scale * in_f32(part[seq]))
+    grad_branch[...] = parts[...].reshape(512, WIDE)
+    out_moves += copies(sems.at[pl.ds(5, 1)], (grad_branch, branch_to))
+    finish(moves[0])
+    for shift in range(4):
+        columns[0, uly ^ shift] = weights[1, :, :, 192 * shift : 192 * (shift + 1)].reshape(WIDE, 192)
+    for group in range(4):
+        w_out[:, 192 * group : 192 * (group + 1)] = columns[0, group]
+    out_moves += copies(sems.at[pl.ds(6, 1)], (w_out, w_out_to))
+    projected = mul(mixed[...], w_out[...])
+    finish(moves[1])
+    middle = in_f32(rows[...].reshape(512, WIDE)) + branch_scale * projected
     normal, unused = norm_stats(middle)
     normed[...] = in_bf16(normal * vectors[2:3] + vectors[3:4])
     chunks = middle.reshape(2, 4, 64, WIDE)
@@ -716,53 +757,64 @@
         jnp.where(uly == 0, chunks[:, 0], chunks[:, 1]),
         jnp.where(uly == 2, chunks[:, 2], chunks[:, 3]),
     )
-    down_from(weights, columns, down)
-    grad_branch[...] = in_bf16(branch_scale * in_f32(parts[...])).reshape(512, WIDE)
-    up_full = weights[:, :, :WIDE].reshape(WIDE, WIDE)
-    pre = mul(normed[...], up_full)
-    grad_act = mul_t(grad_branch[...], down[...])
+    out_moves += copies(sems.at[pl.ds(8, 2)], (normed, normed_to), (middle_own, middle_to))
+    finish(moves[2])
+    w_up = up[...].reshape(WIDE, WIDE)
+    pre = mul(normed[...], w_up)
+    finish(moves[3])
+    for at in range(8):
+        for number in range(4):
+            columns[1, (at // 2) ^ uly, pl.ds(384 * (at % 2) + 96 * number, 96), :] = weights[
+                0, at, :, 192 * number : 192 * (number + 1)
+            ]
+    for group in range(4):
+        w_down[:, 192 * group : 192 * (group + 1)] = columns[1, group]
+    out_moves += copies(sems.at[pl.ds(7, 1)], (w_down, w_down_to))
+    grad_act = mul_t(grad_branch[...], w_down[...])
     square = pre * pre
     bend = jnp.tanh(math.sqrt(2.0 / math.pi) * pre * (1.0 + 0.044715 * square))
     half = 0.5 * (1.0 + bend)
     act_out[...] = in_bf16(pre * half)
+    out_moves += copies(sems.at[pl.ds(10, 1)], (act_out, act_to))
     slope = math.sqrt(2.0 / math.pi) * (1.0 + 3 * 0.044715 * square)
     gate = half + 0.5 * pre * (1.0 - bend * bend) * slope
     pre_out[...] = in_bf16(grad_act * gate)
-    result = in_bf16(mul_t(pre_out[...], up_full)).reshape(2, 4, 64, WIDE)
+    out_moves += copies(sems.at[pl.ds(11, 1)], (pre_out, pre_to))
+    result = in_bf16(mul_t(pre_out[...], w_up)).reshape(2, 4, 64, WIDE)
     for to in range(4):
         slots[to] = result[:, to]
-    for shift, out in enumerate(grad_outs):
-        out[...] = slots[uly ^ shift]
-
-
-def feed_grads_kernel(place, normed, act, grad_pre, grad_branch, weights_in, *refs):
-    feed, keep, send, w_out, weights, up_grad, down_grad, columns, down, sems = refs
+    out_moves += copies(sems.at[pl.ds(12, 4)], *((slots.at[uly ^ n], out) for n, out in enumerate(grad_outs)))
+    finish(*out_moves)
+
+
+def feed_grads_kernel(place, normed, act, grad_pre, branch_in, down_in, feed, keep, send, *refs):
+    up_grad, down_grad, grad_branch, w_down, sems = refs
+    moves = copies(sems, (branch_in, grad_branch), (down_in, w_down))
     blk, uly = place[0], place[1]
-    moves = copies([(weights_in, weights)], sems)
     chip, core = blk // 2, lax.rem(blk, 2)
     up_grad[...] = in_bf16(mul(normed[...].T, grad_pre[...])).reshape(8, 96, WIDE)
+    finish(*moves)
     grad = in_bf16(mul(act[...].T, grad_branch[...]))
     for group in range(4):
         for half in range(2):
             for number in range(4):
                 at = 384 * half + 96 * number
-                down_grad[2 * group + half, :, 192 * number : 192 * (number + 1)] = grad[
+                down_grad[2 * (group ^ uly) + half, :, 192 * number : 192 * (number + 1)] = grad[
                     at : at + 96, 192 * group : 192 * (group + 1)
                 ]
     for shift in range(4):
         same, other = 2 * (chip ^ shift) + core, 2 * (chip ^ shift) + 1 - core
         keep[shift, 0], keep[shift, 1] = up_grad[same], down_grad[same]
         send[shift, 0], send[shift, 1] = up_grad[other], down_grad[other]
-    finish(moves)
-    out_from(weights, uly, columns, w_out)
-    down_from(weights, columns, down)
-    feed[...] = in_bf16(mul(act[...], down[...])).reshape(2, 256, WIDE)
+    feed[...] = in_bf16(mul(act[...], w_down[...])).reshape(2, 256, WIDE)
 
 
 def second_back_kernel(
-    place, g0, g1, g2, g3, middle, out_grad, w_out, vectors, grad_middle, pack, sums, a0, a1, a2, a3, columns
+    place, g0, g1, g2, g3, middle, out_grad, w_out_in, vectors, middle_to, pack, sums, a0, a1, a2, a3, *refs
 ):
+    columns, grad_middle, w_out, sems = refs
     uly = place[1]
+    moves = copies(sems.at[pl.ds(0, 1)], (w_out_in, w_out))
     grad = in_f32(g0[...]) + in_f32(g1[...]) + in_f32(g2[...]) + in_f32(g3[...])
     grad = grad.reshape(128, WIDE)
     normal, scale = norm_stats(middle[...].reshape(128, WIDE))
@@ -777,23 +829,36 @@
     result = in_f32(out_grad[...].reshape(128, WIDE)) + norm_back(grad, normal, scale, vectors[2:3])
     grad_middle[...] = result.reshape(2, 64, WIDE)
     low = in_bf16(branch_scale * result)
+    for group in range(4):
+        columns[group] = low[:, 192 * group : 192 * (group + 1)]
+    outs = copies(sems.at[pl.ds(1, 1)], (grad_middle, middle_to))
+    outs += copies(sems.at[pl.ds(2, 4)], *((columns.at[uly ^ n], out) for n, out in enumerate((a0, a1, a2, a3))))
+    finish(*moves)
     mixed = in_bf16(mul_t(low, w_out[...]))
     for group in range(4):
-        columns[group] = low[:, 192 * group : 192 * (group + 1)]
         for seq in range(2):
             rows = mixed[64 * seq : 64 * (seq + 1)]
             for head in range(3):
                 at = 192 * group + HEAD_DIM * head
                 pack[4 * seq + head, group] = halves_in(rows[:, at : at + HEAD_DIM])
             pack[4 * seq + 3, group] = jnp.zeros((32, 128), jnp.bfloat16)
-    for shift, out in enumerate((a0, a1, a2, a3)):
-        out[...] = columns[uly ^ shift]
-
-
-def last_kernel(place, dpack, weight_in, rows_in, *refs):
-    grad_norm, grad_qkv, sums, weight, rows_low, parts, sems = refs
-    uly = place[1]
-    moves = copies([(weight_in, weight), (rows_in, rows_low)], sems)
+    finish(*outs)
+
+
+TAIL = 832
+
+
+def last_kernel(place, dpack, weight_in, rows_from, normed_from, sums_two, mixed_from, a0, a1, a2, a3, *refs):
+    grad_to, keep, send, grad_qkv, parts, slots, full, columns, weight, rows_in, normed, mixed, sems = refs
+    blk, uly = place[0], place[1]
+    moves = copies(
+        sems.at[pl.ds(0, 4)],
+        (weight_in, weight),
+        (rows_from, rows_in),
+        (normed_from, normed),
+        (mixed_from, mixed),
+    )
+    chip, core = blk // 2, lax.rem(blk, 2)
     for seq in range(2):
         rows = pl.ds(256 * seq, 256)
         for head in range(3):
@@ -802,42 +867,74 @@
             parts[0, rows, at] = pair[:, :HEAD_DIM]
             parts[1, rows, at] = pair[:, HEAD_DIM:]
             parts[2, rows, at] = halves_out(dpack[4 * seq + head, 256:, :])
+        for shift, part in enumerate((a0, a1, a2, a3)):
+            columns[seq, uly ^ shift] = part[64 * seq : 64 * (seq + 1)]
     query, key, value = group_places(uly)
     for number in range(3):
         part = jnp.where(query == number, 0, jnp.where(key == number, 1, 2))
         grad_qkv[:, 192 * number : 192 * (number + 1)] = parts[part]
-    finish(moves)
-    grad = mul_t(grad_qkv[...], weight[:, :576])
-    grad_norm[...] = in_bf16(grad).reshape(2, 256, WIDE)
-    normal, unused = norm_stats(in_f32(rows_low[...].reshape(512, WIDE)))
-    sums[...] = jnp.concatenate(
+    finish(moves[0])
+    grad = mul_t(grad_qkv[...], weight[...].reshape(WIDE, 640)[:, :576])
+    result = in_bf16(grad).reshape(2, 4, 64, WIDE)
+    for to in range(4):
+        slots[to] = result[:, to]
+    out_moves = copies(sems.at[pl.ds(4, 1)], (slots, grad_to))
+    finish(moves[1])
+    normal, unused = norm_stats(in_f32(rows_in[...].reshape(512, WIDE)))
+    sums = jnp.concatenate(
         [
             jnp.sum(grad * normal, axis=0, keepdims=True),
             jnp.sum(grad, axis=0, keepdims=True),
-            jnp.zeros((6, WIDE), jnp.float32),
+            sums_two[0:2],
+            jnp.zeros((60, WIDE), jnp.float32),
         ],
         axis=0,
     )
-
-
-TAIL = 832
-
-
-def late_grads_kernel(
-    place, normed, grad_qkv, sums_one, sums_two, mixed, a0, a1, a2, a3, keep, send, full, columns
-):
-    blk, uly = place[0], place[1]
-    chip, core = blk // 2, lax.rem(blk, 2)
-    for shift, part in enumerate((a0, a1, a2, a3)):
-        for seq in range(2):
-            columns[seq, uly ^ shift] = part[64 * seq : 64 * (seq + 1)]
-    grad = mul(normed[...].T, grad_qkv[...])
-    out_grad = mul(mixed[...].T, columns[...].reshape(512, 192))
-    sums = jnp.concatenate([sums_one[0:2], sums_two[0:2], jnp.zeros((60, WIDE), jnp.float32)], axis=0)
-    full[...] = in_bf16(jnp.concatenate([grad, sums.T, out_grad], axis=1)).reshape(8, 96, TAIL)
+    finish(moves[2], moves[3])
+    grad_weight = mul(normed[...].T, grad_qkv[...])
+    grad_out_weight = mul(mixed[...].T, columns[...].reshape(512, 192))
+    full[...] = in_bf16(jnp.concatenate([grad_weight, sums.T, grad_out_weight], axis=1)).reshape(8, 96, TAIL)
     for shift in range(4):
         keep[shift] = full[2 * (chip ^ shift) + core]
         send[shift] = full[2 * (chip ^ shift) + 1 - core]
+    finish(*out_moves)
+
+
+def join_ud_kernel(own, from_x, from_y, from_xy, up, down):
+    total = own[...] + in_f32(from_x[...]) + in_f32(from_y[...]) + in_f32(from_xy[...])
+    up[...] = total[0]
+    for number in range(4):
+        down[96 * number : 96 * (number + 1), :] = in_bf16(total[1, :, 192 * number : 192 * (number + 1)])
+
+
+def join_tail_kernel(place, own, from_x, from_y, from_xy, kept, sums, w_out, to_one, to_two, to_three):
+    even = lax.rem(place[1], 2) == 0
+    total = own[...] + in_f32(from_x[...]) + in_f32(from_y[...]) + in_f32(from_xy[...])
+    low = in_bf16(total)
+    line = total[:, 512:640].T[64:72]
+    kept[...] = total[:, :192]
+    w_out[...] = total[:, 640:]
+    sums[...] = line
+    to_one[:, :192], to_one[:, 192:] = low[:, 192:384], low[:, 576:640]
+    to_two[:, :192], to_two[:, 192:] = low[:, 384:576], low[:, 576:640]
+    to_three[...] = line
+
+
+def finish_tail_kernel(place, kept, sums, got_one, got_two, got_three, w_qkv, vectors):
+    even = lax.rem(place[1], 2) == 0
+    own, one, two = kept[...], in_f32(got_one[:, :192]), in_f32(got_two[:, :192])
+    w_qkv[:, :192] = jnp.where(even, own, two)
+    w_qkv[:, 192:384] = one
+    w_qkv[:, 384:] = jnp.where(even, two, own)
+    lines = in_f32(got_one[:, 128:256]) + in_f32(got_two[:, 128:256])
+    vectors[...] = lines.T[64:72] + sums[...] + got_three[...]
+
+
+def finish_rows_kernel(grads, inputs, grad_middle, vectors, grad_inputs):
+    grad = in_f32(grads[0]) + in_f32(grads[1]) + in_f32(grads[2]) + in_f32(grads[3])
+    normal, scale = norm_stats(in_f32(inputs[...].reshape(128, WIDE)))
+    result = norm_back(grad.reshape(128, WIDE), normal, scale, vectors[0:1])
+    grad_inputs[...] = grad_middle[...] + result.reshape(2, 64, WIDE)
 
 
 def chip_sum_kernel(keep, got, own, to_x, to_y, to_xy):
@@ -847,32 +944,29 @@
 
 
 VMEM_SPEC = pl.BlockSpec(memory_space=pltpu.VMEM)
-FREE_SPEC = pl.BlockSpec(memory_space=pl.ANY)
-
-
-def on_core(kernel, outs, operands, scratch=(), flops=0, place=False, free=(), sems=0):
-    size = lambda item: math.prod(item.shape) * item.dtype.itemsize
+
+
+FAR_SPEC = pl.BlockSpec(memory_space=pltpu.HBM)
+
+
+def on_core(kernel, outs, operands, scratch=(), grant=16, cost=0, place=False, far=(), far_outs=(), sems=0):
     shapes = [jax.ShapeDtypeStruct(shape, dtype) for shape, dtype in outs]
-    specs = [FREE_SPEC if n in free else VMEM_SPEC for n in range(len(operands))]
+    specs = [FAR_SPEC if n in far else VMEM_SPEC for n in range(len(operands))]
     if place:
         specs[0] = pl.BlockSpec(memory_space=pltpu.SMEM)
     scratch = [pltpu.VMEM(shape, dtype) for shape, dtype in scratch]
     if sems:
         scratch.append(pltpu.SemaphoreType.DMA((sems,)))
-    moved = sum(size(item) for item in operands) + sum(size(item) for item in shapes)
     return pl.pallas_call(
         kernel,
         out_shape=shapes,
         in_specs=specs,
-        out_specs=[VMEM_SPEC] * len(shapes),
+        out_specs=[FAR_SPEC if n in far_outs else VMEM_SPEC for n in range(len(shapes))],
         scratch_shapes=scratch,
-        compiler_params=pltpu.CompilerParams(vmem_limit_bytes=(VMEM_MB if free else 24) * 2**20),
-        cost_estimate=pl.CostEstimate(flops=flops, bytes_accessed=moved, transcendentals=0),
+        compiler_params=pltpu.CompilerParams(vmem_limit_bytes=(56 if far or far_outs else grant) * 2**20),
+        cost_estimate=pl.CostEstimate(flops=int(cost * 10**9), bytes_accessed=0, transcendentals=0),
         name=kernel.__name__,
     )(*operands)
-
-
-VMEM_MB = 56
 
 
 def swap_z(value, shift):
@@ -896,15 +990,15 @@
     return own, to_x, to_y, to_xy
 
 
-def finish_sum(own, to_x, to_y, to_xy):
-    return own + in_f32(swap_blk(to_x, 2)) + in_f32(swap_blk(to_y, 4)) + in_f32(swap_blk(to_xy, 6))
+def swap_sums(own, to_x, to_y, to_xy):
+    return own, swap_blk(to_x, 2), swap_blk(to_y, 4), swap_blk(to_xy, 6)
 
 
 def after(value, *others):
     return lax.optimization_barrier((value,) + others)[0]
 
 
-DOWN_MOVES = [(b * 4 + u, (2 * u + b % 2) * 4 + b // 2) for b in range(8) for u in range(4)]
+DOWN_MOVES = [(b * 4 + u, (2 * (u ^ (b // 2)) + b % 2) * 4 + b // 2) for b in range(8) for u in range(4)]
 
 
 def local_fast(
@@ -923,58 +1017,49 @@
     bf16, f32 = jnp.bfloat16, jnp.float32
     blk, uly = lax.axis_index("blk"), lax.axis_index("uly")
     place = jnp.stack([blk, uly]).astype(jnp.int32)
-    even = lax.rem(uly, 2) == 0
     square = (WIDE, WIDE)
 
-    groups = [query_key_value_weight[:, 192 * n : 192 * (n + 1)] for n in range(3)]
-    own_starts = jnp.concatenate([doc_starts // 128, lax.rem(doc_starts, 128)], axis=1).astype(bf16)
-    shared = jnp.concatenate([attention_out_weight, jnp.pad(own_starts, ((0, 14), (0, 64)))], axis=0)
-    to_one = jnp.concatenate([groups[1], shared], axis=0)
-    to_two = jnp.concatenate([jnp.where(even, groups[2], groups[0]), shared], axis=0)
-    to_three = jnp.concatenate(
-        [inputs.reshape(128, WIDE), jnp.concatenate([shared[28 * n : 28 * (n + 1)] for n in range(4)], axis=1),
-         jnp.zeros((4, WIDE), bf16)], axis=0
+    to_one, to_two, shared = on_core(
+        send_kernel,
+        [((208, 192), bf16), ((208, 192), bf16), ((128, 192), bf16)],
+        [place, query_key_value_weight, attention_out_weight, doc_starts],
+        scratch=[((96, 576), bf16), ((96, 192), bf16), ((2, 64), jnp.int32)],
+        place=True,
+        far=(1, 2, 3),
+        sems=3,
     )
     got_one, got_two = swap_z(to_one, 1), swap_z(to_two, 2)
-    got_three = swap_z(to_three, 3)
     x_own = after(inputs, to_one, to_two)
-    x_parts = [inputs, swap_z(x_own, 1), swap_z(x_own, 2), got_three]
-    shared_three = jnp.concatenate([got_three[128:156, 192 * n : 192 * (n + 1)] for n in range(4)], axis=0)
-    vectors = jnp.stack([first_gain, first_bias, second_gain, second_bias], axis=1)
-    qkv_shard = jnp.concatenate(
-        [
-            jnp.where(even, groups[0], groups[2]),
-            got_one[:96],
-            got_two[:96],
-            jnp.pad(vectors, ((0, 0), (0, 60))),
-        ],
-        axis=1,
-    )
-    starts = jnp.concatenate(
-        [own_starts, got_one[192:194, :128], got_two[192:194, :128], shared_three[96:98, :128]], axis=0
-    )
-    w_qkv = lax.all_gather(qkv_shard, "blk", axis=0, tiled=True)
+    (to_three,) = on_core(third_kernel, [((160, WIDE), bf16)], [x_own, shared], far=(0,), sems=2)
+    x_parts = [inputs, swap_z(x_own, 1), swap_z(x_own, 2), swap_z(to_three, 3)]
+    (qkv_shard,) = on_core(
+        shard_kernel,
+        [((96, 640), bf16)],
+        [place, query_key_value_weight, got_one, got_two]
+        + [jnp.stack([first_gain, first_bias, second_gain, second_bias])],
+        place=True,
+    )
+    w_qkv = lax.all_gather(qkv_shard, "blk", axis=0)
     down_shard = lax.ppermute(down_weight, ("blk", "uly"), DOWN_MOVES)
+    x_parts[0], down_shard = lax.optimization_barrier((inputs, down_shard))
 
     pack, normed_one, rows, vectors = on_core(
         first_kernel,
         [((8, PACK, 128), bf16), ((512, WIDE), bf16), ((2, 4, 64, WIDE), bf16), ((8, WIDE), f32)],
-        [place] + x_parts + [starts, w_qkv],
-        scratch=[((WIDE, 640), bf16), ((2, 4, 64, WIDE), bf16), ((3, 512, 192), bf16)],
-        flops=2 * 512 * 768 * 576,
+        [place] + x_parts + [got_one, got_two, doc_starts, w_qkv],
+        scratch=[((3, 512, 192), bf16)],
         place=True,
-        free=(1, 2, 3, 4, 6),
-        sems=9,
-    )
-    weights = jnp.concatenate(
-        [up_weight]
-        + [down_shard[96 * n : 96 * (n + 1)] for n in range(4)]
-        + [attention_out_weight, got_one[96:192], got_two[96:192], shared_three[:96]],
-        axis=1,
-    )
+    )
+    g_own = after(out_grad, normed_one)
+    g_one, g_three = swap_z(g_own, 1), swap_z(g_own, 3)
+    (weights,) = on_core(
+        weights_kernel,
+        [((96, 2 * WIDE), bf16)],
+        [down_shard, attention_out_weight, after(got_one, pack), got_two, x_parts[3]],
+    )
+    ups = lax.all_gather(up_weight, "blk", axis=0)
     pack = lax.all_to_all(pack, "blk", 0, 0, tiled=True)
-    weights = lax.all_gather(after(weights, pack), "blk", axis=0)
-    g_parts = swap_parts([after(out_grad, normed_one)] * 4)
+    pack, g_one, g_three = lax.optimization_barrier((pack, g_one, g_three))
 
     head_rows = ((FULL_TOK, HEAD_DIM), bf16)
     head_cols = ((HEAD_DIM, FULL_TOK), bf16)
@@ -982,109 +1067,129 @@
         attn_forward_kernel,
         [((8, 128, 128), bf16), ((HEAD_DIM, FULL_TOK), f32), ((1, FULL_TOK), f32)],
         [pack],
-        scratch=[head_rows, head_rows, head_cols],
-        flops=4 * FULL_TOK * FULL_TOK * HEAD_DIM,
-    )
-    attn_pack, *g_parts = lax.optimization_barrier([attn_pack] + g_parts)
+        scratch=[head_rows, head_rows, head_cols, ((2, TILES, TILE, TILE), f32), ((2, FULL_TOK, TILE), bf16)],
+    )
+    weights, g_own = lax.optimization_barrier((weights, out_grad, attn_pack))[:2]
+    weights = lax.all_gather(weights, "blk", axis=0)
     attn_pack = lax.all_to_all(attn_pack, "blk", 0, 0, tiled=True)
-    attn_pack = lax.all_gather(attn_pack.reshape(2, 4, 128, 128)[:, :3], "uly", axis=0)
-
-    big = [((8, 96, 3 * WIDE), bf16), ((4, WIDE, 192), bf16), (square, bf16)]
+    g_two = swap_z(g_own, 2)
+    g_parts = [out_grad, g_one, g_two, g_three]
+
     tok_rows = ((512, WIDE), bf16)
     own_rows = ((2, 64, WIDE), bf16)
-    *grad_norm, mixed, middle_own, normed_two, act, grad_pre, grad_branch = on_core(
+    attn_pack = lax.all_gather(attn_pack.reshape(2, 4, 128, 128)[:, :3], "uly", axis=0)
+    *grad_norm, mixed, middle_own, normed_two, act, grad_pre, w_out, w_down, grad_branch = on_core(
         middle_kernel,
-        [own_rows] * 4 + [tok_rows, ((2, 64, WIDE), f32)] + [tok_rows] * 4,
-        [place, attn_pack, rows] + g_parts + [weights, vectors],
-        scratch=big + [(square, bf16), ((2, 4, 64, WIDE), bf16), ((2, 4, 64, WIDE), bf16), ((4, 2, 64, WIDE), bf16)],
-        flops=8 * 512 * 768 * 768,
+        [own_rows] * 4 + [tok_rows, ((2, 64, WIDE), f32)] + [tok_rows] * 3 + [(square, bf16)] * 2 + [tok_rows],
+        [place, attn_pack, rows, weights, ups] + g_parts + [vectors],
+        scratch=[
+            ((4, 2, 64, WIDE), bf16),
+            tok_rows,
+            ((2, 4, 64, WIDE), bf16),
+            ((2, 8, 96, WIDE), bf16),
+            ((8, 96, WIDE), bf16),
+            ((2, 4, 64, WIDE), bf16),
+            ((2, 4, WIDE, 192), bf16),
+            (square, bf16),
+            (square, bf16),
+            tok_rows,
+            ((2, 64, WIDE), f32),
+            tok_rows,
+            tok_rows,
+            tok_rows,
+        ],
+        cost=5,
         place=True,
-        free=(2, 3, 4, 5, 6, 7),
-        sems=10,
+        far=(2, 3, 4),
+        far_outs=tuple(range(12)),
+        sems=16,
     )
     grad_norm = swap_parts(grad_norm)
-    feed, keep, send, w_out = on_core(
+    feed, keep, send = on_core(
         feed_grads_kernel,
-        [((2, 256, WIDE), bf16), ((4, 2, 96, WIDE), bf16), ((4, 2, 96, WIDE), bf16), (square, bf16)],
-        [place, normed_two, act, grad_pre, grad_branch, weights],
-        scratch=[big[0], ((8, 96, WIDE), bf16), ((8, 96, WIDE), bf16)] + big[1:],
-        flops=6 * 512 * 768 * 768,
+        [((2, 256, WIDE), bf16), ((4, 2, 96, WIDE), bf16), ((4, 2, 96, WIDE), bf16)],
+        [place, normed_two, act, grad_pre, grad_branch, w_down],
+        scratch=[((8, 96, WIDE), bf16), ((8, 96, WIDE), bf16), tok_rows, (square, bf16)],
         place=True,
-        free=(5,),
-        sems=1,
-    )
+        cost=4,
+        far=(4, 5),
+        sems=2,
+    )
+    grad_norm[0], keep, send = lax.optimization_barrier((grad_norm[0], keep, send))
     grad_middle, grad_pack, sums_two, *grad_cols = on_core(
         second_back_kernel,
         [((2, 64, WIDE), f32), ((8, 4, 32, 128), bf16), ((8, WIDE), f32)] + [((128, 192), bf16)] * 4,
         [place] + grad_norm + [middle_own, out_grad, w_out, vectors],
-        scratch=[((4, 128, 192), bf16)],
-        flops=2 * 128 * 768 * 768,
+        scratch=[((4, 128, 192), bf16), ((2, 64, WIDE), f32), (square, bf16)],
         place=True,
+        cost=2,
+        far=(7,),
+        far_outs=(0, 3, 4, 5, 6),
+        sems=6,
     )
     grad_pack = lax.all_to_all(grad_pack.reshape(32, 32, 128), ("blk", "uly"), 0, 0, tiled=True)
     feed = in_f32(lax.psum_scatter(after(feed, grad_pack), "uly", scatter_dimension=1, tiled=True))
     output = in_bf16(middle_own + branch_scale * feed)
-    sums = sum_blk(keep, after(send, sums_two))
-    grad_pack, *sums = lax.optimization_barrier([grad_pack] + list(sums))
+    sums = sum_blk(keep, send)
+    grad_pack = after(grad_pack, *sums)
+    sums = swap_sums(*sums)
 
     (dpack,) = on_core(
         attn_backward_kernel,
         [((8, 384, 128), bf16)],
         [pack, grad_pack, out_cols, log_row],
-        scratch=[head_rows] * 4 + [head_cols] + [((1, FULL_TOK), f32)] * 2 + [((HEAD_DIM, FULL_TOK), f32)],
-        flops=10 * FULL_TOK * FULL_TOK * HEAD_DIM,
-    )
-    up_down, dpack = lax.optimization_barrier((finish_sum(*sums), dpack))
-    g_w_up = up_down[0]
-    g_w_down = jnp.concatenate([up_down[1][:, 192 * n : 192 * (n + 1)] for n in range(4)], axis=0)
-    g_w_down = lax.ppermute(in_bf16(g_w_down), ("blk", "uly"), [(to, at) for at, to in DOWN_MOVES])
+        scratch=[head_rows] * 4 + [head_cols] + [((1, FULL_TOK), f32)] * 2 + [((HEAD_DIM, FULL_TOK), f32)] + [((2, TILE, FULL_TOK), bf16)] * 2,
+    )
+    dpack, *sums = lax.optimization_barrier([dpack] + list(sums))
+    g_w_up, g_w_down = on_core(join_ud_kernel, [((96, WIDE), f32), ((384, 192), bf16)], sums)
     grad_cols = swap_parts([after(part, dpack) for part in grad_cols])
     dpack = lax.all_to_all(dpack, "blk", 0, 0, tiled=True)
-    dpack, g_w_down, *grad_cols = lax.optimization_barrier([dpack, g_w_down] + grad_cols)
-    grad_norm, grad_qkv, sums_one = on_core(
+    grad_norm, keep, send = on_core(
         last_kernel,
-        [((2, 256, WIDE), bf16)] + [((512, 576), bf16), ((8, WIDE), f32)],
-        [place, dpack, w_qkv, rows],
-        scratch=[((WIDE, 640), bf16), ((2, 4, 64, WIDE), bf16), ((3, 512, 192), bf16)],
-        flops=2 * 512 * 768 * 576,
+        [((4, 2, 64, WIDE), bf16)] + [((4, 96, TAIL), bf16)] * 2,
+        [place, dpack, w_qkv, rows, normed_one, sums_two, mixed] + grad_cols,
+        scratch=[
+            ((512, 576), bf16),
+            ((3, 512, 192), bf16),
+            ((4, 2, 64, WIDE), bf16),
+            ((8, 96, TAIL), bf16),
+            ((2, 4, 64, 192), bf16),
+            ((8, 96, 640), bf16),
+            ((2, 4, 64, WIDE), bf16),
+            tok_rows,
+            tok_rows,
+        ],
+        grant=24,
         place=True,
-        free=(2, 3),
-        sems=2,
-    )
-    grad_norm = lax.psum_scatter(grad_norm, "uly", scatter_dimension=1, tiled=True)
-    keep, send = on_core(
-        late_grads_kernel,
-        [((4, 96, TAIL), bf16)] * 2,
-        [place, normed_one, grad_qkv, sums_one, sums_two, mixed] + grad_cols,
-        scratch=[((8, 96, TAIL), bf16), ((2, 4, 64, 192), bf16)],
-        flops=2 * 512 * 768 * 768,
+        far=(2, 3, 4, 6),
+        far_outs=(0,),
+        sems=5,
+        cost=3,
+    )
+    grad_norm = lax.all_to_all(grad_norm, "uly", 0, 0, tiled=True)
+    kept, sums, g_w_out, to_one, to_two, to_three = on_core(
+        join_tail_kernel,
+        [((96, 192), f32), ((8, 96), f32), ((96, 192), f32), ((96, 256), bf16), ((96, 256), bf16), ((8, 96), f32)],
+        [place] + list(swap_sums(*sum_blk(keep, send))),
         place=True,
     )
-    tail = finish_sum(*sum_blk(keep, send))
-    d_vectors = tail[:, 576:580]
-    got_one = in_f32(swap_z(in_bf16(jnp.concatenate([tail[:, 192:384], d_vectors], axis=1)), 1))
-    d_vectors = d_vectors + got_one[:, 192:]
-    got_two = in_f32(swap_z(in_bf16(jnp.concatenate([tail[:, 384:576], d_vectors], axis=1)), 2))
-    d_vectors = (d_vectors + got_two[:, 192:]).T
-    g_w_qkv = jnp.concatenate(
-        [
-            jnp.where(even, tail[:, :192], got_two[:, :192]),
-            got_one[:, :192],
-            jnp.where(even, got_two[:, :192], tail[:, :192]),
-        ],
-        axis=1,
-    )
-
-    grad_norm = in_f32(grad_norm)
-    normal, scale = norm_stats(in_f32(inputs))
-    grad_inputs = grad_middle + norm_back(grad_norm, normal, scale, vectors[0:1])
+    g_w_down = lax.ppermute(after(g_w_down, to_one), ("blk", "uly"), [(to, at) for at, to in DOWN_MOVES])
+    g_w_qkv, d_vectors = on_core(
+        finish_tail_kernel,
+        [((96, 576), f32), ((8, 96), f32)],
+        [place, kept, sums, swap_z(to_one, 1), swap_z(to_two, 2), swap_z(to_three, 3)],
+        place=True,
+    )
+    (grad_inputs,) = on_core(
+        finish_rows_kernel, [((2, 64, WIDE), f32)], [grad_norm, inputs, grad_middle, vectors]
+    )
     return (
         output,
         grad_inputs,
         d_vectors[0],
         d_vectors[1],
         g_w_qkv,
-        tail[:, 640:],
+        g_w_out,
         d_vectors[2],
         d_vectors[3],
         g_w_up,

time: 253 us -> 241 us (0.953)
  blocking collectives: 45.4 us -> 34.6 us
  starting transfers between devices: 54.5 us -> 64.7 us
  other arithmetic: 12.2 us -> 2.95 us
  local copies, waits for them, and re-layouts: 17.8 us -> 8.67 us
  waiting for transfers between devices: 52.9 us -> 59.9 us
    all_to_all x1 -> x0, blocking collectives: 13 us -> none  [local_fast(): attn_pack = lax.all_to_all(attn_pack, 'blk', 0, 0, tiled=True)]
    all_to_all x1, waiting for transfers between devices: 9.46 us -> 0.01 us  [local_fast(): pack = lax.all_to_all(pack, 'blk', 0, 0, tiled=True)]
    all_to_all x0 -> x2, starting transfers between devices: none -> 8.63 us  [the longest x1 4.4 us: local_fast(): grad_norm = lax.all_to_all(grad_norm, 'uly', 0, 0, tiled=True)]
    ppermute x16 -> x17, waiting for transfers between devices: 21.2 us -> 29.2 us  [swap_z(): return lax.ppermute(value, 'uly', [(i, i ^ shift) for i in range(4)])]
    ppermute x1, waiting for transfers between devices: 0.01 us -> 7.17 us  [local_fast(): down_shard = lax.ppermute(down_weight, ('blk', 'uly'), DOWN_MOVES)]
    ppermute x16 -> x17, starting transfers between devices: 21.6 us -> 26.9 us  [swap_z(): return lax.ppermute(value, 'uly', [(i, i ^ shift) for i in range(4)])]
    all_to_all x1, starting transfers between devices: 8.16 us -> 3.63 us  [local_fast(): pack = lax.all_to_all(pack, 'blk', 0, 0, tiled=True)]
    unnamed x87 -> x82, local copies, waits for them, and re-layouts: 12.6 us -> 8.14 us
  transfers between devices with their start and end apart: 32 -> 35, of which waited for: 12 -> 15; matrix products, arithmetic and copies ran while one was open for 5% -> 2% of each run, Pallas kernels for 17% -> 16%
where the time goes in v3:
time: 241 us; the launch traced here: 240 us
  starting transfers between devices  64.7 us (27%)
  waiting for transfers between devices  59.9 us (25%)
  Pallas kernels  55.4 us (23%)
  blocking collectives  34.6 us (14%)
  between operations  14.2 us (6%)
  local copies, waits for them, and re-layouts  8.67 us (4%)
  other arithmetic  2.95 us (1%)
    pallas_call x17, Pallas kernels, on_core(): pl.pallas_call(kernel, out_shape=shapes, in_specs=specs, out_specs=[FAR_S...  55.4 us
    ppermute x17, waiting for transfers between devices, swap_z(): return lax.ppermute(value, 'uly', [(i, i ^ shift) for i in range(4)])  29.2 us
    ppermute x17, starting transfers between devices, swap_z(): return lax.ppermute(value, 'uly', [(i, i ^ shift) for i in range(4)])  26.9 us
    all_gather x1, blocking collectives, local_fast(): lax.all_gather(attn_pack.reshape(2, 4, 128, 128)[:, :3], 'uly', axis=0)  21.2 us
    all_gather x1, blocking collectives, local_fast(): w_qkv = lax.all_gather(qkv_shard, 'blk', axis=0)  13.4 us
    ppermute x8, waiting for transfers between devices, swap_blk(): return lax.ppermute(value, 'blk', [(i, i ^ mask) for i in range(8)])  10 us
    unnamed x82, local copies, waits for them, and re-layouts  8.14 us
    all_to_all x1, starting transfers between devices, local_fast(): lax.all_to_all(grad_pack.reshape(32, 32, 128), ('blk', 'uly'), 0, 0, tile...  7.97 us
  transfers between devices with their start and end apart: 35, of which 15 were waited for; matrix products, arithmetic and copies ran while one was open for 2% of the time, Pallas kernels for 16%

profile of v3, /device:TPU:4, one launch (start us, length us, event | category | flops | bytes accessed | tf_op | source)
XLA Modules:
  0.0 240.4 jit_solution(16132257573522058766)
XLA Ops:
  8.5 2.4 send_kernel.1
  10.9 1.6 collective-permute-start.4
  12.5 2.6 %collective-permute-start.5 = (bf16[208,192]{1,0:T(8,128)(2,1)}, bf16[208,192]{1,0:T(8,128)(2,1)S(1)}, u32[]{:S(2)}, u32[]{:S(2)}) collective-permute-start(bf16[208,192]{1,0:T(8,128)(2,1)} %get-tuple-element.90), channel_id=1, source_target_pairs={{0,2},{1,3},{2,0},{3,1},{4,6},{5,7},{6,4},{7,5},{8,10},{9,11},{10,... | collective-permute-start | bytes 239624 | tf_op jit(solution)/shard_map/ppermute | solution.py:973
  15.9 2.5 %third_kernel.1 = bf16[160,768]{1,0:T(8,128)(2,1)} custom-call(bf16[2,64,768]{2,1,0:T(8,128)(2,1)} %inputs.2, bf16[128,192]{1,0:T(8,128)(2,1)} %get-tuple-element.92.shared), custom_call_target="tpu_custom_call" | custom-call | tf_op jit(solution)/shard_map/third_kernel/pallas_call | solution.py:960
  18.5 3.7 %collective-permute-start.3 = (bf16[160,768]{1,0:T(8,128)(2,1)}, bf16[160,768]{1,0:T(8,128)(2,1)S(1)}, u32[]{:S(2)}, u32[]{:S(2)}) collective-permute-start(bf16[160,768]{1,0:T(8,128)(2,1)} %third_kernel.1), channel_id=1, source_target_pairs={{0,3},{1,2},{2,1},{3,0},{4,7},{5,6},{6,5},{7,4},{8,11},{9,10},{10,... | collective-permute-start | bytes 737288 | tf_op jit(solution)/shard_map/ppermute | solution.py:973
  22.1 0.7 pad_maximum_fusion.vectors
  22.8 1.0 copy.23
  23.9 1.9 collective-permute-start
  26.5 0.7 shard_kernel.1
  27.2 13.4 %all-gather = bf16[768,640]{1,0:T(8,128)(2,1)S(1)} all-gather(bf16[96,640]{1,0:T(8,128)(2,1)S(1)} %shard_kernel.1), channel_id=2, replica_groups=mesh['blk'=8,'uly'=4] {'blk'}, dimensions={0}, use_global_device_ids=true | all-gather | bytes 1105920 | tf_op jit(solution)/shard_map/all_gather | solution.py:1042
  40.6 7.2 %collective-permute-done.down = bf16[384,192]{1,0:T(8,128)(2,1)S(1)} collective-permute-done((bf16[384,192]{1,0:T(8,128)(2,1)S(1)}, bf16[384,192]{1,0:T(8,128)(2,1)S(1)}, u32[]{:S(2)}, u32[]{:S(2)}) %collective-permute-start) | collective-permute-done | bytes 147488 | tf_op jit(solution)/shard_map/ppermute | solution.py:1043
  47.8 3.0 %first_kernel.1 = (bf16[8,400,128]{2,1,0:T(8,128)(2,1)}, bf16[512,768]{1,0:T(8,128)(2,1)S(1)}, bf16[2,4,64,768]{3,2,1,0:T(8,128)(2,1)S(1)}, f32[8,768]{1,0:T(8,128)S(1)}) custom-call(s32[2]{0:T(128)S(1)} %copy-done.17, bf16[2,64,768]{2,1,0:T(8,128)(2,1)S(1)} %copy-done.1, bf16[2,64,768]{2,1,0:T(8,128)(2,1)S(1)} %collective-permute-done.1.x1, ...), custom_call_target="tpu_custom_call" | custom-call | tf_op jit(solution)/shard_map/first_kernel/pallas_call | solution.py:960
  51.4 0.9 copy-done.20
  52.2 0.9 copy-done.21
  53.2 3.6 %all-to-all-start = ((bf16[8,400,128]{2,1,0:T(8,128)(2,1)}), bf16[8,400,128]{2,1,0:T(8,128)(2,1)S(1)}, u32[]{:S(2)}, u32[]{:S(2)}) async-start(bf16[8,400,128]{2,1,0:T(8,128)(2,1)} %get-tuple-element.93), calls=%async_computation | async-start | bytes 1638400 | tf_op jit(solution)/shard_map/all_to_all | solution.py:1061
  56.9 3.5 %collective-permute-start.7 = (bf16[2,64,768]{2,1,0:T(8,128)(2,1)S(1)}, bf16[2,64,768]{2,1,0:T(8,128)(2,1)S(1)}, u32[]{:S(2)}, u32[]{:S(2)}) collective-permute-start(bf16[2,64,768]{2,1,0:T(8,128)(2,1)S(1)} %copy-done.24), channel_id=1, source_target_pairs={{0,3},{1,2},{2,1},{3,0},{4,7},{5,6},{6,5},{7,4},{8,11},{9,10},{10,... | collective-permute-start | bytes 589832 | tf_op jit(solution)/shard_map/ppermute | solution.py:973
  60.4 0.8 weights_kernel.1
  61.3 5.3 %collective-permute-done.7.g3 = bf16[2,64,768]{2,1,0:T(8,128)(2,1)S(1)} collective-permute-done((bf16[2,64,768]{2,1,0:T(8,128)(2,1)S(1)}, bf16[2,64,768]{2,1,0:T(8,128)(2,1)S(1)}, u32[]{:S(2)}, u32[]{:S(2)}) %collective-permute-start.7) | collective-permute-done | bytes 196640 | tf_op jit(solution)/shard_map/ppermute | solution.py:973
  66.5 3.2 %collective-permute-done.6.g1 = bf16[2,64,768]{2,1,0:T(8,128)(2,1)S(1)} collective-permute-done((bf16[2,64,768]{2,1,0:T(8,128)(2,1)S(1)}, bf16[2,64,768]{2,1,0:T(8,128)(2,1)S(1)}, u32[]{:S(2)}, u32[]{:S(2)}) %collective-permute-start.6) | collective-permute-done | bytes 196640 | tf_op jit(solution)/shard_map/ppermute | solution.py:973
  69.8 5.3 %attn_forward_kernel.1 = (bf16[8,128,128]{2,1,0:T(8,128)(2,1)}, f32[64,2048]{1,0:T(8,128)S(1)}, f32[1,2048]{1,0:T(1,128)S(1)}) custom-call(bf16[8,400,128]{2,1,0:T(8,128)(2,1)S(1)} %all-to-all-done.pack), custom_call_target="tpu_custom_call" | custom-call | tf_op jit(solution)/shard_map/attn_forward_kernel/pallas_call | solution.py:960
  75.1 4.2 %all-to-all-start.1 = ((bf16[8,128,128]{2,1,0:T(8,128)(2,1)}), bf16[8,128,128]{2,1,0:T(8,128)(2,1)S(1)}, u32[]{:S(2)}, u32[]{:S(2)}) async-start(bf16[8,128,128]{2,1,0:T(8,128)(2,1)} %get-tuple-element.97), calls=%async_computation.1 | async-start | bytes 524288 | tf_op jit(solution)/shard_map/all_to_all | solution.py:1074
  79.3 1.4 collective-permute-start.8
  80.7 4.4 %all-to-all-done.1 = bf16[8,128,128]{2,1,0:T(8,128)(2,1)S(1)} async-done(((bf16[8,128,128]{2,1,0:T(8,128)(2,1)}), bf16[8,128,128]{2,1,0:T(8,128)(2,1)S(1)}, u32[]{:S(2)}, u32[]{:S(2)}) %all-to-all-start.1) | async-done | bytes 262176 | tf_op jit(solution)/shard_map/all_to_all | solution.py:1074
  85.2 21.2 %all-gather.1 = bf16[8,3,128,128]{3,2,1,0:T(8,128)(2,1)} all-gather(bf16[2,3,128,128]{3,2,1,0:T(8,128)(2,1)S(1)} %slice.20), channel_id=3, replica_groups=mesh['blk'=8,'uly'=4] {'uly'}, dimensions={0}, use_global_device_ids=true | all-gather | bytes 983040 | tf_op jit(solution)/shard_map/all_gather | solution.py:1080
  107.1 9.1 %middle_kernel.1 = (bf16[2,64,768]{2,1,0:T(8,128)(2,1)}, bf16[2,64,768]{2,1,0:T(8,128)(2,1)}, bf16[2,64,768]{2,1,0:T(8,128)(2,1)}, bf16[2,64,768]{2,1,0:T(8,128)...) custom-call(s32[2]{0:T(128)} %pad_add_fusion.place, ...), custom_call_target="tpu_custom_call" | custom-call | flops 5000000000 | tf_op jit(solution)/shard_map/middle_kernel/pallas_call | solution.py:960
  116.2 6.4 %feed_grads_kernel.1 = (bf16[2,256,768]{2,1,0:T(8,128)(2,1)}, bf16[4,2,96,768]{3,2,1,0:T(8,128)(2,1)}, bf16[4,2,96,768]{3,2,1,0:T(8,128)(2,1)}) custom-call(s32[2]{0:T(128)} %pad_add_fusion.place, bf16[512,768]{1,0:T(8,128)(2,1)} %get-tuple-element.107.normed, bf16[512,768]{1,0:T(8,128)(2,1)} %get-tuple-element.108.act, ...), custom_call_target="tpu_custom_call" | custom-call | flops 4000000000 | tf_op jit(solution)/shard_map/feed_grads_kernel/pallas_call | solution.py:960
  122.8 2.6 %collective-permute-start.10 = (bf16[2,64,768]{2,1,0:T(8,128)(2,1)S(1)}, bf16[2,64,768]{2,1,0:T(8,128)(2,1)S(1)}, u32[]{:S(2)}, u32[]{:S(2)}) collective-permute-start(bf16[2,64,768]{2,1,0:T(8,128)(2,1)S(1)} %copy-done.28), channel_id=1, source_target_pairs={{0,2},{1,3},{2,0},{3,1},{4,6},{5,7},{6,4},{7,5},{8,10},{9,11},{10,... | collective-permute-start | bytes 589832 | tf_op jit(solution)/shard_map/ppermute | solution.py:973
  125.5 1.7 collective-permute-start.11
  127.1 6.5 %collective-permute-done.9.g1 = bf16[2,64,768]{2,1,0:T(8,128)(2,1)S(1)} collective-permute-done((bf16[2,64,768]{2,1,0:T(8,128)(2,1)S(1)}, bf16[2,64,768]{2,1,0:T(8,128)(2,1)S(1)}, u32[]{:S(2)}, u32[]{:S(2)}) %collective-permute-start.9) | collective-permute-done | bytes 196640 | tf_op jit(solution)/shard_map/ppermute | solution.py:973
  133.7 6.3 %collective-permute-done.10.g2 = bf16[2,64,768]{2,1,0:T(8,128)(2,1)S(1)} collective-permute-done((bf16[2,64,768]{2,1,0:T(8,128)(2,1)S(1)}, bf16[2,64,768]{2,1,0:T(8,128)(2,1)S(1)}, u32[]{:S(2)}, u32[]{:S(2)}) %collective-permute-start.10) | collective-permute-done | bytes 196640 | tf_op jit(solution)/shard_map/ppermute | solution.py:973
  140.7 4.2 %second_back_kernel.1 = (f32[2,64,768]{2,1,0:T(8,128)}, bf16[8,4,32,128]{3,2,1,0:T(8,128)(2,1)}, f32[8,768]{1,0:T(8,128)}, bf16[128,192]{1,0:T(8,128)(2,1)}, bf1...) custom-call(s32[2]{0:T(128)} %pad_add_fusion.place, ...), custom_call_target="tpu_custom_call" | custom-call | flops 2000000000 | tf_op jit(solution)/shard_map/second_back_kernel/pallas_call | solution.py:960
  144.8 8.0 %all-to-all-start.2 = ((bf16[32,32,128]{2,1,0:T(8,128)(2,1)}), bf16[32,32,128]{2,1,0:T(8,128)(2,1)S(1)}, u32[]{:S(2)}, u32[]{:S(2)}) async-start(bf16[32,32,128]{2,1,0:T(8,128)(2,1)} %bitcast.24), calls=%async_computation.2 | async-start | bytes 524288 | tf_op jit(solution)/shard_map/all_to_all | solution.py:1130
  152.8 2.2 chip_sum_kernel.2
  155.0 0.8 copy-done.4
  155.8 1.5 collective-permute-start.13
  157.9 1.5 collective-permute-start.15
  159.3 3.0 %all-to-all-done.2.grad = bf16[32,32,128]{2,1,0:T(8,128)(2,1)S(1)} async-done(((bf16[32,32,128]{2,1,0:T(8,128)(2,1)}), bf16[32,32,128]{2,1,0:T(8,128)(2,1)S(1)}, u32[]{:S(2)}, u32[]{:S(2)}) %all-to-all-start.2) | async-done | bytes 262176 | tf_op jit(solution)/shard_map/all_to_all | solution.py:1130
  162.3 7.5 %attn_backward_kernel.1 = bf16[8,384,128]{2,1,0:T(8,128)(2,1)} custom-call(bf16[8,400,128]{2,1,0:T(8,128)(2,1)S(1)} %all-to-all-done.pack, bf16[32,32,128]{2,1,0:T(8,128)(2,1)S(1)} %all-to-all-done.2.grad, f32[64,2048]{1,0:T(8,128)S(1)} %get-tuple-element.130.out_cols, f32[1,2048]{1,0:T(1,128)S(1)} %get-tuple-element.131.log_row), custom_call_target="tpu_custom_call" | custom-call | tf_op jit(solution)/shard_map/attn_backward_kernel/pallas_call | solution.py:960
  169.9 3.3 %collective-permute-done.14.from_y = bf16[2,96,768]{2,1,0:T(8,128)(2,1)S(1)} collective-permute-done((bf16[2,96,768]{2,1,0:T(8,128)(2,1)}, bf16[2,96,768]{2,1,0:T(8,128)(2,1)S(1)}, u32[]{:S(2)}, u32[]{:S(2)}) %collective-permute-start.14) | collective-permute-done | bytes 294944 | tf_op jit(solution)/shard_map/ppermute | solution.py:977
  173.2 4.2 %all-to-all-start.3 = ((bf16[8,384,128]{2,1,0:T(8,128)(2,1)}), bf16[8,384,128]{2,1,0:T(8,128)(2,1)S(1)}, u32[]{:S(2)}, u32[]{:S(2)}) async-start(bf16[8,384,128]{2,1,0:T(8,128)(2,1)} %attn_backward_kernel.1), calls=%async_computation.4 | async-start | bytes 1572864 | tf_op jit(solution)/shard_map/all_to_all | solution.py:1146
  177.4 0.7 reduce-scatter.2.cloned.1.call-update
  178.1 1.5 collective-permute-start.16
  179.6 2.1 collective-permute-start.17
  181.7 0.8 collective-permute-start.18
  182.6 4.6 %collective-permute-done.17.a2 = bf16[128,192]{1,0:T(8,128)(2,1)S(1)} collective-permute-done((bf16[128,192]{1,0:T(8,128)(2,1)S(1)}, bf16[128,192]{1,0:T(8,128)(2,1)S(1)}, u32[]{:S(2)}, u32[]{:S(2)}) %collective-permute-start.17) | collective-permute-done | bytes 49184 | tf_op jit(solution)/shard_map/ppermute | solution.py:973
  187.2 0.7 collective-permute-done.18.a3
  188.5 0.9 copy-done.22
  189.4 6.6 %last_kernel.1 = (bf16[4,2,64,768]{3,2,1,0:T(8,128)(2,1)}, bf16[4,96,832]{2,1,0:T(8,128)(2,1)}, bf16[4,96,832]{2,1,0:T(8,128)(2,1)}) custom-call(s32[2]{0:T(128)} %pad_add_fusion.place, bf16[8,384,128]{2,1,0:T(8,128)(2,1)} %copy-done.22, bf16[8,96,640]{2,1,0:T(8,128)(2,1)} %bitcast.21, bf16[2,4,64,768]{3,2,1,0:T(8,128)(2,1)} %copy-done.21, ...), custom_call_target="tpu_custom_call" | custom-call | flops 3000000000 | tf_op jit(solution)/shard_map/last_kernel/pallas_call | solution.py:960
  196.1 4.4 %all-to-all-start.4 = ((bf16[4,2,64,768]{3,2,1,0:T(8,128)(2,1)}), bf16[4,2,64,768]{3,2,1,0:T(8,128)(2,1)S(1)}, u32[]{:S(2)}, u32[]{:S(2)}) async-start(bf16[4,2,64,768]{3,2,1,0:T(8,128)(2,1)} %get-tuple-element.143), calls=%async_computation.5 | async-start | bytes 1572864 | tf_op jit(solution)/shard_map/all_to_all | solution.py:1169
  201.3 1.4 collective-permute-start.21
  202.8 1.5 collective-permute-start.22
  204.3 0.9 join_ud_kernel.1
  205.1 2.8 %collective-permute-done.20.from_x = bf16[96,832]{1,0:T(8,128)(2,1)S(1)} collective-permute-done((bf16[96,832]{1,0:T(8,128)(2,1)S(1)}, bf16[96,832]{1,0:T(8,128)(2,1)S(1)}, u32[]{:S(2)}, u32[]{:S(2)}) %collective-permute-start.20) | collective-permute-done | bytes 159776 | tf_op jit(solution)/shard_map/ppermute | solution.py:977
  208.0 3.9 %collective-permute-done.22.from_xy = bf16[96,832]{1,0:T(8,128)(2,1)S(1)} collective-permute-done((bf16[96,832]{1,0:T(8,128)(2,1)S(1)}, bf16[96,832]{1,0:T(8,128)(2,1)S(1)}, u32[]{:S(2)}, u32[]{:S(2)}) %collective-permute-start.22) | collective-permute-done | bytes 159776 | tf_op jit(solution)/shard_map/ppermute | solution.py:977
  211.8 1.3 join_tail_kernel.1
  213.1 3.5 %collective-permute-start.25 = (f32[8,96]{1,0:T(8,128)S(1)}, f32[8,96]{1,0:T(8,128)S(1)}, u32[]{:S(2)}, u32[]{:S(2)}) collective-permute-start(f32[8,96]{1,0:T(8,128)S(1)} %get-tuple-element.155), channel_id=1, source_target_pairs={{0,3},{1,2},{2,1},{3,0},{4,7},{5,6},{6,5},{7,4},{8,11},{9,10},{10,... | collective-permute-start | bytes 9224 | tf_op jit(solution)/shard_map/ppermute | solution.py:973
  216.7 0.8 collective-permute-start.23
  217.5 1.6 add_convert_fusion
  219.2 4.2 %collective-permute-start.26 = (bf16[384,192]{1,0:T(8,128)(2,1)S(1)}, bf16[384,192]{1,0:T(8,128)(2,1)S(1)}, u32[]{:S(2)}, u32[]{:S(2)}) collective-permute-start(bf16[384,192]{1,0:T(8,128)(2,1)S(1)} %get-tuple-element.165), channel_id=1, source_target_pairs={{0,0},{8,1},{16,2},{24,3},{4,4},{12,5},{20,6},{28,7},{9,8},{1,9},{... | collective-permute-start | bytes 442376 | tf_op jit(solution)/shard_map/ppermute | solution.py:1176
  223.4 2.6 %collective-permute-done.24.got_two = bf16[96,256]{1,0:T(8,128)(2,1)S(1)} collective-permute-done((bf16[96,256]{1,0:T(8,128)(2,1)S(1)}, bf16[96,256]{1,0:T(8,128)(2,1)S(1)}, u32[]{:S(2)}, u32[]{:S(2)}) %collective-permute-start.24) | collective-permute-done | bytes 49184 | tf_op jit(solution)/shard_map/ppermute | solution.py:973
  226.0 1.3 finish_tail_kernel.1
  227.8 4.1 %collective-permute-done.26 = bf16[384,192]{1,0:T(8,128)(2,1)S(1)} collective-permute-done((bf16[384,192]{1,0:T(8,128)(2,1)S(1)}, bf16[384,192]{1,0:T(8,128)(2,1)S(1)}, u32[]{:S(2)}, u32[]{:S(2)}) %collective-permute-start.26) | collective-permute-done | bytes 147488 | tf_op jit(solution)/shard_map/ppermute | solution.py:1176
  231.9 0.8 copy.24
  232.8 1.1 finish_rows_kernel.1
  (115 shorter events, 7.8 us)
Async XLA Ops:
  7.2 18.7 %copy-start.6 = (bf16[96,576]{1,0:T(8,128)(2,1)S(1)}, bf16[96,576]{1,0:T(8,128)(2,1)}, u32[]{:S(2)}) copy-start(bf16[96,576]{1,0:T(8,128)(2,1)} %weight.1) | copy-start | bytes 331780
  7.2 99.3 %all-gather.9.cloned.1.call-start = ((), (), s32[]{:S(2)}) async-start(), calls=%async_computation.8 | async-start | bytes 1327104 | tf_op jit(solution)/shard_map/all_gather | solution.py:1060
  10.9 13.0 %collective-permute-start.4 = (bf16[208,192]{1,0:T(8,128)(2,1)}, bf16[208,192]{1,0:T(8,128)(2,1)S(1)}, u32[]{:S(2)}, u32[]{:S(2)}) collective-permute-start(bf16[208,192]{1,0:T(8,128)(2,1)} %get-tuple-element.89), channel_id=1, source_target_pairs={{0,1},{1,0},{2,3},{3,2},{4,5},{5,4},{6,7},{7,6},{8,9},{9,8},{10,11... | collective-permute-start | bytes 239624 | tf_op jit(solution)/shard_map/ppermute | solution.py:973
  12.5 13.3 %collective-permute-start.5 = (bf16[208,192]{1,0:T(8,128)(2,1)}, bf16[208,192]{1,0:T(8,128)(2,1)S(1)}, u32[]{:S(2)}, u32[]{:S(2)}) collective-permute-start(bf16[208,192]{1,0:T(8,128)(2,1)} %get-tuple-element.90), channel_id=1, source_target_pairs={{0,2},{1,3},{2,0},{3,1},{4,6},{5,7},{6,4},{7,5},{8,10},{9,11},{10,... | collective-permute-start | bytes 239624 | tf_op jit(solution)/shard_map/ppermute | solution.py:973
  15.1 32.6 %collective-permute-start.2 = (bf16[2,64,768]{2,1,0:T(8,128)(2,1)}, bf16[2,64,768]{2,1,0:T(8,128)(2,1)S(1)}, u32[]{:S(2)}, u32[]{:S(2)}) collective-permute-start(bf16[2,64,768]{2,1,0:T(8,128)(2,1)} %inputs.2), channel_id=1, source_target_pairs={{0,2},{1,3},{2,0},{3,1},{4,6},{5,7},{6,4},{7,5},{8,10},{9,11},{10,... | collective-permute-start | bytes 589832 | tf_op jit(solution)/shard_map/ppermute | solution.py:973
  15.5 32.3 %collective-permute-start.1 = (bf16[2,64,768]{2,1,0:T(8,128)(2,1)}, bf16[2,64,768]{2,1,0:T(8,128)(2,1)S(1)}, u32[]{:S(2)}, u32[]{:S(2)}) collective-permute-start(bf16[2,64,768]{2,1,0:T(8,128)(2,1)} %inputs.2), channel_id=1, source_target_pairs={{0,1},{1,0},{2,3},{3,2},{4,5},{5,4},{6,7},{7,6},{8,9},{9,8},{10,11... | collective-permute-start | bytes 589832 | tf_op jit(solution)/shard_map/ppermute | solution.py:973
  15.9 31.8 %copy-start.1 = (bf16[2,64,768]{2,1,0:T(8,128)(2,1)S(1)}, bf16[2,64,768]{2,1,0:T(8,128)(2,1)}, u32[]{:S(2)}) copy-start(bf16[2,64,768]{2,1,0:T(8,128)(2,1)} %inputs.2) | copy-start | bytes 589828
  15.9 31.8 %copy-start.19 = (s32[2,64]{1,0:T(2,128)S(1)}, s32[2,64]{1,0:T(2,128)}, u32[]{:S(2)}) copy-start(s32[2,64]{1,0:T(2,128)} %doc_starts.1) | copy-start | bytes 1540
  18.5 29.3 %collective-permute-start.3 = (bf16[160,768]{1,0:T(8,128)(2,1)}, bf16[160,768]{1,0:T(8,128)(2,1)S(1)}, u32[]{:S(2)}, u32[]{:S(2)}) collective-permute-start(bf16[160,768]{1,0:T(8,128)(2,1)} %third_kernel.1), channel_id=1, source_target_pairs={{0,3},{1,2},{2,1},{3,0},{4,7},{5,6},{6,5},{7,4},{8,11},{9,10},{10,... | collective-permute-start | bytes 737288 | tf_op jit(solution)/shard_map/ppermute | solution.py:973
  23.9 23.8 %collective-permute-start = (bf16[384,192]{1,0:T(8,128)(2,1)S(1)}, bf16[384,192]{1,0:T(8,128)(2,1)S(1)}, u32[]{:S(2)}, u32[]{:S(2)}) collective-permute-start(bf16[384,192]{1,0:T(8,128)(2,1)S(1)} %copy.23), channel_id=1, source_target_pairs={{0,0},{1,8},{2,16},{3,24},{4,4},{5,12},{6,20},{7,28},{8,9},{9,1},{... | collective-permute-start | bytes 442376 | tf_op jit(solution)/shard_map/ppermute | solution.py:1043
  40.6 12.6 %copy-start = (bf16[768,640]{1,0:T(8,128)(2,1)}, bf16[768,640]{1,0:T(8,128)(2,1)S(1)}, u32[]{:S(2)}) copy-start(bf16[768,640]{1,0:T(8,128)(2,1)S(1)} %all-gather) | copy-start | bytes 2949124
  53.2 3.7 %copy-start.24 = (bf16[2,64,768]{2,1,0:T(8,128)(2,1)S(1)}, bf16[2,64,768]{2,1,0:T(8,128)(2,1)}, u32[]{:S(2)}) copy-start(bf16[2,64,768]{2,1,0:T(8,128)(2,1)} %out_grad.1) | copy-start | bytes 589828
  53.2 7.2 %copy-start.14 = (bf16[96,192]{1,0:T(8,128)(2,1)S(1)}, bf16[96,192]{1,0:T(8,128)(2,1)}, u32[]{:S(2)}) copy-start(bf16[96,192]{1,0:T(8,128)(2,1)} %out_weight.1) | copy-start | bytes 110596
  53.2 16.6 %all-to-all-start = ((bf16[8,400,128]{2,1,0:T(8,128)(2,1)}), bf16[8,400,128]{2,1,0:T(8,128)(2,1)S(1)}, u32[]{:S(2)}, u32[]{:S(2)}) async-start(bf16[8,400,128]{2,1,0:T(8,128)(2,1)} %get-tuple-element.93), calls=%async_computation | async-start | bytes 1638400 | tf_op jit(solution)/shard_map/all_to_all | solution.py:1061
  56.8 49.6 %all-gather.7.cloned.1.call-start = ((), (), s32[]{:S(2)}) async-start(), calls=%async_computation.7 | async-start | bytes 2654208 | tf_op jit(solution)/shard_map/all_gather | solution.py:1073
  56.9 9.6 %collective-permute-start.7 = (bf16[2,64,768]{2,1,0:T(8,128)(2,1)S(1)}, bf16[2,64,768]{2,1,0:T(8,128)(2,1)S(1)}, u32[]{:S(2)}, u32[]{:S(2)}) collective-permute-start(bf16[2,64,768]{2,1,0:T(8,128)(2,1)S(1)} %copy-done.24), channel_id=1, source_target_pairs={{0,3},{1,2},{2,1},{3,0},{4,7},{5,6},{6,5},{7,4},{8,11},{9,10},{10,... | collective-permute-start | bytes 589832 | tf_op jit(solution)/shard_map/ppermute | solution.py:973
  60.4 9.3 %collective-permute-start.6 = (bf16[2,64,768]{2,1,0:T(8,128)(2,1)S(1)}, bf16[2,64,768]{2,1,0:T(8,128)(2,1)S(1)}, u32[]{:S(2)}, u32[]{:S(2)}) collective-permute-start(bf16[2,64,768]{2,1,0:T(8,128)(2,1)S(1)} %copy-done.24), channel_id=1, source_target_pairs={{0,1},{1,0},{2,3},{3,2},{4,5},{5,4},{6,7},{7,6},{8,9},{9,8},{10,11... | collective-permute-start | bytes 589832 | tf_op jit(solution)/shard_map/ppermute | solution.py:973
  66.5 39.9 %copy-start.25 = (bf16[2,64,768]{2,1,0:T(8,128)(2,1)}, bf16[2,64,768]{2,1,0:T(8,128)(2,1)S(1)}, u32[]{:S(2)}) copy-start(bf16[2,64,768]{2,1,0:T(8,128)(2,1)S(1)} %collective-permute-done.7.g3) | copy-start | bytes 589828
  69.8 36.6 %copy-start.26 = (bf16[2,64,768]{2,1,0:T(8,128)(2,1)}, bf16[2,64,768]{2,1,0:T(8,128)(2,1)S(1)}, u32[]{:S(2)}) copy-start(bf16[2,64,768]{2,1,0:T(8,128)(2,1)S(1)} %collective-permute-done.6.g1) | copy-start | bytes 589828
  75.1 10.1 %all-to-all-start.1 = ((bf16[8,128,128]{2,1,0:T(8,128)(2,1)}), bf16[8,128,128]{2,1,0:T(8,128)(2,1)S(1)}, u32[]{:S(2)}, u32[]{:S(2)}) async-start(bf16[8,128,128]{2,1,0:T(8,128)(2,1)} %get-tuple-element.97), calls=%async_computation.1 | async-start | bytes 524288 | tf_op jit(solution)/shard_map/all_to_all | solution.py:1074
  79.3 27.1 %collective-permute-start.8 = (bf16[2,64,768]{2,1,0:T(8,128)(2,1)S(1)}, bf16[2,64,768]{2,1,0:T(8,128)(2,1)S(1)}, u32[]{:S(2)}, u32[]{:S(2)}) collective-permute-start(bf16[2,64,768]{2,1,0:T(8,128)(2,1)S(1)} %copy-done.24), channel_id=1, source_target_pairs={{0,2},{1,3},{2,0},{3,1},{4,6},{5,7},{6,4},{7,5},{8,10},{9,11},{10,... | collective-permute-start | bytes 589832 | tf_op jit(solution)/shard_map/ppermute | solution.py:973
  116.2 6.5 %copy-start.29 = (bf16[2,64,768]{2,1,0:T(8,128)(2,1)S(1)}, bf16[2,64,768]{2,1,0:T(8,128)(2,1)}, u32[]{:S(2)}) copy-start(bf16[2,64,768]{2,1,0:T(8,128)(2,1)} %get-tuple-element.117) | copy-start | bytes 589828
  116.2 6.6 %copy-start.28 = (bf16[2,64,768]{2,1,0:T(8,128)(2,1)S(1)}, bf16[2,64,768]{2,1,0:T(8,128)(2,1)}, u32[]{:S(2)}) copy-start(bf16[2,64,768]{2,1,0:T(8,128)(2,1)} %get-tuple-element.118) | copy-start | bytes 589828
  116.2 9.2 %copy-start.27 = (bf16[2,64,768]{2,1,0:T(8,128)(2,1)S(1)}, bf16[2,64,768]{2,1,0:T(8,128)(2,1)}, u32[]{:S(2)}) copy-start(bf16[2,64,768]{2,1,0:T(8,128)(2,1)} %get-tuple-element.119) | copy-start | bytes 589828
  122.6 30.2 %collective-permute-start.12 = (bf16[4,2,96,768]{3,2,1,0:T(8,128)(2,1)}, bf16[4,2,96,768]{3,2,1,0:T(8,128)(2,1)}, u32[]{:S(2)}, u32[]{:S(2)}) collective-permute-start(bf16[4,2,96,768]{3,2,1,0:T(8,128)(2,1)} %get-tuple-element.124), channel_id=1, source_target_pairs={{0,4},{4,0},{8,12},{12,8},{16,20},{20,16},{24,28},{28,24},{1,5},{5... | collective-permute-start | bytes 3538952 | tf_op jit(solution)/shard_map/ppermute | solution.py:977
  122.7 11.0 %collective-permute-start.9 = (bf16[2,64,768]{2,1,0:T(8,128)(2,1)S(1)}, bf16[2,64,768]{2,1,0:T(8,128)(2,1)S(1)}, u32[]{:S(2)}, u32[]{:S(2)}) collective-permute-start(bf16[2,64,768]{2,1,0:T(8,128)(2,1)S(1)} %copy-done.29), channel_id=1, source_target_pairs={{0,1},{1,0},{2,3},{3,2},{4,5},{5,4},{6,7},{7,6},{8,9},{9,8},{10,11... | collective-permute-start | bytes 589832 | tf_op jit(solution)/shard_map/ppermute | solution.py:973
  122.8 17.1 %collective-permute-start.10 = (bf16[2,64,768]{2,1,0:T(8,128)(2,1)S(1)}, bf16[2,64,768]{2,1,0:T(8,128)(2,1)S(1)}, u32[]{:S(2)}, u32[]{:S(2)}) collective-permute-start(bf16[2,64,768]{2,1,0:T(8,128)(2,1)S(1)} %copy-done.28), channel_id=1, source_target_pairs={{0,2},{1,3},{2,0},{3,1},{4,6},{5,7},{6,4},{7,5},{8,10},{9,11},{10,... | collective-permute-start | bytes 589832 | tf_op jit(solution)/shard_map/ppermute | solution.py:973
  125.5 14.5 %collective-permute-start.11 = (bf16[2,64,768]{2,1,0:T(8,128)(2,1)S(1)}, bf16[2,64,768]{2,1,0:T(8,128)(2,1)S(1)}, u32[]{:S(2)}, u32[]{:S(2)}) collective-permute-start(bf16[2,64,768]{2,1,0:T(8,128)(2,1)S(1)} %copy-done.27), channel_id=1, source_target_pairs={{0,3},{1,2},{2,1},{3,0},{4,7},{5,6},{6,5},{7,4},{8,11},{9,10},{10,... | collective-permute-start | bytes 589832 | tf_op jit(solution)/shard_map/ppermute | solution.py:973
  133.7 6.3 %copy-start.31 = (bf16[2,64,768]{2,1,0:T(8,128)(2,1)}, bf16[2,64,768]{2,1,0:T(8,128)(2,1)S(1)}, u32[]{:S(2)}) copy-start(bf16[2,64,768]{2,1,0:T(8,128)(2,1)S(1)} %collective-permute-done.9.g1) | copy-start | bytes 589828
  140.7 12.2 %copy-start.2 = (bf16[4,2,96,768]{3,2,1,0:T(8,128)(2,1)S(1)}, bf16[4,2,96,768]{3,2,1,0:T(8,128)(2,1)}, u32[]{:S(2)}) copy-start(bf16[4,2,96,768]{3,2,1,0:T(8,128)(2,1)} %get-tuple-element.123.keep) | copy-start | bytes 3538948
  144.8 17.5 %all-to-all-start.2 = ((bf16[32,32,128]{2,1,0:T(8,128)(2,1)}), bf16[32,32,128]{2,1,0:T(8,128)(2,1)S(1)}, u32[]{:S(2)}, u32[]{:S(2)}) async-start(bf16[32,32,128]{2,1,0:T(8,128)(2,1)} %bitcast.24), calls=%async_computation.2 | async-start | bytes 524288 | tf_op jit(solution)/shard_map/all_to_all | solution.py:1130
  155.8 14.0 %collective-permute-start.13 = (bf16[2,96,768]{2,1,0:T(8,128)(2,1)}, bf16[2,96,768]{2,1,0:T(8,128)(2,1)S(1)}, u32[]{:S(2)}, u32[]{:S(2)}) collective-permute-start(bf16[2,96,768]{2,1,0:T(8,128)(2,1)} %get-tuple-element.126), channel_id=1, source_target_pairs={{0,8},{4,12},{8,0},{12,4},{16,24},{20,28},{24,16},{28,20},{1,9},{5... | collective-permute-start | bytes 884744 | tf_op jit(solution)/shard_map/ppermute | solution.py:977
  157.3 15.9 %collective-permute-start.14 = (bf16[2,96,768]{2,1,0:T(8,128)(2,1)}, bf16[2,96,768]{2,1,0:T(8,128)(2,1)S(1)}, u32[]{:S(2)}, u32[]{:S(2)}) collective-permute-start(bf16[2,96,768]{2,1,0:T(8,128)(2,1)} %get-tuple-element.127), channel_id=1, source_target_pairs={{0,16},{4,20},{8,24},{12,28},{16,0},{20,4},{24,8},{28,12},{1,17},{... | collective-permute-start | bytes 884744 | tf_op jit(solution)/shard_map/ppermute | solution.py:977
  157.9 15.3 %collective-permute-start.15 = (bf16[2,96,768]{2,1,0:T(8,128)(2,1)S(1)}, bf16[2,96,768]{2,1,0:T(8,128)(2,1)S(1)}, u32[]{:S(2)}, u32[]{:S(2)}) collective-permute-start(bf16[2,96,768]{2,1,0:T(8,128)(2,1)S(1)} %get-tuple-element.128), channel_id=1, source_target_pairs={{0,24},{4,28},{8,16},{12,20},{16,8},{20,12},{24,0},{28,4},{1,25},{... | collective-permute-start | bytes 884744 | tf_op jit(solution)/shard_map/ppermute | solution.py:977
  169.9 8.3 %copy-start.36 = (bf16[128,192]{1,0:T(8,128)(2,1)S(1)}, bf16[128,192]{1,0:T(8,128)(2,1)}, u32[]{:S(2)}) copy-start(bf16[128,192]{1,0:T(8,128)(2,1)} %get-tuple-element.138) | copy-start | bytes 147460
  169.9 9.8 %copy-start.35 = (bf16[128,192]{1,0:T(8,128)(2,1)S(1)}, bf16[128,192]{1,0:T(8,128)(2,1)}, u32[]{:S(2)}) copy-start(bf16[128,192]{1,0:T(8,128)(2,1)} %get-tuple-element.140) | copy-start | bytes 147460
  169.9 11.9 %copy-start.34 = (bf16[128,192]{1,0:T(8,128)(2,1)S(1)}, bf16[128,192]{1,0:T(8,128)(2,1)}, u32[]{:S(2)}) copy-start(bf16[128,192]{1,0:T(8,128)(2,1)} %get-tuple-element.142) | copy-start | bytes 147460
  169.9 8.2 %copy-start.8 = (bf16[2,96,768]{2,1,0:T(8,128)(2,1)}, bf16[2,96,768]{2,1,0:T(8,128)(2,1)S(1)}, u32[]{:S(2)}) copy-start(bf16[2,96,768]{2,1,0:T(8,128)(2,1)S(1)} %collective-permute-done.13.from_x) | copy-start | bytes 884740
  173.2 4.9 %copy-start.10 = (bf16[2,96,768]{2,1,0:T(8,128)(2,1)}, bf16[2,96,768]{2,1,0:T(8,128)(2,1)S(1)}, u32[]{:S(2)}) copy-start(bf16[2,96,768]{2,1,0:T(8,128)(2,1)S(1)} %collective-permute-done.14.from_y) | copy-start | bytes 884740
  173.2 4.9 %copy-start.12 = (bf16[2,96,768]{2,1,0:T(8,128)(2,1)}, bf16[2,96,768]{2,1,0:T(8,128)(2,1)S(1)}, u32[]{:S(2)}) copy-start(bf16[2,96,768]{2,1,0:T(8,128)(2,1)S(1)} %collective-permute-done.15.from_xy) | copy-start | bytes 884740
  173.2 15.3 %all-to-all-start.3 = ((bf16[8,384,128]{2,1,0:T(8,128)(2,1)}), bf16[8,384,128]{2,1,0:T(8,128)(2,1)S(1)}, u32[]{:S(2)}, u32[]{:S(2)}) async-start(bf16[8,384,128]{2,1,0:T(8,128)(2,1)} %attn_backward_kernel.1), calls=%async_computation.4 | async-start | bytes 1572864 | tf_op jit(solution)/shard_map/all_to_all | solution.py:1146
  177.4 40.1 %reduce-scatter.2.cloned.1.call-start = ((), (), s32[]{:S(2)}) async-start(), calls=%async_computation.6 | async-start | bytes 983040 | tf_op jit(solution)/shard_map/reduce_scatter | solution.py:1131
  178.1 4.5 %collective-permute-start.16 = (bf16[128,192]{1,0:T(8,128)(2,1)S(1)}, bf16[128,192]{1,0:T(8,128)(2,1)S(1)}, u32[]{:S(2)}, u32[]{:S(2)}) collective-permute-start(bf16[128,192]{1,0:T(8,128)(2,1)S(1)} %copy-done.36), channel_id=1, source_target_pairs={{0,1},{1,0},{2,3},{3,2},{4,5},{5,4},{6,7},{7,6},{8,9},{9,8},{10,11... | collective-permute-start | bytes 147464 | tf_op jit(solution)/shard_map/ppermute | solution.py:973
  179.6 7.6 %collective-permute-start.17 = (bf16[128,192]{1,0:T(8,128)(2,1)S(1)}, bf16[128,192]{1,0:T(8,128)(2,1)S(1)}, u32[]{:S(2)}, u32[]{:S(2)}) collective-permute-start(bf16[128,192]{1,0:T(8,128)(2,1)S(1)} %copy-done.35), channel_id=1, source_target_pairs={{0,2},{1,3},{2,0},{3,1},{4,6},{5,7},{6,4},{7,5},{8,10},{9,11},{10,... | collective-permute-start | bytes 147464 | tf_op jit(solution)/shard_map/ppermute | solution.py:973
  181.7 6.2 %collective-permute-start.18 = (bf16[128,192]{1,0:T(8,128)(2,1)S(1)}, bf16[128,192]{1,0:T(8,128)(2,1)S(1)}, u32[]{:S(2)}, u32[]{:S(2)}) collective-permute-start(bf16[128,192]{1,0:T(8,128)(2,1)S(1)} %copy-done.34), channel_id=1, source_target_pairs={{0,3},{1,2},{2,1},{3,0},{4,7},{5,6},{6,5},{7,4},{8,11},{9,10},{10,... | collective-permute-start | bytes 147464 | tf_op jit(solution)/shard_map/ppermute | solution.py:973
  182.6 5.9 %copy-start.37 = (bf16[128,192]{1,0:T(8,128)(2,1)}, bf16[128,192]{1,0:T(8,128)(2,1)S(1)}, u32[]{:S(2)}) copy-start(bf16[128,192]{1,0:T(8,128)(2,1)S(1)} %collective-permute-done.16.a1) | copy-start | bytes 147460
  196.0 4.5 %copy-start.3 = (bf16[4,96,832]{2,1,0:T(8,128)(2,1)S(1)}, bf16[4,96,832]{2,1,0:T(8,128)(2,1)}, u32[]{:S(2)}) copy-start(bf16[4,96,832]{2,1,0:T(8,128)(2,1)} %get-tuple-element.145.keep) | copy-start | bytes 1916932
  196.0 4.5 %collective-permute-start.19 = (bf16[4,96,832]{2,1,0:T(8,128)(2,1)}, bf16[4,96,832]{2,1,0:T(8,128)(2,1)S(1)}, u32[]{:S(2)}, u32[]{:S(2)}) collective-permute-start(bf16[4,96,832]{2,1,0:T(8,128)(2,1)} %get-tuple-element.146), channel_id=1, source_target_pairs={{0,4},{4,0},{8,12},{12,8},{16,20},{20,16},{24,28},{28,24},{1,5},{5... | collective-permute-start | bytes 1916936 | tf_op jit(solution)/shard_map/ppermute | solution.py:977
  196.1 8.2 %copy-start.5 = (f32[2,96,768]{2,1,0:T(8,128)S(1)}, f32[2,96,768]{2,1,0:T(8,128)}, u32[]{:S(2)}) copy-start(f32[2,96,768]{2,1,0:T(8,128)} %copy-done.4) | copy-start | bytes 1769476
  196.1 8.2 %copy-start.9 = (bf16[2,96,768]{2,1,0:T(8,128)(2,1)S(1)}, bf16[2,96,768]{2,1,0:T(8,128)(2,1)}, u32[]{:S(2)}) copy-start(bf16[2,96,768]{2,1,0:T(8,128)(2,1)} %copy-done.8) | copy-start | bytes 884740
  196.1 36.7 %all-to-all-start.4 = ((bf16[4,2,64,768]{3,2,1,0:T(8,128)(2,1)}), bf16[4,2,64,768]{3,2,1,0:T(8,128)(2,1)S(1)}, u32[]{:S(2)}, u32[]{:S(2)}) async-start(bf16[4,2,64,768]{3,2,1,0:T(8,128)(2,1)} %get-tuple-element.143), calls=%async_computation.5 | async-start | bytes 1572864 | tf_op jit(solution)/shard_map/all_to_all | solution.py:1169
  200.5 3.8 %copy-start.11 = (bf16[2,96,768]{2,1,0:T(8,128)(2,1)S(1)}, bf16[2,96,768]{2,1,0:T(8,128)(2,1)}, u32[]{:S(2)}) copy-start(bf16[2,96,768]{2,1,0:T(8,128)(2,1)} %copy-done.10) | copy-start | bytes 884740
  200.5 3.8 %copy-start.13 = (bf16[2,96,768]{2,1,0:T(8,128)(2,1)S(1)}, bf16[2,96,768]{2,1,0:T(8,128)(2,1)}, u32[]{:S(2)}) copy-start(bf16[2,96,768]{2,1,0:T(8,128)(2,1)} %copy-done.12) | copy-start | bytes 884740
  200.5 11.3 %copy-start.18 = (s32[2]{0:T(128)S(1)}, s32[2]{0:T(128)}, u32[]{:S(2)}) copy-start(s32[2]{0:T(128)} %pad_add_fusion.place) | copy-start | bytes 28
  200.7 16.8 %copy-start.23 = (f32[2,64,768]{2,1,0:T(8,128)S(1)}, f32[2,64,768]{2,1,0:T(8,128)}, u32[]{:S(2)}) copy-start(f32[2,64,768]{2,1,0:T(8,128)} %get-tuple-element.106.middle) | copy-start | bytes 1179652
  200.7 7.3 %collective-permute-start.20 = (bf16[96,832]{1,0:T(8,128)(2,1)S(1)}, bf16[96,832]{1,0:T(8,128)(2,1)S(1)}, u32[]{:S(2)}, u32[]{:S(2)}) collective-permute-start(bf16[96,832]{1,0:T(8,128)(2,1)S(1)} %get-tuple-element.148), channel_id=1, source_target_pairs={{0,8},{4,12},{8,0},{12,4},{16,24},{20,28},{24,16},{28,20},{1,9},{5... | collective-permute-start | bytes 479240 | tf_op jit(solution)/shard_map/ppermute | solution.py:977
  201.3 6.6 %collective-permute-start.21 = (bf16[96,832]{1,0:T(8,128)(2,1)S(1)}, bf16[96,832]{1,0:T(8,128)(2,1)S(1)}, u32[]{:S(2)}, u32[]{:S(2)}) collective-permute-start(bf16[96,832]{1,0:T(8,128)(2,1)S(1)} %get-tuple-element.149), channel_id=1, source_target_pairs={{0,16},{4,20},{8,24},{12,28},{16,0},{20,4},{24,8},{28,12},{1,17},{... | collective-permute-start | bytes 479240 | tf_op jit(solution)/shard_map/ppermute | solution.py:977
  202.8 9.1 %collective-permute-start.22 = (bf16[96,832]{1,0:T(8,128)(2,1)S(1)}, bf16[96,832]{1,0:T(8,128)(2,1)S(1)}, u32[]{:S(2)}, u32[]{:S(2)}) collective-permute-start(bf16[96,832]{1,0:T(8,128)(2,1)S(1)} %get-tuple-element.150), channel_id=1, source_target_pairs={{0,24},{4,28},{8,16},{12,20},{16,8},{20,12},{24,0},{28,4},{1,25},{... | collective-permute-start | bytes 479240 | tf_op jit(solution)/shard_map/ppermute | solution.py:977
  211.8 20.9 %copy-start.7 = (f32[2,64,768]{2,1,0:T(8,128)S(1)}, f32[2,64,768]{2,1,0:T(8,128)}, u32[]{:S(2)}) copy-start(f32[2,64,768]{2,1,0:T(8,128)} %get-tuple-element.144.grad_middle) | copy-start | bytes 1179652
  211.8 20.9 %copy-start.16 = (f32[8,768]{1,0:T(8,128)S(1)}, f32[8,768]{1,0:T(8,128)}, u32[]{:S(2)}) copy-start(f32[8,768]{1,0:T(8,128)} %copy-done.15) | copy-start | bytes 73732
  213.1 10.3 %collective-permute-start.25 = (f32[8,96]{1,0:T(8,128)S(1)}, f32[8,96]{1,0:T(8,128)S(1)}, u32[]{:S(2)}, u32[]{:S(2)}) collective-permute-start(f32[8,96]{1,0:T(8,128)S(1)} %get-tuple-element.155), channel_id=1, source_target_pairs={{0,3},{1,2},{2,1},{3,0},{4,7},{5,6},{6,5},{7,4},{8,11},{9,10},{10,... | collective-permute-start | bytes 9224 | tf_op jit(solution)/shard_map/ppermute | solution.py:973
  216.7 9.3 %collective-permute-start.24 = (bf16[96,256]{1,0:T(8,128)(2,1)S(1)}, bf16[96,256]{1,0:T(8,128)(2,1)S(1)}, u32[]{:S(2)}, u32[]{:S(2)}) collective-permute-start(bf16[96,256]{1,0:T(8,128)(2,1)S(1)} %get-tuple-element.154), channel_id=1, source_target_pairs={{0,2},{1,3},{2,0},{3,1},{4,6},{5,7},{6,4},{7,5},{8,10},{9,11},{10,... | collective-permute-start | bytes 147464 | tf_op jit(solution)/shard_map/ppermute | solution.py:973
  216.7 9.3 %collective-permute-start.23 = (bf16[96,256]{1,0:T(8,128)(2,1)S(1)}, bf16[96,256]{1,0:T(8,128)(2,1)S(1)}, u32[]{:S(2)}, u32[]{:S(2)}) collective-permute-start(bf16[96,256]{1,0:T(8,128)(2,1)S(1)} %get-tuple-element.153), channel_id=1, source_target_pairs={{0,1},{1,0},{2,3},{3,2},{4,5},{5,4},{6,7},{7,6},{8,9},{9,8},{10,11... | collective-permute-start | bytes 147464 | tf_op jit(solution)/shard_map/ppermute | solution.py:973
  219.2 12.8 %collective-permute-start.26 = (bf16[384,192]{1,0:T(8,128)(2,1)S(1)}, bf16[384,192]{1,0:T(8,128)(2,1)S(1)}, u32[]{:S(2)}, u32[]{:S(2)}) collective-permute-start(bf16[384,192]{1,0:T(8,128)(2,1)S(1)} %get-tuple-element.165), channel_id=1, source_target_pairs={{0,0},{8,1},{16,2},{24,3},{4,4},{12,5},{20,6},{28,7},{9,8},{1,9},{... | collective-permute-start | bytes 442376 | tf_op jit(solution)/shard_map/ppermute | solution.py:1176
  (11 other events, 8.8 us)
Sparse Core Ops, SparseCore 0:
  9.9 26.8 all-gather.8
  75.2 28.1 all-gather.6
  180.5 23.8 reduce-scatter.1

commit v4 on v3

--- a/solution.py
+++ b/solution.py
@@ -535,18 +535,8 @@
     to_two[:96, :] = jnp.where(even, groups[2], groups[0])
     to_one[96:, :] = lines[:112]
     to_two[96:, :] = lines[:112]
-    shared[...] = lines
-
-
-def third_kernel(inputs, shared, to_three, sems):
-    moves = copies(
-        sems,
-        (inputs.at[0], to_three.at[pl.ds(0, 64)]),
-        (inputs.at[1], to_three.at[pl.ds(64, 64)]),
-    )
     for number in range(4):
-        to_three[128:, 192 * number : 192 * (number + 1)] = shared[32 * number : 32 * (number + 1)]
-    finish(*moves)
+        shared[:, 192 * number : 192 * (number + 1)] = lines[32 * number : 32 * (number + 1)]
 
 
 def shard_kernel(place, weight, got_one, got_two, vectors, shard):
@@ -1021,7 +1011,7 @@
 
     to_one, to_two, shared = on_core(
         send_kernel,
-        [((208, 192), bf16), ((208, 192), bf16), ((128, 192), bf16)],
+        [((208, 192), bf16), ((208, 192), bf16), ((32, WIDE), bf16)],
         [place, query_key_value_weight, attention_out_weight, doc_starts],
         scratch=[((96, 576), bf16), ((96, 192), bf16), ((2, 64), jnp.int32)],
         place=True,
@@ -1030,7 +1020,7 @@
     )
     got_one, got_two = swap_z(to_one, 1), swap_z(to_two, 2)
     x_own = after(inputs, to_one, to_two)
-    (to_three,) = on_core(third_kernel, [((160, WIDE), bf16)], [x_own, shared], far=(0,), sems=2)
+    to_three = jnp.concatenate([x_own.reshape(128, WIDE), shared], axis=0)
     x_parts = [inputs, swap_z(x_own, 1), swap_z(x_own, 2), swap_z(to_three, 3)]
     (qkv_shard,) = on_core(
         shard_kernel,
@@ -1059,7 +1049,7 @@
     )
     ups = lax.all_gather(up_weight, "blk", axis=0)
     pack = lax.all_to_all(pack, "blk", 0, 0, tiled=True)
-    pack, g_one, g_three = lax.optimization_barrier((pack, g_one, g_three))
+    pack, g_three = lax.optimization_barrier((pack, g_three))
 
     head_rows = ((FULL_TOK, HEAD_DIM), bf16)
     head_cols = ((HEAD_DIM, FULL_TOK), bf16)

time: 241 us -> 241 us (level)
  Pallas kernels: 55.4 us -> 52.9 us
    all_to_all x1, waiting for transfers between devices: 4.41 us -> 1.58 us  [local_fast(): attn_pack = lax.all_to_all(attn_pack, 'blk', 0, 0, tiled=True)]
    ppermute x17, waiting for transfers between devices: 29.2 us -> 26.4 us  [swap_z(): return lax.ppermute(value, 'uly', [(i, i ^ shift) for i in range(4)])]
    all_to_all x1, waiting for transfers between devices: 0.01 us -> 2.55 us  [local_fast(): pack = lax.all_to_all(pack, 'blk', 0, 0, tiled=True)]
    pallas_call x17 -> x16, Pallas kernels: 55.4 us -> 52.9 us  [on_core(): pl.pallas_call(kernel, out_shape=shapes, in_specs=specs, out_specs=[FAR_S...]
    ppermute x17, starting transfers between devices: 26.9 us -> 29.5 us  [swap_z(): return lax.ppermute(value, 'uly', [(i, i ^ shift) for i in range(4)])]
  transfers between devices with their start and end apart: 35 -> 35, of which waited for: 15 -> 16; matrix products, arithmetic and copies ran while one was open for 2% -> 3% of each run, Pallas kernels for 16% -> 15%
where the time goes in v4:
time: 241 us; the launch traced here: 240 us
  starting transfers between devices  66.3 us (28%)
  waiting for transfers between devices  58.6 us (24%)
  Pallas kernels  52.9 us (22%)
  blocking collectives  35 us (15%)
  between operations  14.2 us (6%)
  local copies, waits for them, and re-layouts  8.73 us (4%)
  other arithmetic  4 us (2%)
    pallas_call x16, Pallas kernels, on_core(): pl.pallas_call(kernel, out_shape=shapes, in_specs=specs, out_specs=[FAR_S...  52.9 us
    ppermute x17, starting transfers between devices, swap_z(): return lax.ppermute(value, 'uly', [(i, i ^ shift) for i in range(4)])  29.5 us
    ppermute x17, waiting for transfers between devices, swap_z(): return lax.ppermute(value, 'uly', [(i, i ^ shift) for i in range(4)])  26.4 us
    all_gather x1, blocking collectives, local_fast(): lax.all_gather(attn_pack.reshape(2, 4, 128, 128)[:, :3], 'uly', axis=0)  22.7 us
    all_gather x1, blocking collectives, local_fast(): w_qkv = lax.all_gather(qkv_shard, 'blk', axis=0)  12.3 us
    ppermute x8, waiting for transfers between devices, swap_blk(): return lax.ppermute(value, 'blk', [(i, i ^ mask) for i in range(8)])  10 us
    ppermute x1, waiting for transfers between devices, local_fast(): down_shard = lax.ppermute(down_weight, ('blk', 'uly'), DOWN_MOVES)  8.99 us
    unnamed x82, local copies, waits for them, and re-layouts  8.19 us
  transfers between devices with their start and end apart: 35, of which 16 were waited for; matrix products, arithmetic and copies ran while one was open for 3% of the time, Pallas kernels for 15%

profile of v4, /device:TPU:4, one launch (start us, length us, event | category | flops | bytes accessed | tf_op | source)
XLA Modules:
  0.0 239.7 jit_solution(1719571678137629570)
XLA Ops:
  8.5 2.4 send_kernel.1
  10.9 1.6 collective-permute-start.4
  12.5 2.6 %collective-permute-start.5 = (bf16[208,192]{1,0:T(8,128)(2,1)}, bf16[208,192]{1,0:T(8,128)(2,1)S(1)}, u32[]{:S(2)}, u32[]{:S(2)}) collective-permute-start(bf16[208,192]{1,0:T(8,128)(2,1)} %get-tuple-element.89), channel_id=1, source_target_pairs={{0,2},{1,3},{2,0},{3,1},{4,6},{5,7},{6,4},{7,5},{8,10},{9,11},{10,... | collective-permute-start | bytes 239624 | tf_op jit(solution)/shard_map/ppermute | solution.py:963
  15.9 1.1 pad_maximum_fusion
  17.0 3.7 %collective-permute-start.3 = (bf16[160,768]{1,0:T(8,128)(2,1)S(1)}, bf16[160,768]{1,0:T(8,128)(2,1)S(1)}, u32[]{:S(2)}, u32[]{:S(2)}) collective-permute-start(bf16[160,768]{1,0:T(8,128)(2,1)S(1)} %pad_maximum_fusion), channel_id=1, source_target_pairs={{0,3},{1,2},{2,1},{3,0},{4,7},{5,6},{6,5},{7,4},{8,11},{9,10},{10,... | collective-permute-start | bytes 737288 | tf_op jit(solution)/shard_map/ppermute | solution.py:963
  21.3 1.1 copy.23
  22.4 1.9 collective-permute-start
  24.3 0.8 collective-permute-done.5.got_two
  26.5 12.3 %all-gather = bf16[768,640]{1,0:T(8,128)(2,1)S(1)} all-gather(bf16[96,640]{1,0:T(8,128)(2,1)S(1)} %shard_kernel.1), channel_id=2, replica_groups=mesh['blk'=8,'uly'=4] {'blk'}, dimensions={0}, use_global_device_ids=true | all-gather | bytes 1105920 | tf_op jit(solution)/shard_map/all_gather | solution.py:1032
  38.8 9.0 %collective-permute-done.down = bf16[384,192]{1,0:T(8,128)(2,1)S(1)} collective-permute-done((bf16[384,192]{1,0:T(8,128)(2,1)S(1)}, bf16[384,192]{1,0:T(8,128)(2,1)S(1)}, u32[]{:S(2)}, u32[]{:S(2)}) %collective-permute-start) | collective-permute-done | bytes 147488 | tf_op jit(solution)/shard_map/ppermute | solution.py:1033
  47.8 3.0 %first_kernel.1 = (bf16[8,400,128]{2,1,0:T(8,128)(2,1)}, bf16[512,768]{1,0:T(8,128)(2,1)S(1)}, bf16[2,4,64,768]{3,2,1,0:T(8,128)(2,1)S(1)}, f32[8,768]{1,0:T(8,128)S(1)}) custom-call(s32[2]{0:T(128)S(1)} %copy-done.17, bf16[2,64,768]{2,1,0:T(8,128)(2,1)S(1)} %copy-done.1, bf16[2,64,768]{2,1,0:T(8,128)(2,1)S(1)} %collective-permute-done.1.x1, ...), custom_call_target="tpu_custom_call" | custom-call | tf_op jit(solution)/shard_map/first_kernel/pallas_call | solution.py:950
  51.4 0.9 copy-done.20
  52.3 0.9 copy-done.21
  53.2 3.6 %all-to-all-start = ((bf16[8,400,128]{2,1,0:T(8,128)(2,1)}), bf16[8,400,128]{2,1,0:T(8,128)(2,1)S(1)}, u32[]{:S(2)}, u32[]{:S(2)}) async-start(bf16[8,400,128]{2,1,0:T(8,128)(2,1)} %get-tuple-element.92), calls=%async_computation | async-start | bytes 1638400 | tf_op jit(solution)/shard_map/all_to_all | solution.py:1051
  56.9 3.5 %collective-permute-start.6 = (bf16[2,64,768]{2,1,0:T(8,128)(2,1)S(1)}, bf16[2,64,768]{2,1,0:T(8,128)(2,1)S(1)}, u32[]{:S(2)}, u32[]{:S(2)}) collective-permute-start(bf16[2,64,768]{2,1,0:T(8,128)(2,1)S(1)} %copy-done.24), channel_id=1, source_target_pairs={{0,3},{1,2},{2,1},{3,0},{4,7},{5,6},{6,5},{7,4},{8,11},{9,10},{10,... | collective-permute-start | bytes 589832 | tf_op jit(solution)/shard_map/ppermute | solution.py:963
  60.4 0.8 weights_kernel.1
  61.2 4.3 %collective-permute-done.6.g3 = bf16[2,64,768]{2,1,0:T(8,128)(2,1)S(1)} collective-permute-done((bf16[2,64,768]{2,1,0:T(8,128)(2,1)S(1)}, bf16[2,64,768]{2,1,0:T(8,128)(2,1)S(1)}, u32[]{:S(2)}, u32[]{:S(2)}) %collective-permute-start.6) | collective-permute-done | bytes 196640 | tf_op jit(solution)/shard_map/ppermute | solution.py:963
  65.6 2.5 %all-to-all-done.pack = bf16[8,400,128]{2,1,0:T(8,128)(2,1)S(1)} async-done(((bf16[8,400,128]{2,1,0:T(8,128)(2,1)}), bf16[8,400,128]{2,1,0:T(8,128)(2,1)S(1)}, u32[]{:S(2)}, u32[]{:S(2)}) %all-to-all-start) | async-done | bytes 819232 | tf_op jit(solution)/shard_map/all_to_all | solution.py:1051
  68.1 5.3 %attn_forward_kernel.1 = (bf16[8,128,128]{2,1,0:T(8,128)(2,1)}, f32[64,2048]{1,0:T(8,128)S(1)}, f32[1,2048]{1,0:T(1,128)S(1)}) custom-call(bf16[8,400,128]{2,1,0:T(8,128)(2,1)S(1)} %all-to-all-done.pack), custom_call_target="tpu_custom_call" | custom-call | tf_op jit(solution)/shard_map/attn_forward_kernel/pallas_call | solution.py:950
  73.5 4.8 %all-to-all-start.1 = ((bf16[8,128,128]{2,1,0:T(8,128)(2,1)}), bf16[8,128,128]{2,1,0:T(8,128)(2,1)S(1)}, u32[]{:S(2)}, u32[]{:S(2)}) async-start(bf16[8,128,128]{2,1,0:T(8,128)(2,1)} %get-tuple-element.96), calls=%async_computation.1 | async-start | bytes 524288 | tf_op jit(solution)/shard_map/all_to_all | solution.py:1064
  78.3 1.4 collective-permute-start.7
  79.7 2.5 %collective-permute-start.8 = (bf16[2,64,768]{2,1,0:T(8,128)(2,1)S(1)}, bf16[2,64,768]{2,1,0:T(8,128)(2,1)S(1)}, u32[]{:S(2)}, u32[]{:S(2)}) collective-permute-start(bf16[2,64,768]{2,1,0:T(8,128)(2,1)S(1)} %copy-done.24), channel_id=1, source_target_pairs={{0,2},{1,3},{2,0},{3,1},{4,6},{5,7},{6,4},{7,5},{8,10},{9,11},{10,... | collective-permute-start | bytes 589832 | tf_op jit(solution)/shard_map/ppermute | solution.py:963
  82.3 1.6 all-to-all-done.1
  83.9 22.7 %all-gather.1 = bf16[8,3,128,128]{3,2,1,0:T(8,128)(2,1)} all-gather(bf16[2,3,128,128]{3,2,1,0:T(8,128)(2,1)S(1)} %slice.20), channel_id=3, replica_groups=mesh['blk'=8,'uly'=4] {'uly'}, dimensions={0}, use_global_device_ids=true | all-gather | bytes 983040 | tf_op jit(solution)/shard_map/all_gather | solution.py:1070
  107.3 9.1 %middle_kernel.1 = (bf16[2,64,768]{2,1,0:T(8,128)(2,1)}, bf16[2,64,768]{2,1,0:T(8,128)(2,1)}, bf16[2,64,768]{2,1,0:T(8,128)(2,1)}, bf16[2,64,768]{2,1,0:T(8,128)...) custom-call(s32[2]{0:T(128)} %pad_add_fusion.place, ...), custom_call_target="tpu_custom_call" | custom-call | flops 5000000000 | tf_op jit(solution)/shard_map/middle_kernel/pallas_call | solution.py:950
  116.4 6.4 %feed_grads_kernel.1 = (bf16[2,256,768]{2,1,0:T(8,128)(2,1)}, bf16[4,2,96,768]{3,2,1,0:T(8,128)(2,1)}, bf16[4,2,96,768]{3,2,1,0:T(8,128)(2,1)}) custom-call(s32[2]{0:T(128)} %pad_add_fusion.place, bf16[512,768]{1,0:T(8,128)(2,1)} %get-tuple-element.105.normed, bf16[512,768]{1,0:T(8,128)(2,1)} %get-tuple-element.106.act, ...), custom_call_target="tpu_custom_call" | custom-call | flops 4000000000 | tf_op jit(solution)/shard_map/feed_grads_kernel/pallas_call | solution.py:950
  122.9 0.7 collective-permute-start.9
  123.6 1.2 collective-permute-start.10
  124.8 2.5 %collective-permute-start.11 = (bf16[2,64,768]{2,1,0:T(8,128)(2,1)S(1)}, bf16[2,64,768]{2,1,0:T(8,128)(2,1)S(1)}, u32[]{:S(2)}, u32[]{:S(2)}) collective-permute-start(bf16[2,64,768]{2,1,0:T(8,128)(2,1)S(1)} %copy-done.26), channel_id=1, source_target_pairs={{0,3},{1,2},{2,1},{3,0},{4,7},{5,6},{6,5},{7,4},{8,11},{9,10},{10,... | collective-permute-start | bytes 589832 | tf_op jit(solution)/shard_map/ppermute | solution.py:963
  127.3 6.0 %collective-permute-done.9.g1 = bf16[2,64,768]{2,1,0:T(8,128)(2,1)S(1)} collective-permute-done((bf16[2,64,768]{2,1,0:T(8,128)(2,1)S(1)}, bf16[2,64,768]{2,1,0:T(8,128)(2,1)S(1)}, u32[]{:S(2)}, u32[]{:S(2)}) %collective-permute-start.9) | collective-permute-done | bytes 196640 | tf_op jit(solution)/shard_map/ppermute | solution.py:963
  133.3 7.4 %collective-permute-done.10.g2 = bf16[2,64,768]{2,1,0:T(8,128)(2,1)S(1)} collective-permute-done((bf16[2,64,768]{2,1,0:T(8,128)(2,1)S(1)}, bf16[2,64,768]{2,1,0:T(8,128)(2,1)S(1)}, u32[]{:S(2)}, u32[]{:S(2)}) %collective-permute-start.10) | collective-permute-done | bytes 196640 | tf_op jit(solution)/shard_map/ppermute | solution.py:963
  141.5 4.2 %second_back_kernel.1 = (f32[2,64,768]{2,1,0:T(8,128)}, bf16[8,4,32,128]{3,2,1,0:T(8,128)(2,1)}, f32[8,768]{1,0:T(8,128)}, bf16[128,192]{1,0:T(8,128)(2,1)}, bf1...) custom-call(s32[2]{0:T(128)} %pad_add_fusion.place, ...), custom_call_target="tpu_custom_call" | custom-call | flops 2000000000 | tf_op jit(solution)/shard_map/second_back_kernel/pallas_call | solution.py:950
  145.7 6.4 %all-to-all-start.2 = ((bf16[32,32,128]{2,1,0:T(8,128)(2,1)}), bf16[32,32,128]{2,1,0:T(8,128)(2,1)S(1)}, u32[]{:S(2)}, u32[]{:S(2)}) async-start(bf16[32,32,128]{2,1,0:T(8,128)(2,1)} %bitcast.26), calls=%async_computation.2 | async-start | bytes 524288 | tf_op jit(solution)/shard_map/all_to_all | solution.py:1120
  152.1 2.2 chip_sum_kernel.2
  154.3 0.8 copy-done.4
  155.1 1.5 collective-permute-start.13
  157.1 1.5 collective-permute-start.15
  158.6 3.0 %all-to-all-done.2.grad = bf16[32,32,128]{2,1,0:T(8,128)(2,1)S(1)} async-done(((bf16[32,32,128]{2,1,0:T(8,128)(2,1)}), bf16[32,32,128]{2,1,0:T(8,128)(2,1)S(1)}, u32[]{:S(2)}, u32[]{:S(2)}) %all-to-all-start.2) | async-done | bytes 262176 | tf_op jit(solution)/shard_map/all_to_all | solution.py:1120
  161.6 7.5 %attn_backward_kernel.1 = bf16[8,384,128]{2,1,0:T(8,128)(2,1)} custom-call(bf16[8,400,128]{2,1,0:T(8,128)(2,1)S(1)} %all-to-all-done.pack, bf16[32,32,128]{2,1,0:T(8,128)(2,1)S(1)} %all-to-all-done.2.grad, f32[64,2048]{1,0:T(8,128)S(1)} %get-tuple-element.128.out_cols, f32[1,2048]{1,0:T(1,128)S(1)} %get-tuple-element.129.log_row), custom_call_target="tpu_custom_call" | custom-call | tf_op jit(solution)/shard_map/attn_backward_kernel/pallas_call | solution.py:950
  169.2 3.3 %collective-permute-done.14.from_y = bf16[2,96,768]{2,1,0:T(8,128)(2,1)S(1)} collective-permute-done((bf16[2,96,768]{2,1,0:T(8,128)(2,1)}, bf16[2,96,768]{2,1,0:T(8,128)(2,1)S(1)}, u32[]{:S(2)}, u32[]{:S(2)}) %collective-permute-start.14) | collective-permute-done | bytes 294944 | tf_op jit(solution)/shard_map/ppermute | solution.py:967
  172.5 4.2 %all-to-all-start.3 = ((bf16[8,384,128]{2,1,0:T(8,128)(2,1)}), bf16[8,384,128]{2,1,0:T(8,128)(2,1)S(1)}, u32[]{:S(2)}, u32[]{:S(2)}) async-start(bf16[8,384,128]{2,1,0:T(8,128)(2,1)} %attn_backward_kernel.1), calls=%async_computation.4 | async-start | bytes 1572864 | tf_op jit(solution)/shard_map/all_to_all | solution.py:1136
  177.4 1.5 collective-permute-start.16
  178.9 2.1 collective-permute-start.17
  181.0 0.8 collective-permute-start.18
  181.9 4.6 %collective-permute-done.17.a2 = bf16[128,192]{1,0:T(8,128)(2,1)S(1)} collective-permute-done((bf16[128,192]{1,0:T(8,128)(2,1)S(1)}, bf16[128,192]{1,0:T(8,128)(2,1)S(1)}, u32[]{:S(2)}, u32[]{:S(2)}) %collective-permute-start.17) | collective-permute-done | bytes 49184 | tf_op jit(solution)/shard_map/ppermute | solution.py:963
  186.4 0.7 collective-permute-done.18.a3
  187.8 0.9 copy-done.22
  188.7 6.6 %last_kernel.1 = (bf16[4,2,64,768]{3,2,1,0:T(8,128)(2,1)}, bf16[4,96,832]{2,1,0:T(8,128)(2,1)}, bf16[4,96,832]{2,1,0:T(8,128)(2,1)}) custom-call(s32[2]{0:T(128)} %pad_add_fusion.place, bf16[8,384,128]{2,1,0:T(8,128)(2,1)} %copy-done.22, bf16[8,96,640]{2,1,0:T(8,128)(2,1)} %bitcast.22, bf16[2,4,64,768]{3,2,1,0:T(8,128)(2,1)} %copy-done.21, ...), custom_call_target="tpu_custom_call" | custom-call | flops 3000000000 | tf_op jit(solution)/shard_map/last_kernel/pallas_call | solution.py:950
  195.3 4.4 %all-to-all-start.4 = ((bf16[4,2,64,768]{3,2,1,0:T(8,128)(2,1)}), bf16[4,2,64,768]{3,2,1,0:T(8,128)(2,1)S(1)}, u32[]{:S(2)}, u32[]{:S(2)}) async-start(bf16[4,2,64,768]{3,2,1,0:T(8,128)(2,1)} %get-tuple-element.141), calls=%async_computation.5 | async-start | bytes 1572864 | tf_op jit(solution)/shard_map/all_to_all | solution.py:1159
  200.6 1.4 collective-permute-start.21
  202.1 1.5 collective-permute-start.22
  203.5 0.9 join_ud_kernel.1
  204.4 2.8 %collective-permute-done.20.from_x = bf16[96,832]{1,0:T(8,128)(2,1)S(1)} collective-permute-done((bf16[96,832]{1,0:T(8,128)(2,1)S(1)}, bf16[96,832]{1,0:T(8,128)(2,1)S(1)}, u32[]{:S(2)}, u32[]{:S(2)}) %collective-permute-start.20) | collective-permute-done | bytes 159776 | tf_op jit(solution)/shard_map/ppermute | solution.py:967
  207.2 3.9 %collective-permute-done.22.from_xy = bf16[96,832]{1,0:T(8,128)(2,1)S(1)} collective-permute-done((bf16[96,832]{1,0:T(8,128)(2,1)S(1)}, bf16[96,832]{1,0:T(8,128)(2,1)S(1)}, u32[]{:S(2)}, u32[]{:S(2)}) %collective-permute-start.22) | collective-permute-done | bytes 159776 | tf_op jit(solution)/shard_map/ppermute | solution.py:967
  211.1 1.3 join_tail_kernel.1
  212.4 3.5 %collective-permute-start.25 = (f32[8,96]{1,0:T(8,128)S(1)}, f32[8,96]{1,0:T(8,128)S(1)}, u32[]{:S(2)}, u32[]{:S(2)}) collective-permute-start(f32[8,96]{1,0:T(8,128)S(1)} %get-tuple-element.153), channel_id=1, source_target_pairs={{0,3},{1,2},{2,1},{3,0},{4,7},{5,6},{6,5},{7,4},{8,11},{9,10},{10,... | collective-permute-start | bytes 9224 | tf_op jit(solution)/shard_map/ppermute | solution.py:963
  215.9 0.8 collective-permute-start.23
  216.8 1.6 add_convert_fusion
  218.4 4.2 %collective-permute-start.26 = (bf16[384,192]{1,0:T(8,128)(2,1)S(1)}, bf16[384,192]{1,0:T(8,128)(2,1)S(1)}, u32[]{:S(2)}, u32[]{:S(2)}) collective-permute-start(bf16[384,192]{1,0:T(8,128)(2,1)S(1)} %get-tuple-element.163), channel_id=1, source_target_pairs={{0,0},{8,1},{16,2},{24,3},{4,4},{12,5},{20,6},{28,7},{9,8},{1,9},{... | collective-permute-start | bytes 442376 | tf_op jit(solution)/shard_map/ppermute | solution.py:1166
  222.7 2.6 %collective-permute-done.24.got_two = bf16[96,256]{1,0:T(8,128)(2,1)S(1)} collective-permute-done((bf16[96,256]{1,0:T(8,128)(2,1)S(1)}, bf16[96,256]{1,0:T(8,128)(2,1)S(1)}, u32[]{:S(2)}, u32[]{:S(2)}) %collective-permute-start.24) | collective-permute-done | bytes 49184 | tf_op jit(solution)/shard_map/ppermute | solution.py:963
  225.3 1.3 finish_tail_kernel.1
  227.1 4.1 %collective-permute-done.26 = bf16[384,192]{1,0:T(8,128)(2,1)S(1)} collective-permute-done((bf16[384,192]{1,0:T(8,128)(2,1)S(1)}, bf16[384,192]{1,0:T(8,128)(2,1)S(1)}, u32[]{:S(2)}, u32[]{:S(2)}) %collective-permute-start.26) | collective-permute-done | bytes 147488 | tf_op jit(solution)/shard_map/ppermute | solution.py:1166
  231.2 0.8 copy.24
  232.0 1.1 finish_rows_kernel.1
  (115 shorter events, 9.8 us)
Async XLA Ops:
  7.2 17.9 %copy-start.6 = (bf16[96,576]{1,0:T(8,128)(2,1)S(1)}, bf16[96,576]{1,0:T(8,128)(2,1)}, u32[]{:S(2)}) copy-start(bf16[96,576]{1,0:T(8,128)(2,1)} %weight.1) | copy-start | bytes 331780
  7.2 99.4 %all-gather.9.cloned.1.call-start = ((), (), s32[]{:S(2)}) async-start(), calls=%async_computation.8 | async-start | bytes 1327104 | tf_op jit(solution)/shard_map/all_gather | solution.py:1050
  10.9 11.5 %collective-permute-start.4 = (bf16[208,192]{1,0:T(8,128)(2,1)}, bf16[208,192]{1,0:T(8,128)(2,1)S(1)}, u32[]{:S(2)}, u32[]{:S(2)}) collective-permute-start(bf16[208,192]{1,0:T(8,128)(2,1)} %get-tuple-element.88), channel_id=1, source_target_pairs={{0,1},{1,0},{2,3},{3,2},{4,5},{5,4},{6,7},{7,6},{8,9},{9,8},{10,11... | collective-permute-start | bytes 239624 | tf_op jit(solution)/shard_map/ppermute | solution.py:963
  12.5 12.6 %collective-permute-start.5 = (bf16[208,192]{1,0:T(8,128)(2,1)}, bf16[208,192]{1,0:T(8,128)(2,1)S(1)}, u32[]{:S(2)}, u32[]{:S(2)}) collective-permute-start(bf16[208,192]{1,0:T(8,128)(2,1)} %get-tuple-element.89), channel_id=1, source_target_pairs={{0,2},{1,3},{2,0},{3,1},{4,6},{5,7},{6,4},{7,5},{8,10},{9,11},{10,... | collective-permute-start | bytes 239624 | tf_op jit(solution)/shard_map/ppermute | solution.py:963
  15.1 32.7 %collective-permute-start.2 = (bf16[2,64,768]{2,1,0:T(8,128)(2,1)}, bf16[2,64,768]{2,1,0:T(8,128)(2,1)S(1)}, u32[]{:S(2)}, u32[]{:S(2)}) collective-permute-start(bf16[2,64,768]{2,1,0:T(8,128)(2,1)} %inputs.1), channel_id=1, source_target_pairs={{0,2},{1,3},{2,0},{3,1},{4,6},{5,7},{6,4},{7,5},{8,10},{9,11},{10,... | collective-permute-start | bytes 589832 | tf_op jit(solution)/shard_map/ppermute | solution.py:963
  15.5 32.3 %collective-permute-start.1 = (bf16[2,64,768]{2,1,0:T(8,128)(2,1)}, bf16[2,64,768]{2,1,0:T(8,128)(2,1)S(1)}, u32[]{:S(2)}, u32[]{:S(2)}) collective-permute-start(bf16[2,64,768]{2,1,0:T(8,128)(2,1)} %inputs.1), channel_id=1, source_target_pairs={{0,1},{1,0},{2,3},{3,2},{4,5},{5,4},{6,7},{7,6},{8,9},{9,8},{10,11... | collective-permute-start | bytes 589832 | tf_op jit(solution)/shard_map/ppermute | solution.py:963
  15.9 31.9 %copy-start.1 = (bf16[2,64,768]{2,1,0:T(8,128)(2,1)S(1)}, bf16[2,64,768]{2,1,0:T(8,128)(2,1)}, u32[]{:S(2)}) copy-start(bf16[2,64,768]{2,1,0:T(8,128)(2,1)} %inputs.1) | copy-start | bytes 589828
  15.9 31.9 %copy-start.19 = (s32[2,64]{1,0:T(2,128)S(1)}, s32[2,64]{1,0:T(2,128)}, u32[]{:S(2)}) copy-start(s32[2,64]{1,0:T(2,128)} %doc_starts.1) | copy-start | bytes 1540
  17.0 30.8 %collective-permute-start.3 = (bf16[160,768]{1,0:T(8,128)(2,1)S(1)}, bf16[160,768]{1,0:T(8,128)(2,1)S(1)}, u32[]{:S(2)}, u32[]{:S(2)}) collective-permute-start(bf16[160,768]{1,0:T(8,128)(2,1)S(1)} %pad_maximum_fusion), channel_id=1, source_target_pairs={{0,3},{1,2},{2,1},{3,0},{4,7},{5,6},{6,5},{7,4},{8,11},{9,10},{10,... | collective-permute-start | bytes 737288 | tf_op jit(solution)/shard_map/ppermute | solution.py:963
  22.4 25.4 %collective-permute-start = (bf16[384,192]{1,0:T(8,128)(2,1)S(1)}, bf16[384,192]{1,0:T(8,128)(2,1)S(1)}, u32[]{:S(2)}, u32[]{:S(2)}) collective-permute-start(bf16[384,192]{1,0:T(8,128)(2,1)S(1)} %copy.23), channel_id=1, source_target_pairs={{0,0},{1,8},{2,16},{3,24},{4,4},{5,12},{6,20},{7,28},{8,9},{9,1},{... | collective-permute-start | bytes 442376 | tf_op jit(solution)/shard_map/ppermute | solution.py:1033
  38.8 14.4 %copy-start = (bf16[768,640]{1,0:T(8,128)(2,1)}, bf16[768,640]{1,0:T(8,128)(2,1)S(1)}, u32[]{:S(2)}) copy-start(bf16[768,640]{1,0:T(8,128)(2,1)S(1)} %all-gather) | copy-start | bytes 2949124
  53.2 3.7 %copy-start.24 = (bf16[2,64,768]{2,1,0:T(8,128)(2,1)S(1)}, bf16[2,64,768]{2,1,0:T(8,128)(2,1)}, u32[]{:S(2)}) copy-start(bf16[2,64,768]{2,1,0:T(8,128)(2,1)} %out_grad.1) | copy-start | bytes 589828
  53.2 7.2 %copy-start.14 = (bf16[96,192]{1,0:T(8,128)(2,1)S(1)}, bf16[96,192]{1,0:T(8,128)(2,1)}, u32[]{:S(2)}) copy-start(bf16[96,192]{1,0:T(8,128)(2,1)} %out_weight.1) | copy-start | bytes 110596
  53.2 14.9 %all-to-all-start = ((bf16[8,400,128]{2,1,0:T(8,128)(2,1)}), bf16[8,400,128]{2,1,0:T(8,128)(2,1)S(1)}, u32[]{:S(2)}, u32[]{:S(2)}) async-start(bf16[8,400,128]{2,1,0:T(8,128)(2,1)} %get-tuple-element.92), calls=%async_computation | async-start | bytes 1638400 | tf_op jit(solution)/shard_map/all_to_all | solution.py:1051
  56.9 49.8 %all-gather.7.cloned.1.call-start = ((), (), s32[]{:S(2)}) async-start(), calls=%async_computation.7 | async-start | bytes 2654208 | tf_op jit(solution)/shard_map/all_gather | solution.py:1063
  56.9 8.7 %collective-permute-start.6 = (bf16[2,64,768]{2,1,0:T(8,128)(2,1)S(1)}, bf16[2,64,768]{2,1,0:T(8,128)(2,1)S(1)}, u32[]{:S(2)}, u32[]{:S(2)}) collective-permute-start(bf16[2,64,768]{2,1,0:T(8,128)(2,1)S(1)} %copy-done.24), channel_id=1, source_target_pairs={{0,3},{1,2},{2,1},{3,0},{4,7},{5,6},{6,5},{7,4},{8,11},{9,10},{10,... | collective-permute-start | bytes 589832 | tf_op jit(solution)/shard_map/ppermute | solution.py:963
  65.6 40.9 %copy-start.25 = (bf16[2,64,768]{2,1,0:T(8,128)(2,1)}, bf16[2,64,768]{2,1,0:T(8,128)(2,1)S(1)}, u32[]{:S(2)}) copy-start(bf16[2,64,768]{2,1,0:T(8,128)(2,1)S(1)} %collective-permute-done.6.g3) | copy-start | bytes 589828
  73.5 10.4 %all-to-all-start.1 = ((bf16[8,128,128]{2,1,0:T(8,128)(2,1)}), bf16[8,128,128]{2,1,0:T(8,128)(2,1)S(1)}, u32[]{:S(2)}, u32[]{:S(2)}) async-start(bf16[8,128,128]{2,1,0:T(8,128)(2,1)} %get-tuple-element.96), calls=%async_computation.1 | async-start | bytes 524288 | tf_op jit(solution)/shard_map/all_to_all | solution.py:1064
  78.3 28.2 %collective-permute-start.7 = (bf16[2,64,768]{2,1,0:T(8,128)(2,1)S(1)}, bf16[2,64,768]{2,1,0:T(8,128)(2,1)S(1)}, u32[]{:S(2)}, u32[]{:S(2)}) collective-permute-start(bf16[2,64,768]{2,1,0:T(8,128)(2,1)S(1)} %copy-done.24), channel_id=1, source_target_pairs={{0,1},{1,0},{2,3},{3,2},{4,5},{5,4},{6,7},{7,6},{8,9},{9,8},{10,11... | collective-permute-start | bytes 589832 | tf_op jit(solution)/shard_map/ppermute | solution.py:963
  79.7 26.8 %collective-permute-start.8 = (bf16[2,64,768]{2,1,0:T(8,128)(2,1)S(1)}, bf16[2,64,768]{2,1,0:T(8,128)(2,1)S(1)}, u32[]{:S(2)}, u32[]{:S(2)}) collective-permute-start(bf16[2,64,768]{2,1,0:T(8,128)(2,1)S(1)} %copy-done.24), channel_id=1, source_target_pairs={{0,2},{1,3},{2,0},{3,1},{4,6},{5,7},{6,4},{7,5},{8,10},{9,11},{10,... | collective-permute-start | bytes 589832 | tf_op jit(solution)/shard_map/ppermute | solution.py:963
  116.4 6.5 %copy-start.30 = (bf16[2,64,768]{2,1,0:T(8,128)(2,1)S(1)}, bf16[2,64,768]{2,1,0:T(8,128)(2,1)}, u32[]{:S(2)}) copy-start(bf16[2,64,768]{2,1,0:T(8,128)(2,1)} %get-tuple-element.115) | copy-start | bytes 589828
  116.4 7.2 %copy-start.28 = (bf16[2,64,768]{2,1,0:T(8,128)(2,1)S(1)}, bf16[2,64,768]{2,1,0:T(8,128)(2,1)}, u32[]{:S(2)}) copy-start(bf16[2,64,768]{2,1,0:T(8,128)(2,1)} %get-tuple-element.116) | copy-start | bytes 589828
  116.4 8.4 %copy-start.26 = (bf16[2,64,768]{2,1,0:T(8,128)(2,1)S(1)}, bf16[2,64,768]{2,1,0:T(8,128)(2,1)}, u32[]{:S(2)}) copy-start(bf16[2,64,768]{2,1,0:T(8,128)(2,1)} %get-tuple-element.117) | copy-start | bytes 589828
  122.8 29.3 %collective-permute-start.12 = (bf16[4,2,96,768]{3,2,1,0:T(8,128)(2,1)}, bf16[4,2,96,768]{3,2,1,0:T(8,128)(2,1)}, u32[]{:S(2)}, u32[]{:S(2)}) collective-permute-start(bf16[4,2,96,768]{3,2,1,0:T(8,128)(2,1)} %get-tuple-element.122), channel_id=1, source_target_pairs={{0,4},{4,0},{8,12},{12,8},{16,20},{20,16},{24,28},{28,24},{1,5},{5... | collective-permute-start | bytes 3538952 | tf_op jit(solution)/shard_map/ppermute | solution.py:967
  122.9 10.4 %collective-permute-start.9 = (bf16[2,64,768]{2,1,0:T(8,128)(2,1)S(1)}, bf16[2,64,768]{2,1,0:T(8,128)(2,1)S(1)}, u32[]{:S(2)}, u32[]{:S(2)}) collective-permute-start(bf16[2,64,768]{2,1,0:T(8,128)(2,1)S(1)} %copy-done.30), channel_id=1, source_target_pairs={{0,1},{1,0},{2,3},{3,2},{4,5},{5,4},{6,7},{7,6},{8,9},{9,8},{10,11... | collective-permute-start | bytes 589832 | tf_op jit(solution)/shard_map/ppermute | solution.py:963
  123.6 17.1 %collective-permute-start.10 = (bf16[2,64,768]{2,1,0:T(8,128)(2,1)S(1)}, bf16[2,64,768]{2,1,0:T(8,128)(2,1)S(1)}, u32[]{:S(2)}, u32[]{:S(2)}) collective-permute-start(bf16[2,64,768]{2,1,0:T(8,128)(2,1)S(1)} %copy-done.28), channel_id=1, source_target_pairs={{0,2},{1,3},{2,0},{3,1},{4,6},{5,7},{6,4},{7,5},{8,10},{9,11},{10,... | collective-permute-start | bytes 589832 | tf_op jit(solution)/shard_map/ppermute | solution.py:963
  124.8 15.9 %collective-permute-start.11 = (bf16[2,64,768]{2,1,0:T(8,128)(2,1)S(1)}, bf16[2,64,768]{2,1,0:T(8,128)(2,1)S(1)}, u32[]{:S(2)}, u32[]{:S(2)}) collective-permute-start(bf16[2,64,768]{2,1,0:T(8,128)(2,1)S(1)} %copy-done.26), channel_id=1, source_target_pairs={{0,3},{1,2},{2,1},{3,0},{4,7},{5,6},{6,5},{7,4},{8,11},{9,10},{10,... | collective-permute-start | bytes 589832 | tf_op jit(solution)/shard_map/ppermute | solution.py:963
  133.3 7.4 %copy-start.31 = (bf16[2,64,768]{2,1,0:T(8,128)(2,1)}, bf16[2,64,768]{2,1,0:T(8,128)(2,1)S(1)}, u32[]{:S(2)}) copy-start(bf16[2,64,768]{2,1,0:T(8,128)(2,1)S(1)} %collective-permute-done.9.g1) | copy-start | bytes 589828
  141.5 10.6 %copy-start.2 = (bf16[4,2,96,768]{3,2,1,0:T(8,128)(2,1)S(1)}, bf16[4,2,96,768]{3,2,1,0:T(8,128)(2,1)}, u32[]{:S(2)}) copy-start(bf16[4,2,96,768]{3,2,1,0:T(8,128)(2,1)} %get-tuple-element.121.keep) | copy-start | bytes 3538948
  145.7 15.9 %all-to-all-start.2 = ((bf16[32,32,128]{2,1,0:T(8,128)(2,1)}), bf16[32,32,128]{2,1,0:T(8,128)(2,1)S(1)}, u32[]{:S(2)}, u32[]{:S(2)}) async-start(bf16[32,32,128]{2,1,0:T(8,128)(2,1)} %bitcast.26), calls=%async_computation.2 | async-start | bytes 524288 | tf_op jit(solution)/shard_map/all_to_all | solution.py:1120
  155.1 14.0 %collective-permute-start.13 = (bf16[2,96,768]{2,1,0:T(8,128)(2,1)}, bf16[2,96,768]{2,1,0:T(8,128)(2,1)S(1)}, u32[]{:S(2)}, u32[]{:S(2)}) collective-permute-start(bf16[2,96,768]{2,1,0:T(8,128)(2,1)} %get-tuple-element.124), channel_id=1, source_target_pairs={{0,8},{4,12},{8,0},{12,4},{16,24},{20,28},{24,16},{28,20},{1,9},{5... | collective-permute-start | bytes 884744 | tf_op jit(solution)/shard_map/ppermute | solution.py:967
  156.6 15.9 %collective-permute-start.14 = (bf16[2,96,768]{2,1,0:T(8,128)(2,1)}, bf16[2,96,768]{2,1,0:T(8,128)(2,1)S(1)}, u32[]{:S(2)}, u32[]{:S(2)}) collective-permute-start(bf16[2,96,768]{2,1,0:T(8,128)(2,1)} %get-tuple-element.125), channel_id=1, source_target_pairs={{0,16},{4,20},{8,24},{12,28},{16,0},{20,4},{24,8},{28,12},{1,17},{... | collective-permute-start | bytes 884744 | tf_op jit(solution)/shard_map/ppermute | solution.py:967
  157.1 15.3 %collective-permute-start.15 = (bf16[2,96,768]{2,1,0:T(8,128)(2,1)S(1)}, bf16[2,96,768]{2,1,0:T(8,128)(2,1)S(1)}, u32[]{:S(2)}, u32[]{:S(2)}) collective-permute-start(bf16[2,96,768]{2,1,0:T(8,128)(2,1)S(1)} %get-tuple-element.126), channel_id=1, source_target_pairs={{0,24},{4,28},{8,16},{12,20},{16,8},{20,12},{24,0},{28,4},{1,25},{... | collective-permute-start | bytes 884744 | tf_op jit(solution)/shard_map/ppermute | solution.py:967
  169.1 8.3 %copy-start.36 = (bf16[128,192]{1,0:T(8,128)(2,1)S(1)}, bf16[128,192]{1,0:T(8,128)(2,1)}, u32[]{:S(2)}) copy-start(bf16[128,192]{1,0:T(8,128)(2,1)} %get-tuple-element.136) | copy-start | bytes 147460
  169.1 9.8 %copy-start.35 = (bf16[128,192]{1,0:T(8,128)(2,1)S(1)}, bf16[128,192]{1,0:T(8,128)(2,1)}, u32[]{:S(2)}) copy-start(bf16[128,192]{1,0:T(8,128)(2,1)} %get-tuple-element.138) | copy-start | bytes 147460
  169.1 11.9 %copy-start.34 = (bf16[128,192]{1,0:T(8,128)(2,1)S(1)}, bf16[128,192]{1,0:T(8,128)(2,1)}, u32[]{:S(2)}) copy-start(bf16[128,192]{1,0:T(8,128)(2,1)} %get-tuple-element.140) | copy-start | bytes 147460
  169.1 8.2 %copy-start.8 = (bf16[2,96,768]{2,1,0:T(8,128)(2,1)}, bf16[2,96,768]{2,1,0:T(8,128)(2,1)S(1)}, u32[]{:S(2)}) copy-start(bf16[2,96,768]{2,1,0:T(8,128)(2,1)S(1)} %collective-permute-done.13.from_x) | copy-start | bytes 884740
  172.4 4.9 %copy-start.10 = (bf16[2,96,768]{2,1,0:T(8,128)(2,1)}, bf16[2,96,768]{2,1,0:T(8,128)(2,1)S(1)}, u32[]{:S(2)}) copy-start(bf16[2,96,768]{2,1,0:T(8,128)(2,1)S(1)} %collective-permute-done.14.from_y) | copy-start | bytes 884740
  172.5 4.9 %copy-start.12 = (bf16[2,96,768]{2,1,0:T(8,128)(2,1)}, bf16[2,96,768]{2,1,0:T(8,128)(2,1)S(1)}, u32[]{:S(2)}) copy-start(bf16[2,96,768]{2,1,0:T(8,128)(2,1)S(1)} %collective-permute-done.15.from_xy) | copy-start | bytes 884740
  172.5 15.3 %all-to-all-start.3 = ((bf16[8,384,128]{2,1,0:T(8,128)(2,1)}), bf16[8,384,128]{2,1,0:T(8,128)(2,1)S(1)}, u32[]{:S(2)}, u32[]{:S(2)}) async-start(bf16[8,384,128]{2,1,0:T(8,128)(2,1)} %attn_backward_kernel.1), calls=%async_computation.4 | async-start | bytes 1572864 | tf_op jit(solution)/shard_map/all_to_all | solution.py:1136
  176.6 40.1 %reduce-scatter.2.cloned.1.call-start = ((), (), s32[]{:S(2)}) async-start(), calls=%async_computation.6 | async-start | bytes 983040 | tf_op jit(solution)/shard_map/reduce_scatter | solution.py:1121
  177.4 4.5 %collective-permute-start.16 = (bf16[128,192]{1,0:T(8,128)(2,1)S(1)}, bf16[128,192]{1,0:T(8,128)(2,1)S(1)}, u32[]{:S(2)}, u32[]{:S(2)}) collective-permute-start(bf16[128,192]{1,0:T(8,128)(2,1)S(1)} %copy-done.36), channel_id=1, source_target_pairs={{0,1},{1,0},{2,3},{3,2},{4,5},{5,4},{6,7},{7,6},{8,9},{9,8},{10,11... | collective-permute-start | bytes 147464 | tf_op jit(solution)/shard_map/ppermute | solution.py:963
  178.9 7.6 %collective-permute-start.17 = (bf16[128,192]{1,0:T(8,128)(2,1)S(1)}, bf16[128,192]{1,0:T(8,128)(2,1)S(1)}, u32[]{:S(2)}, u32[]{:S(2)}) collective-permute-start(bf16[128,192]{1,0:T(8,128)(2,1)S(1)} %copy-done.35), channel_id=1, source_target_pairs={{0,2},{1,3},{2,0},{3,1},{4,6},{5,7},{6,4},{7,5},{8,10},{9,11},{10,... | collective-permute-start | bytes 147464 | tf_op jit(solution)/shard_map/ppermute | solution.py:963
  181.0 6.2 %collective-permute-start.18 = (bf16[128,192]{1,0:T(8,128)(2,1)S(1)}, bf16[128,192]{1,0:T(8,128)(2,1)S(1)}, u32[]{:S(2)}, u32[]{:S(2)}) collective-permute-start(bf16[128,192]{1,0:T(8,128)(2,1)S(1)} %copy-done.34), channel_id=1, source_target_pairs={{0,3},{1,2},{2,1},{3,0},{4,7},{5,6},{6,5},{7,4},{8,11},{9,10},{10,... | collective-permute-start | bytes 147464 | tf_op jit(solution)/shard_map/ppermute | solution.py:963
  181.9 5.9 %copy-start.37 = (bf16[128,192]{1,0:T(8,128)(2,1)}, bf16[128,192]{1,0:T(8,128)(2,1)S(1)}, u32[]{:S(2)}) copy-start(bf16[128,192]{1,0:T(8,128)(2,1)S(1)} %collective-permute-done.16.a1) | copy-start | bytes 147460
  186.4 1.3 copy-start.38
  195.2 4.5 %copy-start.3 = (bf16[4,96,832]{2,1,0:T(8,128)(2,1)S(1)}, bf16[4,96,832]{2,1,0:T(8,128)(2,1)}, u32[]{:S(2)}) copy-start(bf16[4,96,832]{2,1,0:T(8,128)(2,1)} %get-tuple-element.143.keep) | copy-start | bytes 1916932
  195.2 4.5 %collective-permute-start.19 = (bf16[4,96,832]{2,1,0:T(8,128)(2,1)}, bf16[4,96,832]{2,1,0:T(8,128)(2,1)S(1)}, u32[]{:S(2)}, u32[]{:S(2)}) collective-permute-start(bf16[4,96,832]{2,1,0:T(8,128)(2,1)} %get-tuple-element.144), channel_id=1, source_target_pairs={{0,4},{4,0},{8,12},{12,8},{16,20},{20,16},{24,28},{28,24},{1,5},{5... | collective-permute-start | bytes 1916936 | tf_op jit(solution)/shard_map/ppermute | solution.py:967
  195.3 8.2 %copy-start.5 = (f32[2,96,768]{2,1,0:T(8,128)S(1)}, f32[2,96,768]{2,1,0:T(8,128)}, u32[]{:S(2)}) copy-start(f32[2,96,768]{2,1,0:T(8,128)} %copy-done.4) | copy-start | bytes 1769476
  195.3 8.2 %copy-start.9 = (bf16[2,96,768]{2,1,0:T(8,128)(2,1)S(1)}, bf16[2,96,768]{2,1,0:T(8,128)(2,1)}, u32[]{:S(2)}) copy-start(bf16[2,96,768]{2,1,0:T(8,128)(2,1)} %copy-done.8) | copy-start | bytes 884740
  195.3 36.7 %all-to-all-start.4 = ((bf16[4,2,64,768]{3,2,1,0:T(8,128)(2,1)}), bf16[4,2,64,768]{3,2,1,0:T(8,128)(2,1)S(1)}, u32[]{:S(2)}, u32[]{:S(2)}) async-start(bf16[4,2,64,768]{3,2,1,0:T(8,128)(2,1)} %get-tuple-element.141), calls=%async_computation.5 | async-start | bytes 1572864 | tf_op jit(solution)/shard_map/all_to_all | solution.py:1159
  199.7 3.8 %copy-start.11 = (bf16[2,96,768]{2,1,0:T(8,128)(2,1)S(1)}, bf16[2,96,768]{2,1,0:T(8,128)(2,1)}, u32[]{:S(2)}) copy-start(bf16[2,96,768]{2,1,0:T(8,128)(2,1)} %copy-done.10) | copy-start | bytes 884740
  199.8 3.8 %copy-start.13 = (bf16[2,96,768]{2,1,0:T(8,128)(2,1)S(1)}, bf16[2,96,768]{2,1,0:T(8,128)(2,1)}, u32[]{:S(2)}) copy-start(bf16[2,96,768]{2,1,0:T(8,128)(2,1)} %copy-done.12) | copy-start | bytes 884740
  199.8 11.3 %copy-start.18 = (s32[2]{0:T(128)S(1)}, s32[2]{0:T(128)}, u32[]{:S(2)}) copy-start(s32[2]{0:T(128)} %pad_add_fusion.place) | copy-start | bytes 28
  199.9 16.8 %copy-start.23 = (f32[2,64,768]{2,1,0:T(8,128)S(1)}, f32[2,64,768]{2,1,0:T(8,128)}, u32[]{:S(2)}) copy-start(f32[2,64,768]{2,1,0:T(8,128)} %get-tuple-element.104.middle) | copy-start | bytes 1179652
  200.0 7.3 %collective-permute-start.20 = (bf16[96,832]{1,0:T(8,128)(2,1)S(1)}, bf16[96,832]{1,0:T(8,128)(2,1)S(1)}, u32[]{:S(2)}, u32[]{:S(2)}) collective-permute-start(bf16[96,832]{1,0:T(8,128)(2,1)S(1)} %get-tuple-element.146), channel_id=1, source_target_pairs={{0,8},{4,12},{8,0},{12,4},{16,24},{20,28},{24,16},{28,20},{1,9},{5... | collective-permute-start | bytes 479240 | tf_op jit(solution)/shard_map/ppermute | solution.py:967
  200.6 6.6 %collective-permute-start.21 = (bf16[96,832]{1,0:T(8,128)(2,1)S(1)}, bf16[96,832]{1,0:T(8,128)(2,1)S(1)}, u32[]{:S(2)}, u32[]{:S(2)}) collective-permute-start(bf16[96,832]{1,0:T(8,128)(2,1)S(1)} %get-tuple-element.147), channel_id=1, source_target_pairs={{0,16},{4,20},{8,24},{12,28},{16,0},{20,4},{24,8},{28,12},{1,17},{... | collective-permute-start | bytes 479240 | tf_op jit(solution)/shard_map/ppermute | solution.py:967
  202.1 9.1 %collective-permute-start.22 = (bf16[96,832]{1,0:T(8,128)(2,1)S(1)}, bf16[96,832]{1,0:T(8,128)(2,1)S(1)}, u32[]{:S(2)}, u32[]{:S(2)}) collective-permute-start(bf16[96,832]{1,0:T(8,128)(2,1)S(1)} %get-tuple-element.148), channel_id=1, source_target_pairs={{0,24},{4,28},{8,16},{12,20},{16,8},{20,12},{24,0},{28,4},{1,25},{... | collective-permute-start | bytes 479240 | tf_op jit(solution)/shard_map/ppermute | solution.py:967
  211.1 20.9 %copy-start.7 = (f32[2,64,768]{2,1,0:T(8,128)S(1)}, f32[2,64,768]{2,1,0:T(8,128)}, u32[]{:S(2)}) copy-start(f32[2,64,768]{2,1,0:T(8,128)} %get-tuple-element.142.grad_middle) | copy-start | bytes 1179652
  211.1 20.9 %copy-start.16 = (f32[8,768]{1,0:T(8,128)S(1)}, f32[8,768]{1,0:T(8,128)}, u32[]{:S(2)}) copy-start(f32[8,768]{1,0:T(8,128)} %copy-done.15) | copy-start | bytes 73732
  212.4 10.3 %collective-permute-start.25 = (f32[8,96]{1,0:T(8,128)S(1)}, f32[8,96]{1,0:T(8,128)S(1)}, u32[]{:S(2)}, u32[]{:S(2)}) collective-permute-start(f32[8,96]{1,0:T(8,128)S(1)} %get-tuple-element.153), channel_id=1, source_target_pairs={{0,3},{1,2},{2,1},{3,0},{4,7},{5,6},{6,5},{7,4},{8,11},{9,10},{10,... | collective-permute-start | bytes 9224 | tf_op jit(solution)/shard_map/ppermute | solution.py:963
  215.9 9.3 %collective-permute-start.24 = (bf16[96,256]{1,0:T(8,128)(2,1)S(1)}, bf16[96,256]{1,0:T(8,128)(2,1)S(1)}, u32[]{:S(2)}, u32[]{:S(2)}) collective-permute-start(bf16[96,256]{1,0:T(8,128)(2,1)S(1)} %get-tuple-element.152), channel_id=1, source_target_pairs={{0,2},{1,3},{2,0},{3,1},{4,6},{5,7},{6,4},{7,5},{8,10},{9,11},{10,... | collective-permute-start | bytes 147464 | tf_op jit(solution)/shard_map/ppermute | solution.py:963
  215.9 9.3 %collective-permute-start.23 = (bf16[96,256]{1,0:T(8,128)(2,1)S(1)}, bf16[96,256]{1,0:T(8,128)(2,1)S(1)}, u32[]{:S(2)}, u32[]{:S(2)}) collective-permute-start(bf16[96,256]{1,0:T(8,128)(2,1)S(1)} %get-tuple-element.151), channel_id=1, source_target_pairs={{0,1},{1,0},{2,3},{3,2},{4,5},{5,4},{6,7},{7,6},{8,9},{9,8},{10,11... | collective-permute-start | bytes 147464 | tf_op jit(solution)/shard_map/ppermute | solution.py:963
  218.4 12.8 %collective-permute-start.26 = (bf16[384,192]{1,0:T(8,128)(2,1)S(1)}, bf16[384,192]{1,0:T(8,128)(2,1)S(1)}, u32[]{:S(2)}, u32[]{:S(2)}) collective-permute-start(bf16[384,192]{1,0:T(8,128)(2,1)S(1)} %get-tuple-element.163), channel_id=1, source_target_pairs={{0,0},{8,1},{16,2},{24,3},{4,4},{12,5},{20,6},{28,7},{9,8},{1,9},{... | collective-permute-start | bytes 442376 | tf_op jit(solution)/shard_map/ppermute | solution.py:1166
  (11 other events, 8.2 us)
Sparse Core Ops, SparseCore 0:
  9.9 27.3 all-gather.8
  73.6 29.0 all-gather.6
  179.8 23.8 reduce-scatter.1

commit v5 on v4

--- a/solution.py
+++ b/solution.py
@@ -611,10 +611,8 @@
 
 
 def first_row(pack, tile):
-    high, low = (
-        jnp.concatenate([rows[0:1], rows[1:2]], axis=1)
-        for rows in (in_f32(pack[tile, 384:386, :]), in_f32(pack[tile, 386:388, :]))
-    )
+    lines = in_f32(pack[tile, 384:, :])
+    high, low = (jnp.concatenate([lines[at : at + 1], lines[at + 1 : at + 2]], axis=1) for at in (0, 2))
     return high * 128.0 + low
 
 

time: 241 us -> 241 us (level)
  no operation moved by 1% of the time
where the time goes in v5:
time: 241 us; the launch traced here: 240 us
  starting transfers between devices  66.3 us (28%)
  waiting for transfers between devices  58.8 us (24%)
  Pallas kernels  52.9 us (22%)
  blocking collectives  34.9 us (14%)
  between operations  14.2 us (6%)
  local copies, waits for them, and re-layouts  8.73 us (4%)
  other arithmetic  4 us (2%)
    pallas_call x16, Pallas kernels, on_core(): pl.pallas_call(kernel, out_shape=shapes, in_specs=specs, out_specs=[FAR_S...  52.9 us
    ppermute x17, starting transfers between devices, swap_z(): return lax.ppermute(value, 'uly', [(i, i ^ shift) for i in range(4)])  29.5 us
    ppermute x17, waiting for transfers between devices, swap_z(): return lax.ppermute(value, 'uly', [(i, i ^ shift) for i in range(4)])  26.6 us
    all_gather x1, blocking collectives, local_fast(): lax.all_gather(attn_pack.reshape(2, 4, 128, 128)[:, :3], 'uly', axis=0)  22.6 us
    all_gather x1, blocking collectives, local_fast(): w_qkv = lax.all_gather(qkv_shard, 'blk', axis=0)  12.3 us
    ppermute x8, waiting for transfers between devices, swap_blk(): return lax.ppermute(value, 'blk', [(i, i ^ mask) for i in range(8)])  9.99 us
    ppermute x1, waiting for transfers between devices, local_fast(): down_shard = lax.ppermute(down_weight, ('blk', 'uly'), DOWN_MOVES)  8.99 us
    unnamed x82, local copies, waits for them, and re-layouts  8.19 us
  transfers between devices with their start and end apart: 35, of which 16 were waited for; matrix products, arithmetic and copies ran while one was open for 3% of the time, Pallas kernels for 15%

profile of v5, /device:TPU:4, one launch (start us, length us, event | category | flops | bytes accessed | tf_op | source)
XLA Modules:
  0.0 239.7 jit_solution(5803527473440003446)
XLA Ops:
  8.5 2.4 send_kernel.1
  10.9 1.6 collective-permute-start.4
  12.5 2.6 %collective-permute-start.5 = (bf16[208,192]{1,0:T(8,128)(2,1)}, bf16[208,192]{1,0:T(8,128)(2,1)S(1)}, u32[]{:S(2)}, u32[]{:S(2)}) collective-permute-start(bf16[208,192]{1,0:T(8,128)(2,1)} %get-tuple-element.89), channel_id=1, source_target_pairs={{0,2},{1,3},{2,0},{3,1},{4,6},{5,7},{6,4},{7,5},{8,10},{9,11},{10,... | collective-permute-start | bytes 239624 | tf_op jit(solution)/shard_map/ppermute | solution.py:961
  15.9 1.1 pad_maximum_fusion
  17.0 3.7 %collective-permute-start.3 = (bf16[160,768]{1,0:T(8,128)(2,1)S(1)}, bf16[160,768]{1,0:T(8,128)(2,1)S(1)}, u32[]{:S(2)}, u32[]{:S(2)}) collective-permute-start(bf16[160,768]{1,0:T(8,128)(2,1)S(1)} %pad_maximum_fusion), channel_id=1, source_target_pairs={{0,3},{1,2},{2,1},{3,0},{4,7},{5,6},{6,5},{7,4},{8,11},{9,10},{10,... | collective-permute-start | bytes 737288 | tf_op jit(solution)/shard_map/ppermute | solution.py:961
  21.3 1.1 copy.23
  22.4 1.9 collective-permute-start
  24.3 0.8 collective-permute-done.5.got_two
  26.5 12.3 %all-gather = bf16[768,640]{1,0:T(8,128)(2,1)S(1)} all-gather(bf16[96,640]{1,0:T(8,128)(2,1)S(1)} %shard_kernel.1), channel_id=2, replica_groups=mesh['blk'=8,'uly'=4] {'blk'}, dimensions={0}, use_global_device_ids=true | all-gather | bytes 1105920 | tf_op jit(solution)/shard_map/all_gather | solution.py:1030
  38.8 9.0 %collective-permute-done.down = bf16[384,192]{1,0:T(8,128)(2,1)S(1)} collective-permute-done((bf16[384,192]{1,0:T(8,128)(2,1)S(1)}, bf16[384,192]{1,0:T(8,128)(2,1)S(1)}, u32[]{:S(2)}, u32[]{:S(2)}) %collective-permute-start) | collective-permute-done | bytes 147488 | tf_op jit(solution)/shard_map/ppermute | solution.py:1031
  47.8 3.0 %first_kernel.1 = (bf16[8,400,128]{2,1,0:T(8,128)(2,1)}, bf16[512,768]{1,0:T(8,128)(2,1)S(1)}, bf16[2,4,64,768]{3,2,1,0:T(8,128)(2,1)S(1)}, f32[8,768]{1,0:T(8,128)S(1)}) custom-call(s32[2]{0:T(128)S(1)} %copy-done.17, bf16[2,64,768]{2,1,0:T(8,128)(2,1)S(1)} %copy-done.1, bf16[2,64,768]{2,1,0:T(8,128)(2,1)S(1)} %collective-permute-done.1.x1, ...), custom_call_target="tpu_custom_call" | custom-call | tf_op jit(solution)/shard_map/first_kernel/pallas_call | solution.py:948
  51.4 0.9 copy-done.20
  52.3 0.9 copy-done.21
  53.2 3.6 %all-to-all-start = ((bf16[8,400,128]{2,1,0:T(8,128)(2,1)}), bf16[8,400,128]{2,1,0:T(8,128)(2,1)S(1)}, u32[]{:S(2)}, u32[]{:S(2)}) async-start(bf16[8,400,128]{2,1,0:T(8,128)(2,1)} %get-tuple-element.92), calls=%async_computation | async-start | bytes 1638400 | tf_op jit(solution)/shard_map/all_to_all | solution.py:1049
  56.9 3.5 %collective-permute-start.6 = (bf16[2,64,768]{2,1,0:T(8,128)(2,1)S(1)}, bf16[2,64,768]{2,1,0:T(8,128)(2,1)S(1)}, u32[]{:S(2)}, u32[]{:S(2)}) collective-permute-start(bf16[2,64,768]{2,1,0:T(8,128)(2,1)S(1)} %copy-done.24), channel_id=1, source_target_pairs={{0,3},{1,2},{2,1},{3,0},{4,7},{5,6},{6,5},{7,4},{8,11},{9,10},{10,... | collective-permute-start | bytes 589832 | tf_op jit(solution)/shard_map/ppermute | solution.py:961
  60.4 0.8 weights_kernel.1
  61.2 4.3 %collective-permute-done.6.g3 = bf16[2,64,768]{2,1,0:T(8,128)(2,1)S(1)} collective-permute-done((bf16[2,64,768]{2,1,0:T(8,128)(2,1)S(1)}, bf16[2,64,768]{2,1,0:T(8,128)(2,1)S(1)}, u32[]{:S(2)}, u32[]{:S(2)}) %collective-permute-start.6) | collective-permute-done | bytes 196640 | tf_op jit(solution)/shard_map/ppermute | solution.py:961
  65.6 2.5 %all-to-all-done.pack = bf16[8,400,128]{2,1,0:T(8,128)(2,1)S(1)} async-done(((bf16[8,400,128]{2,1,0:T(8,128)(2,1)}), bf16[8,400,128]{2,1,0:T(8,128)(2,1)S(1)}, u32[]{:S(2)}, u32[]{:S(2)}) %all-to-all-start) | async-done | bytes 819232 | tf_op jit(solution)/shard_map/all_to_all | solution.py:1049
  68.1 5.3 %attn_forward_kernel.1 = (bf16[8,128,128]{2,1,0:T(8,128)(2,1)}, f32[64,2048]{1,0:T(8,128)S(1)}, f32[1,2048]{1,0:T(1,128)S(1)}) custom-call(bf16[8,400,128]{2,1,0:T(8,128)(2,1)S(1)} %all-to-all-done.pack), custom_call_target="tpu_custom_call" | custom-call | tf_op jit(solution)/shard_map/attn_forward_kernel/pallas_call | solution.py:948
  73.5 4.8 %all-to-all-start.1 = ((bf16[8,128,128]{2,1,0:T(8,128)(2,1)}), bf16[8,128,128]{2,1,0:T(8,128)(2,1)S(1)}, u32[]{:S(2)}, u32[]{:S(2)}) async-start(bf16[8,128,128]{2,1,0:T(8,128)(2,1)} %get-tuple-element.96), calls=%async_computation.1 | async-start | bytes 524288 | tf_op jit(solution)/shard_map/all_to_all | solution.py:1062
  78.3 1.4 collective-permute-start.7
  79.7 2.5 %collective-permute-start.8 = (bf16[2,64,768]{2,1,0:T(8,128)(2,1)S(1)}, bf16[2,64,768]{2,1,0:T(8,128)(2,1)S(1)}, u32[]{:S(2)}, u32[]{:S(2)}) collective-permute-start(bf16[2,64,768]{2,1,0:T(8,128)(2,1)S(1)} %copy-done.24), channel_id=1, source_target_pairs={{0,2},{1,3},{2,0},{3,1},{4,6},{5,7},{6,4},{7,5},{8,10},{9,11},{10,... | collective-permute-start | bytes 589832 | tf_op jit(solution)/shard_map/ppermute | solution.py:961
  82.3 1.6 all-to-all-done.1
  83.9 22.6 %all-gather.1 = bf16[8,3,128,128]{3,2,1,0:T(8,128)(2,1)} all-gather(bf16[2,3,128,128]{3,2,1,0:T(8,128)(2,1)S(1)} %slice.20), channel_id=3, replica_groups=mesh['blk'=8,'uly'=4] {'uly'}, dimensions={0}, use_global_device_ids=true | all-gather | bytes 983040 | tf_op jit(solution)/shard_map/all_gather | solution.py:1068
  107.2 9.1 %middle_kernel.1 = (bf16[2,64,768]{2,1,0:T(8,128)(2,1)}, bf16[2,64,768]{2,1,0:T(8,128)(2,1)}, bf16[2,64,768]{2,1,0:T(8,128)(2,1)}, bf16[2,64,768]{2,1,0:T(8,128)...) custom-call(s32[2]{0:T(128)} %pad_add_fusion.place, ...), custom_call_target="tpu_custom_call" | custom-call | flops 5000000000 | tf_op jit(solution)/shard_map/middle_kernel/pallas_call | solution.py:948
  116.3 6.4 %feed_grads_kernel.1 = (bf16[2,256,768]{2,1,0:T(8,128)(2,1)}, bf16[4,2,96,768]{3,2,1,0:T(8,128)(2,1)}, bf16[4,2,96,768]{3,2,1,0:T(8,128)(2,1)}) custom-call(s32[2]{0:T(128)} %pad_add_fusion.place, bf16[512,768]{1,0:T(8,128)(2,1)} %get-tuple-element.105.normed, bf16[512,768]{1,0:T(8,128)(2,1)} %get-tuple-element.106.act, ...), custom_call_target="tpu_custom_call" | custom-call | flops 4000000000 | tf_op jit(solution)/shard_map/feed_grads_kernel/pallas_call | solution.py:948
  122.8 0.9 collective-permute-start.9
  123.7 1.2 collective-permute-start.10
  124.9 2.4 collective-permute-start.11
  127.2 5.9 %collective-permute-done.9.g1 = bf16[2,64,768]{2,1,0:T(8,128)(2,1)S(1)} collective-permute-done((bf16[2,64,768]{2,1,0:T(8,128)(2,1)S(1)}, bf16[2,64,768]{2,1,0:T(8,128)(2,1)S(1)}, u32[]{:S(2)}, u32[]{:S(2)}) %collective-permute-start.9) | collective-permute-done | bytes 196640 | tf_op jit(solution)/shard_map/ppermute | solution.py:961
  133.2 7.6 %collective-permute-done.10.g2 = bf16[2,64,768]{2,1,0:T(8,128)(2,1)S(1)} collective-permute-done((bf16[2,64,768]{2,1,0:T(8,128)(2,1)S(1)}, bf16[2,64,768]{2,1,0:T(8,128)(2,1)S(1)}, u32[]{:S(2)}, u32[]{:S(2)}) %collective-permute-start.10) | collective-permute-done | bytes 196640 | tf_op jit(solution)/shard_map/ppermute | solution.py:961
  141.5 4.2 %second_back_kernel.1 = (f32[2,64,768]{2,1,0:T(8,128)}, bf16[8,4,32,128]{3,2,1,0:T(8,128)(2,1)}, f32[8,768]{1,0:T(8,128)}, bf16[128,192]{1,0:T(8,128)(2,1)}, bf1...) custom-call(s32[2]{0:T(128)} %pad_add_fusion.place, ...), custom_call_target="tpu_custom_call" | custom-call | flops 2000000000 | tf_op jit(solution)/shard_map/second_back_kernel/pallas_call | solution.py:948
  145.7 6.4 %all-to-all-start.2 = ((bf16[32,32,128]{2,1,0:T(8,128)(2,1)}), bf16[32,32,128]{2,1,0:T(8,128)(2,1)S(1)}, u32[]{:S(2)}, u32[]{:S(2)}) async-start(bf16[32,32,128]{2,1,0:T(8,128)(2,1)} %bitcast.26), calls=%async_computation.2 | async-start | bytes 524288 | tf_op jit(solution)/shard_map/all_to_all | solution.py:1118
  152.1 2.2 chip_sum_kernel.2
  154.3 0.8 copy-done.4
  155.1 1.5 collective-permute-start.13
  157.1 1.5 collective-permute-start.15
  158.6 3.0 %all-to-all-done.2.grad = bf16[32,32,128]{2,1,0:T(8,128)(2,1)S(1)} async-done(((bf16[32,32,128]{2,1,0:T(8,128)(2,1)}), bf16[32,32,128]{2,1,0:T(8,128)(2,1)S(1)}, u32[]{:S(2)}, u32[]{:S(2)}) %all-to-all-start.2) | async-done | bytes 262176 | tf_op jit(solution)/shard_map/all_to_all | solution.py:1118
  161.6 7.5 %attn_backward_kernel.1 = bf16[8,384,128]{2,1,0:T(8,128)(2,1)} custom-call(bf16[8,400,128]{2,1,0:T(8,128)(2,1)S(1)} %all-to-all-done.pack, bf16[32,32,128]{2,1,0:T(8,128)(2,1)S(1)} %all-to-all-done.2.grad, f32[64,2048]{1,0:T(8,128)S(1)} %get-tuple-element.128.out_cols, f32[1,2048]{1,0:T(1,128)S(1)} %get-tuple-element.129.log_row), custom_call_target="tpu_custom_call" | custom-call | tf_op jit(solution)/shard_map/attn_backward_kernel/pallas_call | solution.py:948
  169.2 3.3 %collective-permute-done.14.from_y = bf16[2,96,768]{2,1,0:T(8,128)(2,1)S(1)} collective-permute-done((bf16[2,96,768]{2,1,0:T(8,128)(2,1)}, bf16[2,96,768]{2,1,0:T(8,128)(2,1)S(1)}, u32[]{:S(2)}, u32[]{:S(2)}) %collective-permute-start.14) | collective-permute-done | bytes 294944 | tf_op jit(solution)/shard_map/ppermute | solution.py:965
  172.5 4.2 %all-to-all-start.3 = ((bf16[8,384,128]{2,1,0:T(8,128)(2,1)}), bf16[8,384,128]{2,1,0:T(8,128)(2,1)S(1)}, u32[]{:S(2)}, u32[]{:S(2)}) async-start(bf16[8,384,128]{2,1,0:T(8,128)(2,1)} %attn_backward_kernel.1), calls=%async_computation.4 | async-start | bytes 1572864 | tf_op jit(solution)/shard_map/all_to_all | solution.py:1134
  177.4 1.5 collective-permute-start.16
  178.9 2.1 collective-permute-start.17
  181.0 0.8 collective-permute-start.18
  181.9 4.6 %collective-permute-done.17.a2 = bf16[128,192]{1,0:T(8,128)(2,1)S(1)} collective-permute-done((bf16[128,192]{1,0:T(8,128)(2,1)S(1)}, bf16[128,192]{1,0:T(8,128)(2,1)S(1)}, u32[]{:S(2)}, u32[]{:S(2)}) %collective-permute-start.17) | collective-permute-done | bytes 49184 | tf_op jit(solution)/shard_map/ppermute | solution.py:961
  186.4 0.7 collective-permute-done.18.a3
  187.8 0.9 copy-done.22
  188.7 6.6 %last_kernel.1 = (bf16[4,2,64,768]{3,2,1,0:T(8,128)(2,1)}, bf16[4,96,832]{2,1,0:T(8,128)(2,1)}, bf16[4,96,832]{2,1,0:T(8,128)(2,1)}) custom-call(s32[2]{0:T(128)} %pad_add_fusion.place, bf16[8,384,128]{2,1,0:T(8,128)(2,1)} %copy-done.22, bf16[8,96,640]{2,1,0:T(8,128)(2,1)} %bitcast.22, bf16[2,4,64,768]{3,2,1,0:T(8,128)(2,1)} %copy-done.21, ...), custom_call_target="tpu_custom_call" | custom-call | flops 3000000000 | tf_op jit(solution)/shard_map/last_kernel/pallas_call | solution.py:948
  195.4 4.4 %all-to-all-start.4 = ((bf16[4,2,64,768]{3,2,1,0:T(8,128)(2,1)}), bf16[4,2,64,768]{3,2,1,0:T(8,128)(2,1)S(1)}, u32[]{:S(2)}, u32[]{:S(2)}) async-start(bf16[4,2,64,768]{3,2,1,0:T(8,128)(2,1)} %get-tuple-element.141), calls=%async_computation.5 | async-start | bytes 1572864 | tf_op jit(solution)/shard_map/all_to_all | solution.py:1157
  200.6 1.4 collective-permute-start.21
  202.0 1.5 collective-permute-start.22
  203.5 0.9 join_ud_kernel.1
  204.4 2.8 %collective-permute-done.20.from_x = bf16[96,832]{1,0:T(8,128)(2,1)S(1)} collective-permute-done((bf16[96,832]{1,0:T(8,128)(2,1)S(1)}, bf16[96,832]{1,0:T(8,128)(2,1)S(1)}, u32[]{:S(2)}, u32[]{:S(2)}) %collective-permute-start.20) | collective-permute-done | bytes 159776 | tf_op jit(solution)/shard_map/ppermute | solution.py:965
  207.2 3.9 %collective-permute-done.22.from_xy = bf16[96,832]{1,0:T(8,128)(2,1)S(1)} collective-permute-done((bf16[96,832]{1,0:T(8,128)(2,1)S(1)}, bf16[96,832]{1,0:T(8,128)(2,1)S(1)}, u32[]{:S(2)}, u32[]{:S(2)}) %collective-permute-start.22) | collective-permute-done | bytes 159776 | tf_op jit(solution)/shard_map/ppermute | solution.py:965
  211.1 1.3 join_tail_kernel.1
  212.4 3.5 %collective-permute-start.25 = (f32[8,96]{1,0:T(8,128)S(1)}, f32[8,96]{1,0:T(8,128)S(1)}, u32[]{:S(2)}, u32[]{:S(2)}) collective-permute-start(f32[8,96]{1,0:T(8,128)S(1)} %get-tuple-element.153), channel_id=1, source_target_pairs={{0,3},{1,2},{2,1},{3,0},{4,7},{5,6},{6,5},{7,4},{8,11},{9,10},{10,... | collective-permute-start | bytes 9224 | tf_op jit(solution)/shard_map/ppermute | solution.py:961
  215.9 0.8 collective-permute-start.23
  216.8 1.6 add_convert_fusion
  218.4 4.2 %collective-permute-start.26 = (bf16[384,192]{1,0:T(8,128)(2,1)S(1)}, bf16[384,192]{1,0:T(8,128)(2,1)S(1)}, u32[]{:S(2)}, u32[]{:S(2)}) collective-permute-start(bf16[384,192]{1,0:T(8,128)(2,1)S(1)} %get-tuple-element.163), channel_id=1, source_target_pairs={{0,0},{8,1},{16,2},{24,3},{4,4},{12,5},{20,6},{28,7},{9,8},{1,9},{... | collective-permute-start | bytes 442376 | tf_op jit(solution)/shard_map/ppermute | solution.py:1164
  222.7 2.6 %collective-permute-done.24.got_two = bf16[96,256]{1,0:T(8,128)(2,1)S(1)} collective-permute-done((bf16[96,256]{1,0:T(8,128)(2,1)S(1)}, bf16[96,256]{1,0:T(8,128)(2,1)S(1)}, u32[]{:S(2)}, u32[]{:S(2)}) %collective-permute-start.24) | collective-permute-done | bytes 49184 | tf_op jit(solution)/shard_map/ppermute | solution.py:961
  225.3 1.3 finish_tail_kernel.1
  227.1 4.1 %collective-permute-done.26 = bf16[384,192]{1,0:T(8,128)(2,1)S(1)} collective-permute-done((bf16[384,192]{1,0:T(8,128)(2,1)S(1)}, bf16[384,192]{1,0:T(8,128)(2,1)S(1)}, u32[]{:S(2)}, u32[]{:S(2)}) %collective-permute-start.26) | collective-permute-done | bytes 147488 | tf_op jit(solution)/shard_map/ppermute | solution.py:1164
  231.2 0.8 copy.24
  232.0 1.1 finish_rows_kernel.1
  (115 shorter events, 9.8 us)
Async XLA Ops:
  7.2 17.9 %copy-start.6 = (bf16[96,576]{1,0:T(8,128)(2,1)S(1)}, bf16[96,576]{1,0:T(8,128)(2,1)}, u32[]{:S(2)}) copy-start(bf16[96,576]{1,0:T(8,128)(2,1)} %weight.1) | copy-start | bytes 331780
  7.2 99.3 %all-gather.9.cloned.1.call-start = ((), (), s32[]{:S(2)}) async-start(), calls=%async_computation.8 | async-start | bytes 1327104 | tf_op jit(solution)/shard_map/all_gather | solution.py:1048
  10.9 11.5 %collective-permute-start.4 = (bf16[208,192]{1,0:T(8,128)(2,1)}, bf16[208,192]{1,0:T(8,128)(2,1)S(1)}, u32[]{:S(2)}, u32[]{:S(2)}) collective-permute-start(bf16[208,192]{1,0:T(8,128)(2,1)} %get-tuple-element.88), channel_id=1, source_target_pairs={{0,1},{1,0},{2,3},{3,2},{4,5},{5,4},{6,7},{7,6},{8,9},{9,8},{10,11... | collective-permute-start | bytes 239624 | tf_op jit(solution)/shard_map/ppermute | solution.py:961
  12.5 12.6 %collective-permute-start.5 = (bf16[208,192]{1,0:T(8,128)(2,1)}, bf16[208,192]{1,0:T(8,128)(2,1)S(1)}, u32[]{:S(2)}, u32[]{:S(2)}) collective-permute-start(bf16[208,192]{1,0:T(8,128)(2,1)} %get-tuple-element.89), channel_id=1, source_target_pairs={{0,2},{1,3},{2,0},{3,1},{4,6},{5,7},{6,4},{7,5},{8,10},{9,11},{10,... | collective-permute-start | bytes 239624 | tf_op jit(solution)/shard_map/ppermute | solution.py:961
  15.1 32.7 %collective-permute-start.2 = (bf16[2,64,768]{2,1,0:T(8,128)(2,1)}, bf16[2,64,768]{2,1,0:T(8,128)(2,1)S(1)}, u32[]{:S(2)}, u32[]{:S(2)}) collective-permute-start(bf16[2,64,768]{2,1,0:T(8,128)(2,1)} %inputs.1), channel_id=1, source_target_pairs={{0,2},{1,3},{2,0},{3,1},{4,6},{5,7},{6,4},{7,5},{8,10},{9,11},{10,... | collective-permute-start | bytes 589832 | tf_op jit(solution)/shard_map/ppermute | solution.py:961
  15.5 32.3 %collective-permute-start.1 = (bf16[2,64,768]{2,1,0:T(8,128)(2,1)}, bf16[2,64,768]{2,1,0:T(8,128)(2,1)S(1)}, u32[]{:S(2)}, u32[]{:S(2)}) collective-permute-start(bf16[2,64,768]{2,1,0:T(8,128)(2,1)} %inputs.1), channel_id=1, source_target_pairs={{0,1},{1,0},{2,3},{3,2},{4,5},{5,4},{6,7},{7,6},{8,9},{9,8},{10,11... | collective-permute-start | bytes 589832 | tf_op jit(solution)/shard_map/ppermute | solution.py:961
  15.9 31.9 %copy-start.1 = (bf16[2,64,768]{2,1,0:T(8,128)(2,1)S(1)}, bf16[2,64,768]{2,1,0:T(8,128)(2,1)}, u32[]{:S(2)}) copy-start(bf16[2,64,768]{2,1,0:T(8,128)(2,1)} %inputs.1) | copy-start | bytes 589828
  15.9 31.9 %copy-start.19 = (s32[2,64]{1,0:T(2,128)S(1)}, s32[2,64]{1,0:T(2,128)}, u32[]{:S(2)}) copy-start(s32[2,64]{1,0:T(2,128)} %doc_starts.1) | copy-start | bytes 1540
  17.0 30.8 %collective-permute-start.3 = (bf16[160,768]{1,0:T(8,128)(2,1)S(1)}, bf16[160,768]{1,0:T(8,128)(2,1)S(1)}, u32[]{:S(2)}, u32[]{:S(2)}) collective-permute-start(bf16[160,768]{1,0:T(8,128)(2,1)S(1)} %pad_maximum_fusion), channel_id=1, source_target_pairs={{0,3},{1,2},{2,1},{3,0},{4,7},{5,6},{6,5},{7,4},{8,11},{9,10},{10,... | collective-permute-start | bytes 737288 | tf_op jit(solution)/shard_map/ppermute | solution.py:961
  22.4 25.4 %collective-permute-start = (bf16[384,192]{1,0:T(8,128)(2,1)S(1)}, bf16[384,192]{1,0:T(8,128)(2,1)S(1)}, u32[]{:S(2)}, u32[]{:S(2)}) collective-permute-start(bf16[384,192]{1,0:T(8,128)(2,1)S(1)} %copy.23), channel_id=1, source_target_pairs={{0,0},{1,8},{2,16},{3,24},{4,4},{5,12},{6,20},{7,28},{8,9},{9,1},{... | collective-permute-start | bytes 442376 | tf_op jit(solution)/shard_map/ppermute | solution.py:1031
  38.8 14.4 %copy-start = (bf16[768,640]{1,0:T(8,128)(2,1)}, bf16[768,640]{1,0:T(8,128)(2,1)S(1)}, u32[]{:S(2)}) copy-start(bf16[768,640]{1,0:T(8,128)(2,1)S(1)} %all-gather) | copy-start | bytes 2949124
  53.2 3.7 %copy-start.24 = (bf16[2,64,768]{2,1,0:T(8,128)(2,1)S(1)}, bf16[2,64,768]{2,1,0:T(8,128)(2,1)}, u32[]{:S(2)}) copy-start(bf16[2,64,768]{2,1,0:T(8,128)(2,1)} %out_grad.1) | copy-start | bytes 589828
  53.2 7.2 %copy-start.14 = (bf16[96,192]{1,0:T(8,128)(2,1)S(1)}, bf16[96,192]{1,0:T(8,128)(2,1)}, u32[]{:S(2)}) copy-start(bf16[96,192]{1,0:T(8,128)(2,1)} %out_weight.1) | copy-start | bytes 110596
  53.2 14.9 %all-to-all-start = ((bf16[8,400,128]{2,1,0:T(8,128)(2,1)}), bf16[8,400,128]{2,1,0:T(8,128)(2,1)S(1)}, u32[]{:S(2)}, u32[]{:S(2)}) async-start(bf16[8,400,128]{2,1,0:T(8,128)(2,1)} %get-tuple-element.92), calls=%async_computation | async-start | bytes 1638400 | tf_op jit(solution)/shard_map/all_to_all | solution.py:1049
  56.9 49.7 %all-gather.7.cloned.1.call-start = ((), (), s32[]{:S(2)}) async-start(), calls=%async_computation.7 | async-start | bytes 2654208 | tf_op jit(solution)/shard_map/all_gather | solution.py:1061
  56.9 8.7 %collective-permute-start.6 = (bf16[2,64,768]{2,1,0:T(8,128)(2,1)S(1)}, bf16[2,64,768]{2,1,0:T(8,128)(2,1)S(1)}, u32[]{:S(2)}, u32[]{:S(2)}) collective-permute-start(bf16[2,64,768]{2,1,0:T(8,128)(2,1)S(1)} %copy-done.24), channel_id=1, source_target_pairs={{0,3},{1,2},{2,1},{3,0},{4,7},{5,6},{6,5},{7,4},{8,11},{9,10},{10,... | collective-permute-start | bytes 589832 | tf_op jit(solution)/shard_map/ppermute | solution.py:961
  65.6 40.9 %copy-start.25 = (bf16[2,64,768]{2,1,0:T(8,128)(2,1)}, bf16[2,64,768]{2,1,0:T(8,128)(2,1)S(1)}, u32[]{:S(2)}) copy-start(bf16[2,64,768]{2,1,0:T(8,128)(2,1)S(1)} %collective-permute-done.6.g3) | copy-start | bytes 589828
  73.5 10.4 %all-to-all-start.1 = ((bf16[8,128,128]{2,1,0:T(8,128)(2,1)}), bf16[8,128,128]{2,1,0:T(8,128)(2,1)S(1)}, u32[]{:S(2)}, u32[]{:S(2)}) async-start(bf16[8,128,128]{2,1,0:T(8,128)(2,1)} %get-tuple-element.96), calls=%async_computation.1 | async-start | bytes 524288 | tf_op jit(solution)/shard_map/all_to_all | solution.py:1062
  78.3 28.2 %collective-permute-start.7 = (bf16[2,64,768]{2,1,0:T(8,128)(2,1)S(1)}, bf16[2,64,768]{2,1,0:T(8,128)(2,1)S(1)}, u32[]{:S(2)}, u32[]{:S(2)}) collective-permute-start(bf16[2,64,768]{2,1,0:T(8,128)(2,1)S(1)} %copy-done.24), channel_id=1, source_target_pairs={{0,1},{1,0},{2,3},{3,2},{4,5},{5,4},{6,7},{7,6},{8,9},{9,8},{10,11... | collective-permute-start | bytes 589832 | tf_op jit(solution)/shard_map/ppermute | solution.py:961
  79.7 26.7 %collective-permute-start.8 = (bf16[2,64,768]{2,1,0:T(8,128)(2,1)S(1)}, bf16[2,64,768]{2,1,0:T(8,128)(2,1)S(1)}, u32[]{:S(2)}, u32[]{:S(2)}) collective-permute-start(bf16[2,64,768]{2,1,0:T(8,128)(2,1)S(1)} %copy-done.24), channel_id=1, source_target_pairs={{0,2},{1,3},{2,0},{3,1},{4,6},{5,7},{6,4},{7,5},{8,10},{9,11},{10,... | collective-permute-start | bytes 589832 | tf_op jit(solution)/shard_map/ppermute | solution.py:961
  116.3 6.5 %copy-start.30 = (bf16[2,64,768]{2,1,0:T(8,128)(2,1)S(1)}, bf16[2,64,768]{2,1,0:T(8,128)(2,1)}, u32[]{:S(2)}) copy-start(bf16[2,64,768]{2,1,0:T(8,128)(2,1)} %get-tuple-element.115) | copy-start | bytes 589828
  116.3 7.4 %copy-start.28 = (bf16[2,64,768]{2,1,0:T(8,128)(2,1)S(1)}, bf16[2,64,768]{2,1,0:T(8,128)(2,1)}, u32[]{:S(2)}) copy-start(bf16[2,64,768]{2,1,0:T(8,128)(2,1)} %get-tuple-element.116) | copy-start | bytes 589828
  116.3 8.5 %copy-start.26 = (bf16[2,64,768]{2,1,0:T(8,128)(2,1)S(1)}, bf16[2,64,768]{2,1,0:T(8,128)(2,1)}, u32[]{:S(2)}) copy-start(bf16[2,64,768]{2,1,0:T(8,128)(2,1)} %get-tuple-element.117) | copy-start | bytes 589828
  122.7 29.4 %collective-permute-start.12 = (bf16[4,2,96,768]{3,2,1,0:T(8,128)(2,1)}, bf16[4,2,96,768]{3,2,1,0:T(8,128)(2,1)}, u32[]{:S(2)}, u32[]{:S(2)}) collective-permute-start(bf16[4,2,96,768]{3,2,1,0:T(8,128)(2,1)} %get-tuple-element.122), channel_id=1, source_target_pairs={{0,4},{4,0},{8,12},{12,8},{16,20},{20,16},{24,28},{28,24},{1,5},{5... | collective-permute-start | bytes 3538952 | tf_op jit(solution)/shard_map/ppermute | solution.py:965
  122.8 10.4 %collective-permute-start.9 = (bf16[2,64,768]{2,1,0:T(8,128)(2,1)S(1)}, bf16[2,64,768]{2,1,0:T(8,128)(2,1)S(1)}, u32[]{:S(2)}, u32[]{:S(2)}) collective-permute-start(bf16[2,64,768]{2,1,0:T(8,128)(2,1)S(1)} %copy-done.30), channel_id=1, source_target_pairs={{0,1},{1,0},{2,3},{3,2},{4,5},{5,4},{6,7},{7,6},{8,9},{9,8},{10,11... | collective-permute-start | bytes 589832 | tf_op jit(solution)/shard_map/ppermute | solution.py:961
  123.7 17.1 %collective-permute-start.10 = (bf16[2,64,768]{2,1,0:T(8,128)(2,1)S(1)}, bf16[2,64,768]{2,1,0:T(8,128)(2,1)S(1)}, u32[]{:S(2)}, u32[]{:S(2)}) collective-permute-start(bf16[2,64,768]{2,1,0:T(8,128)(2,1)S(1)} %copy-done.28), channel_id=1, source_target_pairs={{0,2},{1,3},{2,0},{3,1},{4,6},{5,7},{6,4},{7,5},{8,10},{9,11},{10,... | collective-permute-start | bytes 589832 | tf_op jit(solution)/shard_map/ppermute | solution.py:961
  124.9 15.9 %collective-permute-start.11 = (bf16[2,64,768]{2,1,0:T(8,128)(2,1)S(1)}, bf16[2,64,768]{2,1,0:T(8,128)(2,1)S(1)}, u32[]{:S(2)}, u32[]{:S(2)}) collective-permute-start(bf16[2,64,768]{2,1,0:T(8,128)(2,1)S(1)} %copy-done.26), channel_id=1, source_target_pairs={{0,3},{1,2},{2,1},{3,0},{4,7},{5,6},{6,5},{7,4},{8,11},{9,10},{10,... | collective-permute-start | bytes 589832 | tf_op jit(solution)/shard_map/ppermute | solution.py:961
  133.2 7.6 %copy-start.31 = (bf16[2,64,768]{2,1,0:T(8,128)(2,1)}, bf16[2,64,768]{2,1,0:T(8,128)(2,1)S(1)}, u32[]{:S(2)}) copy-start(bf16[2,64,768]{2,1,0:T(8,128)(2,1)S(1)} %collective-permute-done.9.g1) | copy-start | bytes 589828
  141.5 10.6 %copy-start.2 = (bf16[4,2,96,768]{3,2,1,0:T(8,128)(2,1)S(1)}, bf16[4,2,96,768]{3,2,1,0:T(8,128)(2,1)}, u32[]{:S(2)}) copy-start(bf16[4,2,96,768]{3,2,1,0:T(8,128)(2,1)} %get-tuple-element.121.keep) | copy-start | bytes 3538948
  145.7 15.9 %all-to-all-start.2 = ((bf16[32,32,128]{2,1,0:T(8,128)(2,1)}), bf16[32,32,128]{2,1,0:T(8,128)(2,1)S(1)}, u32[]{:S(2)}, u32[]{:S(2)}) async-start(bf16[32,32,128]{2,1,0:T(8,128)(2,1)} %bitcast.26), calls=%async_computation.2 | async-start | bytes 524288 | tf_op jit(solution)/shard_map/all_to_all | solution.py:1118
  155.1 14.0 %collective-permute-start.13 = (bf16[2,96,768]{2,1,0:T(8,128)(2,1)}, bf16[2,96,768]{2,1,0:T(8,128)(2,1)S(1)}, u32[]{:S(2)}, u32[]{:S(2)}) collective-permute-start(bf16[2,96,768]{2,1,0:T(8,128)(2,1)} %get-tuple-element.124), channel_id=1, source_target_pairs={{0,8},{4,12},{8,0},{12,4},{16,24},{20,28},{24,16},{28,20},{1,9},{5... | collective-permute-start | bytes 884744 | tf_op jit(solution)/shard_map/ppermute | solution.py:965
  156.6 15.9 %collective-permute-start.14 = (bf16[2,96,768]{2,1,0:T(8,128)(2,1)}, bf16[2,96,768]{2,1,0:T(8,128)(2,1)S(1)}, u32[]{:S(2)}, u32[]{:S(2)}) collective-permute-start(bf16[2,96,768]{2,1,0:T(8,128)(2,1)} %get-tuple-element.125), channel_id=1, source_target_pairs={{0,16},{4,20},{8,24},{12,28},{16,0},{20,4},{24,8},{28,12},{1,17},{... | collective-permute-start | bytes 884744 | tf_op jit(solution)/shard_map/ppermute | solution.py:965
  157.1 15.3 %collective-permute-start.15 = (bf16[2,96,768]{2,1,0:T(8,128)(2,1)S(1)}, bf16[2,96,768]{2,1,0:T(8,128)(2,1)S(1)}, u32[]{:S(2)}, u32[]{:S(2)}) collective-permute-start(bf16[2,96,768]{2,1,0:T(8,128)(2,1)S(1)} %get-tuple-element.126), channel_id=1, source_target_pairs={{0,24},{4,28},{8,16},{12,20},{16,8},{20,12},{24,0},{28,4},{1,25},{... | collective-permute-start | bytes 884744 | tf_op jit(solution)/shard_map/ppermute | solution.py:965
  169.1 8.2 %copy-start.36 = (bf16[128,192]{1,0:T(8,128)(2,1)S(1)}, bf16[128,192]{1,0:T(8,128)(2,1)}, u32[]{:S(2)}) copy-start(bf16[128,192]{1,0:T(8,128)(2,1)} %get-tuple-element.136) | copy-start | bytes 147460
  169.1 9.7 %copy-start.35 = (bf16[128,192]{1,0:T(8,128)(2,1)S(1)}, bf16[128,192]{1,0:T(8,128)(2,1)}, u32[]{:S(2)}) copy-start(bf16[128,192]{1,0:T(8,128)(2,1)} %get-tuple-element.138) | copy-start | bytes 147460
  169.1 11.9 %copy-start.34 = (bf16[128,192]{1,0:T(8,128)(2,1)S(1)}, bf16[128,192]{1,0:T(8,128)(2,1)}, u32[]{:S(2)}) copy-start(bf16[128,192]{1,0:T(8,128)(2,1)} %get-tuple-element.140) | copy-start | bytes 147460
  169.2 8.2 %copy-start.8 = (bf16[2,96,768]{2,1,0:T(8,128)(2,1)}, bf16[2,96,768]{2,1,0:T(8,128)(2,1)S(1)}, u32[]{:S(2)}) copy-start(bf16[2,96,768]{2,1,0:T(8,128)(2,1)S(1)} %collective-permute-done.13.from_x) | copy-start | bytes 884740
  172.4 4.9 %copy-start.10 = (bf16[2,96,768]{2,1,0:T(8,128)(2,1)}, bf16[2,96,768]{2,1,0:T(8,128)(2,1)S(1)}, u32[]{:S(2)}) copy-start(bf16[2,96,768]{2,1,0:T(8,128)(2,1)S(1)} %collective-permute-done.14.from_y) | copy-start | bytes 884740
  172.5 4.9 %copy-start.12 = (bf16[2,96,768]{2,1,0:T(8,128)(2,1)}, bf16[2,96,768]{2,1,0:T(8,128)(2,1)S(1)}, u32[]{:S(2)}) copy-start(bf16[2,96,768]{2,1,0:T(8,128)(2,1)S(1)} %collective-permute-done.15.from_xy) | copy-start | bytes 884740
  172.5 15.3 %all-to-all-start.3 = ((bf16[8,384,128]{2,1,0:T(8,128)(2,1)}), bf16[8,384,128]{2,1,0:T(8,128)(2,1)S(1)}, u32[]{:S(2)}, u32[]{:S(2)}) async-start(bf16[8,384,128]{2,1,0:T(8,128)(2,1)} %attn_backward_kernel.1), calls=%async_computation.4 | async-start | bytes 1572864 | tf_op jit(solution)/shard_map/all_to_all | solution.py:1134
  176.6 40.1 %reduce-scatter.2.cloned.1.call-start = ((), (), s32[]{:S(2)}) async-start(), calls=%async_computation.6 | async-start | bytes 983040 | tf_op jit(solution)/shard_map/reduce_scatter | solution.py:1119
  177.4 4.5 %collective-permute-start.16 = (bf16[128,192]{1,0:T(8,128)(2,1)S(1)}, bf16[128,192]{1,0:T(8,128)(2,1)S(1)}, u32[]{:S(2)}, u32[]{:S(2)}) collective-permute-start(bf16[128,192]{1,0:T(8,128)(2,1)S(1)} %copy-done.36), channel_id=1, source_target_pairs={{0,1},{1,0},{2,3},{3,2},{4,5},{5,4},{6,7},{7,6},{8,9},{9,8},{10,11... | collective-permute-start | bytes 147464 | tf_op jit(solution)/shard_map/ppermute | solution.py:961
  178.9 7.6 %collective-permute-start.17 = (bf16[128,192]{1,0:T(8,128)(2,1)S(1)}, bf16[128,192]{1,0:T(8,128)(2,1)S(1)}, u32[]{:S(2)}, u32[]{:S(2)}) collective-permute-start(bf16[128,192]{1,0:T(8,128)(2,1)S(1)} %copy-done.35), channel_id=1, source_target_pairs={{0,2},{1,3},{2,0},{3,1},{4,6},{5,7},{6,4},{7,5},{8,10},{9,11},{10,... | collective-permute-start | bytes 147464 | tf_op jit(solution)/shard_map/ppermute | solution.py:961
  181.0 6.2 %collective-permute-start.18 = (bf16[128,192]{1,0:T(8,128)(2,1)S(1)}, bf16[128,192]{1,0:T(8,128)(2,1)S(1)}, u32[]{:S(2)}, u32[]{:S(2)}) collective-permute-start(bf16[128,192]{1,0:T(8,128)(2,1)S(1)} %copy-done.34), channel_id=1, source_target_pairs={{0,3},{1,2},{2,1},{3,0},{4,7},{5,6},{6,5},{7,4},{8,11},{9,10},{10,... | collective-permute-start | bytes 147464 | tf_op jit(solution)/shard_map/ppermute | solution.py:961
  181.9 5.9 %copy-start.37 = (bf16[128,192]{1,0:T(8,128)(2,1)}, bf16[128,192]{1,0:T(8,128)(2,1)S(1)}, u32[]{:S(2)}) copy-start(bf16[128,192]{1,0:T(8,128)(2,1)S(1)} %collective-permute-done.16.a1) | copy-start | bytes 147460
  186.4 1.3 copy-start.38
  195.2 4.5 %copy-start.3 = (bf16[4,96,832]{2,1,0:T(8,128)(2,1)S(1)}, bf16[4,96,832]{2,1,0:T(8,128)(2,1)}, u32[]{:S(2)}) copy-start(bf16[4,96,832]{2,1,0:T(8,128)(2,1)} %get-tuple-element.143.keep) | copy-start | bytes 1916932
  195.3 4.5 %collective-permute-start.19 = (bf16[4,96,832]{2,1,0:T(8,128)(2,1)}, bf16[4,96,832]{2,1,0:T(8,128)(2,1)S(1)}, u32[]{:S(2)}, u32[]{:S(2)}) collective-permute-start(bf16[4,96,832]{2,1,0:T(8,128)(2,1)} %get-tuple-element.144), channel_id=1, source_target_pairs={{0,4},{4,0},{8,12},{12,8},{16,20},{20,16},{24,28},{28,24},{1,5},{5... | collective-permute-start | bytes 1916936 | tf_op jit(solution)/shard_map/ppermute | solution.py:965
  195.3 8.2 %copy-start.5 = (f32[2,96,768]{2,1,0:T(8,128)S(1)}, f32[2,96,768]{2,1,0:T(8,128)}, u32[]{:S(2)}) copy-start(f32[2,96,768]{2,1,0:T(8,128)} %copy-done.4) | copy-start | bytes 1769476
  195.3 8.2 %copy-start.9 = (bf16[2,96,768]{2,1,0:T(8,128)(2,1)S(1)}, bf16[2,96,768]{2,1,0:T(8,128)(2,1)}, u32[]{:S(2)}) copy-start(bf16[2,96,768]{2,1,0:T(8,128)(2,1)} %copy-done.8) | copy-start | bytes 884740
  195.4 36.7 %all-to-all-start.4 = ((bf16[4,2,64,768]{3,2,1,0:T(8,128)(2,1)}), bf16[4,2,64,768]{3,2,1,0:T(8,128)(2,1)S(1)}, u32[]{:S(2)}, u32[]{:S(2)}) async-start(bf16[4,2,64,768]{3,2,1,0:T(8,128)(2,1)} %get-tuple-element.141), calls=%async_computation.5 | async-start | bytes 1572864 | tf_op jit(solution)/shard_map/all_to_all | solution.py:1157
  199.7 3.8 %copy-start.11 = (bf16[2,96,768]{2,1,0:T(8,128)(2,1)S(1)}, bf16[2,96,768]{2,1,0:T(8,128)(2,1)}, u32[]{:S(2)}) copy-start(bf16[2,96,768]{2,1,0:T(8,128)(2,1)} %copy-done.10) | copy-start | bytes 884740
  199.8 3.8 %copy-start.13 = (bf16[2,96,768]{2,1,0:T(8,128)(2,1)S(1)}, bf16[2,96,768]{2,1,0:T(8,128)(2,1)}, u32[]{:S(2)}) copy-start(bf16[2,96,768]{2,1,0:T(8,128)(2,1)} %copy-done.12) | copy-start | bytes 884740
  199.8 11.3 %copy-start.18 = (s32[2]{0:T(128)S(1)}, s32[2]{0:T(128)}, u32[]{:S(2)}) copy-start(s32[2]{0:T(128)} %pad_add_fusion.place) | copy-start | bytes 28
  199.9 16.8 %copy-start.23 = (f32[2,64,768]{2,1,0:T(8,128)S(1)}, f32[2,64,768]{2,1,0:T(8,128)}, u32[]{:S(2)}) copy-start(f32[2,64,768]{2,1,0:T(8,128)} %get-tuple-element.104.middle) | copy-start | bytes 1179652
  200.0 7.3 %collective-permute-start.20 = (bf16[96,832]{1,0:T(8,128)(2,1)S(1)}, bf16[96,832]{1,0:T(8,128)(2,1)S(1)}, u32[]{:S(2)}, u32[]{:S(2)}) collective-permute-start(bf16[96,832]{1,0:T(8,128)(2,1)S(1)} %get-tuple-element.146), channel_id=1, source_target_pairs={{0,8},{4,12},{8,0},{12,4},{16,24},{20,28},{24,16},{28,20},{1,9},{5... | collective-permute-start | bytes 479240 | tf_op jit(solution)/shard_map/ppermute | solution.py:965
  200.6 6.6 %collective-permute-start.21 = (bf16[96,832]{1,0:T(8,128)(2,1)S(1)}, bf16[96,832]{1,0:T(8,128)(2,1)S(1)}, u32[]{:S(2)}, u32[]{:S(2)}) collective-permute-start(bf16[96,832]{1,0:T(8,128)(2,1)S(1)} %get-tuple-element.147), channel_id=1, source_target_pairs={{0,16},{4,20},{8,24},{12,28},{16,0},{20,4},{24,8},{28,12},{1,17},{... | collective-permute-start | bytes 479240 | tf_op jit(solution)/shard_map/ppermute | solution.py:965
  202.0 9.1 %collective-permute-start.22 = (bf16[96,832]{1,0:T(8,128)(2,1)S(1)}, bf16[96,832]{1,0:T(8,128)(2,1)S(1)}, u32[]{:S(2)}, u32[]{:S(2)}) collective-permute-start(bf16[96,832]{1,0:T(8,128)(2,1)S(1)} %get-tuple-element.148), channel_id=1, source_target_pairs={{0,24},{4,28},{8,16},{12,20},{16,8},{20,12},{24,0},{28,4},{1,25},{... | collective-permute-start | bytes 479240 | tf_op jit(solution)/shard_map/ppermute | solution.py:965
  211.1 20.9 %copy-start.7 = (f32[2,64,768]{2,1,0:T(8,128)S(1)}, f32[2,64,768]{2,1,0:T(8,128)}, u32[]{:S(2)}) copy-start(f32[2,64,768]{2,1,0:T(8,128)} %get-tuple-element.142.grad_middle) | copy-start | bytes 1179652
  211.1 20.9 %copy-start.16 = (f32[8,768]{1,0:T(8,128)S(1)}, f32[8,768]{1,0:T(8,128)}, u32[]{:S(2)}) copy-start(f32[8,768]{1,0:T(8,128)} %copy-done.15) | copy-start | bytes 73732
  212.4 10.3 %collective-permute-start.25 = (f32[8,96]{1,0:T(8,128)S(1)}, f32[8,96]{1,0:T(8,128)S(1)}, u32[]{:S(2)}, u32[]{:S(2)}) collective-permute-start(f32[8,96]{1,0:T(8,128)S(1)} %get-tuple-element.153), channel_id=1, source_target_pairs={{0,3},{1,2},{2,1},{3,0},{4,7},{5,6},{6,5},{7,4},{8,11},{9,10},{10,... | collective-permute-start | bytes 9224 | tf_op jit(solution)/shard_map/ppermute | solution.py:961
  215.9 9.3 %collective-permute-start.24 = (bf16[96,256]{1,0:T(8,128)(2,1)S(1)}, bf16[96,256]{1,0:T(8,128)(2,1)S(1)}, u32[]{:S(2)}, u32[]{:S(2)}) collective-permute-start(bf16[96,256]{1,0:T(8,128)(2,1)S(1)} %get-tuple-element.152), channel_id=1, source_target_pairs={{0,2},{1,3},{2,0},{3,1},{4,6},{5,7},{6,4},{7,5},{8,10},{9,11},{10,... | collective-permute-start | bytes 147464 | tf_op jit(solution)/shard_map/ppermute | solution.py:961
  215.9 9.3 %collective-permute-start.23 = (bf16[96,256]{1,0:T(8,128)(2,1)S(1)}, bf16[96,256]{1,0:T(8,128)(2,1)S(1)}, u32[]{:S(2)}, u32[]{:S(2)}) collective-permute-start(bf16[96,256]{1,0:T(8,128)(2,1)S(1)} %get-tuple-element.151), channel_id=1, source_target_pairs={{0,1},{1,0},{2,3},{3,2},{4,5},{5,4},{6,7},{7,6},{8,9},{9,8},{10,11... | collective-permute-start | bytes 147464 | tf_op jit(solution)/shard_map/ppermute | solution.py:961
  218.4 12.8 %collective-permute-start.26 = (bf16[384,192]{1,0:T(8,128)(2,1)S(1)}, bf16[384,192]{1,0:T(8,128)(2,1)S(1)}, u32[]{:S(2)}, u32[]{:S(2)}) collective-permute-start(bf16[384,192]{1,0:T(8,128)(2,1)S(1)} %get-tuple-element.163), channel_id=1, source_target_pairs={{0,0},{8,1},{16,2},{24,3},{4,4},{12,5},{20,6},{28,7},{9,8},{1,9},{... | collective-permute-start | bytes 442376 | tf_op jit(solution)/shard_map/ppermute | solution.py:1164
  (11 other events, 8.2 us)
Sparse Core Ops, SparseCore 0:
  9.9 27.3 all-gather.8
  73.6 29.0 all-gather.6
  179.8 23.8 reduce-scatter.1
